TPU v7x, 128 devices: a whole 4x4x4 slice. The times are simulated.
128 devices in a mesh: slab: 16 (over z, x), level: 2 (over core), bottom: 4 (over y).
Axes of the slice: x: 4, y: 4, z: 4, core: 2. Of those that a mesh axis runs over, the one named last changes fastest.
Arguments:
- u_init: float32 [128, 32, 32, 128], P(('slab', 'level', 'bottom')), may hold values from -6 to 6
- source: float32 [128, 32, 32, 128], P(('slab', 'level', 'bottom')), may hold values from -10 to 13
- coeffs: float32 [128, 32, 32, 128], P(('slab', 'level', 'bottom')), may hold values from 0.01 to 1
- brick_map: int32 [16, 8], replicated, may hold values from 0 to 7, each once within a row
Outputs:
- solution: float32 [128, 32, 32, 128], P(('slab', 'level', 'bottom'))
Inputs may be any that keep to these rules, and one draw needn't show every extreme that they name: `brick_map`: each row is a permutation of 0 to 7.
All inputs are finite; a program needn't handle non-finite values.
Results may differ from a plain program's by a relative error of at most 0.0003.
Values sent between devices are 32-bit elements; how exact they have to be, the bound alone decides.
No kernel may reach another device: no remote copies, remote signals or barrier semaphores. Data moves between devices by JAX's collectives and lax.ppermute only.
A program may use at most 128 MiB of HBM per device.

v0:
```python
import jax
import jax.numpy as jnp
from jax import lax
from jax.sharding import PartitionSpec as P

SWEEPS_FINE = 2
SWEEPS_COARSE = 2
SWEEPS_BOTTOM = 8


def with_halo(cells, sides, width):
    for axis, dim in sides:
        count = lax.axis_size(axis)
        ends = count - 1
        head = lax.slice_in_dim(cells, 0, width, axis=dim)
        tail = lax.slice_in_dim(cells, cells.shape[dim] - width, cells.shape[dim], axis=dim)
        cells = jnp.concatenate(
            [
                lax.ppermute(tail, axis, [(i, (i + 1) % count) for i in range(ends)]),
                cells,
                lax.ppermute(head, axis, [((i + 1) % count, i) for i in range(ends)]),
            ],
            axis=dim,
        )
    return cells


def neighbours(padded):
    total = padded[2:, 1:-1, 1:-1] + padded[:-2, 1:-1, 1:-1]
    total = total + padded[1:-1, 2:, 1:-1] + padded[1:-1, :-2, 1:-1]
    return total + padded[1:-1, 1:-1, 2:] + padded[1:-1, 1:-1, :-2]


def parity_mask(shape):
    total = lax.broadcasted_iota(jnp.int32, shape, 0) + lax.broadcasted_iota(jnp.int32, shape, 1)
    total = total + lax.broadcasted_iota(jnp.int32, shape, 2)
    return total % 2


def relax_colour(values, padded, forcing, diag_coef, inv_h2, colour):
    update = (forcing + inv_h2 * neighbours(padded)) / (diag_coef + 6.0 * inv_h2)
    return jnp.where(parity_mask(values.shape) == colour, update, values)


def apply_operator(values, padded, diag_coef, inv_h2):
    return diag_coef * values + inv_h2 * (6.0 * values - neighbours(padded))


def restrict(values):
    shaped = values.reshape(
        values.shape[0] // 2, 2, values.shape[1] // 2, 2, values.shape[2] // 2, 2
    )
    return shaped.mean(axis=(1, 3, 5))


def prolong(values):
    return jnp.repeat(jnp.repeat(jnp.repeat(values, 2, 0), 2, 1), 2, 2)


def smooth(values, forcing, diag_coef, inv_h2, sweeps, fill_ghosts):
    for repeat in range(sweeps):
        for colour in (0, 1):
            values = relax_colour(values, fill_ghosts(values), forcing, diag_coef, inv_h2, colour)
    return values


def assemble(blocks_in, brick_map):
    slabs = brick_map.shape[0]
    inner = blocks_in.shape[1:]
    blocks = blocks_in.reshape((slabs, 8) + inner)
    ordered = jax.vmap(lambda members, mapping: members[mapping])(blocks, brick_map)
    ordered = ordered.reshape((slabs, 2, 2, 2) + inner)
    ordered = ordered.transpose(0, 1, 4, 2, 5, 3, 6)
    return ordered.reshape(slabs * 2 * inner[0], 2 * inner[1], 2 * inner[2])


def zero_fill(values):
    return jnp.pad(values, 1)


def flat_padded(face, length):
    flat = face.reshape(-1)
    return jnp.pad(flat, (0, length - flat.shape[0]))


def body(u_init, source, coeffs, brick_map):
    values = u_init[0]
    forcing = source[0]
    diag_coef = coeffs[0]
    slab_index = lax.axis_index("slab")
    member = lax.axis_index(("level", "bottom"))
    slab_count = lax.axis_size("slab")
    map_row = brick_map[slab_index]
    slots = jnp.arange(8, dtype=jnp.int32)
    brick_place = jnp.sum(slots * (map_row == member))
    bit_x = brick_place % 2
    bit_y = brick_place // 2 % 2
    bit_z = brick_place // 4
    partner_x = map_row[brick_place + 1 - 2 * bit_x]
    partner_y = map_row[brick_place + 2 - 4 * bit_y]
    twin_place = brick_place + 4 - 8 * bit_z
    partner_z = map_row[twin_place]
    map_below = brick_map[jnp.maximum(slab_index - 1, 0)]
    map_above = brick_map[jnp.minimum(slab_index + 1, slab_count - 1)]
    cross_member = jnp.where(bit_z == 0, map_below[twin_place], map_above[twin_place])

    def fill_ghosts(values):
        depth, height, width = values.shape
        row_length = max(depth * height, depth * width, height * width)
        face_x = jnp.where(bit_x == 0, values[:, :, -1], values[:, :, 0])
        face_y = jnp.where(bit_y == 0, values[:, -1, :], values[:, 0, :])
        face_z = jnp.where(bit_z == 0, values[-1], values[0])
        outbox = jnp.zeros((8, row_length), jnp.float32)
        outbox = outbox.at[partner_x].set(flat_padded(face_x, row_length))
        outbox = outbox.at[partner_y].set(flat_padded(face_y, row_length))
        outbox = outbox.at[partner_z].set(flat_padded(face_z, row_length))
        received = lax.all_to_all(
            outbox, ("level", "bottom"), split_axis=0, concat_axis=0, tiled=True
        )
        ghost_x = received[partner_x][: depth * height].reshape(depth, height)
        ghost_y = received[partner_y].reshape(depth, width)
        ghost_z = received[partner_z].reshape(height, width)
        outgoing = jnp.where(bit_z == 1, values[-1], values[0])
        layer_faces = lax.all_gather(outgoing[None], ("level", "bottom"), axis=0, tiled=True)
        rim_cells = with_halo(layer_faces[None], (("slab", 0),), 1)
        from_below = rim_cells[0][cross_member]
        from_above = rim_cells[2][cross_member]
        cross_face = jnp.where(bit_z == 0, from_below, from_above)
        padded = jnp.pad(values, 1)
        padded = padded.at[0, 1:-1, 1:-1].set(jnp.where(bit_z == 0, cross_face, ghost_z))
        padded = padded.at[-1, 1:-1, 1:-1].set(jnp.where(bit_z == 0, ghost_z, cross_face))
        padded = padded.at[1:-1, 0, 1:-1].set(jnp.where(bit_y == 1, ghost_y, 0.0))
        padded = padded.at[1:-1, -1, 1:-1].set(jnp.where(bit_y == 0, ghost_y, 0.0))
        padded = padded.at[1:-1, 1:-1, 0].set(jnp.where(bit_x == 1, ghost_x, 0.0))
        padded = padded.at[1:-1, 1:-1, -1].set(jnp.where(bit_x == 0, ghost_x, 0.0))
        return padded

    coarse_coef = restrict(diag_coef)
    bottom_coef = restrict(coarse_coef)
    values = smooth(values, forcing, diag_coef, 1.0, SWEEPS_FINE, fill_ghosts)
    fine_resid = forcing - apply_operator(values, fill_ghosts(values), diag_coef, 1.0)
    coarse_rhs = restrict(fine_resid)
    coarse_err = smooth(
        jnp.zeros_like(coarse_rhs), coarse_rhs, coarse_coef, 0.25, SWEEPS_COARSE, fill_ghosts
    )
    coarse_resid = coarse_rhs - apply_operator(
        coarse_err, fill_ghosts(coarse_err), coarse_coef, 0.25
    )
    bottom_rhs = restrict(coarse_resid)
    inner = bottom_rhs.shape
    all_rhs, all_coef = (
        lax.all_gather(bottom_rhs[None], ("slab", "level", "bottom"), axis=0, tiled=True),
        lax.all_gather(bottom_coef[None], ("slab", "level", "bottom"), axis=0, tiled=True),
    )
    grid_rhs = assemble(all_rhs, brick_map)
    grid_coef = assemble(all_coef, brick_map)
    grid_err = smooth(
        jnp.zeros_like(grid_rhs), grid_rhs, grid_coef, 0.0625, SWEEPS_BOTTOM, zero_fill
    )
    grid_err = grid_err - jnp.mean(grid_err)
    start_z = (slab_index * 2 + bit_z) * inner[0]
    bottom_err = lax.dynamic_slice(grid_err, (start_z, bit_y * inner[1], bit_x * inner[2]), inner)
    coarse_err = coarse_err + prolong(bottom_err)
    coarse_err = smooth(coarse_err, coarse_rhs, coarse_coef, 0.25, SWEEPS_COARSE, fill_ghosts)
    values = values + prolong(coarse_err)
    values = smooth(values, forcing, diag_coef, 1.0, SWEEPS_FINE, fill_ghosts)
    return values[None]


def solution(mesh):
    placed = (
        P(("slab", "level", "bottom"), None, None, None),
        P(("slab", "level", "bottom"), None, None, None),
        P(("slab", "level", "bottom"), None, None, None),
        P(),
    )
    return jax.shard_map(
        body,
        mesh=mesh,
        in_specs=placed,
        out_specs=P(("slab", "level", "bottom"), None, None, None),
        check_vma=False,
    )
```

profile of v0, /device:TPU:1, one launch (start us, length us, event | category | flops | bytes accessed | tf_op | source)
XLA Modules:
  0.0 1384.3 jit_solution(2570226735702980641)
XLA Ops:
  11.4 23.3 %all-gather = f32[8,1,32,128]{3,2,1,0:T(8,128)S(1)} all-gather(f32[1,1,32,128]{3,2,1,0:T(8,128)S(1)} %get-tuple-element.2017), channel_id=2, replica_groups=mesh['slab'=16,'level'=2,'bottom'=4] {'level','bottom'}, dimensions={0}, use_global_device_ids=true | all-gather | bytes 147456 | tf_op jit(solution)/shard_map/all_gather | solution.py:124
  70.2 34.9 %reshape_squeeze.81 = f32[16,2,16,2,64,2]{5,4,3,2,1,0:T(8,128)} reshape(f32[1,32,32,128]{3,2,1,0:T(8,128)S(1)} %copy-done.1) | data formatting | bytes 1048576 | tf_op jit(solution)/shard_map/reshape;squeeze | solution.py:50
  105.2 12.9 reduce_sum.56
  118.0 5.0 all-to-all-start
  136.8 4.9 scatter.545
  141.8 5.0 scatter.546
  150.7 7.3 scatter.554
  169.6 24.1 %all_gather.59 = f32[8,32,128]{2,1,0:T(8,128)} all-gather(f32[1,32,128]{2,1,0:T(8,128)S(1)} %bitcast.491), channel_id=1, replica_groups=mesh['slab'=16,'level'=2,'bottom'=4] {'level','bottom'}, dimensions={0}, use_global_device_ids=true | all-gather | bytes 147456 | tf_op jit(solution)/shard_map/all_gather | solution.py:124
  206.8 5.5 scatter.560
  212.4 5.0 scatter.561
  221.3 7.3 scatter.569
  238.9 24.1 %all_gather.60 = f32[8,32,128]{2,1,0:T(8,128)} all-gather(f32[1,32,128]{2,1,0:T(8,128)S(1)} %bitcast.492), channel_id=1, replica_groups=mesh['slab'=16,'level'=2,'bottom'=4] {'level','bottom'}, dimensions={0}, use_global_device_ids=true | all-gather | bytes 147456 | tf_op jit(solution)/shard_map/all_gather | solution.py:124
  277.8 5.5 scatter.575
  283.3 5.0 scatter.576
  292.2 7.3 scatter.584
  309.5 24.1 %all_gather.61 = f32[8,32,128]{2,1,0:T(8,128)} all-gather(f32[1,32,128]{2,1,0:T(8,128)S(1)} %bitcast.493), channel_id=1, replica_groups=mesh['slab'=16,'level'=2,'bottom'=4] {'level','bottom'}, dimensions={0}, use_global_device_ids=true | all-gather | bytes 147456 | tf_op jit(solution)/shard_map/all_gather | solution.py:124
  333.6 6.1 collective-permute-start.6
  347.9 5.5 scatter.590
  353.4 5.0 scatter.591
  362.3 7.3 scatter.599
  379.9 24.1 %all_gather.62 = f32[8,32,128]{2,1,0:T(8,128)} all-gather(f32[1,32,128]{2,1,0:T(8,128)S(1)} %bitcast.494), channel_id=1, replica_groups=mesh['slab'=16,'level'=2,'bottom'=4] {'level','bottom'}, dimensions={0}, use_global_device_ids=true | all-gather | bytes 147456 | tf_op jit(solution)/shard_map/all_gather | solution.py:124
  416.3 5.5 scatter.605
  421.8 5.0 scatter.606
  430.8 7.3 scatter.614
  439.2 34.9 %reshape.7007 = f32[16,2,16,2,64,2]{5,4,3,2,1,0:T(8,128)} reshape(f32[32,32,128]{2,1,0:T(8,128)S(1)} %copy.386) | data formatting | bytes 1048576 | tf_op jit(solution)/shard_map/reshape | solution.py:50
  474.0 12.3 reduce_sum.55
  494.7 22.1 %all_gather.63 = f32[8,16,64]{2,1,0:T(8,128)S(1)} all-gather(f32[1,16,64]{2,1,0:T(8,128)S(1)} %get-tuple-element.2085), channel_id=1, replica_groups=mesh['slab'=16,'level'=2,'bottom'=4] {'level','bottom'}, dimensions={0}, use_global_device_ids=true | all-gather | bytes 36864 | tf_op jit(solution)/shard_map/all_gather | solution.py:124
  538.8 5.2 all-to-all-start.7
  544.0 22.1 %all_gather.64 = f32[8,16,64]{2,1,0:T(8,128)S(1)} all-gather(f32[1,16,64]{2,1,0:T(8,128)S(1)} %get-tuple-element.2083), channel_id=1, replica_groups=mesh['slab'=16,'level'=2,'bottom'=4] {'level','bottom'}, dimensions={0}, use_global_device_ids=true | all-gather | bytes 36864 | tf_op jit(solution)/shard_map/all_gather | solution.py:124
  593.7 22.1 %all_gather.65 = f32[8,16,64]{2,1,0:T(8,128)S(1)} all-gather(f32[1,16,64]{2,1,0:T(8,128)S(1)} %get-tuple-element.2081), channel_id=1, replica_groups=mesh['slab'=16,'level'=2,'bottom'=4] {'level','bottom'}, dimensions={0}, use_global_device_ids=true | all-gather | bytes 36864 | tf_op jit(solution)/shard_map/all_gather | solution.py:124
  638.6 4.9 all-to-all-start.9
  643.5 22.3 %all_gather.66 = f32[8,16,64]{2,1,0:T(8,128)S(1)} all-gather(f32[1,16,64]{2,1,0:T(8,128)S(1)} %get-tuple-element.2079), channel_id=1, replica_groups=mesh['slab'=16,'level'=2,'bottom'=4] {'level','bottom'}, dimensions={0}, use_global_device_ids=true | all-gather | bytes 36864 | tf_op jit(solution)/shard_map/all_gather | solution.py:124
  684.8 5.6 div.150
  693.7 5.6 reshape.7014
  702.7 61.9 %all-gather.8.cloned.1.call-done = f32[1024,8,32]{2,1,0:T(8,128)} async-done(((f32[8,8,32]{2,1,0:T(8,128)}), f32[1024,8,32]{2,1,0:T(8,128)}) %all-gather.8.cloned.1.call-update) | async-done | bytes 1048592 | tf_op jit(solution)/shard_map/all_gather | solution.py:153
  764.6 5.0 gather_fusion.1
  772.2 5.3 copy.414
  781.8 50.3 %all-gather.6.cloned.1.call-done = f32[1024,8,32]{2,1,0:T(8,128)} async-done(((f32[8,8,32]{2,1,0:T(8,128)}), f32[1024,8,32]{2,1,0:T(8,128)}) %all-gather.6.cloned.1.call-update) | async-done | bytes 1048592 | tf_op jit(solution)/shard_map/all_gather | solution.py:152
  832.1 5.0 gather_fusion
  837.1 7.5 copy.413
  844.6 5.8 reshape.7017
  907.5 22.1 %all_gather.69 = f32[8,16,64]{2,1,0:T(8,128)S(1)} all-gather(f32[1,16,64]{2,1,0:T(8,128)S(1)} %get-tuple-element.2075), channel_id=1, replica_groups=mesh['slab'=16,'level'=2,'bottom'=4] {'level','bottom'}, dimensions={0}, use_global_device_ids=true | all-gather | bytes 36864 | tf_op jit(solution)/shard_map/all_gather | solution.py:124
  950.0 5.2 all-to-all-start.11
  955.2 22.1 %all_gather.70 = f32[8,16,64]{2,1,0:T(8,128)S(1)} all-gather(f32[1,16,64]{2,1,0:T(8,128)S(1)} %get-tuple-element.2073), channel_id=1, replica_groups=mesh['slab'=16,'level'=2,'bottom'=4] {'level','bottom'}, dimensions={0}, use_global_device_ids=true | all-gather | bytes 36864 | tf_op jit(solution)/shard_map/all_gather | solution.py:124
  998.7 5.2 all-to-all-start.12
  1003.9 22.1 %all_gather.71 = f32[8,16,64]{2,1,0:T(8,128)S(1)} all-gather(f32[1,16,64]{2,1,0:T(8,128)S(1)} %get-tuple-element.2071), channel_id=1, replica_groups=mesh['slab'=16,'level'=2,'bottom'=4] {'level','bottom'}, dimensions={0}, use_global_device_ids=true | all-gather | bytes 36864 | tf_op jit(solution)/shard_map/all_gather | solution.py:124
  1054.5 22.1 %all_gather.72 = f32[8,16,64]{2,1,0:T(8,128)S(1)} all-gather(f32[1,16,64]{2,1,0:T(8,128)S(1)} %get-tuple-element.2069), channel_id=1, replica_groups=mesh['slab'=16,'level'=2,'bottom'=4] {'level','bottom'}, dimensions={0}, use_global_device_ids=true | all-gather | bytes 36864 | tf_op jit(solution)/shard_map/all_gather | solution.py:124
  1111.1 24.1 %all_gather.73 = f32[8,32,128]{2,1,0:T(8,128)} all-gather(f32[1,32,128]{2,1,0:T(8,128)S(1)} %bitcast.495), channel_id=1, replica_groups=mesh['slab'=16,'level'=2,'bottom'=4] {'level','bottom'}, dimensions={0}, use_global_device_ids=true | all-gather | bytes 147456 | tf_op jit(solution)/shard_map/all_gather | solution.py:124
  1147.7 5.7 scatter.755
  1153.5 5.0 scatter.756
  1162.4 7.3 scatter.764
  1180.0 24.1 %all_gather.74 = f32[8,32,128]{2,1,0:T(8,128)} all-gather(f32[1,32,128]{2,1,0:T(8,128)S(1)} %bitcast.496), channel_id=1, replica_groups=mesh['slab'=16,'level'=2,'bottom'=4] {'level','bottom'}, dimensions={0}, use_global_device_ids=true | all-gather | bytes 147456 | tf_op jit(solution)/shard_map/all_gather | solution.py:124
  1216.3 5.8 scatter.770
  1222.0 5.0 scatter.771
  1230.9 7.3 scatter.779
  1243.8 5.2 all-to-all-start.16
  1249.0 24.1 %all_gather.75 = f32[8,32,128]{2,1,0:T(8,128)} all-gather(f32[1,32,128]{2,1,0:T(8,128)S(1)} %bitcast.497), channel_id=1, replica_groups=mesh['slab'=16,'level'=2,'bottom'=4] {'level','bottom'}, dimensions={0}, use_global_device_ids=true | all-gather | bytes 147456 | tf_op jit(solution)/shard_map/all_gather | solution.py:124
  1285.4 5.2 scatter.785
  1290.7 5.0 scatter.786
  1299.6 7.3 scatter.794
  1317.2 24.1 %all_gather.76 = f32[8,32,128]{2,1,0:T(8,128)} all-gather(f32[1,32,128]{2,1,0:T(8,128)S(1)} %bitcast.490), channel_id=1, replica_groups=mesh['slab'=16,'level'=2,'bottom'=4] {'level','bottom'}, dimensions={0}, use_global_device_ids=true | all-gather | bytes 147456 | tf_op jit(solution)/shard_map/all_gather | solution.py:124
  1353.7 5.3 scatter.800
  1358.9 5.0 scatter.801
  1367.8 7.3 scatter.809
  (671 shorter events, 519.0 us)
Async XLA Ops:
  34.7 101.4 %collective-permute-start = (f32[1,8,32,128]{3,2,1,0:T(8,128)S(1)}, f32[1,8,32,128]{3,2,1,0:T(8,128)S(1)}, u32[]{:S(2)}, u32[]{:S(2)}) collective-permute-start(f32[1,8,32,128]{3,2,1,0:T(8,128)S(1)} %bitcast.479), channel_id=1, source_target_pairs={{0,8},{8,16},{16,24},{24,32},{32,40},{40,48},{48,56},{56,64},{64,7... | collective-permute-start | bytes 393224 | tf_op jit(solution)/shard_map/ppermute | solution.py:19
  37.8 98.3 %collective-permute-start.1 = (f32[1,8,32,128]{3,2,1,0:T(8,128)S(1)}, f32[1,8,32,128]{3,2,1,0:T(8,128)}, u32[]{:S(2)}, u32[]{:S(2)}) collective-permute-start(f32[1,8,32,128]{3,2,1,0:T(8,128)S(1)} %bitcast.480), channel_id=1, source_target_pairs={{8,0},{16,8},{24,16},{32,24},{40,32},{48,40},{56,48},{64,56},{72,6... | collective-permute-start | bytes 393224 | tf_op jit(solution)/shard_map/ppermute | solution.py:21
  39.1 84.6 %collective-permute-start.10 = (f32[1,8,16,64]{3,2,1,0:T(8,128)S(1)}, f32[1,8,16,64]{3,2,1,0:T(8,128)S(1)}, u32[]{:S(2)}, u32[]{:S(2)}) collective-permute-start(f32[1,8,16,64]{3,2,1,0:T(8,128)S(1)} %broadcast_in_dim.247), channel_id=1, source_target_pairs={{0,8},{8,16},{16,24},{24,32},{32,40},{40,48},{48,56},{56,64},{64,7... | collective-permute-start | bytes 98312 | tf_op jit(solution)/shard_map/ppermute | solution.py:19
  43.1 80.6 %collective-permute-start.11 = (f32[1,8,16,64]{3,2,1,0:T(8,128)S(1)}, f32[1,8,16,64]{3,2,1,0:T(8,128)}, u32[]{:S(2)}, u32[]{:S(2)}) collective-permute-start(f32[1,8,16,64]{3,2,1,0:T(8,128)S(1)} %broadcast_in_dim.247), channel_id=1, source_target_pairs={{8,0},{16,8},{24,16},{32,24},{40,32},{48,40},{56,48},{64,56},{72,6... | collective-permute-start | bytes 98312 | tf_op jit(solution)/shard_map/ppermute | solution.py:21
  57.8 60.3 %all-to-all-start.5 = ((f32[8,1,1024]{2,1,0:T(1,128)}), f32[8,1,1024]{2,1,0:T(1,128)S(1)}, u32[]{:S(2)}, u32[]{:S(2)}) async-start(f32[8,1,1024]{2,1,0:T(1,128)} %copy.387), calls=%async_computation.5 | async-start | bytes 65536 | tf_op jit(solution)/shard_map/all_to_all | solution.py:117
  63.9 6.2 copy-start.1
  118.0 16.1 %all-to-all-start = ((f32[8,1,4096]{2,1,0:T(1,128)}), f32[8,1,4096]{2,1,0:T(1,128)S(1)}, u32[]{:S(2)}, u32[]{:S(2)}) async-start(f32[8,1,4096]{2,1,0:T(1,128)} %copy.342), calls=%async_computation | async-start | bytes 262144 | tf_op jit(solution)/shard_map/all_to_all | solution.py:117
  125.1 32.8 %copy-start.2 = (f32[1,32,32,128]{3,2,1,0:T(8,128)S(1)}, f32[1,32,32,128]{3,2,1,0:T(8,128)}, u32[]{:S(2)}) copy-start(f32[1,32,32,128]{3,2,1,0:T(8,128)} %param.329) | copy-start | bytes 1572868
  134.1 26.1 %copy-start.8 = (f32[18,18,66]{2,1,0:T(8,128)}, f32[18,18,66]{2,1,0:T(8,128)S(1)}, u32[]{:S(2)}) copy-start(f32[18,18,66]{2,1,0:T(8,128)S(1)} %scatter.629) | copy-start | bytes 256612
  164.8 35.8 %all-to-all-start.1 = ((f32[8,1,4096]{2,1,0:T(1,128)}), f32[8,1,4096]{2,1,0:T(1,128)S(1)}, u32[]{:S(2)}, u32[]{:S(2)}) async-start(f32[8,1,4096]{2,1,0:T(1,128)} %copy.352), calls=%async_computation.1 | async-start | bytes 262144 | tf_op jit(solution)/shard_map/all_to_all | solution.py:117
  193.8 10.1 collective-permute-start.2
  198.7 6.8 collective-permute-start.3
  234.1 35.4 %all-to-all-start.2 = ((f32[8,1,4096]{2,1,0:T(1,128)}), f32[8,1,4096]{2,1,0:T(1,128)S(1)}, u32[]{:S(2)}, u32[]{:S(2)}) async-start(f32[8,1,4096]{2,1,0:T(1,128)} %copy.361), calls=%async_computation.2 | async-start | bytes 262144 | tf_op jit(solution)/shard_map/all_to_all | solution.py:117
  263.0 9.8 collective-permute-start.4
  267.5 8.9 collective-permute-start.5
  305.0 36.9 %all-to-all-start.3 = ((f32[8,1,4096]{2,1,0:T(1,128)}), f32[8,1,4096]{2,1,0:T(1,128)S(1)}, u32[]{:S(2)}, u32[]{:S(2)}) async-start(f32[8,1,4096]{2,1,0:T(1,128)} %copy.370), calls=%async_computation.3 | async-start | bytes 262144 | tf_op jit(solution)/shard_map/all_to_all | solution.py:117
  333.6 11.6 collective-permute-start.6
  339.7 6.8 collective-permute-start.7
  370.5 67.5 %copy-start.3 = (f32[32,32,128]{2,0,1:T(8,128)}, f32[32,32,128]{2,0,1:T(8,128)S(1)}, u32[]{:S(2)}) copy-start(f32[32,32,128]{2,0,1:T(8,128)S(1)} %fusion.166) | copy-start | bytes 1572868
  375.2 34.9 %all-to-all-start.4 = ((f32[8,1,4096]{2,1,0:T(1,128)}), f32[8,1,4096]{2,1,0:T(1,128)S(1)}, u32[]{:S(2)}, u32[]{:S(2)}) async-start(f32[8,1,4096]{2,1,0:T(1,128)} %copy.379), calls=%async_computation.4 | async-start | bytes 262144 | tf_op jit(solution)/shard_map/all_to_all | solution.py:117
  404.1 9.3 collective-permute-start.8
  408.2 6.8 collective-permute-start.9
  474.0 12.3 copy-start.7
  474.0 12.3 copy-start.9
  490.0 32.2 %all-to-all-start.6 = ((f32[8,1,1024]{2,1,0:T(1,128)}), f32[8,1,1024]{2,1,0:T(1,128)S(1)}, u32[]{:S(2)}, u32[]{:S(2)}) async-start(f32[8,1,1024]{2,1,0:T(1,128)} %copy.392), calls=%async_computation.6 | async-start | bytes 65536 | tf_op jit(solution)/shard_map/all_to_all | solution.py:117
  516.8 6.0 collective-permute-start.12
  520.3 5.0 collective-permute-start.13
  538.8 32.8 %all-to-all-start.7 = ((f32[8,1,1024]{2,1,0:T(1,128)}), f32[8,1,1024]{2,1,0:T(1,128)S(1)}, u32[]{:S(2)}, u32[]{:S(2)}) async-start(f32[8,1,1024]{2,1,0:T(1,128)} %copy.397), calls=%async_computation.7 | async-start | bytes 65536 | tf_op jit(solution)/shard_map/all_to_all | solution.py:117
  566.1 6.2 collective-permute-start.14
  570.1 5.3 collective-permute-start.15
  588.8 32.5 %all-to-all-start.8 = ((f32[8,1,1024]{2,1,0:T(1,128)}), f32[8,1,1024]{2,1,0:T(1,128)S(1)}, u32[]{:S(2)}, u32[]{:S(2)}) async-start(f32[8,1,1024]{2,1,0:T(1,128)} %copy.402), calls=%async_computation.8 | async-start | bytes 65536 | tf_op jit(solution)/shard_map/all_to_all | solution.py:117
  615.8 6.2 collective-permute-start.16
  619.9 5.3 collective-permute-start.17
  638.6 32.4 %all-to-all-start.9 = ((f32[8,1,1024]{2,1,0:T(1,128)}), f32[8,1,1024]{2,1,0:T(1,128)S(1)}, u32[]{:S(2)}, u32[]{:S(2)}) async-start(f32[8,1,1024]{2,1,0:T(1,128)} %copy.407), calls=%async_computation.9 | async-start | bytes 65536 | tf_op jit(solution)/shard_map/all_to_all | solution.py:117
  643.5 121.1 %all-gather.8.cloned.1.call-start = ((), (), s32[]{:S(2)}) async-start(), calls=%async_computation.19 | async-start | bytes 4227072 | tf_op jit(solution)/shard_map/all_gather | solution.py:153
  665.8 5.9 collective-permute-start.18
  669.5 5.3 collective-permute-start.19
  693.6 138.5 %all-gather.6.cloned.1.call-start = ((), (), s32[]{:S(2)}) async-start(), calls=%async_computation.18 | async-start | bytes 4227072 | tf_op jit(solution)/shard_map/all_gather | solution.py:152
  903.9 29.0 %all-to-all-start.10 = ((f32[8,1,1024]{2,1,0:T(1,128)}), f32[8,1,1024]{2,1,0:T(1,128)S(1)}, u32[]{:S(2)}, u32[]{:S(2)}) async-start(f32[8,1,1024]{2,1,0:T(1,128)} %copy.418), calls=%async_computation.10 | async-start | bytes 65536 | tf_op jit(solution)/shard_map/all_to_all | solution.py:117
  929.5 4.2 collective-permute-start.20
  931.6 5.0 collective-permute-start.21
  950.0 31.7 %all-to-all-start.11 = ((f32[8,1,1024]{2,1,0:T(1,128)}), f32[8,1,1024]{2,1,0:T(1,128)S(1)}, u32[]{:S(2)}, u32[]{:S(2)}) async-start(f32[8,1,1024]{2,1,0:T(1,128)} %copy.423), calls=%async_computation.11 | async-start | bytes 65536 | tf_op jit(solution)/shard_map/all_to_all | solution.py:117
  977.3 5.1 collective-permute-start.22
  980.2 5.0 collective-permute-start.23
  998.7 33.3 %all-to-all-start.12 = ((f32[8,1,1024]{2,1,0:T(1,128)}), f32[8,1,1024]{2,1,0:T(1,128)S(1)}, u32[]{:S(2)}, u32[]{:S(2)}) async-start(f32[8,1,1024]{2,1,0:T(1,128)} %copy.428), calls=%async_computation.12 | async-start | bytes 65536 | tf_op jit(solution)/shard_map/all_to_all | solution.py:117
  1026.0 6.7 collective-permute-start.24
  1030.5 5.3 collective-permute-start.25
  1049.6 32.2 %all-to-all-start.13 = ((f32[8,1,1024]{2,1,0:T(1,128)}), f32[8,1,1024]{2,1,0:T(1,128)S(1)}, u32[]{:S(2)}, u32[]{:S(2)}) async-start(f32[8,1,1024]{2,1,0:T(1,128)} %copy.433), calls=%async_computation.13 | async-start | bytes 65536 | tf_op jit(solution)/shard_map/all_to_all | solution.py:117
  1076.6 5.9 collective-permute-start.26
  1080.4 5.3 collective-permute-start.27
  1106.1 35.2 %all-to-all-start.14 = ((f32[8,1,4096]{2,1,0:T(1,128)}), f32[8,1,4096]{2,1,0:T(1,128)S(1)}, u32[]{:S(2)}, u32[]{:S(2)}) async-start(f32[8,1,4096]{2,1,0:T(1,128)} %copy.443), calls=%async_computation.14 | async-start | bytes 262144 | tf_op jit(solution)/shard_map/all_to_all | solution.py:117
  1135.2 9.4 collective-permute-start.28
  1139.6 6.8 collective-permute-start.29
  1175.2 34.6 %all-to-all-start.15 = ((f32[8,1,4096]{2,1,0:T(1,128)}), f32[8,1,4096]{2,1,0:T(1,128)S(1)}, u32[]{:S(2)}, u32[]{:S(2)}) async-start(f32[8,1,4096]{2,1,0:T(1,128)} %copy.452), calls=%async_computation.15 | async-start | bytes 262144 | tf_op jit(solution)/shard_map/all_to_all | solution.py:117
  1204.1 9.0 collective-permute-start.30
  1208.1 6.8 collective-permute-start.31
  1239.1 39.7 %copy-start.5 = (f32[32,32,128]{2,0,1:T(8,128)}, f32[32,32,128]{2,0,1:T(8,128)S(1)}, u32[]{:S(2)}) copy-start(f32[32,32,128]{2,0,1:T(8,128)S(1)} %fusion.157) | copy-start | bytes 1572868
  1243.8 35.1 %all-to-all-start.16 = ((f32[8,1,4096]{2,1,0:T(1,128)}), f32[8,1,4096]{2,1,0:T(1,128)}, u32[]{:S(2)}, u32[]{:S(2)}) async-start(f32[8,1,4096]{2,1,0:T(1,128)} %copy.461), calls=%async_computation.16 | async-start | bytes 262144 | tf_op jit(solution)/shard_map/all_to_all | solution.py:117
  1273.1 8.6 collective-permute-start.32
  1277.2 6.8 collective-permute-start.33
  1278.9 28.0 %copy-start.6 = (f32[32,32,128]{2,0,1:T(8,128)S(1)}, f32[32,32,128]{2,0,1:T(8,128)}, u32[]{:S(2)}) copy-start(f32[32,32,128]{2,0,1:T(8,128)} %copy-done.5) | copy-start | bytes 1572868
  1312.4 34.7 %all-to-all-start.17 = ((f32[8,1,4096]{2,1,0:T(1,128)}), f32[8,1,4096]{2,1,0:T(1,128)S(1)}, u32[]{:S(2)}, u32[]{:S(2)}) async-start(f32[8,1,4096]{2,1,0:T(1,128)} %copy.468), calls=%async_computation.17 | async-start | bytes 262144 | tf_op jit(solution)/shard_map/all_to_all | solution.py:117
  1341.3 8.3 collective-permute-start.34
  1345.4 6.8 collective-permute-start.35
  (4 other events, 8.3 us)
Sparse Core Ops, SparseCore 0:
  693.7 70.7 all-gather.7
  767.7 64.3 all-gather.5
where the time goes:
time: 1400 us; the launch traced here: 1380 us
  local copies, waits for them, and re-layouts  472 us (34%)
  blocking collectives  393 us (28%)
  starting transfers between devices  183 us (13%)
  other arithmetic  153 us (11%)
  waiting for transfers between devices  153 us (11%)
  between operations  29.4 us (2%)
    all_gather x17, blocking collectives, fill_ghosts(): lax.all_gather(outgoing[None], ('level', 'bottom'), axis=0, tiled=True)  393 us
    scatter x18, local copies, waits for them, and re-layouts, fill_ghosts(): padded = padded.at[1:-1, 1:-1, -1].set(jnp.where(bit_x == 0, ghost_x, 0.0))  89 us
    all_to_all x18, starting transfers between devices, fill_ghosts(): lax.all_to_all(outbox, ('level', 'bottom'), split_axis=0, concat_axis=0,...  86.7 us
    ppermute x18, starting transfers between devices, with_halo(): lax.ppermute(tail, axis, [(i, (i + 1) % count) for i in range(ends)])  71.9 us
    all_gather x1, waiting for transfers between devices, body(): lax.all_gather(bottom_coef[None], ('slab', 'level', 'bottom'), axis=0, ti...  61.9 us
    scatter x18, local copies, waits for them, and re-layouts, fill_ghosts(): padded.at[0, 1:-1, 1:-1].set(jnp.where(bit_z == 0, cross_face, ghost_z))  56.1 us
    scatter x18, local copies, waits for them, and re-layouts, fill_ghosts(): padded.at[-1, 1:-1, 1:-1].set(jnp.where(bit_z == 0, ghost_z, cross_face))  51.9 us
    select_n x30, other arithmetic, relax_colour(): return jnp.where(parity_mask(values.shape) == colour, update, values)  51.4 us
  transfers between devices with their start and end apart: 56, of which 18 were waited for; matrix products, arithmetic and copies ran while one was open for 10% of the time, Pallas kernels for 0%

commit v1 on v0

v1 whole, which is shorter than its diff:
```python
import functools
import math

import jax
import jax.numpy as jnp
from jax import lax
from jax.experimental import pallas as pl
from jax.experimental.pallas import tpu as pltpu
from jax.sharding import PartitionSpec as P

LB = ("level", "bottom")
ALL = ("slab", "level", "bottom")
SLABS = 16
F32 = jnp.float32
VMEM_SPEC = pl.BlockSpec(memory_space=pltpu.VMEM)
SMEM_SPEC = pl.BlockSpec(memory_space=pltpu.SMEM)
EXACT = lax.Precision.HIGHEST


def run(kernel, outs, smem, vmem, scratch=()):
    shapes = [jax.ShapeDtypeStruct(s, F32) for s in outs]
    single = len(shapes) == 1
    return pl.pallas_call(
        kernel,
        out_shape=shapes[0] if single else shapes,
        in_specs=[SMEM_SPEC] * len(smem) + [VMEM_SPEC] * len(vmem),
        out_specs=VMEM_SPEC if single else [VMEM_SPEC] * len(shapes),
        scratch_shapes=[pltpu.VMEM(s, F32) for s in scratch],
        compiler_params=pltpu.CompilerParams(vmem_limit_bytes=50 << 20),
    )(*smem, *vmem)


def iota(shape, dim):
    return lax.broadcasted_iota(jnp.int32, shape, dim)


def odd(rows, cols):
    return ((iota((rows, cols), 0) + iota((rows, cols), 1)) & 1) == 1


def place_of(meta, bricks):
    slab, me = meta[0], meta[1]
    place = jnp.int32(0)
    for i in range(8):
        place = place + jnp.where(bricks[slab, i] == me, i, 0)
    return slab, me, place & 1, (place >> 1) & 1, place >> 2


def is_zero(scalar, shape=(8, 128)):
    return jnp.full(shape, scalar, jnp.int32) == 0


class Shell:
    def __init__(self, low, high, comps, arrays):
        self.low, self.high, self.comps, self.arrays = low, high, comps, arrays
        self.planes = math.ceil(len(low) / 4)
        self.nz = 4 * self.planes
        self.ny = 2 * len(comps)
        self.strips = 8 * arrays
        self.nx = math.ceil(self.strips / 16)
        self.sent = self.nz + self.ny + self.nx
        self.nz2 = 5 * self.planes
        self.y2 = self.nz2 + 1
        self.x2 = self.y2 + self.ny
        self.got = self.x2 + self.nx
        assert 5 * self.planes <= 16 and self.strips % 16 + self.ny <= 16


DOWN = Shell(
    [(0, 0), (0, 1), (0, 2)] + [(c, t) for c in (1, 2, 3, 4) for t in (0, 1)],
    [(0, 13), (0, 14), (0, 15)] + [(c, t) for c in (1, 2, 3, 4) for t in (14, 15)],
    [(0,), (1, 2), (3, 4)],
    5,
)
UP = Shell([(0, 0), (0, 1)], [(0, 14), (0, 15)], [(0,)], 1)


def merge_strips(strips, first=0, base=None):
    group = iota((8, 128), 1) // 8
    total = jnp.zeros((8, 128), F32) if base is None else base
    for i, strip in enumerate(strips):
        pos = first + i
        moved = pltpu.roll(strip, 8 * pos, 1) if pos else strip
        total = jnp.where(group == pos, moved, total)
    return total


def pack_shell(shell, get, out, bit_x, bit_y):
    row = iota((8, 128), 0)
    x0, y0 = is_zero(bit_x), is_zero(bit_y)
    for first, faces in ((0, shell.low), (4, shell.high)):
        for i, (c, t) in enumerate(faces):
            j = 4 * (i % shell.planes)
            out[first + i // shell.planes, j : j + 4] = get(c, t).reshape(4, 8, 128)
    for k in range(8):
        strips = []
        for tl in range(2):
            cells = [get(c, 2 * k + tl) for c in range(shell.arrays)]
            rows = [jnp.where(y0, v[24:32], v[0:8]) for v in cells]
            for ci, comp in enumerate(shell.comps):
                tile = rows[comp[0]]
                if len(comp) == 2:
                    red, black = rows[comp[0]], rows[comp[1]]
                    red = jnp.where(y0, pltpu.roll(red, 4, 0), red)
                    black = jnp.where(y0, black, pltpu.roll(black, 4, 0))
                    tile = jnp.where(row < 4, red, black)
                out[k, shell.nz + tl * len(shell.comps) + ci] = tile
            for v in cells:
                for g in range(4):
                    tile = v[8 * g : 8 * g + 8]
                    strips.append(jnp.where(x0, pltpu.roll(tile, 8, 1), tile))
        for i in range(shell.nx):
            out[k, shell.nz + shell.ny + i] = merge_strips(strips[16 * i : 16 * i + 16])


def cross_kernel(shell, meta, bricks, recv, out):
    slab, me = meta[0], meta[1]
    for i in range(4):
        src = jnp.where(me >= 4, bricks[slab, 4 + i], bricks[slab, i])
        out[i] = recv[src, 0 : shell.nz]


def mid_kernel(shell, meta, bricks, recv, cross, out, faces):
    slab, me = meta[0], meta[1]
    faces[0:8] = recv[:, 0 : shell.nz]
    faces[8:12] = cross[...]
    for p in range(8):
        bx, by, bz = p & 1, (p >> 1) & 1, p >> 2
        dest = bricks[slab, p]
        same = me >= 4 if bz else me < 4

        def src(q):
            return jnp.where(same, bricks[slab, (q & 3) + 4 * (1 - bz)], 8 + (q & 3))

        def strip_of(tile):
            return pltpu.roll(tile, 8, 1) if bx else tile

        at_own, at_y, at_x, at_xy = src(p), src(p ^ 2), src(p ^ 1), src(p ^ 3)
        gy = 3 if by else 0
        strips = []
        for j in range(shell.planes):
            out[dest, 5 * j : 5 * j + 4] = faces[at_own, 4 * j : 4 * j + 4]
            out[dest, 5 * j + 4] = faces[at_y, 4 * j + gy]
            strips += [strip_of(faces[at_x, 4 * j + g]) for g in range(4)]
            strips.append(strip_of(faces[at_xy, 4 * j + gy]))
        out[dest, shell.nz2] = merge_strips(strips)
        from_y, from_x, from_xy = bricks[slab, p ^ 2], bricks[slab, p ^ 1], bricks[slab, p ^ 3]
        y1 = shell.nz
        out[dest, shell.y2 : shell.x2] = recv[from_y, y1 : y1 + shell.ny]
        x1 = shell.nz + shell.ny
        if shell.nx > 1:
            out[dest, shell.x2 : shell.x2 + shell.nx - 1] = recv[from_x, x1 : x1 + shell.nx - 1]
        edge = [strip_of(recv[from_xy, y1 + i]) for i in range(shell.ny)]
        out[dest, shell.x2 + shell.nx - 1] = merge_strips(
            edge, shell.strips % 16, recv[from_x, x1 + shell.nx - 1]
        )


def unpack_shell(shell, recv, grids, bit_x, bit_y):
    row, lane = iota((8, 128), 0), iota((8, 128), 1)
    x0, y0 = is_zero(bit_x), is_zero(bit_y)
    in_x = (x0 & (lane < 8)) | (jnp.logical_not(x0) & (lane >= 120))
    in_y = (y0 & (row != 7)) | (jnp.logical_not(y0) & (row != 0))

    def strip(tile, pos):
        shift = (jnp.where(bit_x == 0, 0, 120) + 128 - 8 * pos) % 128
        return jnp.where(in_x, pltpu.roll(tile, shift, 1), 0.0)

    def split(comp, tile):
        if len(comp) == 1:
            return [tile]
        moved = pltpu.roll(tile, 4, 0)
        return [jnp.where(y0, tile, moved), jnp.where(y0, moved, tile)]

    for first, faces, shift in ((0, shell.low, 19), (4, shell.high, -13)):
        for i, (c, t) in enumerate(faces):
            k, j = first + i // shell.planes, i % shell.planes
            for g in range(5):
                tile, side = recv[k, 5 * j + g], strip(recv[k, shell.nz2], 5 * j + g)
                if g == 4:
                    tile, side = jnp.where(in_y, tile, 0.0), jnp.where(in_y, side, 0.0)
                grids[c][shift + t, 8 * g : 8 * g + 8, 0:128] = tile
                grids[c][shift + t, 8 * g : 8 * g + 8, 128:256] = side
    for t in range(16):
        k, tl = t // 2, t % 2
        for ci, comp in enumerate(shell.comps):
            i = tl * len(shell.comps) + ci
            tile = recv[k, shell.y2 + i]
            side = strip(recv[k, shell.x2 + shell.nx - 1], shell.strips % 16 + i)
            for c, one, two in zip(comp, split(comp, tile), split(comp, side)):
                grids[c][3 + t, 32:40, 0:128] = jnp.where(in_y, one, 0.0)
                grids[c][3 + t, 32:40, 128:256] = jnp.where(in_y, two, 0.0)
        for c in range(shell.arrays):
            for g in range(4):
                i = 4 * (tl * shell.arrays + c) + g
                grids[c][3 + t, 8 * g : 8 * g + 8, 128:256] = strip(recv[k, shell.x2 + i // 16], i % 16)


def pair_of(cells, t, red, mask):
    low, high = cells[0, 2 * t], cells[0, 2 * t + 1]
    return jnp.where(mask, high, low) if red else jnp.where(mask, low, high)


def first_kernel(meta, bricks, u, f, a, out):
    _, _, bit_x, bit_y, _ = place_of(meta, bricks)
    mask = odd(32, 128)
    sources = ((u, False), (f, True), (f, False), (a, True), (a, False))

    def get(c, t):
        return pair_of(sources[c][0], t, sources[c][1], mask)

    pack_shell(DOWN, get, out, bit_x, bit_y)


def around(src, k, red, mask, edges):
    here = src[k]
    rows, cols = here.shape
    above, below = src[k + 1], src[k - 1]
    other = jnp.where(mask, above, below) if red else jnp.where(mask, below, above)
    up, down = pltpu.roll(here, 1, 0), pltpu.roll(here, rows - 1, 0)
    left, right = pltpu.roll(here, 1, 1), pltpu.roll(here, cols - 1, 1)
    if edges:
        row, lane = iota((rows, cols), 0), iota((rows, cols), 1)
        up, down = jnp.where(row == 0, 0.0, up), jnp.where(row == rows - 1, 0.0, down)
        if edges == 2:
            left, right = jnp.where(lane == 0, 0.0, left), jnp.where(lane == cols - 1, 0.0, right)
    return ((here + other) + (up + down)) + (left + right)


def half_sweep(dst, src, force, inverse, lo, hi, red, mask, scale, edges, unroll=2):
    def step(k, carry):
        total = around(src, k, red, mask, edges)
        if scale != 1.0:
            total = scale * total
        dst[k] = (force[k] + total) * inverse[k]
        return carry

    lax.fori_loop(lo, hi, step, 0, unroll=unroll)


def pick(rows, cols, keep):
    return jnp.where(keep(iota((rows, cols), 0), iota((rows, cols), 1)), 1.0, 0.0).astype(F32)


def fine_down_kernel(meta, bricks, u, f, a, recv, rc, u_b, f_r, f_b, i_r, i_b, u_r, resid, small):
    slab, _, bit_x, bit_y, bit_z = place_of(meta, bricks)
    own = odd(32, 128)
    grids = (u_b, f_r, f_b, i_r, i_b)
    sources = ((u, False), (f, True), (f, False), (a, True), (a, False))
    for t in range(16):
        for grid, (cells, red) in zip(grids, sources):
            grid[3 + t, 0:32, 0:128] = pair_of(cells, t, red, own)
    unpack_shell(DOWN, recv, grids, bit_x, bit_y)
    u_r[0] = jnp.zeros((40, 256), F32)
    u_r[21] = jnp.zeros((40, 256), F32)
    row, lane = iota((40, 256), 0), iota((40, 256), 1)
    x0, y0 = is_zero(bit_x, (40, 256)), is_zero(bit_y, (40, 256))
    x1, y1 = jnp.logical_not(x0), jnp.logical_not(y0)
    inside = (row < 32) | (y0 & (row < 36)) | (y1 & (row >= 36))
    inside = inside & ((lane < 128) | (x0 & (lane < 136)) | (x1 & (lane >= 248)))
    no_low = (slab == 0) & (bit_z == 0)
    no_high = (slab == SLABS - 1) & (bit_z == 1)

    def invert(k, carry):
        gone = jnp.where((no_low & (k < 3)) | (no_high & (k >= 19)), 1, 0)
        keep = inside & is_zero(gone, (40, 256))
        i_r[k] = jnp.where(keep, 1.0 / (i_r[k] + 6.0), 0.0)
        i_b[k] = jnp.where(keep, 1.0 / (i_b[k] + 6.0), 0.0)
        return carry

    lax.fori_loop(1, 21, invert, 0)
    mask = odd(40, 256)
    for _ in range(2):
        half_sweep(u_r, u_b, f_r, i_r, 1, 21, True, mask, 1.0, 0)
        half_sweep(u_b, u_r, f_b, i_b, 1, 21, False, mask, 1.0, 0)
    for t in range(16):
        total = around(u_b, 3 + t, True, mask, 0)[0:32, 0:128]
        diag = pair_of(a, t, True, own) + 6.0
        resid[0, t] = pair_of(f, t, True, own) + total - diag * u_r[3 + t, 0:32, 0:128]
        resid[1, t] = a[0, 2 * t] + a[0, 2 * t + 1]
    twice = pick(128, 128, lambda r, c: (r >> 1) == (c & 63)) * 0.125
    row, lane = iota((16, 128), 0), iota((16, 128), 1)
    even = ((row + lane + (lane >> 6)) & 1) == 0
    for i in range(2):
        for t in range(16):
            small[16 * t : 16 * t + 16] = (
                resid[i, t, pl.ds(0, 16, stride=2), :] + resid[i, t, pl.ds(1, 16, stride=2), :]
            )
        summed = jnp.dot(small[...], twice, precision=EXACT, preferred_element_type=F32)
        summed = summed.reshape(16, 16, 128)
        for j in range(8):
            rc[i, j] = jnp.where(even, summed[2 * j], summed[2 * j + 1])


def up_pack_kernel(meta, bricks, u_b, out):
    _, _, bit_x, bit_y, _ = place_of(meta, bricks)
    pack_shell(UP, lambda c, t: u_b[3 + t, 0:32, 0:128], out, bit_x, bit_y)


def slot_of(member, me):
    return jnp.where((member >> 2) == (me >> 2), 0, 4) + ((me - member) & 3)


def faces_kernel(meta, bricks, *refs):
    boxes, (out, held) = refs[:8], refs[8:]
    slab, me = meta[0], meta[1]
    for i, box in enumerate(boxes):
        held[i] = box[...]
    start = jnp.where(me < 4, 3, 0)
    for i in range(4):
        member = jnp.where(me < 4, bricks[slab, 4 + i], bricks[slab, i])
        out[i] = held[slot_of(member, me), :, pl.ds(start, 5)]


def coarse_down_kernel(meta, bricks, *refs):
    boxes, (one, two) = refs[:8], refs[8:10]
    rb, rb_send, e_b, r_r, r_b, i_r, i_b = refs[10:17]
    held, low, high, e_r, a_r, a_b, resid, small = refs[17:]
    slab, me = meta[0], meta[1]
    for i, box in enumerate(boxes):
        held[i] = box[...]

    @pl.when(me < 4)
    def _():
        low[...] = one[...]
        high[...] = two[...]

    @pl.when(me >= 4)
    def _():
        low[...] = two[...]
        high[...] = one[...]

    left = iota((16, 128), 1) < 64
    for q, (red, black) in enumerate(((r_r, r_b), (a_r, a_b))):

        def put(k, by, west, east):
            rows = slice(16 * by, 16 * by + 16)
            red[k, rows] = jnp.where(left, west, pltpu.roll(east, 64, 1))
            black[k, rows] = jnp.where(left, pltpu.roll(west, 64, 1), east)

        for by in range(2):
            for bz in range(2):
                west = slot_of(bricks[slab, 2 * by + 4 * bz], me)
                east = slot_of(bricks[slab, 2 * by + 4 * bz + 1], me)
                for j in range(8):
                    put(6 + 8 * bz + j, by, held[west, q, j], held[east, q, j])
            for j in range(5):
                put(1 + j, by, low[2 * by, q, j], low[2 * by + 1, q, j])
                put(22 + j, by, high[2 * by, q, j], high[2 * by + 1, q, j])
    for k in (0, 27):
        e_r[k] = jnp.zeros((32, 128), F32)
        e_b[k] = jnp.zeros((32, 128), F32)

    def start(k, carry):
        gone = jnp.where(((slab == 0) & (k < 6)) | ((slab == SLABS - 1) & (k >= 22)), 1, 0)
        keep = is_zero(gone, (32, 128))
        inverse = jnp.where(keep, 1.0 / (a_r[k] + 1.5), 0.0)
        i_r[k] = inverse
        i_b[k] = jnp.where(keep, 1.0 / (a_b[k] + 1.5), 0.0)
        e_r[k] = r_r[k] * inverse
        return carry

    lax.fori_loop(1, 27, start, 0)
    mask = odd(32, 128)
    half_sweep(e_b, e_r, r_b, i_b, 1, 27, False, mask, 0.25, 2)
    half_sweep(e_r, e_b, r_r, i_r, 1, 27, True, mask, 0.25, 2)
    half_sweep(e_b, e_r, r_b, i_b, 1, 27, False, mask, 0.25, 2)

    def residual(n, carry):
        k = n + 3
        total = 0.25 * around(e_b, k, True, mask, 2)
        resid[0, n] = r_r[k] + total - (a_r[k] + 1.5) * e_r[k]
        resid[1, n] = a_r[k] + a_b[k]
        return carry

    lax.fori_loop(0, 22, residual, 0, unroll=2)
    total = jnp.zeros((352, 128), F32)
    for i in range(2):
        for n in range(22):
            small[16 * n : 16 * n + 16] = (
                resid[i, n, pl.ds(0, 16, stride=2), :] + resid[i, n, pl.ds(1, 16, stride=2), :]
            )
        half = pick(128, 128, lambda r, c: (r >> 1) == c - 64 * i) * 0.125
        total = total + jnp.dot(small[...], half, precision=EXACT, preferred_element_type=F32)
    rb[...] = total.reshape(22, 16, 128)
    rb_send[...] = rb[pl.ds(jnp.where(me < 4, 1, 3), 18)]


def bottom_kernel(meta, rb, one, two, es, part, e_r, e_b, g_r, g_b, i_r, i_b, low, high):
    slab, me = meta[0], meta[1]

    @pl.when(me < 4)
    def _():
        low[...] = one[...]
        high[...] = two[...]

    @pl.when(me >= 4)
    def _():
        low[...] = two[...]
        high[...] = one[...]

    mask = odd(16, 128)
    left = iota((16, 128), 1) < 64
    zero = jnp.zeros((16, 128), F32)
    for k in (0, 27):
        e_r[k] = zero
        e_b[k] = zero
    for j in range(26):
        planes = []
        for n in (2 * j, 2 * j + 1):
            planes.append(low[n] if n < 18 else rb[n - 15] if n < 34 else high[n - 34])
        keep = left
        if j < 9:
            keep = left & jnp.logical_not(is_zero(slab, (16, 128)))
        if j >= 17:
            keep = left & jnp.logical_not(is_zero(slab - (SLABS - 1), (16, 128)))
        for red in (True, False):
            cells = jnp.where(mask, planes[1], planes[0]) if red else jnp.where(mask, planes[0], planes[1])
            force = jnp.where(left, cells, 0.0)
            inverse = jnp.where(keep, 1.0 / (pltpu.roll(cells, 64, 1) + 0.375), 0.0)
            if red:
                g_r[1 + j], i_r[1 + j], e_r[1 + j] = force, inverse, force * inverse
            else:
                g_b[1 + j], i_b[1 + j] = force, inverse
    half_sweep(e_b, e_r, g_b, i_b, 1, 27, False, mask, 0.0625, 1, unroll=True)

    def sweep(n, carry):
        half_sweep(e_r, e_b, g_r, i_r, 1, 27, True, mask, 0.0625, 1, unroll=True)
        half_sweep(e_b, e_r, g_b, i_b, 1, 27, False, mask, 0.0625, 1, unroll=True)
        return carry

    lax.fori_loop(0, 7, sweep, 0)
    for i in range(22):
        k, upper = (15 + i) // 2 + 1, (15 + i) % 2
        es[i] = jnp.where(mask, e_r[k], e_b[k]) if upper else jnp.where(mask, e_b[k], e_r[k])
    total = zero
    for k in range(10, 18):
        total = total + (e_r[k] + e_b[k])
    total = total[0:8] + total[8:16]
    for i in range(SLABS):
        part[i] = total


def up_kernel(
    meta, bricks, sums, es, ec_b, r_r, r_b, ci_r, ci_b, u1_b, f_r, f_b, i_r, i_b, recv, out,
    e_r, e_b, small, wide, planes, tall, u_r, u_b,
):
    slab, _, bit_x, bit_y, bit_z = place_of(meta, bricks)
    total = sums[0]
    for i in range(1, SLABS):
        total = total + sums[i]
    mean = jnp.sum(total) * (1.0 / (SLABS * 16 * 16 * 64))
    for i in range(22):
        shifted = es[i] - mean
        if i < 3:
            shifted = jnp.where(is_zero(slab, (16, 128)), 0.0, shifted)
        if i >= 19:
            shifted = jnp.where(is_zero(slab - (SLABS - 1), (16, 128)), 0.0, shifted)
        small[16 * i : 16 * i + 16] = shifted
    spread = pick(128, 128, lambda r, c: r == (c >> 1))
    small[...] = jnp.dot(small[...], spread, precision=EXACT, preferred_element_type=F32)
    for i in range(22):
        rows = small[16 * i : 16 * i + 16]
        wide[i, pl.ds(0, 16, stride=2), :] = rows
        wide[i, pl.ds(1, 16, stride=2), :] = rows
    for k in (0, 1, 2, 25, 26, 27):
        e_r[k] = jnp.zeros((32, 128), F32)
        e_b[k] = jnp.zeros((32, 128), F32)
    for i in range(22):
        e_b[3 + i] = ec_b[3 + i] + wide[i]
    coarse = odd(32, 128)
    for _ in range(2):
        half_sweep(e_r, e_b, r_r, ci_r, 3, 25, True, coarse, 0.25, 2)
        half_sweep(e_b, e_r, r_b, ci_b, 3, 25, False, coarse, 0.25, 2)
    for n in range(20):
        z = n - 2
        k = 8 * bit_z + (z // 2 + 6)
        red, black = e_r[k], e_b[k]
        planes[32 * n : 32 * n + 32] = jnp.where(coarse, red, black) if z % 2 else jnp.where(coarse, black, red)

    lane = iota((128, 256), 1)
    x0 = is_zero(bit_x, (128, 256))
    start = jnp.where(lane < 128, 64 * bit_x + (lane >> 1), (lane >> 1) + jnp.where(x0, 0, -64))
    usable = (lane < 128) | (x0 & (lane < 136)) | (jnp.logical_not(x0) & (lane >= 248))
    spread = jnp.where(usable & (iota((128, 256), 0) == start), 1.0, 0.0).astype(F32)
    tall_rows = jnp.dot(planes[...], spread, precision=EXACT, preferred_element_type=F32)
    for n in range(20):
        rows = tall_rows[32 * n : 32 * n + 32]
        for h in range(2):
            tall[n, h, pl.ds(0, 32, stride=2), :] = rows[:, 128 * h : 128 * h + 128]
            tall[n, h, pl.ds(1, 32, stride=2), :] = rows[:, 128 * h : 128 * h + 128]
    u_b[...] = u1_b[...]
    unpack_shell(UP, recv, (u_b,), bit_x, bit_y)
    for k in (0, 21):
        u_r[k] = jnp.zeros((40, 256), F32)
        u_b[k] = jnp.zeros((40, 256), F32)
    row = iota((8, 128), 0)
    y0 = is_zero(bit_y)
    in_y = (y0 & (row != 7)) | (jnp.logical_not(y0) & (row != 0))
    own_start = pl.multiple_of(32 * bit_y, 32)
    side_start = pl.multiple_of(32 - 8 * bit_y, 8)
    for n in range(20):
        for h in range(2):
            lanes = slice(128 * h, 128 * h + 128)
            side = jnp.where(in_y, tall[n, h, pl.ds(side_start, 8), :], 0.0)
            u_b[1 + n, 0:32, lanes] = u_b[1 + n, 0:32, lanes] + tall[n, h, pl.ds(own_start, 32), :]
            u_b[1 + n, 32:40, lanes] = u_b[1 + n, 32:40, lanes] + side
    mask = odd(40, 256)
    for _ in range(2):
        half_sweep(u_r, u_b, f_r, i_r, 1, 21, True, mask, 1.0, 0)
        half_sweep(u_b, u_r, f_b, i_b, 1, 21, False, mask, 1.0, 0)
    own = odd(32, 128)
    for t in range(16):
        red, black = u_r[3 + t, 0:32, 0:128], u_b[3 + t, 0:32, 0:128]
        out[0, 2 * t] = jnp.where(own, black, red)
        out[0, 2 * t + 1] = jnp.where(own, red, black)


def swap_cores(x):
    return lax.ppermute(x, "level", [(0, 1), (1, 0)])


def to_slabs(x, up_first):
    pairs = []
    for s in range(SLABS - 1):
        for m in range(8):
            low, high = s * 8 + m, (s + 1) * 8 + m
            pairs.append((low, high) if (m < 4) == up_first else (high, low))
    return lax.ppermute(x, ALL, pairs)


def exchange(shell, packed, smem):
    got = lax.all_to_all(packed, LB, split_axis=0, concat_axis=0, tiled=True)
    leaving = run(functools.partial(cross_kernel, shell), [(4, shell.nz, 8, 128)], smem, [got])
    cross = to_slabs(leaving, False)
    sent = run(
        functools.partial(mid_kernel, shell), [(8, shell.got, 8, 128)], smem, [got, cross],
        [(12, shell.nz, 8, 128)],
    )
    return lax.all_to_all(sent, LB, split_axis=0, concat_axis=0, tiled=True)


def body(u_init, source, coeffs, brick_map):
    meta = jnp.stack([lax.axis_index("slab"), lax.axis_index(LB)]).astype(jnp.int32)
    smem = [meta, brick_map]
    fine = (22, 40, 256)
    packed = run(first_kernel, [(8, DOWN.sent, 8, 128)], smem, [u_init, source, coeffs])
    halo = exchange(DOWN, packed, smem)
    rc, u_b, f_r, f_b, i_r, i_b = run(
        fine_down_kernel, [(2, 8, 16, 128)] + [fine] * 5, smem, [u_init, source, coeffs, halo],
        [fine, (2, 16, 32, 128), (256, 128)],
    )
    boxes = [rc] + [
        lax.ppermute(rc, "bottom", [(i, (i + d) % 4) for i in range(4)]) for d in range(1, 4)
    ]
    boxes = boxes + [swap_cores(box) for box in boxes]
    leaving = run(faces_kernel, [(4, 2, 5, 16, 128)], smem, boxes, [(8, 2, 8, 16, 128)])
    cross = to_slabs(leaving, True)
    other = swap_cores(cross)
    coarse = (28, 32, 128)
    faces = (4, 2, 5, 16, 128)
    rb, rb_send, ec_b, r_r, r_b, ci_r, ci_b = run(
        coarse_down_kernel, [(22, 16, 128), (18, 16, 128)] + [coarse] * 5, smem, boxes + [cross, other],
        [(8, 2, 8, 16, 128), faces, faces, coarse, coarse, coarse, (2, 22, 32, 128), (352, 128)],
    )
    packed = run(up_pack_kernel, [(8, UP.sent, 8, 128)], smem, [u_b])
    up_halo = exchange(UP, packed, smem)
    cross = to_slabs(rb_send, True)
    other = swap_cores(cross)
    bottom = (28, 16, 128)
    es, part = run(
        bottom_kernel, [(22, 16, 128), (SLABS, 8, 128)], [meta], [rb, cross, other],
        [bottom] * 6 + [(18, 16, 128)] * 2,
    )
    sums = lax.all_to_all(part, "slab", split_axis=0, concat_axis=0, tiled=True)
    return run(
        up_kernel, [(1, 32, 32, 128)], smem,
        [sums, es, ec_b, r_r, r_b, ci_r, ci_b, u_b, f_r, f_b, i_r, i_b, up_halo],
        [coarse, coarse, (352, 128), (22, 32, 128), (640, 128), (20, 2, 64, 128), fine, fine],
    )


def solution(mesh):
    placed = P(ALL, None, None, None)
    return jax.shard_map(
        body, mesh=mesh, in_specs=(placed, placed, placed, P()), out_specs=placed, check_vma=False
    )
```

time: 1400 us -> 150 us (0.11); the launches traced: 1380 us -> 149 us
  local copies, waits for them, and re-layouts: 472 us -> 7.04 us
  blocking collectives: 393 us -> 63.8 us
  starting transfers between devices: 183 us -> 23.8 us
  other arithmetic: 153 us -> 0.07 us
  waiting for transfers between devices: 153 us -> 14.1 us
  Pallas kernels: 0 us -> 39.5 us
  between operations: 29.4 us -> 0.15 us
    all_gather x17 -> x0, blocking collectives: 393 us -> none  [fill_ghosts(): lax.all_gather(outgoing[None], ('level', 'bottom'), axis=0, tiled=True)]
    scatter x180 -> x0, local copies, waits for them, and re-layouts: 308 us -> none  [the longest x18 89 us: fill_ghosts(): padded = padded.at[1:-1, 1:-1, -1].set(jnp.where(bit_x == 0, ghost_x, 0.0))]
    all_gather x2 -> x0, waiting for transfers between devices: 112 us -> none  [the longest x1 61.9 us: body(): lax.all_gather(bottom_coef[None], ('slab', 'level', 'bottom'), axis=0, ti...]
    all_to_all x18 -> x1, starting transfers between devices: 86.7 us -> 5.28 us  [exchange(): return lax.all_to_all(sent, LB, split_axis=0, concat_axis=0, tiled=True)]
    ppermute x36 -> x13, starting transfers between devices: 96.6 us -> 18.5 us  [the longest x4 9.81 us: to_slabs(): return lax.ppermute(x, ALL, pairs)]
    select_n x128 -> x0, other arithmetic: 72.8 us -> none  [the longest x30 51.4 us: relax_colour(): return jnp.where(parity_mask(values.shape) == colour, update, values)]
    all_to_all x0 -> x4, blocking collectives: none -> 63.8 us  [the longest x2 26.9 us: exchange(): got = lax.all_to_all(packed, LB, split_axis=0, concat_axis=0, tiled=True)]
    reshape x8 -> x0, local copies, waits for them, and re-layouts: 50.6 us -> none  [the longest x2 40.5 us: restrict(): values.reshape(values.shape[0] // 2, 2, values.shape[1] // 2, 2, values.s...]
  transfers between devices with their start and end apart: 56 -> 14, of which waited for: 18 -> 7; matrix products, arithmetic and copies ran while one was open for 10% -> 0% of each run, Pallas kernels for 0% -> 9%
where the time goes in v1:
time: 150 us; the launch traced here: 149 us
  blocking collectives  63.8 us (43%)
  Pallas kernels  39.5 us (26%)
  starting transfers between devices  23.8 us (16%)
  waiting for transfers between devices  14.1 us (9%)
  local copies, waits for them, and re-layouts  7.04 us (5%)
    pallas_call x11, Pallas kernels, run(): pl.pallas_call(kernel, out_shape=shapes[0] if single else shapes, in_spec...  39.5 us
    all_to_all x2, blocking collectives, exchange(): got = lax.all_to_all(packed, LB, split_axis=0, concat_axis=0, tiled=True)  26.9 us
    all_to_all x1, blocking collectives, body(): sums = lax.all_to_all(part, 'slab', split_axis=0, concat_axis=0, tiled=True)  18.8 us
    all_to_all x1, blocking collectives, exchange(): return lax.all_to_all(sent, LB, split_axis=0, concat_axis=0, tiled=True)  18.2 us
    ppermute x4, starting transfers between devices, to_slabs(): return lax.ppermute(x, ALL, pairs)  9.81 us
    ppermute x4, waiting for transfers between devices, to_slabs(): return lax.ppermute(x, ALL, pairs)  9.11 us
    unnamed x25, local copies, waits for them, and re-layouts  7.04 us
    ppermute x6, starting transfers between devices, swap_cores(): return lax.ppermute(x, 'level', [(0, 1), (1, 0)])  5.74 us
  transfers between devices with their start and end apart: 14, of which 7 were waited for; matrix products, arithmetic and copies ran while one was open for 0% of the time, Pallas kernels for 9%

profile of v1, /device:TPU:1, one launch (start us, length us, event | category | flops | bytes accessed | tf_op | source)
XLA Modules:
  0.0 148.6 jit_solution(5410856108204994638)
XLA Ops:
  0.0 0.0 copy-start.11
  0.0 0.7 copy-done.11
  0.7 0.1 copy.14.bricks
  0.8 0.1 pad_add_fusion.meta
  0.8 1.0 copy-done
  1.9 0.0 copy-start.1
  1.9 1.0 copy-done.1
  2.9 0.0 copy-start.3
  2.9 1.0 copy-done.3
  4.0 1.6 %shard_map.46 = f32[8,21,8,128]{3,2,1,0:T(8,128)S(1)} custom-call(s32[2]{0:T(128)S(1)} %pad_add_fusion.meta, s32[16,8]{1,0:T(8,128)S(1)} %copy.14.bricks, f32[1,32,32,128]{3,2,1,0:T(8,128)S(1)} %copy-done, f32[1,32,32,128]{3,2,1,0:T(8,128)S(1)} %copy-done.1, f32[1,32,32,128]{3,2,1,0:T(8,128)S(1)} %copy-done.3), custom_call_target="tpu_custom_call" | custom-call | tf_op jit(solution)/shard_map/pallas_call | solution.py:23
  5.6 16.9 %all_to_all.25.recv = f32[8,21,8,128]{3,2,1,0:T(8,128)S(1)} all-to-all(f32[8,21,8,128]{3,2,1,0:T(8,128)S(1)} %shard_map.46), channel_id=1, replica_groups=mesh['slab'=16,'level'=2,'bottom'=4] {'level','bottom'}, dimensions={0} | all-to-all | bytes 1376256 | tf_op jit(solution)/shard_map/all_to_all | solution.py:533
  22.5 0.7 shard_map.47
  23.2 3.1 %collective-permute-start = (f32[4,12,8,128]{3,2,1,0:T(8,128)S(1)}, f32[4,12,8,128]{3,2,1,0:T(8,128)S(1)}, u32[]{:S(2)}, u32[]{:S(2)}) collective-permute-start(f32[4,12,8,128]{3,2,1,0:T(8,128)S(1)} %shard_map.47), channel_id=1, source_target_pairs={{8,0},{9,1},{10,2},{11,3},{4,12},{5,13},{6,14},{7,15},{16,8},{17,9... | collective-permute-start | bytes 589832 | tf_op jit(solution)/shard_map/ppermute | solution.py:529
  26.3 2.6 %collective-permute-done.cross = f32[4,12,8,128]{3,2,1,0:T(8,128)S(1)} collective-permute-done((f32[4,12,8,128]{3,2,1,0:T(8,128)S(1)}, f32[4,12,8,128]{3,2,1,0:T(8,128)S(1)}, u32[]{:S(2)}, u32[]{:S(2)}) %collective-permute-start) | collective-permute-done | bytes 196640 | tf_op jit(solution)/shard_map/ppermute | solution.py:529
  28.9 1.3 shard_map.48
  30.2 0.0 copy-start.2
  30.2 0.0 copy-start.4
  30.3 18.2 %all_to_all.26.recv = f32[8,25,8,128]{3,2,1,0:T(8,128)S(1)} all-to-all(f32[8,25,8,128]{3,2,1,0:T(8,128)S(1)} %shard_map.48), channel_id=1, replica_groups=mesh['slab'=16,'level'=2,'bottom'=4] {'level','bottom'}, dimensions={0} | all-to-all | bytes 1638400 | tf_op jit(solution)/shard_map/all_to_all | solution.py:540
  48.4 0.0 copy-done.2
  48.4 0.0 copy-done.4
  48.4 8.3 %shard_map.49 = (f32[2,8,16,128]{3,2,1,0:T(8,128)S(1)}, f32[22,40,256]{2,1,0:T(8,128)S(1)}, f32[22,40,256]{2,1,0:T(8,128)}, f32[22,40,256]{2,1,0:T(8,128)}, f32[...) custom-call(s32[2]{0:T(128)S(1)} %pad_add_fusion.meta, s32[16,8]{1,0:T(8,128)S(1)} %copy.14.bricks, ...), custom_call_target="tpu_custom_call" | custom-call | tf_op jit(solution)/shard_map/pallas_call | solution.py:23
  56.7 0.4 collective-permute-start.1
  57.1 1.7 %collective-permute-start.2 = (f32[2,8,16,128]{3,2,1,0:T(8,128)S(1)}, f32[2,8,16,128]{3,2,1,0:T(8,128)S(1)}, u32[]{:S(2)}, u32[]{:S(2)}) collective-permute-start(f32[2,8,16,128]{3,2,1,0:T(8,128)S(1)} %get-tuple-element.20.refs_0_), channel_id=1, source_target_pairs={{0,2},{1,3},{2,0},{3,1},{4,6},{5,7},{6,4},{7,5},{8,10},{9,11},{10,... | collective-permute-start | bytes 393224 | tf_op jit(solution)/shard_map/ppermute | solution.py:554
  58.8 0.9 collective-permute-start.3
  59.7 1.2 collective-permute-start.4
  60.9 2.6 %collective-permute-done.1.refs_1_ = f32[2,8,16,128]{3,2,1,0:T(8,128)S(1)} collective-permute-done((f32[2,8,16,128]{3,2,1,0:T(8,128)S(1)}, f32[2,8,16,128]{3,2,1,0:T(8,128)S(1)}, u32[]{:S(2)}, u32[]{:S(2)}) %collective-permute-start.1) | collective-permute-done | bytes 131104 | tf_op jit(solution)/shard_map/ppermute | solution.py:554
  63.5 3.2 %collective-permute-start.5 = (f32[2,8,16,128]{3,2,1,0:T(8,128)S(1)}, f32[2,8,16,128]{3,2,1,0:T(8,128)S(1)}, u32[]{:S(2)}, u32[]{:S(2)}) collective-permute-start(f32[2,8,16,128]{3,2,1,0:T(8,128)S(1)} %collective-permute-done.1.refs_1_), channel_id=1, source_target_pairs={{0,4},{4,0},{1,5},{5,1},{2,6},{6,2},{3,7},{7,3},{8,12},{12,8},{9,1... | collective-permute-start | bytes 393224 | tf_op jit(solution)/shard_map/ppermute | solution.py:520
  66.7 0.0 collective-permute-done.2.refs_2_
  66.7 0.0 collective-permute-start.6
  66.7 0.0 collective-permute-done.3.refs_3_
  66.7 0.6 collective-permute-start.7
  67.3 0.0 collective-permute-done.4.refs_4_
  67.3 0.4 collective-permute-done.5.refs_5_
  67.7 0.4 collective-permute-done.6.refs_6_
  68.0 0.3 collective-permute-done.7.refs_7_
  68.3 0.8 shard_map.50
  69.1 1.3 collective-permute-start.8
  70.4 6.5 %collective-permute-done.8.refs_8_ = f32[4,2,5,16,128]{4,3,2,1,0:T(8,128)S(1)} collective-permute-done((f32[4,2,5,16,128]{4,3,2,1,0:T(8,128)S(1)}, f32[4,2,5,16,128]{4,3,2,1,0:T(8,128)S(1)}, u32[]{:S(2)}, u32[]{:S(2)}) %collective-permute-start.8) | collective-permute-done | bytes 327712 | tf_op jit(solution)/shard_map/ppermute | solution.py:529
  76.9 0.5 collective-permute-start.9
  77.4 0.9 shard_map.53
  78.3 10.0 %all_to_all.27.recv = f32[8,7,8,128]{3,2,1,0:T(8,128)S(1)} all-to-all(f32[8,7,8,128]{3,2,1,0:T(8,128)S(1)} %shard_map.53), channel_id=1, replica_groups=mesh['slab'=16,'level'=2,'bottom'=4] {'level','bottom'}, dimensions={0} | all-to-all | bytes 458752 | tf_op jit(solution)/shard_map/all_to_all | solution.py:533
  88.3 0.7 shard_map.54
  89.0 4.1 %collective-permute-start.12 = (f32[4,4,8,128]{3,2,1,0:T(8,128)S(1)}, f32[4,4,8,128]{3,2,1,0:T(8,128)S(1)}, u32[]{:S(2)}, u32[]{:S(2)}) collective-permute-start(f32[4,4,8,128]{3,2,1,0:T(8,128)S(1)} %shard_map.54), channel_id=1, source_target_pairs={{8,0},{9,1},{10,2},{11,3},{4,12},{5,13},{6,14},{7,15},{16,8},{17,9... | collective-permute-start | bytes 196616 | tf_op jit(solution)/shard_map/ppermute | solution.py:529
  93.1 0.0 collective-permute-done.9.refs_9_
  93.1 7.3 %shard_map.51 = (f32[22,16,128]{2,1,0:T(8,128)S(1)}, f32[18,16,128]{2,1,0:T(8,128)}, f32[28,32,128]{2,1,0:T(8,128)S(1)}, f32[28,32,128]{2,1,0:T(8,128)S(1)}, f32...) custom-call(s32[2]{0:T(128)S(1)} %pad_add_fusion.meta, s32[16,8]{1,0:T(8,128)S(1)} %copy.14.bricks, ...), custom_call_target="tpu_custom_call" | custom-call | tf_op jit(solution)/shard_map/pallas_call | solution.py:23
  100.5 0.0 copy-start.6
  100.5 1.3 collective-permute-start.10
  101.8 0.0 collective-permute-done.12.cross
  101.8 1.6 %shard_map.55 = f32[8,9,8,128]{3,2,1,0:T(8,128)} custom-call(s32[2]{0:T(128)S(1)} %pad_add_fusion.meta, s32[16,8]{1,0:T(8,128)S(1)} %copy.14.bricks, f32[8,7,8,128]{3,2,1,0:T(8,128)S(1)} %all_to_all.27.recv, f32[4,4,8,128]{3,2,1,0:T(8,128)S(1)} %collective-permute-done.12.cross), custom_call_target="tpu_custom_call" | custom-call | tf_op jit(solution)/shard_map/pallas_call | solution.py:23
  103.4 0.0 copy-done.6
  103.4 5.3 %all-to-all-start.4 = ((f32[8,9,8,128]{3,2,1,0:T(8,128)}), f32[8,9,8,128]{3,2,1,0:T(8,128)S(1)}, u32[]{:S(2)}, u32[]{:S(2)}) async-start(f32[8,9,8,128]{3,2,1,0:T(8,128)} %shard_map.55), calls=%async_computation.4 | async-start | bytes 589824 | tf_op jit(solution)/shard_map/all_to_all | solution.py:540
  108.6 0.0 collective-permute-done.10.one
  108.6 0.2 collective-permute-start.11
  108.8 1.5 collective-permute-done.11.two
  110.3 0.9 copy-done.7
  111.2 3.3 %shard_map.52 = (f32[22,16,128]{2,1,0:T(8,128)S(1)}, f32[16,8,128]{2,1,0:T(8,128)S(1)}) custom-call(s32[2]{0:T(128)S(1)} %pad_add_fusion.meta, f32[22,16,128]{2,1,0:T(8,128)S(1)} %copy-done.7, f32[18,16,128]{2,1,0:T(8,128)} %collective-permute-done.10.one, f32[18,16,128]{2,1,0:T(8,128)S(1)} %collective-permute-done.11.two), custom_call_target="tpu_custom_call" | custom-call | tf_op jit(solution)/shard_map/pallas_call | solution.py:23
  114.5 0.0 copy-start.8
  114.5 0.7 copy-done.8
  115.2 0.6 copy-done.10
  115.8 0.0 all-to-all-done.4.recv
  115.8 18.8 %all_to_all.28.sums = f32[16,8,128]{2,1,0:T(8,128)S(1)} all-to-all(f32[16,8,128]{2,1,0:T(8,128)} %copy-done.10), channel_id=1, replica_groups=mesh['slab'=16,'level'=2,'bottom'=4] {'slab'}, dimensions={0} | all-to-all | bytes 131072 | tf_op jit(solution)/shard_map/all_to_all | solution.py:575
  134.6 0.0 copy-done.5
  134.6 0.9 copy-done.9
  135.5 13.1 %shard_map.56 = f32[1,32,32,128]{3,2,1,0:T(8,128)} custom-call(s32[2]{0:T(128)S(1)} %pad_add_fusion.meta, s32[16,8]{1,0:T(8,128)S(1)} %copy.14.bricks, f32[16,8,128]{2,1,0:T(8,128)S(1)} %all_to_all.28.sums, f32[22,16,128]{2,1,0:T(8,128)S(1)} %copy-done.9, f32[28,32,128]{2,1,0:T(8,128)S(1)} %get-tuple-element.25.ec_b, ...), custom_call_target="tpu_custom_call" | custom-call | tf_op jit(solution)/shard_map/pallas_call | solution.py:23
  (5 shorter events, 0.0 us)
Async XLA Ops:
  0.0 0.7 copy-start.11
  0.8 1.0 copy-start
  1.9 1.0 copy-start.1
  2.9 1.0 copy-start.3
  23.2 5.7 %collective-permute-start = (f32[4,12,8,128]{3,2,1,0:T(8,128)S(1)}, f32[4,12,8,128]{3,2,1,0:T(8,128)S(1)}, u32[]{:S(2)}, u32[]{:S(2)}) collective-permute-start(f32[4,12,8,128]{3,2,1,0:T(8,128)S(1)} %shard_map.47), channel_id=1, source_target_pairs={{8,0},{9,1},{10,2},{11,3},{4,12},{5,13},{6,14},{7,15},{16,8},{17,9... | collective-permute-start | bytes 589832 | tf_op jit(solution)/shard_map/ppermute | solution.py:529
  30.2 18.2 %copy-start.2 = (f32[1,32,32,128]{3,2,1,0:T(8,128)S(1)}, f32[1,32,32,128]{3,2,1,0:T(8,128)}, u32[]{:S(2)}) copy-start(f32[1,32,32,128]{3,2,1,0:T(8,128)} %f.3) | copy-start | bytes 1572868
  30.2 18.2 %copy-start.4 = (f32[1,32,32,128]{3,2,1,0:T(8,128)S(1)}, f32[1,32,32,128]{3,2,1,0:T(8,128)}, u32[]{:S(2)}) copy-start(f32[1,32,32,128]{3,2,1,0:T(8,128)} %a.3) | copy-start | bytes 1572868
  56.7 6.7 %collective-permute-start.1 = (f32[2,8,16,128]{3,2,1,0:T(8,128)S(1)}, f32[2,8,16,128]{3,2,1,0:T(8,128)S(1)}, u32[]{:S(2)}, u32[]{:S(2)}) collective-permute-start(f32[2,8,16,128]{3,2,1,0:T(8,128)S(1)} %get-tuple-element.20.refs_0_), channel_id=1, source_target_pairs={{0,1},{1,2},{2,3},{3,0},{4,5},{5,6},{6,7},{7,4},{8,9},{9,10},{10,1... | collective-permute-start | bytes 393224 | tf_op jit(solution)/shard_map/ppermute | solution.py:554
  57.1 9.6 %collective-permute-start.2 = (f32[2,8,16,128]{3,2,1,0:T(8,128)S(1)}, f32[2,8,16,128]{3,2,1,0:T(8,128)S(1)}, u32[]{:S(2)}, u32[]{:S(2)}) collective-permute-start(f32[2,8,16,128]{3,2,1,0:T(8,128)S(1)} %get-tuple-element.20.refs_0_), channel_id=1, source_target_pairs={{0,2},{1,3},{2,0},{3,1},{4,6},{5,7},{6,4},{7,5},{8,10},{9,11},{10,... | collective-permute-start | bytes 393224 | tf_op jit(solution)/shard_map/ppermute | solution.py:554
  58.8 7.9 %collective-permute-start.3 = (f32[2,8,16,128]{3,2,1,0:T(8,128)S(1)}, f32[2,8,16,128]{3,2,1,0:T(8,128)S(1)}, u32[]{:S(2)}, u32[]{:S(2)}) collective-permute-start(f32[2,8,16,128]{3,2,1,0:T(8,128)S(1)} %get-tuple-element.20.refs_0_), channel_id=1, source_target_pairs={{0,3},{1,0},{2,1},{3,2},{4,7},{5,4},{6,5},{7,6},{8,11},{9,8},{10,9... | collective-permute-start | bytes 393224 | tf_op jit(solution)/shard_map/ppermute | solution.py:554
  59.7 7.6 %collective-permute-start.4 = (f32[2,8,16,128]{3,2,1,0:T(8,128)S(1)}, f32[2,8,16,128]{3,2,1,0:T(8,128)S(1)}, u32[]{:S(2)}, u32[]{:S(2)}) collective-permute-start(f32[2,8,16,128]{3,2,1,0:T(8,128)S(1)} %get-tuple-element.20.refs_0_), channel_id=1, source_target_pairs={{0,4},{4,0},{1,5},{5,1},{2,6},{6,2},{3,7},{7,3},{8,12},{12,8},{9,1... | collective-permute-start | bytes 393224 | tf_op jit(solution)/shard_map/ppermute | solution.py:520
  63.5 4.2 %collective-permute-start.5 = (f32[2,8,16,128]{3,2,1,0:T(8,128)S(1)}, f32[2,8,16,128]{3,2,1,0:T(8,128)S(1)}, u32[]{:S(2)}, u32[]{:S(2)}) collective-permute-start(f32[2,8,16,128]{3,2,1,0:T(8,128)S(1)} %collective-permute-done.1.refs_1_), channel_id=1, source_target_pairs={{0,4},{4,0},{1,5},{5,1},{2,6},{6,2},{3,7},{7,3},{8,12},{12,8},{9,1... | collective-permute-start | bytes 393224 | tf_op jit(solution)/shard_map/ppermute | solution.py:520
  66.7 1.3 collective-permute-start.6
  66.7 1.6 %collective-permute-start.7 = (f32[2,8,16,128]{3,2,1,0:T(8,128)S(1)}, f32[2,8,16,128]{3,2,1,0:T(8,128)S(1)}, u32[]{:S(2)}, u32[]{:S(2)}) collective-permute-start(f32[2,8,16,128]{3,2,1,0:T(8,128)S(1)} %collective-permute-done.3.refs_3_), channel_id=1, source_target_pairs={{0,4},{4,0},{1,5},{5,1},{2,6},{6,2},{3,7},{7,3},{8,12},{12,8},{9,1... | collective-permute-start | bytes 393224 | tf_op jit(solution)/shard_map/ppermute | solution.py:520
  69.1 7.8 %collective-permute-start.8 = (f32[4,2,5,16,128]{4,3,2,1,0:T(8,128)S(1)}, f32[4,2,5,16,128]{4,3,2,1,0:T(8,128)S(1)}, u32[]{:S(2)}, u32[]{:S(2)}) collective-permute-start(f32[4,2,5,16,128]{4,3,2,1,0:T(8,128)S(1)} %shard_map.50), channel_id=1, source_target_pairs={{0,8},{1,9},{2,10},{3,11},{12,4},{13,5},{14,6},{15,7},{8,16},{9,17... | collective-permute-start | bytes 983048 | tf_op jit(solution)/shard_map/ppermute | solution.py:529
  76.9 16.2 %collective-permute-start.9 = (f32[4,2,5,16,128]{4,3,2,1,0:T(8,128)S(1)}, f32[4,2,5,16,128]{4,3,2,1,0:T(8,128)S(1)}, u32[]{:S(2)}, u32[]{:S(2)}) collective-permute-start(f32[4,2,5,16,128]{4,3,2,1,0:T(8,128)S(1)} %collective-permute-done.8.refs_8_), channel_id=1, source_target_pairs={{0,4},{4,0},{1,5},{5,1},{2,6},{6,2},{3,7},{7,3},{8,12},{12,8},{9,1... | collective-permute-start | bytes 983048 | tf_op jit(solution)/shard_map/ppermute | solution.py:520
  89.0 12.8 %collective-permute-start.12 = (f32[4,4,8,128]{3,2,1,0:T(8,128)S(1)}, f32[4,4,8,128]{3,2,1,0:T(8,128)S(1)}, u32[]{:S(2)}, u32[]{:S(2)}) collective-permute-start(f32[4,4,8,128]{3,2,1,0:T(8,128)S(1)} %shard_map.54), channel_id=1, source_target_pairs={{8,0},{9,1},{10,2},{11,3},{4,12},{5,13},{6,14},{7,15},{16,8},{17,9... | collective-permute-start | bytes 196616 | tf_op jit(solution)/shard_map/ppermute | solution.py:529
  100.5 2.9 %copy-start.6 = (f32[22,16,128]{2,1,0:T(8,128)}, f32[22,16,128]{2,1,0:T(8,128)S(1)}, u32[]{:S(2)}) copy-start(f32[22,16,128]{2,1,0:T(8,128)S(1)} %get-tuple-element.21.rb) | copy-start | bytes 540676
  100.5 8.2 %collective-permute-start.10 = (f32[18,16,128]{2,1,0:T(8,128)}, f32[18,16,128]{2,1,0:T(8,128)}, u32[]{:S(2)}, u32[]{:S(2)}) collective-permute-start(f32[18,16,128]{2,1,0:T(8,128)} %get-tuple-element.22), channel_id=1, source_target_pairs={{0,8},{1,9},{2,10},{3,11},{12,4},{13,5},{14,6},{15,7},{8,16},{9,17... | collective-permute-start | bytes 442376 | tf_op jit(solution)/shard_map/ppermute | solution.py:529
  103.4 12.5 %all-to-all-start.4 = ((f32[8,9,8,128]{3,2,1,0:T(8,128)}), f32[8,9,8,128]{3,2,1,0:T(8,128)S(1)}, u32[]{:S(2)}, u32[]{:S(2)}) async-start(f32[8,9,8,128]{3,2,1,0:T(8,128)} %shard_map.55), calls=%async_computation.4 | async-start | bytes 589824 | tf_op jit(solution)/shard_map/all_to_all | solution.py:540
  108.6 26.0 %copy-start.5 = (f32[28,32,128]{2,1,0:T(8,128)S(1)}, f32[28,32,128]{2,1,0:T(8,128)}, u32[]{:S(2)}) copy-start(f32[28,32,128]{2,1,0:T(8,128)} %get-tuple-element.29.ci_b) | copy-start | bytes 1376260
  108.6 1.7 %collective-permute-start.11 = (f32[18,16,128]{2,1,0:T(8,128)}, f32[18,16,128]{2,1,0:T(8,128)S(1)}, u32[]{:S(2)}, u32[]{:S(2)}) collective-permute-start(f32[18,16,128]{2,1,0:T(8,128)} %collective-permute-done.10.one), channel_id=1, source_target_pairs={{0,4},{4,0},{1,5},{5,1},{2,6},{6,2},{3,7},{7,3},{8,12},{12,8},{9,1... | collective-permute-start | bytes 442376 | tf_op jit(solution)/shard_map/ppermute | solution.py:520
  110.3 0.9 copy-start.7
  114.5 0.7 copy-start.8
  115.2 0.6 copy-start.10
  134.6 0.9 copy-start.9

commit v2 on v1

--- a/solution.py
+++ b/solution.py
@@ -11,6 +11,7 @@
 LB = ("level", "bottom")
 ALL = ("slab", "level", "bottom")
 SLABS = 16
+OWN = 5
 F32 = jnp.float32
 VMEM_SPEC = pl.BlockSpec(memory_space=pltpu.VMEM)
 SMEM_SPEC = pl.BlockSpec(memory_space=pltpu.SMEM)
@@ -51,42 +52,47 @@
 
 
 class Shell:
-    def __init__(self, low, high, comps, arrays):
-        self.low, self.high, self.comps, self.arrays = low, high, comps, arrays
+    def __init__(self, low, high, arrays):
+        self.low, self.high, self.arrays = low, high, arrays
         self.planes = math.ceil(len(low) / 4)
         self.nz = 4 * self.planes
-        self.ny = 2 * len(comps)
+        self.ny = 2 * arrays
         self.strips = 8 * arrays
         self.nx = math.ceil(self.strips / 16)
         self.sent = self.nz + self.ny + self.nx
         self.nz2 = 5 * self.planes
-        self.y2 = self.nz2 + 1
+        self.side = math.ceil(self.nz2 / 16)
+        self.y2 = self.nz2 + self.side
         self.x2 = self.y2 + self.ny
         self.got = self.x2 + self.nx
-        assert 5 * self.planes <= 16 and self.strips % 16 + self.ny <= 16
+        self.first = min(16 * self.side - self.nz2, self.ny)
+        assert self.strips + self.ny - self.first <= 16 * self.nx
+
+    def edge(self, i):
+        if i < self.first:
+            pos = self.nz2 + i
+            return self.nz2 + pos // 16, pos % 16
+        pos = self.strips + i - self.first
+        return self.x2 + pos // 16, pos % 16
 
 
 DOWN = Shell(
-    [(0, 0), (0, 1), (0, 2)] + [(c, t) for c in (1, 2, 3, 4) for t in (0, 1)],
-    [(0, 13), (0, 14), (0, 15)] + [(c, t) for c in (1, 2, 3, 4) for t in (14, 15)],
-    [(0,), (1, 2), (3, 4)],
+    [(c, t) for c in (0, 1, 3) for t in range(4)] + [(c, t) for c in (2, 4) for t in range(3)],
+    [(c, 15 - t) for c in (0, 1, 3) for t in range(4)] + [(c, 15 - t) for c in (2, 4) for t in range(3)],
     5,
 )
-UP = Shell([(0, 0), (0, 1)], [(0, 14), (0, 15)], [(0,)], 1)
-
-
-def merge_strips(strips, first=0, base=None):
+
+
+def merge_strips(placed, base=None):
     group = iota((8, 128), 1) // 8
     total = jnp.zeros((8, 128), F32) if base is None else base
-    for i, strip in enumerate(strips):
-        pos = first + i
+    for pos, strip in placed:
         moved = pltpu.roll(strip, 8 * pos, 1) if pos else strip
         total = jnp.where(group == pos, moved, total)
     return total
 
 
 def pack_shell(shell, get, out, bit_x, bit_y):
-    row = iota((8, 128), 0)
     x0, y0 = is_zero(bit_x), is_zero(bit_y)
     for first, faces in ((0, shell.low), (4, shell.high)):
         for i, (c, t) in enumerate(faces):
@@ -95,22 +101,14 @@
     for k in range(8):
         strips = []
         for tl in range(2):
-            cells = [get(c, 2 * k + tl) for c in range(shell.arrays)]
-            rows = [jnp.where(y0, v[24:32], v[0:8]) for v in cells]
-            for ci, comp in enumerate(shell.comps):
-                tile = rows[comp[0]]
-                if len(comp) == 2:
-                    red, black = rows[comp[0]], rows[comp[1]]
-                    red = jnp.where(y0, pltpu.roll(red, 4, 0), red)
-                    black = jnp.where(y0, black, pltpu.roll(black, 4, 0))
-                    tile = jnp.where(row < 4, red, black)
-                out[k, shell.nz + tl * len(shell.comps) + ci] = tile
-            for v in cells:
+            for c in range(shell.arrays):
+                v = get(c, 2 * k + tl)
+                out[k, shell.nz + tl * shell.arrays + c] = jnp.where(y0, v[24:32], v[0:8])
                 for g in range(4):
                     tile = v[8 * g : 8 * g + 8]
                     strips.append(jnp.where(x0, pltpu.roll(tile, 8, 1), tile))
         for i in range(shell.nx):
-            out[k, shell.nz + shell.ny + i] = merge_strips(strips[16 * i : 16 * i + 16])
+            out[k, shell.nz + shell.ny + i] = merge_strips(list(enumerate(strips[16 * i : 16 * i + 16])))
 
 
 def cross_kernel(shell, meta, bricks, recv, out):
@@ -143,57 +141,49 @@
             out[dest, 5 * j + 4] = faces[at_y, 4 * j + gy]
             strips += [strip_of(faces[at_x, 4 * j + g]) for g in range(4)]
             strips.append(strip_of(faces[at_xy, 4 * j + gy]))
-        out[dest, shell.nz2] = merge_strips(strips)
         from_y, from_x, from_xy = bricks[slab, p ^ 2], bricks[slab, p ^ 1], bricks[slab, p ^ 3]
-        y1 = shell.nz
-        out[dest, shell.y2 : shell.x2] = recv[from_y, y1 : y1 + shell.ny]
-        x1 = shell.nz + shell.ny
-        if shell.nx > 1:
-            out[dest, shell.x2 : shell.x2 + shell.nx - 1] = recv[from_x, x1 : x1 + shell.nx - 1]
-        edge = [strip_of(recv[from_xy, y1 + i]) for i in range(shell.ny)]
-        out[dest, shell.x2 + shell.nx - 1] = merge_strips(
-            edge, shell.strips % 16, recv[from_x, x1 + shell.nx - 1]
-        )
-
-
-def unpack_shell(shell, recv, grids, bit_x, bit_y):
-    row, lane = iota((8, 128), 0), iota((8, 128), 1)
-    x0, y0 = is_zero(bit_x), is_zero(bit_y)
+        y1, x1 = shell.nz, shell.nz + shell.ny
+        out[dest, shell.y2 : shell.x2] = recv[from_y, y1:x1]
+        placed = {}
+        for i, strip in enumerate(strips):
+            placed.setdefault(shell.nz2 + i // 16, []).append((i % 16, strip))
+        for i in range(shell.ny):
+            tile, pos = shell.edge(i)
+            placed.setdefault(tile, []).append((pos, strip_of(recv[from_xy, y1 + i])))
+        for i in range(shell.nx):
+            tile = recv[from_x, x1 + i]
+            out[dest, shell.x2 + i] = merge_strips(placed.get(shell.x2 + i, []), tile)
+        for i in range(shell.side):
+            out[dest, shell.nz2 + i] = merge_strips(placed[shell.nz2 + i])
+
+
+def unpack_shell(shell, recv, grids, bit_x):
+    lane = iota((8, 128), 1)
+    x0 = is_zero(bit_x)
     in_x = (x0 & (lane < 8)) | (jnp.logical_not(x0) & (lane >= 120))
-    in_y = (y0 & (row != 7)) | (jnp.logical_not(y0) & (row != 0))
 
     def strip(tile, pos):
         shift = (jnp.where(bit_x == 0, 0, 120) + 128 - 8 * pos) % 128
         return jnp.where(in_x, pltpu.roll(tile, shift, 1), 0.0)
 
-    def split(comp, tile):
-        if len(comp) == 1:
-            return [tile]
-        moved = pltpu.roll(tile, 4, 0)
-        return [jnp.where(y0, tile, moved), jnp.where(y0, moved, tile)]
-
-    for first, faces, shift in ((0, shell.low, 19), (4, shell.high, -13)):
+    for first, faces, shift in ((0, shell.low, OWN + 16), (4, shell.high, OWN - 16)):
         for i, (c, t) in enumerate(faces):
             k, j = first + i // shell.planes, i % shell.planes
             for g in range(5):
-                tile, side = recv[k, 5 * j + g], strip(recv[k, shell.nz2], 5 * j + g)
-                if g == 4:
-                    tile, side = jnp.where(in_y, tile, 0.0), jnp.where(in_y, side, 0.0)
-                grids[c][shift + t, 8 * g : 8 * g + 8, 0:128] = tile
-                grids[c][shift + t, 8 * g : 8 * g + 8, 128:256] = side
+                n = 5 * j + g
+                rows = slice(8 * g, 8 * g + 8)
+                grids[c][shift + t, rows, 0:128] = recv[k, n]
+                grids[c][shift + t, rows, 128:256] = strip(recv[k, shell.nz2 + n // 16], n % 16)
     for t in range(16):
         k, tl = t // 2, t % 2
-        for ci, comp in enumerate(shell.comps):
-            i = tl * len(shell.comps) + ci
-            tile = recv[k, shell.y2 + i]
-            side = strip(recv[k, shell.x2 + shell.nx - 1], shell.strips % 16 + i)
-            for c, one, two in zip(comp, split(comp, tile), split(comp, side)):
-                grids[c][3 + t, 32:40, 0:128] = jnp.where(in_y, one, 0.0)
-                grids[c][3 + t, 32:40, 128:256] = jnp.where(in_y, two, 0.0)
         for c in range(shell.arrays):
+            i = tl * shell.arrays + c
+            tile, pos = shell.edge(i)
+            grids[c][OWN + t, 32:40, 0:128] = recv[k, shell.y2 + i]
+            grids[c][OWN + t, 32:40, 128:256] = strip(recv[k, tile], pos)
             for g in range(4):
-                i = 4 * (tl * shell.arrays + c) + g
-                grids[c][3 + t, 8 * g : 8 * g + 8, 128:256] = strip(recv[k, shell.x2 + i // 16], i % 16)
+                n = 4 * i + g
+                grids[c][OWN + t, 8 * g : 8 * g + 8, 128:256] = strip(recv[k, shell.x2 + n // 16], n % 16)
 
 
 def pair_of(cells, t, red, mask):
@@ -212,7 +202,7 @@
     pack_shell(DOWN, get, out, bit_x, bit_y)
 
 
-def around(src, k, red, mask, edges):
+def around(src, k, red, mask, edges, cut=None):
     here = src[k]
     rows, cols = here.shape
     above, below = src[k + 1], src[k - 1]
@@ -224,18 +214,20 @@
         up, down = jnp.where(row == 0, 0.0, up), jnp.where(row == rows - 1, 0.0, down)
         if edges == 2:
             left, right = jnp.where(lane == 0, 0.0, left), jnp.where(lane == cols - 1, 0.0, right)
+    if cut is not None:
+        up, down = jnp.where(cut[0], 0.0, up), jnp.where(cut[1], 0.0, down)
     return ((here + other) + (up + down)) + (left + right)
 
 
-def half_sweep(dst, src, force, inverse, lo, hi, red, mask, scale, edges, unroll=2):
+def half_sweep(dst, src, force, inverse, lo, hi, red, mask, scale, edges, cut=None):
     def step(k, carry):
-        total = around(src, k, red, mask, edges)
+        total = around(src, k, red, mask, edges, cut)
         if scale != 1.0:
             total = scale * total
         dst[k] = (force[k] + total) * inverse[k]
         return carry
 
-    lax.fori_loop(lo, hi, step, 0, unroll=unroll)
+    lax.fori_loop(lo, hi, step, 0, unroll=True)
 
 
 def pick(rows, cols, keep):
@@ -249,34 +241,42 @@
     sources = ((u, False), (f, True), (f, False), (a, True), (a, False))
     for t in range(16):
         for grid, (cells, red) in zip(grids, sources):
-            grid[3 + t, 0:32, 0:128] = pair_of(cells, t, red, own)
-    unpack_shell(DOWN, recv, grids, bit_x, bit_y)
-    u_r[0] = jnp.zeros((40, 256), F32)
-    u_r[21] = jnp.zeros((40, 256), F32)
+            grid[OWN + t, 0:32, 0:128] = pair_of(cells, t, red, own)
+    unpack_shell(DOWN, recv, grids, bit_x)
+    zero = jnp.zeros((40, 256), F32)
+    for k in (0, 25):
+        u_r[k] = zero
+        u_b[k] = zero
+    for k in (1, 24):
+        f_b[k] = zero
+        i_b[k] = zero
     row, lane = iota((40, 256), 0), iota((40, 256), 1)
     x0, y0 = is_zero(bit_x, (40, 256)), is_zero(bit_y, (40, 256))
     x1, y1 = jnp.logical_not(x0), jnp.logical_not(y0)
-    inside = (row < 32) | (y0 & (row < 36)) | (y1 & (row >= 36))
+    inside = (row < 32) | (y0 & (row < 39)) | (y1 & (row >= 33))
     inside = inside & ((lane < 128) | (x0 & (lane < 136)) | (x1 & (lane >= 248)))
     no_low = (slab == 0) & (bit_z == 0)
     no_high = (slab == SLABS - 1) & (bit_z == 1)
 
     def invert(k, carry):
-        gone = jnp.where((no_low & (k < 3)) | (no_high & (k >= 19)), 1, 0)
+        gone = jnp.where((no_low & (k < OWN)) | (no_high & (k >= OWN + 16)), 1, 0)
         keep = inside & is_zero(gone, (40, 256))
         i_r[k] = jnp.where(keep, 1.0 / (i_r[k] + 6.0), 0.0)
-        i_b[k] = jnp.where(keep, 1.0 / (i_b[k] + 6.0), 0.0)
+        ends = jnp.where((k == 1) | (k == 24), 1, 0)
+        i_b[k] = jnp.where(keep & is_zero(ends, (40, 256)), 1.0 / (i_b[k] + 6.0), 0.0)
         return carry
 
-    lax.fori_loop(1, 21, invert, 0)
+    lax.fori_loop(1, 25, invert, 0, unroll=4)
     mask = odd(40, 256)
-    for _ in range(2):
-        half_sweep(u_r, u_b, f_r, i_r, 1, 21, True, mask, 1.0, 0)
-        half_sweep(u_b, u_r, f_b, i_b, 1, 21, False, mask, 1.0, 0)
+    cut = (y0 & (row == 0), y1 & (row == 31))
+    half_sweep(u_r, u_b, f_r, i_r, 1, 25, True, mask, 1.0, 0, cut)
+    half_sweep(u_b, u_r, f_b, i_b, 1, 25, False, mask, 1.0, 0)
+    half_sweep(u_r, u_b, f_r, i_r, 2, 24, True, mask, 1.0, 0)
+    half_sweep(u_b, u_r, f_b, i_b, 3, 23, False, mask, 1.0, 0)
     for t in range(16):
-        total = around(u_b, 3 + t, True, mask, 0)[0:32, 0:128]
+        total = around(u_b, OWN + t, True, mask, 0)[0:32, 0:128]
         diag = pair_of(a, t, True, own) + 6.0
-        resid[0, t] = pair_of(f, t, True, own) + total - diag * u_r[3 + t, 0:32, 0:128]
+        resid[0, t] = pair_of(f, t, True, own) + total - diag * u_r[OWN + t, 0:32, 0:128]
         resid[1, t] = a[0, 2 * t] + a[0, 2 * t + 1]
     twice = pick(128, 128, lambda r, c: (r >> 1) == (c & 63)) * 0.125
     row, lane = iota((16, 128), 0), iota((16, 128), 1)
@@ -292,11 +292,6 @@
             rc[i, j] = jnp.where(even, summed[2 * j], summed[2 * j + 1])
 
 
-def up_pack_kernel(meta, bricks, u_b, out):
-    _, _, bit_x, bit_y, _ = place_of(meta, bricks)
-    pack_shell(UP, lambda c, t: u_b[3 + t, 0:32, 0:128], out, bit_x, bit_y)
-
-
 def slot_of(member, me):
     return jnp.where((member >> 2) == (me >> 2), 0, 4) + ((me - member) & 3)
 
@@ -360,7 +355,7 @@
         e_r[k] = r_r[k] * inverse
         return carry
 
-    lax.fori_loop(1, 27, start, 0)
+    lax.fori_loop(1, 27, start, 0, unroll=13)
     mask = odd(32, 128)
     half_sweep(e_b, e_r, r_b, i_b, 1, 27, False, mask, 0.25, 2)
     half_sweep(e_r, e_b, r_r, i_r, 1, 27, True, mask, 0.25, 2)
@@ -373,7 +368,7 @@
         resid[1, n] = a_r[k] + a_b[k]
         return carry
 
-    lax.fori_loop(0, 22, residual, 0, unroll=2)
+    lax.fori_loop(0, 22, residual, 0, unroll=True)
     total = jnp.zeros((352, 128), F32)
     for i in range(2):
         for n in range(22):
@@ -422,11 +417,11 @@
                 g_r[1 + j], i_r[1 + j], e_r[1 + j] = force, inverse, force * inverse
             else:
                 g_b[1 + j], i_b[1 + j] = force, inverse
-    half_sweep(e_b, e_r, g_b, i_b, 1, 27, False, mask, 0.0625, 1, unroll=True)
+    half_sweep(e_b, e_r, g_b, i_b, 1, 27, False, mask, 0.0625, 1)
 
     def sweep(n, carry):
-        half_sweep(e_r, e_b, g_r, i_r, 1, 27, True, mask, 0.0625, 1, unroll=True)
-        half_sweep(e_b, e_r, g_b, i_b, 1, 27, False, mask, 0.0625, 1, unroll=True)
+        half_sweep(e_r, e_b, g_r, i_r, 1, 27, True, mask, 0.0625, 1)
+        half_sweep(e_b, e_r, g_b, i_b, 1, 27, False, mask, 0.0625, 1)
         return carry
 
     lax.fori_loop(0, 7, sweep, 0)
@@ -442,7 +437,7 @@
 
 
 def up_kernel(
-    meta, bricks, sums, es, ec_b, r_r, r_b, ci_r, ci_b, u1_b, f_r, f_b, i_r, i_b, recv, out,
+    meta, bricks, sums, es, ec_b, r_r, r_b, ci_r, ci_b, u1_b, f_r, f_b, i_r, i_b, out,
     e_r, e_b, small, wide, planes, tall, u_r, u_b,
 ):
     slab, _, bit_x, bit_y, bit_z = place_of(meta, bricks)
@@ -489,8 +484,6 @@
         for h in range(2):
             tall[n, h, pl.ds(0, 32, stride=2), :] = rows[:, 128 * h : 128 * h + 128]
             tall[n, h, pl.ds(1, 32, stride=2), :] = rows[:, 128 * h : 128 * h + 128]
-    u_b[...] = u1_b[...]
-    unpack_shell(UP, recv, (u_b,), bit_x, bit_y)
     for k in (0, 21):
         u_r[k] = jnp.zeros((40, 256), F32)
         u_b[k] = jnp.zeros((40, 256), F32)
@@ -503,12 +496,14 @@
         for h in range(2):
             lanes = slice(128 * h, 128 * h + 128)
             side = jnp.where(in_y, tall[n, h, pl.ds(side_start, 8), :], 0.0)
-            u_b[1 + n, 0:32, lanes] = u_b[1 + n, 0:32, lanes] + tall[n, h, pl.ds(own_start, 32), :]
-            u_b[1 + n, 32:40, lanes] = u_b[1 + n, 32:40, lanes] + side
+            u_b[1 + n, 0:32, lanes] = u1_b[3 + n, 0:32, lanes] + tall[n, h, pl.ds(own_start, 32), :]
+            u_b[1 + n, 32:40, lanes] = u1_b[3 + n, 32:40, lanes] + side
     mask = odd(40, 256)
-    for _ in range(2):
-        half_sweep(u_r, u_b, f_r, i_r, 1, 21, True, mask, 1.0, 0)
-        half_sweep(u_b, u_r, f_b, i_b, 1, 21, False, mask, 1.0, 0)
+    f_r, f_b, i_r, i_b = (grid.at[2:24] for grid in (f_r, f_b, i_r, i_b))
+    half_sweep(u_r, u_b, f_r, i_r, 1, 21, True, mask, 1.0, 0)
+    half_sweep(u_b, u_r, f_b, i_b, 2, 20, False, mask, 1.0, 0)
+    half_sweep(u_r, u_b, f_r, i_r, 2, 20, True, mask, 1.0, 0)
+    half_sweep(u_b, u_r, f_b, i_b, 3, 19, False, mask, 1.0, 0)
     own = odd(32, 128)
     for t in range(16):
         red, black = u_r[3 + t, 0:32, 0:128], u_b[3 + t, 0:32, 0:128]
@@ -529,23 +524,26 @@
     return lax.ppermute(x, ALL, pairs)
 
 
-def exchange(shell, packed, smem):
-    got = lax.all_to_all(packed, LB, split_axis=0, concat_axis=0, tiled=True)
+def among(x):
+    return lax.all_to_all(x, LB, split_axis=0, concat_axis=0, tiled=True)
+
+
+def deliver(shell, got, smem):
     leaving = run(functools.partial(cross_kernel, shell), [(4, shell.nz, 8, 128)], smem, [got])
     cross = to_slabs(leaving, False)
     sent = run(
         functools.partial(mid_kernel, shell), [(8, shell.got, 8, 128)], smem, [got, cross],
         [(12, shell.nz, 8, 128)],
     )
-    return lax.all_to_all(sent, LB, split_axis=0, concat_axis=0, tiled=True)
+    return among(sent)
 
 
 def body(u_init, source, coeffs, brick_map):
     meta = jnp.stack([lax.axis_index("slab"), lax.axis_index(LB)]).astype(jnp.int32)
     smem = [meta, brick_map]
-    fine = (22, 40, 256)
+    fine = (26, 40, 256)
     packed = run(first_kernel, [(8, DOWN.sent, 8, 128)], smem, [u_init, source, coeffs])
-    halo = exchange(DOWN, packed, smem)
+    halo = deliver(DOWN, among(packed), smem)
     rc, u_b, f_r, f_b, i_r, i_b = run(
         fine_down_kernel, [(2, 8, 16, 128)] + [fine] * 5, smem, [u_init, source, coeffs, halo],
         [fine, (2, 16, 32, 128), (256, 128)],
@@ -563,8 +561,6 @@
         coarse_down_kernel, [(22, 16, 128), (18, 16, 128)] + [coarse] * 5, smem, boxes + [cross, other],
         [(8, 2, 8, 16, 128), faces, faces, coarse, coarse, coarse, (2, 22, 32, 128), (352, 128)],
     )
-    packed = run(up_pack_kernel, [(8, UP.sent, 8, 128)], smem, [u_b])
-    up_halo = exchange(UP, packed, smem)
     cross = to_slabs(rb_send, True)
     other = swap_cores(cross)
     bottom = (28, 16, 128)
@@ -575,8 +571,8 @@
     sums = lax.all_to_all(part, "slab", split_axis=0, concat_axis=0, tiled=True)
     return run(
         up_kernel, [(1, 32, 32, 128)], smem,
-        [sums, es, ec_b, r_r, r_b, ci_r, ci_b, u_b, f_r, f_b, i_r, i_b, up_halo],
-        [coarse, coarse, (352, 128), (22, 32, 128), (640, 128), (20, 2, 64, 128), fine, fine],
+        [sums, es, ec_b, r_r, r_b, ci_r, ci_b, u_b, f_r, f_b, i_r, i_b],
+        [coarse, coarse, (352, 128), (22, 32, 128), (640, 128), (20, 2, 64, 128), (22, 40, 256), (22, 40, 256)],
     )
 
 

time: 150 us -> 132 us (0.88)
  Pallas kernels: 39.5 us -> 24.4 us
  starting transfers between devices: 23.8 us -> 16.5 us
  waiting for transfers between devices: 14.1 us -> 20.6 us
    pallas_call x11 -> x8, Pallas kernels: 39.5 us -> 24.4 us  [run(): pl.pallas_call(kernel, out_shape=shapes[0] if single else shapes, in_spec...]
    ppermute x4 -> x3, waiting for transfers between devices: 9.11 us -> 15.8 us  [to_slabs(): return lax.ppermute(x, ALL, pairs)]
    all_to_all x1 -> x0, starting transfers between devices: 5.28 us -> none  [exchange(): return lax.all_to_all(sent, LB, split_axis=0, concat_axis=0, tiled=True)]
    ppermute x4 -> x3, starting transfers between devices: 9.81 us -> 5.71 us  [to_slabs(): return lax.ppermute(x, ALL, pairs)]
    ppermute x6, starting transfers between devices: 5.74 us -> 8.44 us  [swap_cores(): return lax.ppermute(x, 'level', [(0, 1), (1, 0)])]
    unnamed x25 -> x13, local copies, waits for them, and re-layouts: 7.04 us -> 5.9 us
    all_to_all x3 -> x2, blocking collectives: 45.1 us -> 44.9 us  [among(): return lax.all_to_all(x, LB, split_axis=0, concat_axis=0, tiled=True)]
  transfers between devices with their start and end apart: 14 -> 12, of which waited for: 7 -> 8; matrix products, arithmetic and copies ran while one was open for 0% -> 0% of each run, Pallas kernels for 9% -> 0%
where the time goes in v2:
time: 132 us; the launch traced here: 131 us
  blocking collectives  63.4 us (48%)
  Pallas kernels  24.4 us (18%)
  waiting for transfers between devices  20.6 us (16%)
  starting transfers between devices  16.5 us (12%)
  local copies, waits for them, and re-layouts  5.9 us (4%)
    all_to_all x2, blocking collectives, among(): return lax.all_to_all(x, LB, split_axis=0, concat_axis=0, tiled=True)  44.9 us
    pallas_call x8, Pallas kernels, run(): pl.pallas_call(kernel, out_shape=shapes[0] if single else shapes, in_spec...  24.4 us
    all_to_all x1, blocking collectives, body(): sums = lax.all_to_all(part, 'slab', split_axis=0, concat_axis=0, tiled=True)  18.5 us
    ppermute x3, waiting for transfers between devices, to_slabs(): return lax.ppermute(x, ALL, pairs)  15.8 us
    ppermute x6, starting transfers between devices, swap_cores(): return lax.ppermute(x, 'level', [(0, 1), (1, 0)])  8.44 us
    unnamed x13, local copies, waits for them, and re-layouts  5.9 us
    ppermute x3, starting transfers between devices, to_slabs(): return lax.ppermute(x, ALL, pairs)  5.71 us
    ppermute x6, waiting for transfers between devices, swap_cores(): return lax.ppermute(x, 'level', [(0, 1), (1, 0)])  3.25 us
  transfers between devices with their start and end apart: 12, of which 8 were waited for; matrix products, arithmetic and copies ran while one was open for 0% of the time, Pallas kernels for 0%

profile of v2, /device:TPU:1, one launch (start us, length us, event | category | flops | bytes accessed | tf_op | source)
XLA Modules:
  0.0 131.0 jit_solution(6371867544797544985)
XLA Ops:
  0.0 0.8 copy.11.bricks
  0.8 0.1 pad_add_fusion.meta
  0.8 0.0 copy-start
  0.8 1.0 copy-done
  1.9 0.0 copy-start.1
  1.9 1.0 copy-done.1
  2.9 0.0 copy-start.2
  2.9 1.0 copy-done.2
  4.0 1.6 %shard_map.46 = f32[8,33,8,128]{3,2,1,0:T(8,128)S(1)} custom-call(s32[2]{0:T(128)S(1)} %pad_add_fusion.meta, s32[16,8]{1,0:T(8,128)S(1)} %copy.11.bricks, f32[1,32,32,128]{3,2,1,0:T(8,128)S(1)} %copy-done, f32[1,32,32,128]{3,2,1,0:T(8,128)S(1)} %copy-done.1, f32[1,32,32,128]{3,2,1,0:T(8,128)S(1)} %copy-done.2), custom_call_target="tpu_custom_call" | custom-call | tf_op jit(solution)/shard_map/pallas_call | solution.py:24
  5.6 21.6 %all_to_all.15.recv = f32[8,33,8,128]{3,2,1,0:T(8,128)S(1)} all-to-all(f32[8,33,8,128]{3,2,1,0:T(8,128)S(1)} %shard_map.46), channel_id=1, replica_groups=mesh['slab'=16,'level'=2,'bottom'=4] {'level','bottom'}, dimensions={0} | all-to-all | bytes 2162688 | tf_op jit(solution)/shard_map/all_to_all | solution.py:528
  27.2 0.7 shard_map.47
  27.9 3.1 %collective-permute-start = (f32[4,20,8,128]{3,2,1,0:T(8,128)S(1)}, f32[4,20,8,128]{3,2,1,0:T(8,128)S(1)}, u32[]{:S(2)}, u32[]{:S(2)}) collective-permute-start(f32[4,20,8,128]{3,2,1,0:T(8,128)S(1)} %shard_map.47), channel_id=1, source_target_pairs={{8,0},{9,1},{10,2},{11,3},{4,12},{5,13},{6,14},{7,15},{16,8},{17,9... | collective-permute-start | bytes 983048 | tf_op jit(solution)/shard_map/ppermute | solution.py:524
  31.0 4.0 %collective-permute-done.cross = f32[4,20,8,128]{3,2,1,0:T(8,128)S(1)} collective-permute-done((f32[4,20,8,128]{3,2,1,0:T(8,128)S(1)}, f32[4,20,8,128]{3,2,1,0:T(8,128)S(1)}, u32[]{:S(2)}, u32[]{:S(2)}) %collective-permute-start) | collective-permute-done | bytes 327712 | tf_op jit(solution)/shard_map/ppermute | solution.py:524
  35.0 1.5 %shard_map.48 = f32[8,40,8,128]{3,2,1,0:T(8,128)S(1)} custom-call(s32[2]{0:T(128)S(1)} %pad_add_fusion.meta, s32[16,8]{1,0:T(8,128)S(1)} %copy.11.bricks, f32[8,33,8,128]{3,2,1,0:T(8,128)S(1)} %all_to_all.15.recv, f32[4,20,8,128]{3,2,1,0:T(8,128)S(1)} %collective-permute-done.cross), custom_call_target="tpu_custom_call" | custom-call | tf_op jit(solution)/shard_map/pallas_call | solution.py:24
  36.5 0.0 copy-start.3
  36.5 23.3 %all_to_all.16.recv = f32[8,40,8,128]{3,2,1,0:T(8,128)} all-to-all(f32[8,40,8,128]{3,2,1,0:T(8,128)S(1)} %shard_map.48), channel_id=1, replica_groups=mesh['slab'=16,'level'=2,'bottom'=4] {'level','bottom'}, dimensions={0} | all-to-all | bytes 2621440 | tf_op jit(solution)/shard_map/all_to_all | solution.py:528
  59.8 0.0 copy-done.3
  59.8 6.6 %shard_map.49 = (f32[2,8,16,128]{3,2,1,0:T(8,128)S(1)}, f32[26,40,256]{2,1,0:T(8,128)S(1)}, f32[26,40,256]{2,1,0:T(8,128)S(1)}, f32[26,40,256]{2,1,0:T(8,128)}, ...) custom-call(s32[2]{0:T(128)S(1)} %pad_add_fusion.meta, s32[16,8]{1,0:T(8,128)S(1)} %copy.11.bricks, ...), custom_call_target="tpu_custom_call" | custom-call | tf_op jit(solution)/shard_map/pallas_call | solution.py:24
  66.4 0.0 copy-start.4
  66.4 1.0 copy-done.4
  67.4 0.8 collective-permute-start.3
  68.2 1.5 %collective-permute-start.2 = (f32[2,8,16,128]{3,2,1,0:T(8,128)S(1)}, f32[2,8,16,128]{3,2,1,0:T(8,128)S(1)}, u32[]{:S(2)}, u32[]{:S(2)}) collective-permute-start(f32[2,8,16,128]{3,2,1,0:T(8,128)S(1)} %get-tuple-element.20.refs_0_), channel_id=1, source_target_pairs={{0,2},{1,3},{2,0},{3,1},{4,6},{5,7},{6,4},{7,5},{8,10},{9,11},{10,... | collective-permute-start | bytes 393224 | tf_op jit(solution)/shard_map/ppermute | solution.py:552
  69.7 0.0 collective-permute-start.1
  69.7 0.9 collective-permute-start.4
  70.6 1.5 %collective-permute-done.3.refs_3_ = f32[2,8,16,128]{3,2,1,0:T(8,128)S(1)} collective-permute-done((f32[2,8,16,128]{3,2,1,0:T(8,128)S(1)}, f32[2,8,16,128]{3,2,1,0:T(8,128)S(1)}, u32[]{:S(2)}, u32[]{:S(2)}) %collective-permute-start.3) | collective-permute-done | bytes 131104 | tf_op jit(solution)/shard_map/ppermute | solution.py:552
  72.1 2.0 %collective-permute-start.7 = (f32[2,8,16,128]{3,2,1,0:T(8,128)S(1)}, f32[2,8,16,128]{3,2,1,0:T(8,128)S(1)}, u32[]{:S(2)}, u32[]{:S(2)}) collective-permute-start(f32[2,8,16,128]{3,2,1,0:T(8,128)S(1)} %collective-permute-done.3.refs_3_), channel_id=1, source_target_pairs={{0,4},{4,0},{1,5},{5,1},{2,6},{6,2},{3,7},{7,3},{8,12},{12,8},{9,1... | collective-permute-start | bytes 393224 | tf_op jit(solution)/shard_map/ppermute | solution.py:515
  74.1 0.0 collective-permute-done.2.refs_2_
  74.1 3.0 %collective-permute-start.6 = (f32[2,8,16,128]{3,2,1,0:T(8,128)S(1)}, f32[2,8,16,128]{3,2,1,0:T(8,128)S(1)}, u32[]{:S(2)}, u32[]{:S(2)}) collective-permute-start(f32[2,8,16,128]{3,2,1,0:T(8,128)S(1)} %collective-permute-done.2.refs_2_), channel_id=1, source_target_pairs={{0,4},{4,0},{1,5},{5,1},{2,6},{6,2},{3,7},{7,3},{8,12},{12,8},{9,1... | collective-permute-start | bytes 393224 | tf_op jit(solution)/shard_map/ppermute | solution.py:515
  77.1 0.1 collective-permute-done.1.refs_1_
  77.2 1.3 collective-permute-start.5
  78.4 0.0 collective-permute-done.4.refs_4_
  78.4 0.0 collective-permute-done.7.refs_7_
  78.4 0.0 collective-permute-done.6.refs_6_
  78.4 1.0 collective-permute-done.5.refs_5_
  79.4 0.8 shard_map.50
  80.2 1.3 collective-permute-start.8
  81.5 6.5 %collective-permute-done.8.refs_8_ = f32[4,2,5,16,128]{4,3,2,1,0:T(8,128)S(1)} collective-permute-done((f32[4,2,5,16,128]{4,3,2,1,0:T(8,128)S(1)}, f32[4,2,5,16,128]{4,3,2,1,0:T(8,128)S(1)}, u32[]{:S(2)}, u32[]{:S(2)}) %collective-permute-start.8) | collective-permute-done | bytes 327712 | tf_op jit(solution)/shard_map/ppermute | solution.py:524
  88.0 0.5 collective-permute-start.9
  88.5 1.3 collective-permute-done.9.refs_9_
  89.8 3.4 %shard_map.51 = (f32[22,16,128]{2,1,0:T(8,128)S(1)}, f32[18,16,128]{2,1,0:T(8,128)S(1)}, f32[28,32,128]{2,1,0:T(8,128)S(1)}, f32[28,32,128]{2,1,0:T(8,128)S(1)},...) custom-call(s32[2]{0:T(128)S(1)} %pad_add_fusion.meta, s32[16,8]{1,0:T(8,128)S(1)} %copy.11.bricks, ...), custom_call_target="tpu_custom_call" | custom-call | tf_op jit(solution)/shard_map/pallas_call | solution.py:24
  93.2 1.3 collective-permute-start.10
  94.5 5.3 %collective-permute-done.10.one = f32[18,16,128]{2,1,0:T(8,128)S(1)} collective-permute-done((f32[18,16,128]{2,1,0:T(8,128)S(1)}, f32[18,16,128]{2,1,0:T(8,128)S(1)}, u32[]{:S(2)}, u32[]{:S(2)}) %collective-permute-start.10) | collective-permute-done | bytes 147488 | tf_op jit(solution)/shard_map/ppermute | solution.py:524
  99.8 0.8 collective-permute-start.11
  100.6 1.0 collective-permute-done.11.two
  101.6 2.9 %shard_map.52 = (f32[22,16,128]{2,1,0:T(8,128)S(1)}, f32[16,8,128]{2,1,0:T(8,128)S(1)}) custom-call(s32[2]{0:T(128)S(1)} %pad_add_fusion.meta, f32[22,16,128]{2,1,0:T(8,128)S(1)} %get-tuple-element.21.rb, f32[18,16,128]{2,1,0:T(8,128)S(1)} %collective-permute-done.10.one, f32[18,16,128]{2,1,0:T(8,128)S(1)} %collective-permute-done.11.two), custom_call_target="tpu_custom_call" | custom-call | tf_op jit(solution)/shard_map/pallas_call | solution.py:24
  104.6 18.5 %all_to_all.17.sums = f32[16,8,128]{2,1,0:T(8,128)S(1)} all-to-all(f32[16,8,128]{2,1,0:T(8,128)S(1)} %get-tuple-element.23), channel_id=1, replica_groups=mesh['slab'=16,'level'=2,'bottom'=4] {'slab'}, dimensions={0} | all-to-all | bytes 131072 | tf_op jit(solution)/shard_map/all_to_all | solution.py:571
  123.0 0.0 copy-start.5
  123.1 1.0 copy-done.5
  124.1 6.9 %shard_map.53 = f32[1,32,32,128]{3,2,1,0:T(8,128)} custom-call(s32[2]{0:T(128)S(1)} %pad_add_fusion.meta, s32[16,8]{1,0:T(8,128)S(1)} %copy.11.bricks, f32[16,8,128]{2,1,0:T(8,128)S(1)} %all_to_all.17.sums, f32[22,16,128]{2,1,0:T(8,128)S(1)} %get-tuple-element.24.es, f32[28,32,128]{2,1,0:T(8,128)S(1)} %get-tuple-element.25.ec_b, ...), custom_call_target="tpu_custom_call" | custom-call | tf_op jit(solution)/shard_map/pallas_call | solution.py:24
Async XLA Ops:
  0.8 1.0 copy-start
  1.9 1.0 copy-start.1
  2.9 1.0 copy-start.2
  27.9 7.1 %collective-permute-start = (f32[4,20,8,128]{3,2,1,0:T(8,128)S(1)}, f32[4,20,8,128]{3,2,1,0:T(8,128)S(1)}, u32[]{:S(2)}, u32[]{:S(2)}) collective-permute-start(f32[4,20,8,128]{3,2,1,0:T(8,128)S(1)} %shard_map.47), channel_id=1, source_target_pairs={{8,0},{9,1},{10,2},{11,3},{4,12},{5,13},{6,14},{7,15},{16,8},{17,9... | collective-permute-start | bytes 983048 | tf_op jit(solution)/shard_map/ppermute | solution.py:524
  36.5 23.3 %copy-start.3 = (f32[1,32,32,128]{3,2,1,0:T(8,128)S(1)}, f32[1,32,32,128]{3,2,1,0:T(8,128)}, u32[]{:S(2)}) copy-start(f32[1,32,32,128]{3,2,1,0:T(8,128)} %a.3) | copy-start | bytes 1572868
  66.4 1.0 copy-start.4
  67.4 4.7 %collective-permute-start.3 = (f32[2,8,16,128]{3,2,1,0:T(8,128)S(1)}, f32[2,8,16,128]{3,2,1,0:T(8,128)S(1)}, u32[]{:S(2)}, u32[]{:S(2)}) collective-permute-start(f32[2,8,16,128]{3,2,1,0:T(8,128)S(1)} %get-tuple-element.20.refs_0_), channel_id=1, source_target_pairs={{0,3},{1,0},{2,1},{3,2},{4,7},{5,4},{6,5},{7,6},{8,11},{9,8},{10,9... | collective-permute-start | bytes 393224 | tf_op jit(solution)/shard_map/ppermute | solution.py:552
  68.2 5.9 %collective-permute-start.2 = (f32[2,8,16,128]{3,2,1,0:T(8,128)S(1)}, f32[2,8,16,128]{3,2,1,0:T(8,128)S(1)}, u32[]{:S(2)}, u32[]{:S(2)}) collective-permute-start(f32[2,8,16,128]{3,2,1,0:T(8,128)S(1)} %get-tuple-element.20.refs_0_), channel_id=1, source_target_pairs={{0,2},{1,3},{2,0},{3,1},{4,6},{5,7},{6,4},{7,5},{8,10},{9,11},{10,... | collective-permute-start | bytes 393224 | tf_op jit(solution)/shard_map/ppermute | solution.py:552
  69.7 7.4 %collective-permute-start.1 = (f32[2,8,16,128]{3,2,1,0:T(8,128)S(1)}, f32[2,8,16,128]{3,2,1,0:T(8,128)S(1)}, u32[]{:S(2)}, u32[]{:S(2)}) collective-permute-start(f32[2,8,16,128]{3,2,1,0:T(8,128)S(1)} %get-tuple-element.20.refs_0_), channel_id=1, source_target_pairs={{0,1},{1,2},{2,3},{3,0},{4,5},{5,6},{6,7},{7,4},{8,9},{9,10},{10,1... | collective-permute-start | bytes 393224 | tf_op jit(solution)/shard_map/ppermute | solution.py:552
  69.7 8.7 %collective-permute-start.4 = (f32[2,8,16,128]{3,2,1,0:T(8,128)S(1)}, f32[2,8,16,128]{3,2,1,0:T(8,128)S(1)}, u32[]{:S(2)}, u32[]{:S(2)}) collective-permute-start(f32[2,8,16,128]{3,2,1,0:T(8,128)S(1)} %get-tuple-element.20.refs_0_), channel_id=1, source_target_pairs={{0,4},{4,0},{1,5},{5,1},{2,6},{6,2},{3,7},{7,3},{8,12},{12,8},{9,1... | collective-permute-start | bytes 393224 | tf_op jit(solution)/shard_map/ppermute | solution.py:515
  72.1 6.3 %collective-permute-start.7 = (f32[2,8,16,128]{3,2,1,0:T(8,128)S(1)}, f32[2,8,16,128]{3,2,1,0:T(8,128)S(1)}, u32[]{:S(2)}, u32[]{:S(2)}) collective-permute-start(f32[2,8,16,128]{3,2,1,0:T(8,128)S(1)} %collective-permute-done.3.refs_3_), channel_id=1, source_target_pairs={{0,4},{4,0},{1,5},{5,1},{2,6},{6,2},{3,7},{7,3},{8,12},{12,8},{9,1... | collective-permute-start | bytes 393224 | tf_op jit(solution)/shard_map/ppermute | solution.py:515
  74.1 4.3 %collective-permute-start.6 = (f32[2,8,16,128]{3,2,1,0:T(8,128)S(1)}, f32[2,8,16,128]{3,2,1,0:T(8,128)S(1)}, u32[]{:S(2)}, u32[]{:S(2)}) collective-permute-start(f32[2,8,16,128]{3,2,1,0:T(8,128)S(1)} %collective-permute-done.2.refs_2_), channel_id=1, source_target_pairs={{0,4},{4,0},{1,5},{5,1},{2,6},{6,2},{3,7},{7,3},{8,12},{12,8},{9,1... | collective-permute-start | bytes 393224 | tf_op jit(solution)/shard_map/ppermute | solution.py:515
  77.2 2.3 %collective-permute-start.5 = (f32[2,8,16,128]{3,2,1,0:T(8,128)S(1)}, f32[2,8,16,128]{3,2,1,0:T(8,128)S(1)}, u32[]{:S(2)}, u32[]{:S(2)}) collective-permute-start(f32[2,8,16,128]{3,2,1,0:T(8,128)S(1)} %collective-permute-done.1.refs_1_), channel_id=1, source_target_pairs={{0,4},{4,0},{1,5},{5,1},{2,6},{6,2},{3,7},{7,3},{8,12},{12,8},{9,1... | collective-permute-start | bytes 393224 | tf_op jit(solution)/shard_map/ppermute | solution.py:515
  80.2 7.8 %collective-permute-start.8 = (f32[4,2,5,16,128]{4,3,2,1,0:T(8,128)S(1)}, f32[4,2,5,16,128]{4,3,2,1,0:T(8,128)S(1)}, u32[]{:S(2)}, u32[]{:S(2)}) collective-permute-start(f32[4,2,5,16,128]{4,3,2,1,0:T(8,128)S(1)} %shard_map.50), channel_id=1, source_target_pairs={{0,8},{1,9},{2,10},{3,11},{12,4},{13,5},{14,6},{15,7},{8,16},{9,17... | collective-permute-start | bytes 983048 | tf_op jit(solution)/shard_map/ppermute | solution.py:524
  88.0 1.8 %collective-permute-start.9 = (f32[4,2,5,16,128]{4,3,2,1,0:T(8,128)S(1)}, f32[4,2,5,16,128]{4,3,2,1,0:T(8,128)S(1)}, u32[]{:S(2)}, u32[]{:S(2)}) collective-permute-start(f32[4,2,5,16,128]{4,3,2,1,0:T(8,128)S(1)} %collective-permute-done.8.refs_8_), channel_id=1, source_target_pairs={{0,4},{4,0},{1,5},{5,1},{2,6},{6,2},{3,7},{7,3},{8,12},{12,8},{9,1... | collective-permute-start | bytes 983048 | tf_op jit(solution)/shard_map/ppermute | solution.py:515
  93.2 6.6 %collective-permute-start.10 = (f32[18,16,128]{2,1,0:T(8,128)S(1)}, f32[18,16,128]{2,1,0:T(8,128)S(1)}, u32[]{:S(2)}, u32[]{:S(2)}) collective-permute-start(f32[18,16,128]{2,1,0:T(8,128)S(1)} %get-tuple-element.22), channel_id=1, source_target_pairs={{0,8},{1,9},{2,10},{3,11},{12,4},{13,5},{14,6},{15,7},{8,16},{9,17... | collective-permute-start | bytes 442376 | tf_op jit(solution)/shard_map/ppermute | solution.py:524
  99.8 1.8 %collective-permute-start.11 = (f32[18,16,128]{2,1,0:T(8,128)S(1)}, f32[18,16,128]{2,1,0:T(8,128)S(1)}, u32[]{:S(2)}, u32[]{:S(2)}) collective-permute-start(f32[18,16,128]{2,1,0:T(8,128)S(1)} %collective-permute-done.10.one), channel_id=1, source_target_pairs={{0,4},{4,0},{1,5},{5,1},{2,6},{6,2},{3,7},{7,3},{8,12},{12,8},{9,1... | collective-permute-start | bytes 442376 | tf_op jit(solution)/shard_map/ppermute | solution.py:515
  123.0 1.0 copy-start.5

commit v3 on v2

--- a/solution.py
+++ b/solution.py
@@ -27,7 +27,7 @@
         in_specs=[SMEM_SPEC] * len(smem) + [VMEM_SPEC] * len(vmem),
         out_specs=VMEM_SPEC if single else [VMEM_SPEC] * len(shapes),
         scratch_shapes=[pltpu.VMEM(s, F32) for s in scratch],
-        compiler_params=pltpu.CompilerParams(vmem_limit_bytes=50 << 20),
+        compiler_params=pltpu.CompilerParams(vmem_limit_bytes=20 << 20),
     )(*smem, *vmem)
 
 
@@ -59,7 +59,8 @@
         self.ny = 2 * arrays
         self.strips = 8 * arrays
         self.nx = math.ceil(self.strips / 16)
-        self.sent = self.nz + self.ny + self.nx
+        self.coef = self.nz + self.ny + self.nx
+        self.sent = self.coef + 2
         self.nz2 = 5 * self.planes
         self.side = math.ceil(self.nz2 / 16)
         self.y2 = self.nz2 + self.side
@@ -115,13 +116,20 @@
     slab, me = meta[0], meta[1]
     for i in range(4):
         src = jnp.where(me >= 4, bricks[slab, 4 + i], bricks[slab, i])
-        out[i] = recv[src, 0 : shell.nz]
-
-
-def mid_kernel(shell, meta, bricks, recv, cross, out, faces):
+        out[i, 0 : shell.nz] = recv[src, 0 : shell.nz]
+        for j in range(2):
+            coef = recv[bricks[slab, 2 * i + j], shell.coef : shell.coef + 2]
+            out[i, shell.nz + 2 * j : shell.nz + 2 * j + 2] = coef
+
+
+def mid_kernel(shell, meta, bricks, recv, cross, out, coef, faces):
     slab, me = meta[0], meta[1]
     faces[0:8] = recv[:, 0 : shell.nz]
-    faces[8:12] = cross[...]
+    faces[8:12] = cross[:, 0 : shell.nz]
+    for p in range(8):
+        coef[0, p] = recv[bricks[slab, p], shell.coef : shell.coef + 2]
+        j = shell.nz + 2 * (p & 1)
+        coef[1, p] = cross[p >> 1, j : j + 2]
     for p in range(8):
         bx, by, bz = p & 1, (p >> 1) & 1, p >> 2
         dest = bricks[slab, p]
@@ -191,7 +199,26 @@
     return jnp.where(mask, high, low) if red else jnp.where(mask, low, high)
 
 
-def first_kernel(meta, bricks, u, f, a, out):
+def pack_bottom_coef(a, out, small):
+    for i in range(8):
+        planes = (a[0, 4 * i] + a[0, 4 * i + 1]) + (a[0, 4 * i + 2] + a[0, 4 * i + 3])
+        small[i] = planes
+    rows = []
+    for i in range(8):
+        first = small[i, pl.ds(0, 8, stride=4), :] + small[i, pl.ds(1, 8, stride=4), :]
+        rows.append(first + (small[i, pl.ds(2, 8, stride=4), :] + small[i, pl.ds(3, 8, stride=4), :]))
+    fold = pick(128, 128, lambda r, c: (r >> 2) == (c & 31)) * (1.0 / 64)
+    cells = jnp.dot(jnp.concatenate(rows, 0), fold, precision=EXACT, preferred_element_type=F32)
+    group = iota((8, 128), 1) >> 5
+    for h in range(2):
+        tile = cells[32 * h : 32 * h + 8]
+        for j in range(1, 4):
+            tile = jnp.where(group == j, cells[32 * h + 8 * j : 32 * h + 8 * j + 8], tile)
+        for k in range(8):
+            out[k, DOWN.coef + h] = tile
+
+
+def first_kernel(meta, bricks, u, f, a, out, small):
     _, _, bit_x, bit_y, _ = place_of(meta, bricks)
     mask = odd(32, 128)
     sources = ((u, False), (f, True), (f, False), (a, True), (a, False))
@@ -200,6 +227,7 @@
         return pair_of(sources[c][0], t, sources[c][1], mask)
 
     pack_shell(DOWN, get, out, bit_x, bit_y)
+    pack_bottom_coef(a, out, small)
 
 
 def around(src, k, red, mask, edges, cut=None):
@@ -308,9 +336,9 @@
 
 
 def coarse_down_kernel(meta, bricks, *refs):
-    boxes, (one, two) = refs[:8], refs[8:10]
-    rb, rb_send, e_b, r_r, r_b, i_r, i_b = refs[10:17]
-    held, low, high, e_r, a_r, a_b, resid, small = refs[17:]
+    boxes, (one, two, weights) = refs[:8], refs[8:11]
+    rb, rb_send, part, e_b, r_r, r_b, i_r, i_b = refs[11:19]
+    held, low, high, e_r, a_r, a_b, resid, small = refs[19:]
     slab, me = meta[0], meta[1]
     for i, box in enumerate(boxes):
         held[i] = box[...]
@@ -379,9 +407,15 @@
         total = total + jnp.dot(small[...], half, precision=EXACT, preferred_element_type=F32)
     rb[...] = total.reshape(22, 16, 128)
     rb_send[...] = rb[pl.ds(jnp.where(me < 4, 1, 3), 18)]
-
-
-def bottom_kernel(meta, rb, one, two, es, part, e_r, e_b, g_r, g_b, i_r, i_b, low, high):
+    total = jnp.zeros((16, 128), F32)
+    for i in range(16):
+        total = total + rb[3 + i] * weights[i]
+    total = total[0:8] + total[8:16]
+    for i in range(SLABS):
+        part[i] = total
+
+
+def bottom_kernel(meta, rb, one, two, es, e_r, e_b, g_r, g_b, i_r, i_b, low, high):
     slab, me = meta[0], meta[1]
 
     @pl.when(me < 4)
@@ -428,12 +462,72 @@
     for i in range(22):
         k, upper = (15 + i) // 2 + 1, (15 + i) % 2
         es[i] = jnp.where(mask, e_r[k], e_b[k]) if upper else jnp.where(mask, e_b[k], e_r[k])
-    total = zero
-    for k in range(10, 18):
-        total = total + (e_r[k] + e_b[k])
-    total = total[0:8] + total[8:16]
-    for i in range(SLABS):
-        part[i] = total
+
+
+def weights_kernel(meta, here, there, out, t_r, t_b, w_r, w_b, i_r, i_b, low, high):
+    slab, me = meta[0], meta[1]
+
+    @pl.when(me < 4)
+    def _():
+        low[...] = there[1]
+        high[...] = here[1]
+
+    @pl.when(me >= 4)
+    def _():
+        low[...] = here[1]
+        high[...] = there[1]
+
+    lane = iota((8, 128), 1)
+
+    def plane(boxes, z):
+        rows = []
+        for by in range(2):
+            place, shift = 4 * (z >> 3) + 2 * by, 32 * (z & 3)
+            west = pltpu.roll(boxes(place, (z & 7) >> 2), (128 - shift) % 128, 1)
+            east = pltpu.roll(boxes(place + 1, (z & 7) >> 2), (160 - shift) % 128, 1)
+            rows.append(jnp.where(lane < 32, west, east))
+        return jnp.concatenate(rows, 0)
+
+    parts = (lambda p, h: low[p, h], lambda p, h: here[0, p, h], lambda p, h: high[p, h])
+    mask = odd(16, 128)
+    left = iota((16, 128), 1) < 64
+    zero = jnp.zeros((16, 128), F32)
+    for k in (0, 25):
+        t_r[k] = zero
+        t_b[k] = zero
+    for j in range(24):
+        lower, upper = (plane(parts[(2 * j + i) // 16], (2 * j + i) % 16) for i in range(2))
+        keep = left
+        if j < 8:
+            keep = left & jnp.logical_not(is_zero(slab, (16, 128)))
+        if j >= 16:
+            keep = left & jnp.logical_not(is_zero(slab - (SLABS - 1), (16, 128)))
+        i_r[1 + j] = jnp.where(keep, 1.0 / (jnp.where(mask, upper, lower) + 0.375), 0.0)
+        i_b[1 + j] = jnp.where(keep, 1.0 / (jnp.where(mask, lower, upper) + 0.375), 0.0)
+    for k in range(1, 25):
+        t_b[k] = i_b[k]
+        w_b[k] = i_b[k]
+    for k in range(1, 25):
+        t = i_r[k] * (1.0 + 0.0625 * around(t_b, k, True, mask, 1))
+        t_r[k] = t
+        w_r[k] = t
+
+    def sweep(n, carry):
+        for k in range(1, 25):
+            t = i_b[k] * (0.0625 * around(t_r, k, False, mask, 1))
+            t_b[k] = t
+            w_b[k] = w_b[k] + t
+        for k in range(1, 25):
+            t = i_r[k] * (0.0625 * around(t_b, k, True, mask, 1))
+            t_r[k] = t
+            w_r[k] = w_r[k] + t
+        return carry
+
+    lax.fori_loop(0, 7, sweep, 0)
+    for j in range(8):
+        red, black = w_r[9 + j], w_b[9 + j]
+        out[2 * j] = jnp.where(mask, black, red)
+        out[2 * j + 1] = jnp.where(mask, red, black)
 
 
 def up_kernel(
@@ -528,22 +622,25 @@
     return lax.all_to_all(x, LB, split_axis=0, concat_axis=0, tiled=True)
 
 
-def deliver(shell, got, smem):
-    leaving = run(functools.partial(cross_kernel, shell), [(4, shell.nz, 8, 128)], smem, [got])
-    cross = to_slabs(leaving, False)
-    sent = run(
-        functools.partial(mid_kernel, shell), [(8, shell.got, 8, 128)], smem, [got, cross],
-        [(12, shell.nz, 8, 128)],
-    )
-    return among(sent)
-
-
 def body(u_init, source, coeffs, brick_map):
     meta = jnp.stack([lax.axis_index("slab"), lax.axis_index(LB)]).astype(jnp.int32)
     smem = [meta, brick_map]
     fine = (26, 40, 256)
-    packed = run(first_kernel, [(8, DOWN.sent, 8, 128)], smem, [u_init, source, coeffs])
-    halo = deliver(DOWN, among(packed), smem)
+    packed = run(first_kernel, [(8, DOWN.sent, 8, 128)], smem, [u_init, source, coeffs], [(8, 32, 128)])
+    got = among(packed)
+    leaving = run(functools.partial(cross_kernel, DOWN), [(4, DOWN.nz + 4, 8, 128)], smem, [got])
+    cross = to_slabs(leaving, False)
+    sent, coef = run(
+        functools.partial(mid_kernel, DOWN), [(8, DOWN.got, 8, 128), (2, 8, 2, 8, 128)], smem, [got, cross],
+        [(12, DOWN.nz, 8, 128)],
+    )
+    coef_other = swap_cores(coef)
+    halo = among(sent)
+    weights = run(
+        weights_kernel, [(16, 16, 128)], [meta], [coef, coef_other],
+        [(26, 16, 128)] * 6 + [(8, 2, 8, 128)] * 2,
+    )
+    halo, weights = lax.optimization_barrier((halo, weights))
     rc, u_b, f_r, f_b, i_r, i_b = run(
         fine_down_kernel, [(2, 8, 16, 128)] + [fine] * 5, smem, [u_init, source, coeffs, halo],
         [fine, (2, 16, 32, 128), (256, 128)],
@@ -557,18 +654,20 @@
     other = swap_cores(cross)
     coarse = (28, 32, 128)
     faces = (4, 2, 5, 16, 128)
-    rb, rb_send, ec_b, r_r, r_b, ci_r, ci_b = run(
-        coarse_down_kernel, [(22, 16, 128), (18, 16, 128)] + [coarse] * 5, smem, boxes + [cross, other],
+    rb, rb_send, part, ec_b, r_r, r_b, ci_r, ci_b = run(
+        coarse_down_kernel, [(22, 16, 128), (18, 16, 128), (SLABS, 8, 128)] + [coarse] * 5, smem,
+        boxes + [cross, other, weights],
         [(8, 2, 8, 16, 128), faces, faces, coarse, coarse, coarse, (2, 22, 32, 128), (352, 128)],
     )
     cross = to_slabs(rb_send, True)
+    sums = lax.all_to_all(part, "slab", split_axis=0, concat_axis=0, tiled=True)
+    cross, sums = lax.optimization_barrier((cross, sums))
     other = swap_cores(cross)
     bottom = (28, 16, 128)
-    es, part = run(
-        bottom_kernel, [(22, 16, 128), (SLABS, 8, 128)], [meta], [rb, cross, other],
+    es = run(
+        bottom_kernel, [(22, 16, 128)], [meta], [rb, cross, other],
         [bottom] * 6 + [(18, 16, 128)] * 2,
     )
-    sums = lax.all_to_all(part, "slab", split_axis=0, concat_axis=0, tiled=True)
     return run(
         up_kernel, [(1, 32, 32, 128)], smem,
         [sums, es, ec_b, r_r, r_b, ci_r, ci_b, u_b, f_r, f_b, i_r, i_b],

time: 132 us -> 125 us (0.947)
  blocking collectives: 63.4 us -> 40.5 us
  waiting for transfers between devices: 20.6 us -> 31 us
  starting transfers between devices: 16.5 us -> 24.4 us
    all_to_all x2 -> x1, blocking collectives: 44.9 us -> 22 us  [among(): return lax.all_to_all(x, LB, split_axis=0, concat_axis=0, tiled=True)]
    all_to_all x0 -> x1, waiting for transfers between devices: none -> 13.5 us  [among(): return lax.all_to_all(x, LB, split_axis=0, concat_axis=0, tiled=True)]
    all_to_all x0 -> x1, starting transfers between devices: none -> 5.86 us  [among(): return lax.all_to_all(x, LB, split_axis=0, concat_axis=0, tiled=True)]
    ppermute x3, waiting for transfers between devices: 15.8 us -> 11.2 us  [to_slabs(): return lax.ppermute(x, ALL, pairs)]
    ppermute x6 -> x7, starting transfers between devices: 8.44 us -> 10.4 us  [swap_cores(): return lax.ppermute(x, 'level', [(0, 1), (1, 0)])]
    ppermute x6 -> x7, waiting for transfers between devices: 3.25 us -> 4.43 us  [swap_cores(): return lax.ppermute(x, 'level', [(0, 1), (1, 0)])]
    unnamed x13 -> x15, local copies, waits for them, and re-layouts: 5.9 us -> 4.95 us
    pallas_call x8 -> x9, Pallas kernels: 24.4 us -> 23.8 us  [run(): pl.pallas_call(kernel, out_shape=shapes[0] if single else shapes, in_spec...]
  transfers between devices with their start and end apart: 12 -> 14, of which waited for: 8 -> 9; matrix products, arithmetic and copies ran while one was open for 0% -> 0% of each run, Pallas kernels for 0% -> 2%
where the time goes in v3:
time: 125 us
  blocking collectives  40.5 us (32%)
  waiting for transfers between devices  31 us (25%)
  starting transfers between devices  24.4 us (20%)
  Pallas kernels  23.8 us (19%)
  local copies, waits for them, and re-layouts  4.95 us (4%)
    pallas_call x9, Pallas kernels, run(): pl.pallas_call(kernel, out_shape=shapes[0] if single else shapes, in_spec...  23.8 us
    all_to_all x1, blocking collectives, among(): return lax.all_to_all(x, LB, split_axis=0, concat_axis=0, tiled=True)  22 us
    all_to_all x1, blocking collectives, body(): sums = lax.all_to_all(part, 'slab', split_axis=0, concat_axis=0, tiled=True)  18.5 us
    all_to_all x1, waiting for transfers between devices, among(): return lax.all_to_all(x, LB, split_axis=0, concat_axis=0, tiled=True)  13.5 us
    ppermute x3, waiting for transfers between devices, to_slabs(): return lax.ppermute(x, ALL, pairs)  11.2 us
    ppermute x7, starting transfers between devices, swap_cores(): return lax.ppermute(x, 'level', [(0, 1), (1, 0)])  10.4 us
    all_to_all x1, starting transfers between devices, among(): return lax.all_to_all(x, LB, split_axis=0, concat_axis=0, tiled=True)  5.86 us
    ppermute x3, starting transfers between devices, to_slabs(): return lax.ppermute(x, ALL, pairs)  5.72 us
  transfers between devices with their start and end apart: 14, of which 9 were waited for; matrix products, arithmetic and copies ran while one was open for 0% of the time, Pallas kernels for 2%

profile of v3, /device:TPU:1, one launch (start us, length us, event | category | flops | bytes accessed | tf_op | source)
XLA Modules:
  0.0 124.8 jit_solution(905464563789266523)
XLA Ops:
  0.0 0.8 copy.11.bricks
  0.8 0.1 pad_add_fusion.meta
  0.8 0.0 copy-start
  0.8 1.0 copy-done
  1.9 0.0 copy-start.2
  1.9 1.0 copy-done.2
  2.9 0.0 copy-start.4
  2.9 1.0 copy-done.4
  4.0 1.7 %shard_map.46 = f32[8,35,8,128]{3,2,1,0:T(8,128)S(1)} custom-call(s32[2]{0:T(128)S(1)} %pad_add_fusion.meta, s32[16,8]{1,0:T(8,128)S(1)} %copy.11.bricks, f32[1,32,32,128]{3,2,1,0:T(8,128)S(1)} %copy-done, f32[1,32,32,128]{3,2,1,0:T(8,128)S(1)} %copy-done.2, f32[1,32,32,128]{3,2,1,0:T(8,128)S(1)} %copy-done.4), custom_call_target="tpu_custom_call" | custom-call | tf_op jit(solution)/shard_map/pallas_call | solution.py:24
  5.6 22.0 %all_to_all.15.recv = f32[8,35,8,128]{3,2,1,0:T(8,128)S(1)} all-to-all(f32[8,35,8,128]{3,2,1,0:T(8,128)S(1)} %shard_map.46), channel_id=1, replica_groups=mesh['slab'=16,'level'=2,'bottom'=4] {'level','bottom'}, dimensions={0} | all-to-all | bytes 2293760 | tf_op jit(solution)/shard_map/all_to_all | solution.py:622
  27.6 0.7 shard_map.47
  28.4 3.1 %collective-permute-start = (f32[4,24,8,128]{3,2,1,0:T(8,128)S(1)}, f32[4,24,8,128]{3,2,1,0:T(8,128)S(1)}, u32[]{:S(2)}, u32[]{:S(2)}) collective-permute-start(f32[4,24,8,128]{3,2,1,0:T(8,128)S(1)} %shard_map.47), channel_id=1, source_target_pairs={{8,0},{9,1},{10,2},{11,3},{4,12},{5,13},{6,14},{7,15},{16,8},{17,9... | collective-permute-start | bytes 1179656 | tf_op jit(solution)/shard_map/ppermute | solution.py:618
  31.5 4.7 %collective-permute-done.cross = f32[4,24,8,128]{3,2,1,0:T(8,128)S(1)} collective-permute-done((f32[4,24,8,128]{3,2,1,0:T(8,128)S(1)}, f32[4,24,8,128]{3,2,1,0:T(8,128)S(1)}, u32[]{:S(2)}, u32[]{:S(2)}) %collective-permute-start) | collective-permute-done | bytes 393248 | tf_op jit(solution)/shard_map/ppermute | solution.py:618
  36.2 1.5 %shard_map.48 = (f32[8,40,8,128]{3,2,1,0:T(8,128)S(1)}, f32[2,8,2,8,128]{4,3,2,1,0:T(8,128)S(1)}) custom-call(s32[2]{0:T(128)S(1)} %pad_add_fusion.meta, s32[16,8]{1,0:T(8,128)S(1)} %copy.11.bricks, f32[8,35,8,128]{3,2,1,0:T(8,128)S(1)} %all_to_all.15.recv, f32[4,24,8,128]{3,2,1,0:T(8,128)S(1)} %collective-permute-done.cross), custom_call_target="tpu_custom_call" | custom-call | tf_op jit(solution)/shard_map/pallas_call | solution.py:24
  37.6 0.0 copy-start.6
  37.7 1.1 copy-done.6
  38.7 0.0 copy-start.1
  38.7 0.0 copy-start.3
  38.7 0.0 copy-start.5
  38.7 5.9 %all-to-all-start.1 = ((f32[8,40,8,128]{3,2,1,0:T(8,128)}), f32[8,40,8,128]{3,2,1,0:T(8,128)S(1)}, u32[]{:S(2)}, u32[]{:S(2)}) async-start(f32[8,40,8,128]{3,2,1,0:T(8,128)} %copy-done.6), calls=%async_computation.1 | async-start | bytes 2621440 | tf_op jit(solution)/shard_map/all_to_all | solution.py:622
  44.6 0.2 collective-permute-start.1
  44.7 1.2 collective-permute-done.1.there
  45.9 3.0 %shard_map.49.refs_10_ = f32[16,16,128]{2,1,0:T(8,128)S(1)} custom-call(s32[2]{0:T(128)S(1)} %pad_add_fusion.meta, f32[2,8,2,8,128]{4,3,2,1,0:T(8,128)S(1)} %get-tuple-element.26.here, f32[2,8,2,8,128]{4,3,2,1,0:T(8,128)S(1)} %collective-permute-done.1.there), custom_call_target="tpu_custom_call" | custom-call | tf_op jit(solution)/shard_map/pallas_call | solution.py:24
  48.9 13.5 %all-to-all-done.1.recv = f32[8,40,8,128]{3,2,1,0:T(8,128)S(1)} async-done(((f32[8,40,8,128]{3,2,1,0:T(8,128)}), f32[8,40,8,128]{3,2,1,0:T(8,128)S(1)}, u32[]{:S(2)}, u32[]{:S(2)}) %all-to-all-start.1) | async-done | bytes 1310752 | tf_op jit(solution)/shard_map/all_to_all | solution.py:622
  62.4 0.0 copy-done.1
  62.4 0.0 copy-done.3
  62.4 0.0 copy-done.5
  62.4 4.6 %shard_map.50 = (f32[2,8,16,128]{3,2,1,0:T(8,128)S(1)}, f32[26,40,256]{2,1,0:T(8,128)S(1)}, f32[26,40,256]{2,1,0:T(8,128)S(1)}, f32[26,40,256]{2,1,0:T(8,128)S(1...) custom-call(s32[2]{0:T(128)S(1)} %pad_add_fusion.meta, s32[16,8]{1,0:T(8,128)S(1)} %copy.11.bricks, ...), custom_call_target="tpu_custom_call" | custom-call | tf_op jit(solution)/shard_map/pallas_call | solution.py:24
  67.0 1.1 collective-permute-start.4
  68.0 1.4 %collective-permute-start.3 = (f32[2,8,16,128]{3,2,1,0:T(8,128)S(1)}, f32[2,8,16,128]{3,2,1,0:T(8,128)S(1)}, u32[]{:S(2)}, u32[]{:S(2)}) collective-permute-start(f32[2,8,16,128]{3,2,1,0:T(8,128)S(1)} %get-tuple-element.28.refs_0_), channel_id=1, source_target_pairs={{0,2},{1,3},{2,0},{3,1},{4,6},{5,7},{6,4},{7,5},{8,10},{9,11},{10,... | collective-permute-start | bytes 393224 | tf_op jit(solution)/shard_map/ppermute | solution.py:649
  69.4 0.0 collective-permute-start.2
  69.4 0.8 collective-permute-start.5
  70.2 1.6 %collective-permute-done.4.refs_3_ = f32[2,8,16,128]{3,2,1,0:T(8,128)S(1)} collective-permute-done((f32[2,8,16,128]{3,2,1,0:T(8,128)S(1)}, f32[2,8,16,128]{3,2,1,0:T(8,128)S(1)}, u32[]{:S(2)}, u32[]{:S(2)}) %collective-permute-start.4) | collective-permute-done | bytes 131104 | tf_op jit(solution)/shard_map/ppermute | solution.py:649
  71.8 2.0 %collective-permute-start.8 = (f32[2,8,16,128]{3,2,1,0:T(8,128)S(1)}, f32[2,8,16,128]{3,2,1,0:T(8,128)S(1)}, u32[]{:S(2)}, u32[]{:S(2)}) collective-permute-start(f32[2,8,16,128]{3,2,1,0:T(8,128)S(1)} %collective-permute-done.4.refs_3_), channel_id=1, source_target_pairs={{0,4},{4,0},{1,5},{5,1},{2,6},{6,2},{3,7},{7,3},{8,12},{12,8},{9,1... | collective-permute-start | bytes 393224 | tf_op jit(solution)/shard_map/ppermute | solution.py:609
  73.8 0.0 collective-permute-done.3.refs_2_
  73.8 3.1 %collective-permute-start.7 = (f32[2,8,16,128]{3,2,1,0:T(8,128)S(1)}, f32[2,8,16,128]{3,2,1,0:T(8,128)S(1)}, u32[]{:S(2)}, u32[]{:S(2)}) collective-permute-start(f32[2,8,16,128]{3,2,1,0:T(8,128)S(1)} %collective-permute-done.3.refs_2_), channel_id=1, source_target_pairs={{0,4},{4,0},{1,5},{5,1},{2,6},{6,2},{3,7},{7,3},{8,12},{12,8},{9,1... | collective-permute-start | bytes 393224 | tf_op jit(solution)/shard_map/ppermute | solution.py:609
  76.9 0.4 collective-permute-done.2.refs_1_
  77.2 1.0 collective-permute-start.6
  78.3 0.0 collective-permute-done.5.refs_4_
  78.3 0.0 collective-permute-done.8.refs_7_
  78.3 0.0 collective-permute-done.7.refs_6_
  78.3 1.0 collective-permute-done.6.refs_5_
  79.3 0.8 shard_map.51
  80.0 1.3 %collective-permute-start.9 = (f32[4,2,5,16,128]{4,3,2,1,0:T(8,128)S(1)}, f32[4,2,5,16,128]{4,3,2,1,0:T(8,128)S(1)}, u32[]{:S(2)}, u32[]{:S(2)}) collective-permute-start(f32[4,2,5,16,128]{4,3,2,1,0:T(8,128)S(1)} %shard_map.51), channel_id=1, source_target_pairs={{0,8},{1,9},{2,10},{3,11},{12,4},{13,5},{14,6},{15,7},{8,16},{9,17... | collective-permute-start | bytes 983048 | tf_op jit(solution)/shard_map/ppermute | solution.py:618
  81.3 6.5 %collective-permute-done.9.refs_8_ = f32[4,2,5,16,128]{4,3,2,1,0:T(8,128)S(1)} collective-permute-done((f32[4,2,5,16,128]{4,3,2,1,0:T(8,128)S(1)}, f32[4,2,5,16,128]{4,3,2,1,0:T(8,128)S(1)}, u32[]{:S(2)}, u32[]{:S(2)}) %collective-permute-start.9) | collective-permute-done | bytes 327712 | tf_op jit(solution)/shard_map/ppermute | solution.py:618
  87.8 0.5 collective-permute-start.10
  88.4 1.3 %collective-permute-done.10.refs_9_ = f32[4,2,5,16,128]{4,3,2,1,0:T(8,128)S(1)} collective-permute-done((f32[4,2,5,16,128]{4,3,2,1,0:T(8,128)S(1)}, f32[4,2,5,16,128]{4,3,2,1,0:T(8,128)S(1)}, u32[]{:S(2)}, u32[]{:S(2)}) %collective-permute-start.10) | collective-permute-done | bytes 327712 | tf_op jit(solution)/shard_map/ppermute | solution.py:609
  89.6 3.1 %shard_map.52 = (f32[22,16,128]{2,1,0:T(8,128)S(1)}, f32[18,16,128]{2,1,0:T(8,128)S(1)}, f32[16,8,128]{2,1,0:T(8,128)S(1)}, f32[28,32,128]{2,1,0:T(8,128)S(1)}, ...) custom-call(s32[2]{0:T(128)S(1)} %pad_add_fusion.meta, ...), custom_call_target="tpu_custom_call" | custom-call | tf_op jit(solution)/shard_map/pallas_call | solution.py:24
  92.7 1.3 %collective-permute-start.11 = (f32[18,16,128]{2,1,0:T(8,128)S(1)}, f32[18,16,128]{2,1,0:T(8,128)S(1)}, u32[]{:S(2)}, u32[]{:S(2)}) collective-permute-start(f32[18,16,128]{2,1,0:T(8,128)S(1)} %get-tuple-element.30), channel_id=1, source_target_pairs={{0,8},{1,9},{2,10},{3,11},{12,4},{13,5},{14,6},{15,7},{8,16},{9,17... | collective-permute-start | bytes 442376 | tf_op jit(solution)/shard_map/ppermute | solution.py:618
  94.0 18.5 %all_to_all.16.sums = f32[16,8,128]{2,1,0:T(8,128)S(1)} all-to-all(f32[16,8,128]{2,1,0:T(8,128)S(1)} %get-tuple-element.31), channel_id=1, replica_groups=mesh['slab'=16,'level'=2,'bottom'=4] {'slab'}, dimensions={0} | all-to-all | bytes 131072 | tf_op jit(solution)/shard_map/all_to_all | solution.py:663
  112.5 0.0 collective-permute-done.11.one
  112.5 2.7 %collective-permute-start.12 = (f32[18,16,128]{2,1,0:T(8,128)S(1)}, f32[18,16,128]{2,1,0:T(8,128)S(1)}, u32[]{:S(2)}, u32[]{:S(2)}) collective-permute-start(f32[18,16,128]{2,1,0:T(8,128)S(1)} %collective-permute-done.11.one), channel_id=1, source_target_pairs={{0,4},{4,0},{1,5},{5,1},{2,6},{6,2},{3,7},{7,3},{8,12},{12,8},{9,1... | collective-permute-start | bytes 442376 | tf_op jit(solution)/shard_map/ppermute | solution.py:609
  115.2 1.0 collective-permute-done.12.two
  116.2 3.1 %shard_map.53.es = f32[22,16,128]{2,1,0:T(8,128)S(1)} custom-call(s32[2]{0:T(128)S(1)} %pad_add_fusion.meta, f32[22,16,128]{2,1,0:T(8,128)S(1)} %get-tuple-element.33.rb, f32[18,16,128]{2,1,0:T(8,128)S(1)} %collective-permute-done.11.one, f32[18,16,128]{2,1,0:T(8,128)S(1)} %collective-permute-done.12.two), custom_call_target="tpu_custom_call" | custom-call | tf_op jit(solution)/shard_map/pallas_call | solution.py:24
  119.3 5.5 %shard_map.54 = f32[1,32,32,128]{3,2,1,0:T(8,128)} custom-call(s32[2]{0:T(128)S(1)} %pad_add_fusion.meta, s32[16,8]{1,0:T(8,128)S(1)} %copy.11.bricks, f32[16,8,128]{2,1,0:T(8,128)S(1)} %all_to_all.16.sums, f32[22,16,128]{2,1,0:T(8,128)S(1)} %shard_map.53.es, f32[28,32,128]{2,1,0:T(8,128)S(1)} %get-tuple-element.35.ec_b, ...), custom_call_target="tpu_custom_call" | custom-call | tf_op jit(solution)/shard_map/pallas_call | solution.py:24
Async XLA Ops:
  0.8 1.0 copy-start
  1.9 1.0 copy-start.2
  2.9 1.0 copy-start.4
  28.4 7.8 %collective-permute-start = (f32[4,24,8,128]{3,2,1,0:T(8,128)S(1)}, f32[4,24,8,128]{3,2,1,0:T(8,128)S(1)}, u32[]{:S(2)}, u32[]{:S(2)}) collective-permute-start(f32[4,24,8,128]{3,2,1,0:T(8,128)S(1)} %shard_map.47), channel_id=1, source_target_pairs={{8,0},{9,1},{10,2},{11,3},{4,12},{5,13},{6,14},{7,15},{16,8},{17,9... | collective-permute-start | bytes 1179656 | tf_op jit(solution)/shard_map/ppermute | solution.py:618
  37.6 1.1 copy-start.6
  38.7 23.7 %copy-start.1 = (f32[1,32,32,128]{3,2,1,0:T(8,128)S(1)}, f32[1,32,32,128]{3,2,1,0:T(8,128)}, u32[]{:S(2)}) copy-start(f32[1,32,32,128]{3,2,1,0:T(8,128)} %u.3) | copy-start | bytes 1572868
  38.7 23.7 %copy-start.3 = (f32[1,32,32,128]{3,2,1,0:T(8,128)S(1)}, f32[1,32,32,128]{3,2,1,0:T(8,128)}, u32[]{:S(2)}) copy-start(f32[1,32,32,128]{3,2,1,0:T(8,128)} %f.3) | copy-start | bytes 1572868
  38.7 23.7 %copy-start.5 = (f32[1,32,32,128]{3,2,1,0:T(8,128)S(1)}, f32[1,32,32,128]{3,2,1,0:T(8,128)}, u32[]{:S(2)}) copy-start(f32[1,32,32,128]{3,2,1,0:T(8,128)} %a.3) | copy-start | bytes 1572868
  38.7 23.7 %all-to-all-start.1 = ((f32[8,40,8,128]{3,2,1,0:T(8,128)}), f32[8,40,8,128]{3,2,1,0:T(8,128)S(1)}, u32[]{:S(2)}, u32[]{:S(2)}) async-start(f32[8,40,8,128]{3,2,1,0:T(8,128)} %copy-done.6), calls=%async_computation.1 | async-start | bytes 2621440 | tf_op jit(solution)/shard_map/all_to_all | solution.py:622
  44.6 1.3 %collective-permute-start.1 = (f32[2,8,2,8,128]{4,3,2,1,0:T(8,128)S(1)}, f32[2,8,2,8,128]{4,3,2,1,0:T(8,128)S(1)}, u32[]{:S(2)}, u32[]{:S(2)}) collective-permute-start(f32[2,8,2,8,128]{4,3,2,1,0:T(8,128)S(1)} %get-tuple-element.26.here), channel_id=1, source_target_pairs={{0,4},{4,0},{1,5},{5,1},{2,6},{6,2},{3,7},{7,3},{8,12},{12,8},{9,1... | collective-permute-start | bytes 393224 | tf_op jit(solution)/shard_map/ppermute | solution.py:609
  67.0 4.8 %collective-permute-start.4 = (f32[2,8,16,128]{3,2,1,0:T(8,128)S(1)}, f32[2,8,16,128]{3,2,1,0:T(8,128)S(1)}, u32[]{:S(2)}, u32[]{:S(2)}) collective-permute-start(f32[2,8,16,128]{3,2,1,0:T(8,128)S(1)} %get-tuple-element.28.refs_0_), channel_id=1, source_target_pairs={{0,3},{1,0},{2,1},{3,2},{4,7},{5,4},{6,5},{7,6},{8,11},{9,8},{10,9... | collective-permute-start | bytes 393224 | tf_op jit(solution)/shard_map/ppermute | solution.py:649
  68.0 5.7 %collective-permute-start.3 = (f32[2,8,16,128]{3,2,1,0:T(8,128)S(1)}, f32[2,8,16,128]{3,2,1,0:T(8,128)S(1)}, u32[]{:S(2)}, u32[]{:S(2)}) collective-permute-start(f32[2,8,16,128]{3,2,1,0:T(8,128)S(1)} %get-tuple-element.28.refs_0_), channel_id=1, source_target_pairs={{0,2},{1,3},{2,0},{3,1},{4,6},{5,7},{6,4},{7,5},{8,10},{9,11},{10,... | collective-permute-start | bytes 393224 | tf_op jit(solution)/shard_map/ppermute | solution.py:649
  69.4 7.8 %collective-permute-start.2 = (f32[2,8,16,128]{3,2,1,0:T(8,128)S(1)}, f32[2,8,16,128]{3,2,1,0:T(8,128)S(1)}, u32[]{:S(2)}, u32[]{:S(2)}) collective-permute-start(f32[2,8,16,128]{3,2,1,0:T(8,128)S(1)} %get-tuple-element.28.refs_0_), channel_id=1, source_target_pairs={{0,1},{1,2},{2,3},{3,0},{4,5},{5,6},{6,7},{7,4},{8,9},{9,10},{10,1... | collective-permute-start | bytes 393224 | tf_op jit(solution)/shard_map/ppermute | solution.py:649
  69.4 8.9 %collective-permute-start.5 = (f32[2,8,16,128]{3,2,1,0:T(8,128)S(1)}, f32[2,8,16,128]{3,2,1,0:T(8,128)S(1)}, u32[]{:S(2)}, u32[]{:S(2)}) collective-permute-start(f32[2,8,16,128]{3,2,1,0:T(8,128)S(1)} %get-tuple-element.28.refs_0_), channel_id=1, source_target_pairs={{0,4},{4,0},{1,5},{5,1},{2,6},{6,2},{3,7},{7,3},{8,12},{12,8},{9,1... | collective-permute-start | bytes 393224 | tf_op jit(solution)/shard_map/ppermute | solution.py:609
  71.8 6.5 %collective-permute-start.8 = (f32[2,8,16,128]{3,2,1,0:T(8,128)S(1)}, f32[2,8,16,128]{3,2,1,0:T(8,128)S(1)}, u32[]{:S(2)}, u32[]{:S(2)}) collective-permute-start(f32[2,8,16,128]{3,2,1,0:T(8,128)S(1)} %collective-permute-done.4.refs_3_), channel_id=1, source_target_pairs={{0,4},{4,0},{1,5},{5,1},{2,6},{6,2},{3,7},{7,3},{8,12},{12,8},{9,1... | collective-permute-start | bytes 393224 | tf_op jit(solution)/shard_map/ppermute | solution.py:609
  73.8 4.5 %collective-permute-start.7 = (f32[2,8,16,128]{3,2,1,0:T(8,128)S(1)}, f32[2,8,16,128]{3,2,1,0:T(8,128)S(1)}, u32[]{:S(2)}, u32[]{:S(2)}) collective-permute-start(f32[2,8,16,128]{3,2,1,0:T(8,128)S(1)} %collective-permute-done.3.refs_2_), channel_id=1, source_target_pairs={{0,4},{4,0},{1,5},{5,1},{2,6},{6,2},{3,7},{7,3},{8,12},{12,8},{9,1... | collective-permute-start | bytes 393224 | tf_op jit(solution)/shard_map/ppermute | solution.py:609
  77.2 2.0 %collective-permute-start.6 = (f32[2,8,16,128]{3,2,1,0:T(8,128)S(1)}, f32[2,8,16,128]{3,2,1,0:T(8,128)S(1)}, u32[]{:S(2)}, u32[]{:S(2)}) collective-permute-start(f32[2,8,16,128]{3,2,1,0:T(8,128)S(1)} %collective-permute-done.2.refs_1_), channel_id=1, source_target_pairs={{0,4},{4,0},{1,5},{5,1},{2,6},{6,2},{3,7},{7,3},{8,12},{12,8},{9,1... | collective-permute-start | bytes 393224 | tf_op jit(solution)/shard_map/ppermute | solution.py:609
  80.0 7.8 %collective-permute-start.9 = (f32[4,2,5,16,128]{4,3,2,1,0:T(8,128)S(1)}, f32[4,2,5,16,128]{4,3,2,1,0:T(8,128)S(1)}, u32[]{:S(2)}, u32[]{:S(2)}) collective-permute-start(f32[4,2,5,16,128]{4,3,2,1,0:T(8,128)S(1)} %shard_map.51), channel_id=1, source_target_pairs={{0,8},{1,9},{2,10},{3,11},{12,4},{13,5},{14,6},{15,7},{8,16},{9,17... | collective-permute-start | bytes 983048 | tf_op jit(solution)/shard_map/ppermute | solution.py:618
  87.8 1.8 %collective-permute-start.10 = (f32[4,2,5,16,128]{4,3,2,1,0:T(8,128)S(1)}, f32[4,2,5,16,128]{4,3,2,1,0:T(8,128)S(1)}, u32[]{:S(2)}, u32[]{:S(2)}) collective-permute-start(f32[4,2,5,16,128]{4,3,2,1,0:T(8,128)S(1)} %collective-permute-done.9.refs_8_), channel_id=1, source_target_pairs={{0,4},{4,0},{1,5},{5,1},{2,6},{6,2},{3,7},{7,3},{8,12},{12,8},{9,1... | collective-permute-start | bytes 983048 | tf_op jit(solution)/shard_map/ppermute | solution.py:609
  92.7 19.8 %collective-permute-start.11 = (f32[18,16,128]{2,1,0:T(8,128)S(1)}, f32[18,16,128]{2,1,0:T(8,128)S(1)}, u32[]{:S(2)}, u32[]{:S(2)}) collective-permute-start(f32[18,16,128]{2,1,0:T(8,128)S(1)} %get-tuple-element.30), channel_id=1, source_target_pairs={{0,8},{1,9},{2,10},{3,11},{12,4},{13,5},{14,6},{15,7},{8,16},{9,17... | collective-permute-start | bytes 442376 | tf_op jit(solution)/shard_map/ppermute | solution.py:618
  112.5 3.8 %collective-permute-start.12 = (f32[18,16,128]{2,1,0:T(8,128)S(1)}, f32[18,16,128]{2,1,0:T(8,128)S(1)}, u32[]{:S(2)}, u32[]{:S(2)}) collective-permute-start(f32[18,16,128]{2,1,0:T(8,128)S(1)} %collective-permute-done.11.one), channel_id=1, source_target_pairs={{0,4},{4,0},{1,5},{5,1},{2,6},{6,2},{3,7},{7,3},{8,12},{12,8},{9,1... | collective-permute-start | bytes 442376 | tf_op jit(solution)/shard_map/ppermute | solution.py:609

commit v4 on v3

--- a/solution.py
+++ b/solution.py
@@ -1,6 +1,3 @@
-import functools
-import math
-
 import jax
 import jax.numpy as jnp
 from jax import lax
@@ -51,37 +48,14 @@
     return jnp.full(shape, scalar, jnp.int32) == 0
 
 
-class Shell:
-    def __init__(self, low, high, arrays):
-        self.low, self.high, self.arrays = low, high, arrays
-        self.planes = math.ceil(len(low) / 4)
-        self.nz = 4 * self.planes
-        self.ny = 2 * arrays
-        self.strips = 8 * arrays
-        self.nx = math.ceil(self.strips / 16)
-        self.coef = self.nz + self.ny + self.nx
-        self.sent = self.coef + 2
-        self.nz2 = 5 * self.planes
-        self.side = math.ceil(self.nz2 / 16)
-        self.y2 = self.nz2 + self.side
-        self.x2 = self.y2 + self.ny
-        self.got = self.x2 + self.nx
-        self.first = min(16 * self.side - self.nz2, self.ny)
-        assert self.strips + self.ny - self.first <= 16 * self.nx
-
-    def edge(self, i):
-        if i < self.first:
-            pos = self.nz2 + i
-            return self.nz2 + pos // 16, pos % 16
-        pos = self.strips + i - self.first
-        return self.x2 + pos // 16, pos % 16
-
-
-DOWN = Shell(
-    [(c, t) for c in (0, 1, 3) for t in range(4)] + [(c, t) for c in (2, 4) for t in range(3)],
-    [(c, 15 - t) for c in (0, 1, 3) for t in range(4)] + [(c, 15 - t) for c in (2, 4) for t in range(3)],
-    5,
-)
+ARRAYS = 5
+FACE = 17
+SENT_Y, SENT_X, SENT_COEF, SENT = 17, 27, 30, 32
+GOT_ROWS, GOT_STRIPS, GOT_Y, GOT_X, GOT = 17, 20, 22, 32, 35
+
+
+def face_planes(j):
+    return [(1 + j, 0), (1 + j, 1), (1 + j, 2), (0, j)]
 
 
 def merge_strips(placed, base=None):
@@ -93,43 +67,53 @@
     return total
 
 
-def pack_shell(shell, get, out, bit_x, bit_y):
+def swap_lanes(cells):
+    lane = iota(cells.shape, 1)
+    return jnp.where((lane & 1) == 0, pltpu.roll(cells, cells.shape[1] - 1, 1), pltpu.roll(cells, 1, 1))
+
+
+def pack_shell(get, out, bit_x, bit_y):
     x0, y0 = is_zero(bit_x), is_zero(bit_y)
-    for first, faces in ((0, shell.low), (4, shell.high)):
-        for i, (c, t) in enumerate(faces):
-            j = 4 * (i % shell.planes)
-            out[first + i // shell.planes, j : j + 4] = get(c, t).reshape(4, 8, 128)
+    mask = odd(32, 128)
     for k in range(8):
+        high, j = k >= 4, k % 4
+        for i, (c, far) in enumerate(face_planes(j)):
+            out[k, 4 * i : 4 * i + 4] = get(c, 15 - far if high else far).reshape(4, 8, 128)
+        t = 12 if high else 3
+        one, two = get(1, t), swap_lanes(get(3, t))
+        both = jnp.where(mask, one, two) if high else jnp.where(mask, two, one)
+        out[k, 16] = both[8 * j : 8 * j + 8]
         strips = []
         for tl in range(2):
-            for c in range(shell.arrays):
+            for c in range(ARRAYS):
                 v = get(c, 2 * k + tl)
-                out[k, shell.nz + tl * shell.arrays + c] = jnp.where(y0, v[24:32], v[0:8])
+                out[k, SENT_Y + tl * ARRAYS + c] = jnp.where(y0, v[24:32], v[0:8])
                 for g in range(4):
                     tile = v[8 * g : 8 * g + 8]
                     strips.append(jnp.where(x0, pltpu.roll(tile, 8, 1), tile))
-        for i in range(shell.nx):
-            out[k, shell.nz + shell.ny + i] = merge_strips(list(enumerate(strips[16 * i : 16 * i + 16])))
-
-
-def cross_kernel(shell, meta, bricks, recv, out):
+        for i in range(3):
+            out[k, SENT_X + i] = merge_strips(list(enumerate(strips[16 * i : 16 * i + 16])))
+
+
+def cross_kernel(meta, bricks, recv, out):
     slab, me = meta[0], meta[1]
     for i in range(4):
         src = jnp.where(me >= 4, bricks[slab, 4 + i], bricks[slab, i])
-        out[i, 0 : shell.nz] = recv[src, 0 : shell.nz]
+        out[i, 0:FACE] = recv[src, 0:FACE]
         for j in range(2):
-            coef = recv[bricks[slab, 2 * i + j], shell.coef : shell.coef + 2]
-            out[i, shell.nz + 2 * j : shell.nz + 2 * j + 2] = coef
-
-
-def mid_kernel(shell, meta, bricks, recv, cross, out, coef, faces):
+            coef = recv[bricks[slab, 2 * i + j], SENT_COEF:SENT]
+            out[i, FACE + 2 * j : FACE + 2 * j + 2] = coef
+
+
+def mid_kernel(meta, bricks, recv, cross, out, coef, faces):
     slab, me = meta[0], meta[1]
-    faces[0:8] = recv[:, 0 : shell.nz]
-    faces[8:12] = cross[:, 0 : shell.nz]
+    faces[0:8] = recv[:, 0:FACE]
+    faces[8:12] = cross[:, 0:FACE]
     for p in range(8):
-        coef[0, p] = recv[bricks[slab, p], shell.coef : shell.coef + 2]
-        j = shell.nz + 2 * (p & 1)
+        coef[0, p] = recv[bricks[slab, p], SENT_COEF:SENT]
+        j = FACE + 2 * (p & 1)
         coef[1, p] = cross[p >> 1, j : j + 2]
+    row = iota((8, 128), 0)
     for p in range(8):
         bx, by, bz = p & 1, (p >> 1) & 1, p >> 2
         dest = bricks[slab, p]
@@ -141,57 +125,70 @@
         def strip_of(tile):
             return pltpu.roll(tile, 8, 1) if bx else tile
 
+        def rows_of(at):
+            one, two, three, last = (faces[at, 4 * i + (3 if by else 0)] for i in range(4))
+            if by:
+                shared = jnp.where(row >= 3, two, pltpu.roll(three, 3, 0))
+            else:
+                shared = jnp.where(row < 5, two, pltpu.roll(three, 5, 0))
+            return [one, shared, last]
+
         at_own, at_y, at_x, at_xy = src(p), src(p ^ 2), src(p ^ 1), src(p ^ 3)
-        gy = 3 if by else 0
-        strips = []
-        for j in range(shell.planes):
-            out[dest, 5 * j : 5 * j + 4] = faces[at_own, 4 * j : 4 * j + 4]
-            out[dest, 5 * j + 4] = faces[at_y, 4 * j + gy]
-            strips += [strip_of(faces[at_x, 4 * j + g]) for g in range(4)]
-            strips.append(strip_of(faces[at_xy, 4 * j + gy]))
+        out[dest, 0:FACE] = faces[at_own]
+        for i, tile in enumerate(rows_of(at_y)):
+            out[dest, GOT_ROWS + i] = tile
+        strips = [strip_of(faces[at_x, i]) for i in range(16)] + [strip_of(tile) for tile in rows_of(at_xy)]
         from_y, from_x, from_xy = bricks[slab, p ^ 2], bricks[slab, p ^ 1], bricks[slab, p ^ 3]
-        y1, x1 = shell.nz, shell.nz + shell.ny
-        out[dest, shell.y2 : shell.x2] = recv[from_y, y1:x1]
-        placed = {}
-        for i, strip in enumerate(strips):
-            placed.setdefault(shell.nz2 + i // 16, []).append((i % 16, strip))
-        for i in range(shell.ny):
-            tile, pos = shell.edge(i)
-            placed.setdefault(tile, []).append((pos, strip_of(recv[from_xy, y1 + i])))
-        for i in range(shell.nx):
-            tile = recv[from_x, x1 + i]
-            out[dest, shell.x2 + i] = merge_strips(placed.get(shell.x2 + i, []), tile)
-        for i in range(shell.side):
-            out[dest, shell.nz2 + i] = merge_strips(placed[shell.nz2 + i])
-
-
-def unpack_shell(shell, recv, grids, bit_x):
-    lane = iota((8, 128), 1)
-    x0 = is_zero(bit_x)
+        strips += [strip_of(recv[from_xy, SENT_Y + i]) for i in range(2 * ARRAYS)]
+        for i in range(2):
+            out[dest, GOT_STRIPS + i] = merge_strips(list(enumerate(strips[16 * i : 16 * i + 16])))
+        out[dest, GOT_Y:GOT_X] = recv[from_y, SENT_Y:SENT_X]
+        out[dest, GOT_X:GOT] = recv[from_x, SENT_X:SENT_COEF]
+
+
+def unpack_shell(recv, grids, bit_x, bit_y):
+    row, lane = iota((8, 128), 0), iota((8, 128), 1)
+    x0, y0 = is_zero(bit_x), is_zero(bit_y)
     in_x = (x0 & (lane < 8)) | (jnp.logical_not(x0) & (lane >= 120))
+    five = (y0 & (row < 5)) | (jnp.logical_not(y0) & (row >= 3))
+    three = (y0 & (row < 3)) | (jnp.logical_not(y0) & (row >= 5))
 
     def strip(tile, pos):
         shift = (jnp.where(bit_x == 0, 0, 120) + 128 - 8 * pos) % 128
         return jnp.where(in_x, pltpu.roll(tile, shift, 1), 0.0)
 
-    for first, faces, shift in ((0, shell.low, OWN + 16), (4, shell.high, OWN - 16)):
-        for i, (c, t) in enumerate(faces):
-            k, j = first + i // shell.planes, i % shell.planes
-            for g in range(5):
-                n = 5 * j + g
-                rows = slice(8 * g, 8 * g + 8)
-                grids[c][shift + t, rows, 0:128] = recv[k, n]
-                grids[c][shift + t, rows, 128:256] = strip(recv[k, shell.nz2 + n // 16], n % 16)
-    for t in range(16):
-        k, tl = t // 2, t % 2
-        for c in range(shell.arrays):
-            i = tl * shell.arrays + c
-            tile, pos = shell.edge(i)
-            grids[c][OWN + t, 32:40, 0:128] = recv[k, shell.y2 + i]
-            grids[c][OWN + t, 32:40, 128:256] = strip(recv[k, tile], pos)
+    def rows_of(tiles):
+        one, shared, last = tiles
+        moved = jnp.where(y0, pltpu.roll(shared, 3, 0), pltpu.roll(shared, 5, 0))
+        return [one, jnp.where(five, shared, 0.0), jnp.where(three, moved, 0.0), last]
+
+    for k in range(8):
+        high, j = k >= 4, k % 4
+        rows = rows_of([recv[k, GOT_ROWS + i] for i in range(3)])
+        sides = rows_of([strip(recv[k, GOT_STRIPS + 1], i) for i in range(3)])
+        for i, (c, far) in enumerate(face_planes(j)):
+            at = OWN - 1 - far if high else OWN + 16 + far
             for g in range(4):
-                n = 4 * i + g
-                grids[c][OWN + t, 8 * g : 8 * g + 8, 128:256] = strip(recv[k, shell.x2 + n // 16], n % 16)
+                grids[c][at, 8 * g : 8 * g + 8, 0:128] = recv[k, 4 * i + g]
+                grids[c][at, 8 * g : 8 * g + 8, 128:256] = strip(recv[k, GOT_STRIPS], 4 * i + g)
+            grids[c][at, 32:40, 0:128] = rows[i]
+            grids[c][at, 32:40, 128:256] = sides[i]
+        at = 1 if high else 24
+        both = recv[k, 16]
+        for c, cells in ((1, both), (3, swap_lanes(both))):
+            grids[c][at, 8 * j : 8 * j + 8, 0:128] = cells
+            grids[c][at, 8 * j : 8 * j + 8, 128:256] = jnp.zeros((8, 128), F32)
+            grids[c][at, 32:40] = jnp.zeros((8, 256), F32)
+        for tl in range(2):
+            for c in range(ARRAYS):
+                i = tl * ARRAYS + c
+                at = OWN + 2 * k + tl
+                grids[c][at, 32:40, 0:128] = recv[k, GOT_Y + i]
+                grids[c][at, 32:40, 128:256] = strip(recv[k, GOT_STRIPS + 1], 3 + i)
+                for g in range(4):
+                    n = 4 * i + g
+                    side = strip(recv[k, GOT_X + n // 16], n % 16)
+                    grids[c][at, 8 * g : 8 * g + 8, 128:256] = side
 
 
 def pair_of(cells, t, red, mask):
@@ -215,7 +212,7 @@
         for j in range(1, 4):
             tile = jnp.where(group == j, cells[32 * h + 8 * j : 32 * h + 8 * j + 8], tile)
         for k in range(8):
-            out[k, DOWN.coef + h] = tile
+            out[k, SENT_COEF + h] = tile
 
 
 def first_kernel(meta, bricks, u, f, a, out, small):
@@ -226,7 +223,7 @@
     def get(c, t):
         return pair_of(sources[c][0], t, sources[c][1], mask)
 
-    pack_shell(DOWN, get, out, bit_x, bit_y)
+    pack_shell(get, out, bit_x, bit_y)
     pack_bottom_coef(a, out, small)
 
 
@@ -270,7 +267,7 @@
     for t in range(16):
         for grid, (cells, red) in zip(grids, sources):
             grid[OWN + t, 0:32, 0:128] = pair_of(cells, t, red, own)
-    unpack_shell(DOWN, recv, grids, bit_x)
+    unpack_shell(recv, grids, bit_x, bit_y)
     zero = jnp.zeros((40, 256), F32)
     for k in (0, 25):
         u_r[k] = zero
@@ -286,10 +283,13 @@
     no_low = (slab == 0) & (bit_z == 0)
     no_high = (slab == SLABS - 1) & (bit_z == 1)
 
+    mask_int = (row + lane) & 1
+
     def invert(k, carry):
         gone = jnp.where((no_low & (k < OWN)) | (no_high & (k >= OWN + 16)), 1, 0)
         keep = inside & is_zero(gone, (40, 256))
-        i_r[k] = jnp.where(keep, 1.0 / (i_r[k] + 6.0), 0.0)
+        far = jnp.where(k == 1, mask_int, jnp.where(k == 24, 1 - mask_int, 1)) == 1
+        i_r[k] = jnp.where(keep & far, 1.0 / (i_r[k] + 6.0), 0.0)
         ends = jnp.where((k == 1) | (k == 24), 1, 0)
         i_b[k] = jnp.where(keep & is_zero(ends, (40, 256)), 1.0 / (i_b[k] + 6.0), 0.0)
         return carry
@@ -410,9 +410,7 @@
     total = jnp.zeros((16, 128), F32)
     for i in range(16):
         total = total + rb[3 + i] * weights[i]
-    total = total[0:8] + total[8:16]
-    for i in range(SLABS):
-        part[i] = total
+    part[...] = total[0:8] + total[8:16]
 
 
 def bottom_kernel(meta, rb, one, two, es, e_r, e_b, g_r, g_b, i_r, i_b, low, high):
@@ -531,13 +529,11 @@
 
 
 def up_kernel(
-    meta, bricks, sums, es, ec_b, r_r, r_b, ci_r, ci_b, u1_b, f_r, f_b, i_r, i_b, out,
+    meta, bricks, sum_0, sum_1, sum_2, sum_3, es, ec_b, r_r, r_b, ci_r, ci_b, u1_b, f_r, f_b, i_r, i_b, out,
     e_r, e_b, small, wide, planes, tall, u_r, u_b,
 ):
     slab, _, bit_x, bit_y, bit_z = place_of(meta, bricks)
-    total = sums[0]
-    for i in range(1, SLABS):
-        total = total + sums[i]
+    total = (sum_0[...] + sum_1[...]) + (sum_2[...] + sum_3[...])
     mean = jnp.sum(total) * (1.0 / (SLABS * 16 * 16 * 64))
     for i in range(22):
         shifted = es[i] - mean
@@ -618,6 +614,14 @@
     return lax.ppermute(x, ALL, pairs)
 
 
+def around_ring(x, stride, step):
+    pairs = []
+    for s in range(SLABS):
+        at = s // stride % 4
+        pairs.append((s, s + ((at + step) % 4 - at) * stride))
+    return lax.ppermute(x, "slab", pairs)
+
+
 def among(x):
     return lax.all_to_all(x, LB, split_axis=0, concat_axis=0, tiled=True)
 
@@ -626,13 +630,14 @@
     meta = jnp.stack([lax.axis_index("slab"), lax.axis_index(LB)]).astype(jnp.int32)
     smem = [meta, brick_map]
     fine = (26, 40, 256)
-    packed = run(first_kernel, [(8, DOWN.sent, 8, 128)], smem, [u_init, source, coeffs], [(8, 32, 128)])
+    packed = run(
+        first_kernel, [(8, SENT, 8, 128)], smem, [u_init, source, coeffs], [(8, 32, 128)],
+    )
     got = among(packed)
-    leaving = run(functools.partial(cross_kernel, DOWN), [(4, DOWN.nz + 4, 8, 128)], smem, [got])
+    leaving = run(cross_kernel, [(4, FACE + 4, 8, 128)], smem, [got])
     cross = to_slabs(leaving, False)
     sent, coef = run(
-        functools.partial(mid_kernel, DOWN), [(8, DOWN.got, 8, 128), (2, 8, 2, 8, 128)], smem, [got, cross],
-        [(12, DOWN.nz, 8, 128)],
+        mid_kernel, [(8, GOT, 8, 128), (2, 8, 2, 8, 128)], smem, [got, cross], [(12, FACE, 8, 128)],
     )
     coef_other = swap_cores(coef)
     halo = among(sent)
@@ -655,14 +660,16 @@
     coarse = (28, 32, 128)
     faces = (4, 2, 5, 16, 128)
     rb, rb_send, part, ec_b, r_r, r_b, ci_r, ci_b = run(
-        coarse_down_kernel, [(22, 16, 128), (18, 16, 128), (SLABS, 8, 128)] + [coarse] * 5, smem,
+        coarse_down_kernel, [(22, 16, 128), (18, 16, 128), (8, 128)] + [coarse] * 5, smem,
         boxes + [cross, other, weights],
         [(8, 2, 8, 16, 128), faces, faces, coarse, coarse, coarse, (2, 22, 32, 128), (352, 128)],
     )
     cross = to_slabs(rb_send, True)
-    sums = lax.all_to_all(part, "slab", split_axis=0, concat_axis=0, tiled=True)
-    cross, sums = lax.optimization_barrier((cross, sums))
+    rows = [around_ring(part, 1, d) for d in range(1, 4)]
+    cross, *rows = lax.optimization_barrier((cross, *rows))
     other = swap_cores(cross)
+    part = (part + rows[0]) + (rows[1] + rows[2])
+    sums = [part] + [around_ring(part, 4, d) for d in range(1, 4)]
     bottom = (28, 16, 128)
     es = run(
         bottom_kernel, [(22, 16, 128)], [meta], [rb, cross, other],
@@ -670,7 +677,7 @@
     )
     return run(
         up_kernel, [(1, 32, 32, 128)], smem,
-        [sums, es, ec_b, r_r, r_b, ci_r, ci_b, u_b, f_r, f_b, i_r, i_b],
+        sums + [es, ec_b, r_r, r_b, ci_r, ci_b, u_b, f_r, f_b, i_r, i_b],
         [coarse, coarse, (352, 128), (22, 32, 128), (640, 128), (20, 2, 64, 128), (22, 40, 256), (22, 40, 256)],
     )
 

time: 125 us -> 118 us (0.944)
  blocking collectives: 40.5 us -> 20.8 us
  starting transfers between devices: 24.4 us -> 36.8 us
    all_to_all x1 -> x0, blocking collectives: 18.5 us -> none  [body(): sums = lax.all_to_all(part, 'slab', split_axis=0, concat_axis=0, tiled=True)]
    ppermute x0 -> x6, starting transfers between devices: none -> 12.4 us  [around_ring(): return lax.ppermute(x, 'slab', pairs)]
    ppermute x0 -> x6, waiting for transfers between devices: none -> 3.38 us  [around_ring(): return lax.ppermute(x, 'slab', pairs)]
    all_to_all x1, waiting for transfers between devices: 13.5 us -> 11.7 us  [among(): return lax.all_to_all(x, LB, split_axis=0, concat_axis=0, tiled=True)]
    all_to_all x1, blocking collectives: 22 us -> 20.8 us  [among(): return lax.all_to_all(x, LB, split_axis=0, concat_axis=0, tiled=True)]
  transfers between devices with their start and end apart: 14 -> 20, of which waited for: 9 -> 10; matrix products, arithmetic and copies ran while one was open for 0% -> 0% of each run, Pallas kernels for 2% -> 5%
where the time goes in v4:
time: 118 us; the launch traced here: 117 us
  starting transfers between devices  36.8 us (31%)
  waiting for transfers between devices  31.1 us (26%)
  Pallas kernels  23.5 us (20%)
  blocking collectives  20.8 us (18%)
  local copies, waits for them, and re-layouts  4.91 us (4%)
    pallas_call x9, Pallas kernels, run(): pl.pallas_call(kernel, out_shape=shapes[0] if single else shapes, in_spec...  23.5 us
    all_to_all x1, blocking collectives, among(): return lax.all_to_all(x, LB, split_axis=0, concat_axis=0, tiled=True)  20.8 us
    ppermute x6, starting transfers between devices, around_ring(): return lax.ppermute(x, 'slab', pairs)  12.4 us
    all_to_all x1, waiting for transfers between devices, among(): return lax.all_to_all(x, LB, split_axis=0, concat_axis=0, tiled=True)  11.7 us
    ppermute x3, waiting for transfers between devices, to_slabs(): return lax.ppermute(x, ALL, pairs)  10.7 us
    ppermute x7, starting transfers between devices, swap_cores(): return lax.ppermute(x, 'level', [(0, 1), (1, 0)])  10.5 us
    all_to_all x1, starting transfers between devices, among(): return lax.all_to_all(x, LB, split_axis=0, concat_axis=0, tiled=True)  5.82 us
    ppermute x3, starting transfers between devices, to_slabs(): return lax.ppermute(x, ALL, pairs)  5.72 us
  transfers between devices with their start and end apart: 20, of which 10 were waited for; matrix products, arithmetic and copies ran while one was open for 0% of the time, Pallas kernels for 5%

profile of v4, /device:TPU:1, one launch (start us, length us, event | category | flops | bytes accessed | tf_op | source)
XLA Modules:
  0.0 117.3 jit_solution(378695438696350692)
XLA Ops:
  0.0 0.8 copy.11.bricks
  0.8 0.1 pad_add_fusion.meta
  0.8 0.0 copy-start
  0.8 1.0 copy-done
  1.9 0.0 copy-start.2
  1.9 1.0 copy-done.2
  2.9 0.0 copy-start.4
  2.9 1.0 copy-done.4
  4.0 1.7 %shard_map.46 = f32[8,32,8,128]{3,2,1,0:T(8,128)S(1)} custom-call(s32[2]{0:T(128)S(1)} %pad_add_fusion.meta, s32[16,8]{1,0:T(8,128)S(1)} %copy.11.bricks, f32[1,32,32,128]{3,2,1,0:T(8,128)S(1)} %copy-done, f32[1,32,32,128]{3,2,1,0:T(8,128)S(1)} %copy-done.2, f32[1,32,32,128]{3,2,1,0:T(8,128)S(1)} %copy-done.4), custom_call_target="tpu_custom_call" | custom-call | tf_op jit(solution)/shard_map/pallas_call | solution.py:21
  5.6 20.8 %all_to_all.10.recv = f32[8,32,8,128]{3,2,1,0:T(8,128)S(1)} all-to-all(f32[8,32,8,128]{3,2,1,0:T(8,128)S(1)} %shard_map.46), channel_id=1, replica_groups=mesh['slab'=16,'level'=2,'bottom'=4] {'level','bottom'}, dimensions={0} | all-to-all | bytes 2097152 | tf_op jit(solution)/shard_map/all_to_all | solution.py:626
  26.4 0.7 shard_map.47
  27.1 3.1 %collective-permute-start = (f32[4,21,8,128]{3,2,1,0:T(8,128)S(1)}, f32[4,21,8,128]{3,2,1,0:T(8,128)S(1)}, u32[]{:S(2)}, u32[]{:S(2)}) collective-permute-start(f32[4,21,8,128]{3,2,1,0:T(8,128)S(1)} %shard_map.47), channel_id=1, source_target_pairs={{8,0},{9,1},{10,2},{11,3},{4,12},{5,13},{6,14},{7,15},{16,8},{17,9... | collective-permute-start | bytes 1032200 | tf_op jit(solution)/shard_map/ppermute | solution.py:614
  30.3 4.2 %collective-permute-done.cross = f32[4,21,8,128]{3,2,1,0:T(8,128)S(1)} collective-permute-done((f32[4,21,8,128]{3,2,1,0:T(8,128)S(1)}, f32[4,21,8,128]{3,2,1,0:T(8,128)S(1)}, u32[]{:S(2)}, u32[]{:S(2)}) %collective-permute-start) | collective-permute-done | bytes 344096 | tf_op jit(solution)/shard_map/ppermute | solution.py:614
  34.4 1.3 %shard_map.48 = (f32[8,35,8,128]{3,2,1,0:T(8,128)S(1)}, f32[2,8,2,8,128]{4,3,2,1,0:T(8,128)S(1)}) custom-call(s32[2]{0:T(128)S(1)} %pad_add_fusion.meta, s32[16,8]{1,0:T(8,128)S(1)} %copy.11.bricks, f32[8,32,8,128]{3,2,1,0:T(8,128)S(1)} %all_to_all.10.recv, f32[4,21,8,128]{3,2,1,0:T(8,128)S(1)} %collective-permute-done.cross), custom_call_target="tpu_custom_call" | custom-call | tf_op jit(solution)/shard_map/pallas_call | solution.py:21
  35.7 0.0 copy-start.6
  35.8 1.0 copy-done.6
  36.8 0.0 copy-start.1
  36.8 5.8 %all-to-all-start.1 = ((f32[8,35,8,128]{3,2,1,0:T(8,128)}), f32[8,35,8,128]{3,2,1,0:T(8,128)S(1)}, u32[]{:S(2)}, u32[]{:S(2)}) async-start(f32[8,35,8,128]{3,2,1,0:T(8,128)} %copy-done.6), calls=%async_computation.1 | async-start | bytes 2293760 | tf_op jit(solution)/shard_map/all_to_all | solution.py:626
  42.6 0.2 collective-permute-start.1
  42.8 1.2 %collective-permute-done.1.there = f32[2,8,2,8,128]{4,3,2,1,0:T(8,128)S(1)} collective-permute-done((f32[2,8,2,8,128]{4,3,2,1,0:T(8,128)S(1)}, f32[2,8,2,8,128]{4,3,2,1,0:T(8,128)S(1)}, u32[]{:S(2)}, u32[]{:S(2)}) %collective-permute-start.1) | collective-permute-done | bytes 131104 | tf_op jit(solution)/shard_map/ppermute | solution.py:605
  43.9 3.0 %shard_map.49.refs_10_ = f32[16,16,128]{2,1,0:T(8,128)S(1)} custom-call(s32[2]{0:T(128)S(1)} %pad_add_fusion.meta, f32[2,8,2,8,128]{4,3,2,1,0:T(8,128)S(1)} %get-tuple-element.28.here, f32[2,8,2,8,128]{4,3,2,1,0:T(8,128)S(1)} %collective-permute-done.1.there), custom_call_target="tpu_custom_call" | custom-call | tf_op jit(solution)/shard_map/pallas_call | solution.py:21
  46.9 11.7 %all-to-all-done.1.recv = f32[8,35,8,128]{3,2,1,0:T(8,128)S(1)} async-done(((f32[8,35,8,128]{3,2,1,0:T(8,128)}), f32[8,35,8,128]{3,2,1,0:T(8,128)S(1)}, u32[]{:S(2)}, u32[]{:S(2)}) %all-to-all-start.1) | async-done | bytes 1146912 | tf_op jit(solution)/shard_map/all_to_all | solution.py:626
  58.6 0.0 copy-done.1
  58.6 0.0 copy-done.3
  58.6 0.0 copy-done.5
  58.7 4.7 %shard_map.50 = (f32[2,8,16,128]{3,2,1,0:T(8,128)S(1)}, f32[26,40,256]{2,1,0:T(8,128)S(1)}, f32[26,40,256]{2,1,0:T(8,128)S(1)}, f32[26,40,256]{2,1,0:T(8,128)S(1...) custom-call(s32[2]{0:T(128)S(1)} %pad_add_fusion.meta, s32[16,8]{1,0:T(8,128)S(1)} %copy.11.bricks, ...), custom_call_target="tpu_custom_call" | custom-call | tf_op jit(solution)/shard_map/pallas_call | solution.py:21
  63.3 1.1 collective-permute-start.4
  64.4 1.4 %collective-permute-start.3 = (f32[2,8,16,128]{3,2,1,0:T(8,128)S(1)}, f32[2,8,16,128]{3,2,1,0:T(8,128)S(1)}, u32[]{:S(2)}, u32[]{:S(2)}) collective-permute-start(f32[2,8,16,128]{3,2,1,0:T(8,128)S(1)} %get-tuple-element.30.refs_0_), channel_id=1, source_target_pairs={{0,2},{1,3},{2,0},{3,1},{4,6},{5,7},{6,4},{7,5},{8,10},{9,11},{10,... | collective-permute-start | bytes 393224 | tf_op jit(solution)/shard_map/ppermute | solution.py:654
  65.8 0.0 collective-permute-start.2
  65.8 0.8 collective-permute-start.5
  66.5 1.6 %collective-permute-done.4.refs_3_ = f32[2,8,16,128]{3,2,1,0:T(8,128)S(1)} collective-permute-done((f32[2,8,16,128]{3,2,1,0:T(8,128)S(1)}, f32[2,8,16,128]{3,2,1,0:T(8,128)S(1)}, u32[]{:S(2)}, u32[]{:S(2)}) %collective-permute-start.4) | collective-permute-done | bytes 131104 | tf_op jit(solution)/shard_map/ppermute | solution.py:654
  68.1 2.0 %collective-permute-start.8 = (f32[2,8,16,128]{3,2,1,0:T(8,128)S(1)}, f32[2,8,16,128]{3,2,1,0:T(8,128)S(1)}, u32[]{:S(2)}, u32[]{:S(2)}) collective-permute-start(f32[2,8,16,128]{3,2,1,0:T(8,128)S(1)} %collective-permute-done.4.refs_3_), channel_id=1, source_target_pairs={{0,4},{4,0},{1,5},{5,1},{2,6},{6,2},{3,7},{7,3},{8,12},{12,8},{9,1... | collective-permute-start | bytes 393224 | tf_op jit(solution)/shard_map/ppermute | solution.py:605
  70.1 0.0 collective-permute-done.3.refs_2_
  70.1 3.1 %collective-permute-start.7 = (f32[2,8,16,128]{3,2,1,0:T(8,128)S(1)}, f32[2,8,16,128]{3,2,1,0:T(8,128)S(1)}, u32[]{:S(2)}, u32[]{:S(2)}) collective-permute-start(f32[2,8,16,128]{3,2,1,0:T(8,128)S(1)} %collective-permute-done.3.refs_2_), channel_id=1, source_target_pairs={{0,4},{4,0},{1,5},{5,1},{2,6},{6,2},{3,7},{7,3},{8,12},{12,8},{9,1... | collective-permute-start | bytes 393224 | tf_op jit(solution)/shard_map/ppermute | solution.py:605
  73.2 0.4 collective-permute-done.2.refs_1_
  73.6 1.0 collective-permute-start.6
  74.6 0.0 collective-permute-done.5.refs_4_
  74.6 0.0 collective-permute-done.8.refs_7_
  74.6 0.0 collective-permute-done.7.refs_6_
  74.6 1.0 collective-permute-done.6.refs_5_
  75.6 0.8 shard_map.51
  76.4 1.3 %collective-permute-start.9 = (f32[4,2,5,16,128]{4,3,2,1,0:T(8,128)S(1)}, f32[4,2,5,16,128]{4,3,2,1,0:T(8,128)S(1)}, u32[]{:S(2)}, u32[]{:S(2)}) collective-permute-start(f32[4,2,5,16,128]{4,3,2,1,0:T(8,128)S(1)} %shard_map.51), channel_id=1, source_target_pairs={{0,8},{1,9},{2,10},{3,11},{12,4},{13,5},{14,6},{15,7},{8,16},{9,17... | collective-permute-start | bytes 983048 | tf_op jit(solution)/shard_map/ppermute | solution.py:614
  77.7 6.5 %collective-permute-done.9.refs_8_ = f32[4,2,5,16,128]{4,3,2,1,0:T(8,128)S(1)} collective-permute-done((f32[4,2,5,16,128]{4,3,2,1,0:T(8,128)S(1)}, f32[4,2,5,16,128]{4,3,2,1,0:T(8,128)S(1)}, u32[]{:S(2)}, u32[]{:S(2)}) %collective-permute-start.9) | collective-permute-done | bytes 327712 | tf_op jit(solution)/shard_map/ppermute | solution.py:614
  84.2 0.5 collective-permute-start.10
  84.7 1.3 %collective-permute-done.10.refs_9_ = f32[4,2,5,16,128]{4,3,2,1,0:T(8,128)S(1)} collective-permute-done((f32[4,2,5,16,128]{4,3,2,1,0:T(8,128)S(1)}, f32[4,2,5,16,128]{4,3,2,1,0:T(8,128)S(1)}, u32[]{:S(2)}, u32[]{:S(2)}) %collective-permute-start.10) | collective-permute-done | bytes 327712 | tf_op jit(solution)/shard_map/ppermute | solution.py:605
  86.0 3.0 %shard_map.52 = (f32[22,16,128]{2,1,0:T(8,128)S(1)}, f32[18,16,128]{2,1,0:T(8,128)S(1)}, f32[8,128]{1,0:T(8,128)S(1)}, f32[28,32,128]{2,1,0:T(8,128)S(1)}, f32[2...) custom-call(s32[2]{0:T(128)S(1)} %pad_add_fusion.meta, ...), custom_call_target="tpu_custom_call" | custom-call | tf_op jit(solution)/shard_map/pallas_call | solution.py:21
  89.0 1.3 %collective-permute-start.11 = (f32[18,16,128]{2,1,0:T(8,128)S(1)}, f32[18,16,128]{2,1,0:T(8,128)S(1)}, u32[]{:S(2)}, u32[]{:S(2)}) collective-permute-start(f32[18,16,128]{2,1,0:T(8,128)S(1)} %get-tuple-element.33), channel_id=1, source_target_pairs={{0,8},{1,9},{2,10},{3,11},{12,4},{13,5},{14,6},{15,7},{8,16},{9,17... | collective-permute-start | bytes 442376 | tf_op jit(solution)/shard_map/ppermute | solution.py:614
  90.3 7.2 %collective-permute-start.14 = (f32[8,128]{1,0:T(8,128)S(1)}, f32[8,128]{1,0:T(8,128)S(1)}, u32[]{:S(2)}, u32[]{:S(2)}) collective-permute-start(f32[8,128]{1,0:T(8,128)S(1)} %get-tuple-element.32), channel_id=1, source_target_pairs={{0,24},{8,0},{16,8},{24,16},{32,56},{40,32},{48,40},{56,48},{64,88... | collective-permute-start | bytes 12296 | tf_op jit(solution)/shard_map/ppermute | solution.py:622
  97.5 0.0 collective-permute-start.13
  97.5 0.7 collective-permute-start.12
  98.2 0.1 collective-permute-done.14
  98.3 3.3 %collective-permute-done.13 = f32[8,128]{1,0:T(8,128)S(1)} collective-permute-done((f32[8,128]{1,0:T(8,128)S(1)}, f32[8,128]{1,0:T(8,128)S(1)}, u32[]{:S(2)}, u32[]{:S(2)}) %collective-permute-start.13) | collective-permute-done | bytes 4128 | tf_op jit(solution)/shard_map/ppermute | solution.py:622
  101.5 0.0 collective-permute-done.12
  101.6 0.0 collective-permute-done.11.one
  101.6 2.9 %collective-permute-start.18 = (f32[18,16,128]{2,1,0:T(8,128)S(1)}, f32[18,16,128]{2,1,0:T(8,128)S(1)}, u32[]{:S(2)}, u32[]{:S(2)}) collective-permute-start(f32[18,16,128]{2,1,0:T(8,128)S(1)} %collective-permute-done.11.one), channel_id=1, source_target_pairs={{0,4},{4,0},{1,5},{5,1},{2,6},{6,2},{3,7},{7,3},{8,12},{12,8},{9,1... | collective-permute-start | bytes 442376 | tf_op jit(solution)/shard_map/ppermute | solution.py:605
  104.4 1.6 %collective-permute-start.17 = (f32[8,128]{1,0:T(8,128)S(1)}, f32[8,128]{1,0:T(8,128)S(1)}, u32[]{:S(2)}, u32[]{:S(2)}) collective-permute-start(f32[8,128]{1,0:T(8,128)S(1)} %add_add_fusion.sum_0), channel_id=1, source_target_pairs={{0,96},{8,104},{16,112},{24,120},{32,0},{40,8},{48,16},{56,24},{64... | collective-permute-start | bytes 12296 | tf_op jit(solution)/shard_map/ppermute | solution.py:622
  106.0 2.1 %collective-permute-start.16 = (f32[8,128]{1,0:T(8,128)S(1)}, f32[8,128]{1,0:T(8,128)S(1)}, u32[]{:S(2)}, u32[]{:S(2)}) collective-permute-start(f32[8,128]{1,0:T(8,128)S(1)} %add_add_fusion.sum_0), channel_id=1, source_target_pairs={{0,64},{8,72},{16,80},{24,88},{32,96},{40,104},{48,112},{56,120},{... | collective-permute-start | bytes 12296 | tf_op jit(solution)/shard_map/ppermute | solution.py:622
  108.1 0.8 collective-permute-start.15
  108.9 0.0 collective-permute-done.18.two
  108.9 2.9 %shard_map.53.es = f32[22,16,128]{2,1,0:T(8,128)S(1)} custom-call(s32[2]{0:T(128)S(1)} %pad_add_fusion.meta, f32[22,16,128]{2,1,0:T(8,128)S(1)} %get-tuple-element.37.rb, f32[18,16,128]{2,1,0:T(8,128)S(1)} %collective-permute-done.11.one, f32[18,16,128]{2,1,0:T(8,128)S(1)} %collective-permute-done.18.two), custom_call_target="tpu_custom_call" | custom-call | tf_op jit(solution)/shard_map/pallas_call | solution.py:21
  111.8 0.0 collective-permute-done.17.sum_3
  111.8 0.0 collective-permute-done.16.sum_2
  111.8 0.0 collective-permute-done.15.sum_1
  111.8 5.5 %shard_map.54 = f32[1,32,32,128]{3,2,1,0:T(8,128)} custom-call(s32[2]{0:T(128)S(1)} %pad_add_fusion.meta, s32[16,8]{1,0:T(8,128)S(1)} %copy.11.bricks, f32[8,128]{1,0:T(8,128)S(1)} %add_add_fusion.sum_0, f32[8,128]{1,0:T(8,128)S(1)} %collective-permute-done.15.sum_1, f32[8,128]{1,0:T(8,128)S(1)} %collective-permute-done.16.sum_2, ...), custom_call_target="tpu_custom_call" | custom-call | tf_op jit(solution)/shard_map/pallas_call | solution.py:21
  (3 shorter events, 0.0 us)
Async XLA Ops:
  0.8 1.0 copy-start
  1.9 1.0 copy-start.2
  2.9 1.0 copy-start.4
  27.1 7.3 %collective-permute-start = (f32[4,21,8,128]{3,2,1,0:T(8,128)S(1)}, f32[4,21,8,128]{3,2,1,0:T(8,128)S(1)}, u32[]{:S(2)}, u32[]{:S(2)}) collective-permute-start(f32[4,21,8,128]{3,2,1,0:T(8,128)S(1)} %shard_map.47), channel_id=1, source_target_pairs={{8,0},{9,1},{10,2},{11,3},{4,12},{5,13},{6,14},{7,15},{16,8},{17,9... | collective-permute-start | bytes 1032200 | tf_op jit(solution)/shard_map/ppermute | solution.py:614
  35.7 1.0 copy-start.6
  36.8 21.9 %copy-start.1 = (f32[1,32,32,128]{3,2,1,0:T(8,128)S(1)}, f32[1,32,32,128]{3,2,1,0:T(8,128)}, u32[]{:S(2)}) copy-start(f32[1,32,32,128]{3,2,1,0:T(8,128)} %u.3) | copy-start | bytes 1572868
  36.8 21.9 %copy-start.3 = (f32[1,32,32,128]{3,2,1,0:T(8,128)S(1)}, f32[1,32,32,128]{3,2,1,0:T(8,128)}, u32[]{:S(2)}) copy-start(f32[1,32,32,128]{3,2,1,0:T(8,128)} %f.3) | copy-start | bytes 1572868
  36.8 21.9 %copy-start.5 = (f32[1,32,32,128]{3,2,1,0:T(8,128)S(1)}, f32[1,32,32,128]{3,2,1,0:T(8,128)}, u32[]{:S(2)}) copy-start(f32[1,32,32,128]{3,2,1,0:T(8,128)} %a.3) | copy-start | bytes 1572868
  36.8 21.9 %all-to-all-start.1 = ((f32[8,35,8,128]{3,2,1,0:T(8,128)}), f32[8,35,8,128]{3,2,1,0:T(8,128)S(1)}, u32[]{:S(2)}, u32[]{:S(2)}) async-start(f32[8,35,8,128]{3,2,1,0:T(8,128)} %copy-done.6), calls=%async_computation.1 | async-start | bytes 2293760 | tf_op jit(solution)/shard_map/all_to_all | solution.py:626
  42.6 1.3 %collective-permute-start.1 = (f32[2,8,2,8,128]{4,3,2,1,0:T(8,128)S(1)}, f32[2,8,2,8,128]{4,3,2,1,0:T(8,128)S(1)}, u32[]{:S(2)}, u32[]{:S(2)}) collective-permute-start(f32[2,8,2,8,128]{4,3,2,1,0:T(8,128)S(1)} %get-tuple-element.28.here), channel_id=1, source_target_pairs={{0,4},{4,0},{1,5},{5,1},{2,6},{6,2},{3,7},{7,3},{8,12},{12,8},{9,1... | collective-permute-start | bytes 393224 | tf_op jit(solution)/shard_map/ppermute | solution.py:605
  63.3 4.8 %collective-permute-start.4 = (f32[2,8,16,128]{3,2,1,0:T(8,128)S(1)}, f32[2,8,16,128]{3,2,1,0:T(8,128)S(1)}, u32[]{:S(2)}, u32[]{:S(2)}) collective-permute-start(f32[2,8,16,128]{3,2,1,0:T(8,128)S(1)} %get-tuple-element.30.refs_0_), channel_id=1, source_target_pairs={{0,3},{1,0},{2,1},{3,2},{4,7},{5,4},{6,5},{7,6},{8,11},{9,8},{10,9... | collective-permute-start | bytes 393224 | tf_op jit(solution)/shard_map/ppermute | solution.py:654
  64.4 5.7 %collective-permute-start.3 = (f32[2,8,16,128]{3,2,1,0:T(8,128)S(1)}, f32[2,8,16,128]{3,2,1,0:T(8,128)S(1)}, u32[]{:S(2)}, u32[]{:S(2)}) collective-permute-start(f32[2,8,16,128]{3,2,1,0:T(8,128)S(1)} %get-tuple-element.30.refs_0_), channel_id=1, source_target_pairs={{0,2},{1,3},{2,0},{3,1},{4,6},{5,7},{6,4},{7,5},{8,10},{9,11},{10,... | collective-permute-start | bytes 393224 | tf_op jit(solution)/shard_map/ppermute | solution.py:654
  65.8 7.8 %collective-permute-start.2 = (f32[2,8,16,128]{3,2,1,0:T(8,128)S(1)}, f32[2,8,16,128]{3,2,1,0:T(8,128)S(1)}, u32[]{:S(2)}, u32[]{:S(2)}) collective-permute-start(f32[2,8,16,128]{3,2,1,0:T(8,128)S(1)} %get-tuple-element.30.refs_0_), channel_id=1, source_target_pairs={{0,1},{1,2},{2,3},{3,0},{4,5},{5,6},{6,7},{7,4},{8,9},{9,10},{10,1... | collective-permute-start | bytes 393224 | tf_op jit(solution)/shard_map/ppermute | solution.py:654
  65.8 8.9 %collective-permute-start.5 = (f32[2,8,16,128]{3,2,1,0:T(8,128)S(1)}, f32[2,8,16,128]{3,2,1,0:T(8,128)S(1)}, u32[]{:S(2)}, u32[]{:S(2)}) collective-permute-start(f32[2,8,16,128]{3,2,1,0:T(8,128)S(1)} %get-tuple-element.30.refs_0_), channel_id=1, source_target_pairs={{0,4},{4,0},{1,5},{5,1},{2,6},{6,2},{3,7},{7,3},{8,12},{12,8},{9,1... | collective-permute-start | bytes 393224 | tf_op jit(solution)/shard_map/ppermute | solution.py:605
  68.1 6.5 %collective-permute-start.8 = (f32[2,8,16,128]{3,2,1,0:T(8,128)S(1)}, f32[2,8,16,128]{3,2,1,0:T(8,128)S(1)}, u32[]{:S(2)}, u32[]{:S(2)}) collective-permute-start(f32[2,8,16,128]{3,2,1,0:T(8,128)S(1)} %collective-permute-done.4.refs_3_), channel_id=1, source_target_pairs={{0,4},{4,0},{1,5},{5,1},{2,6},{6,2},{3,7},{7,3},{8,12},{12,8},{9,1... | collective-permute-start | bytes 393224 | tf_op jit(solution)/shard_map/ppermute | solution.py:605
  70.1 4.5 %collective-permute-start.7 = (f32[2,8,16,128]{3,2,1,0:T(8,128)S(1)}, f32[2,8,16,128]{3,2,1,0:T(8,128)S(1)}, u32[]{:S(2)}, u32[]{:S(2)}) collective-permute-start(f32[2,8,16,128]{3,2,1,0:T(8,128)S(1)} %collective-permute-done.3.refs_2_), channel_id=1, source_target_pairs={{0,4},{4,0},{1,5},{5,1},{2,6},{6,2},{3,7},{7,3},{8,12},{12,8},{9,1... | collective-permute-start | bytes 393224 | tf_op jit(solution)/shard_map/ppermute | solution.py:605
  73.6 2.0 %collective-permute-start.6 = (f32[2,8,16,128]{3,2,1,0:T(8,128)S(1)}, f32[2,8,16,128]{3,2,1,0:T(8,128)S(1)}, u32[]{:S(2)}, u32[]{:S(2)}) collective-permute-start(f32[2,8,16,128]{3,2,1,0:T(8,128)S(1)} %collective-permute-done.2.refs_1_), channel_id=1, source_target_pairs={{0,4},{4,0},{1,5},{5,1},{2,6},{6,2},{3,7},{7,3},{8,12},{12,8},{9,1... | collective-permute-start | bytes 393224 | tf_op jit(solution)/shard_map/ppermute | solution.py:605
  76.4 7.8 %collective-permute-start.9 = (f32[4,2,5,16,128]{4,3,2,1,0:T(8,128)S(1)}, f32[4,2,5,16,128]{4,3,2,1,0:T(8,128)S(1)}, u32[]{:S(2)}, u32[]{:S(2)}) collective-permute-start(f32[4,2,5,16,128]{4,3,2,1,0:T(8,128)S(1)} %shard_map.51), channel_id=1, source_target_pairs={{0,8},{1,9},{2,10},{3,11},{12,4},{13,5},{14,6},{15,7},{8,16},{9,17... | collective-permute-start | bytes 983048 | tf_op jit(solution)/shard_map/ppermute | solution.py:614
  84.2 1.8 %collective-permute-start.10 = (f32[4,2,5,16,128]{4,3,2,1,0:T(8,128)S(1)}, f32[4,2,5,16,128]{4,3,2,1,0:T(8,128)S(1)}, u32[]{:S(2)}, u32[]{:S(2)}) collective-permute-start(f32[4,2,5,16,128]{4,3,2,1,0:T(8,128)S(1)} %collective-permute-done.9.refs_8_), channel_id=1, source_target_pairs={{0,4},{4,0},{1,5},{5,1},{2,6},{6,2},{3,7},{7,3},{8,12},{12,8},{9,1... | collective-permute-start | bytes 983048 | tf_op jit(solution)/shard_map/ppermute | solution.py:605
  89.0 12.6 %collective-permute-start.11 = (f32[18,16,128]{2,1,0:T(8,128)S(1)}, f32[18,16,128]{2,1,0:T(8,128)S(1)}, u32[]{:S(2)}, u32[]{:S(2)}) collective-permute-start(f32[18,16,128]{2,1,0:T(8,128)S(1)} %get-tuple-element.33), channel_id=1, source_target_pairs={{0,8},{1,9},{2,10},{3,11},{12,4},{13,5},{14,6},{15,7},{8,16},{9,17... | collective-permute-start | bytes 442376 | tf_op jit(solution)/shard_map/ppermute | solution.py:614
  90.3 8.0 %collective-permute-start.14 = (f32[8,128]{1,0:T(8,128)S(1)}, f32[8,128]{1,0:T(8,128)S(1)}, u32[]{:S(2)}, u32[]{:S(2)}) collective-permute-start(f32[8,128]{1,0:T(8,128)S(1)} %get-tuple-element.32), channel_id=1, source_target_pairs={{0,24},{8,0},{16,8},{24,16},{32,56},{40,32},{48,40},{56,48},{64,88... | collective-permute-start | bytes 12296 | tf_op jit(solution)/shard_map/ppermute | solution.py:622
  97.5 4.0 %collective-permute-start.13 = (f32[8,128]{1,0:T(8,128)S(1)}, f32[8,128]{1,0:T(8,128)S(1)}, u32[]{:S(2)}, u32[]{:S(2)}) collective-permute-start(f32[8,128]{1,0:T(8,128)S(1)} %get-tuple-element.32), channel_id=1, source_target_pairs={{0,16},{8,24},{16,0},{24,8},{32,48},{40,56},{48,32},{56,40},{64,80... | collective-permute-start | bytes 12296 | tf_op jit(solution)/shard_map/ppermute | solution.py:622
  97.5 4.0 %collective-permute-start.12 = (f32[8,128]{1,0:T(8,128)S(1)}, f32[8,128]{1,0:T(8,128)S(1)}, u32[]{:S(2)}, u32[]{:S(2)}) collective-permute-start(f32[8,128]{1,0:T(8,128)S(1)} %get-tuple-element.32), channel_id=1, source_target_pairs={{0,8},{8,16},{16,24},{24,0},{32,40},{40,48},{48,56},{56,32},{64,72... | collective-permute-start | bytes 12296 | tf_op jit(solution)/shard_map/ppermute | solution.py:622
  101.6 7.3 %collective-permute-start.18 = (f32[18,16,128]{2,1,0:T(8,128)S(1)}, f32[18,16,128]{2,1,0:T(8,128)S(1)}, u32[]{:S(2)}, u32[]{:S(2)}) collective-permute-start(f32[18,16,128]{2,1,0:T(8,128)S(1)} %collective-permute-done.11.one), channel_id=1, source_target_pairs={{0,4},{4,0},{1,5},{5,1},{2,6},{6,2},{3,7},{7,3},{8,12},{12,8},{9,1... | collective-permute-start | bytes 442376 | tf_op jit(solution)/shard_map/ppermute | solution.py:605
  104.4 7.4 %collective-permute-start.17 = (f32[8,128]{1,0:T(8,128)S(1)}, f32[8,128]{1,0:T(8,128)S(1)}, u32[]{:S(2)}, u32[]{:S(2)}) collective-permute-start(f32[8,128]{1,0:T(8,128)S(1)} %add_add_fusion.sum_0), channel_id=1, source_target_pairs={{0,96},{8,104},{16,112},{24,120},{32,0},{40,8},{48,16},{56,24},{64... | collective-permute-start | bytes 12296 | tf_op jit(solution)/shard_map/ppermute | solution.py:622
  106.0 5.8 %collective-permute-start.16 = (f32[8,128]{1,0:T(8,128)S(1)}, f32[8,128]{1,0:T(8,128)S(1)}, u32[]{:S(2)}, u32[]{:S(2)}) collective-permute-start(f32[8,128]{1,0:T(8,128)S(1)} %add_add_fusion.sum_0), channel_id=1, source_target_pairs={{0,64},{8,72},{16,80},{24,88},{32,96},{40,104},{48,112},{56,120},{... | collective-permute-start | bytes 12296 | tf_op jit(solution)/shard_map/ppermute | solution.py:622
  108.1 3.7 %collective-permute-start.15 = (f32[8,128]{1,0:T(8,128)S(1)}, f32[8,128]{1,0:T(8,128)S(1)}, u32[]{:S(2)}, u32[]{:S(2)}) collective-permute-start(f32[8,128]{1,0:T(8,128)S(1)} %add_add_fusion.sum_0), channel_id=1, source_target_pairs={{0,32},{8,40},{16,48},{24,56},{32,64},{40,72},{48,80},{56,88},{64,... | collective-permute-start | bytes 12296 | tf_op jit(solution)/shard_map/ppermute | solution.py:622

commit v5 on v4

--- a/solution.py
+++ b/solution.py
@@ -215,7 +215,19 @@
             out[k, SENT_COEF + h] = tile
 
 
-def first_kernel(meta, bricks, u, f, a, out, small):
+def pack_coarse(planes, small, out):
+    twice = pick(128, 128, lambda r, c: (r >> 1) == (c & 63)) * 0.125
+    row, lane = iota((16, 128), 0), iota((16, 128), 1)
+    even = ((row + lane + (lane >> 6)) & 1) == 0
+    for t in range(16):
+        small[16 * t : 16 * t + 16] = planes[t, pl.ds(0, 16, stride=2), :] + planes[t, pl.ds(1, 16, stride=2), :]
+    summed = jnp.dot(small[...], twice, precision=EXACT, preferred_element_type=F32)
+    summed = summed.reshape(16, 16, 128)
+    for j in range(8):
+        out[j] = jnp.where(even, summed[2 * j], summed[2 * j + 1])
+
+
+def first_kernel(meta, bricks, u, f, a, out, ac, small, planes, rows):
     _, _, bit_x, bit_y, _ = place_of(meta, bricks)
     mask = odd(32, 128)
     sources = ((u, False), (f, True), (f, False), (a, True), (a, False))
@@ -225,6 +237,9 @@
 
     pack_shell(get, out, bit_x, bit_y)
     pack_bottom_coef(a, out, small)
+    for t in range(16):
+        planes[t] = a[0, 2 * t] + a[0, 2 * t + 1]
+    pack_coarse(planes, rows, ac)
 
 
 def around(src, k, red, mask, edges, cut=None):
@@ -304,20 +319,8 @@
     for t in range(16):
         total = around(u_b, OWN + t, True, mask, 0)[0:32, 0:128]
         diag = pair_of(a, t, True, own) + 6.0
-        resid[0, t] = pair_of(f, t, True, own) + total - diag * u_r[OWN + t, 0:32, 0:128]
-        resid[1, t] = a[0, 2 * t] + a[0, 2 * t + 1]
-    twice = pick(128, 128, lambda r, c: (r >> 1) == (c & 63)) * 0.125
-    row, lane = iota((16, 128), 0), iota((16, 128), 1)
-    even = ((row + lane + (lane >> 6)) & 1) == 0
-    for i in range(2):
-        for t in range(16):
-            small[16 * t : 16 * t + 16] = (
-                resid[i, t, pl.ds(0, 16, stride=2), :] + resid[i, t, pl.ds(1, 16, stride=2), :]
-            )
-        summed = jnp.dot(small[...], twice, precision=EXACT, preferred_element_type=F32)
-        summed = summed.reshape(16, 16, 128)
-        for j in range(8):
-            rc[i, j] = jnp.where(even, summed[2 * j], summed[2 * j + 1])
+        resid[t] = pair_of(f, t, True, own) + total - diag * u_r[OWN + t, 0:32, 0:128]
+    pack_coarse(resid, small, rc)
 
 
 def slot_of(member, me):
@@ -332,17 +335,10 @@
     start = jnp.where(me < 4, 3, 0)
     for i in range(4):
         member = jnp.where(me < 4, bricks[slab, 4 + i], bricks[slab, i])
-        out[i] = held[slot_of(member, me), :, pl.ds(start, 5)]
-
-
-def coarse_down_kernel(meta, bricks, *refs):
-    boxes, (one, two, weights) = refs[:8], refs[8:11]
-    rb, rb_send, part, e_b, r_r, r_b, i_r, i_b = refs[11:19]
-    held, low, high, e_r, a_r, a_b, resid, small = refs[19:]
-    slab, me = meta[0], meta[1]
-    for i, box in enumerate(boxes):
-        held[i] = box[...]
-
+        out[i] = held[slot_of(member, me), pl.ds(start, 5)]
+
+
+def sort_sides(me, one, two, low, high):
     @pl.when(me < 4)
     def _():
         low[...] = one[...]
@@ -353,59 +349,76 @@
         low[...] = two[...]
         high[...] = one[...]
 
+
+def assemble(meta, bricks, boxes, one, two, red, black, held, low, high):
+    slab, me = meta[0], meta[1]
+    for i, box in enumerate(boxes):
+        held[i] = box[...]
+    sort_sides(me, one, two, low, high)
     left = iota((16, 128), 1) < 64
-    for q, (red, black) in enumerate(((r_r, r_b), (a_r, a_b))):
-
-        def put(k, by, west, east):
-            rows = slice(16 * by, 16 * by + 16)
-            red[k, rows] = jnp.where(left, west, pltpu.roll(east, 64, 1))
-            black[k, rows] = jnp.where(left, pltpu.roll(west, 64, 1), east)
-
-        for by in range(2):
-            for bz in range(2):
-                west = slot_of(bricks[slab, 2 * by + 4 * bz], me)
-                east = slot_of(bricks[slab, 2 * by + 4 * bz + 1], me)
-                for j in range(8):
-                    put(6 + 8 * bz + j, by, held[west, q, j], held[east, q, j])
-            for j in range(5):
-                put(1 + j, by, low[2 * by, q, j], low[2 * by + 1, q, j])
-                put(22 + j, by, high[2 * by, q, j], high[2 * by + 1, q, j])
+
+    def put(k, by, west, east):
+        rows = slice(16 * by, 16 * by + 16)
+        red[k, rows] = jnp.where(left, west, pltpu.roll(east, 64, 1))
+        black[k, rows] = jnp.where(left, pltpu.roll(west, 64, 1), east)
+
+    for by in range(2):
+        for bz in range(2):
+            west = slot_of(bricks[slab, 2 * by + 4 * bz], me)
+            east = slot_of(bricks[slab, 2 * by + 4 * bz + 1], me)
+            for j in range(8):
+                put(6 + 8 * bz + j, by, held[west, j], held[east, j])
+        for j in range(5):
+            put(1 + j, by, low[2 * by, j], low[2 * by + 1, j])
+            put(22 + j, by, high[2 * by, j], high[2 * by + 1, j])
+
+
+def to_bottom(planes, small, half):
+    for n in range(22):
+        small[16 * n : 16 * n + 16] = planes[n, pl.ds(0, 16, stride=2), :] + planes[n, pl.ds(1, 16, stride=2), :]
+    fold = pick(128, 128, lambda r, c: (r >> 1) == c - 64 * half) * 0.125
+    return jnp.dot(small[...], fold, precision=EXACT, preferred_element_type=F32).reshape(22, 16, 128)
+
+
+def coarse_coef_kernel(meta, bricks, *refs):
+    boxes, (one, two) = refs[:8], refs[8:10]
+    a_r, i_r, i_b, ab = refs[10:14]
+    held, low, high, a_b, planes, small = refs[14:]
+    slab = meta[0]
+    assemble(meta, bricks, boxes, one, two, a_r, a_b, held, low, high)
+    for k in range(1, 27):
+        keep = jnp.full((32, 128), 0, jnp.int32) == 0
+        if k < 6:
+            keep = jnp.logical_not(is_zero(slab, (32, 128)))
+        if k >= 22:
+            keep = jnp.logical_not(is_zero(slab - (SLABS - 1), (32, 128)))
+        i_r[k] = jnp.where(keep, 1.0 / (a_r[k] + 1.5), 0.0)
+        i_b[k] = jnp.where(keep, 1.0 / (a_b[k] + 1.5), 0.0)
+    for n in range(22):
+        planes[n] = a_r[3 + n] + a_b[3 + n]
+    ab[...] = to_bottom(planes, small, 1)
+
+
+def coarse_down_kernel(meta, bricks, *refs):
+    boxes, (one, two, weights, a_r, i_r, i_b, ab) = refs[:8], refs[8:15]
+    rb, rb_send, part, e_b, r_r, r_b = refs[15:21]
+    held, low, high, e_r, resid, small = refs[21:]
+    me = meta[1]
+    assemble(meta, bricks, boxes, one, two, r_r, r_b, held, low, high)
     for k in (0, 27):
         e_r[k] = jnp.zeros((32, 128), F32)
         e_b[k] = jnp.zeros((32, 128), F32)
-
-    def start(k, carry):
-        gone = jnp.where(((slab == 0) & (k < 6)) | ((slab == SLABS - 1) & (k >= 22)), 1, 0)
-        keep = is_zero(gone, (32, 128))
-        inverse = jnp.where(keep, 1.0 / (a_r[k] + 1.5), 0.0)
-        i_r[k] = inverse
-        i_b[k] = jnp.where(keep, 1.0 / (a_b[k] + 1.5), 0.0)
-        e_r[k] = r_r[k] * inverse
-        return carry
-
-    lax.fori_loop(1, 27, start, 0, unroll=13)
+    for k in range(1, 27):
+        e_r[k] = r_r[k] * i_r[k]
     mask = odd(32, 128)
     half_sweep(e_b, e_r, r_b, i_b, 1, 27, False, mask, 0.25, 2)
     half_sweep(e_r, e_b, r_r, i_r, 1, 27, True, mask, 0.25, 2)
     half_sweep(e_b, e_r, r_b, i_b, 1, 27, False, mask, 0.25, 2)
-
-    def residual(n, carry):
+    for n in range(22):
         k = n + 3
         total = 0.25 * around(e_b, k, True, mask, 2)
-        resid[0, n] = r_r[k] + total - (a_r[k] + 1.5) * e_r[k]
-        resid[1, n] = a_r[k] + a_b[k]
-        return carry
-
-    lax.fori_loop(0, 22, residual, 0, unroll=True)
-    total = jnp.zeros((352, 128), F32)
-    for i in range(2):
-        for n in range(22):
-            small[16 * n : 16 * n + 16] = (
-                resid[i, n, pl.ds(0, 16, stride=2), :] + resid[i, n, pl.ds(1, 16, stride=2), :]
-            )
-        half = pick(128, 128, lambda r, c: (r >> 1) == c - 64 * i) * 0.125
-        total = total + jnp.dot(small[...], half, precision=EXACT, preferred_element_type=F32)
-    rb[...] = total.reshape(22, 16, 128)
+        resid[n] = r_r[k] + total - (a_r[k] + 1.5) * e_r[k]
+    rb[...] = to_bottom(resid, small, 0) + ab[...]
     rb_send[...] = rb[pl.ds(jnp.where(me < 4, 1, 3), 18)]
     total = jnp.zeros((16, 128), F32)
     for i in range(16):
@@ -415,17 +428,7 @@
 
 def bottom_kernel(meta, rb, one, two, es, e_r, e_b, g_r, g_b, i_r, i_b, low, high):
     slab, me = meta[0], meta[1]
-
-    @pl.when(me < 4)
-    def _():
-        low[...] = one[...]
-        high[...] = two[...]
-
-    @pl.when(me >= 4)
-    def _():
-        low[...] = two[...]
-        high[...] = one[...]
-
+    sort_sides(me, one, two, low, high)
     mask = odd(16, 128)
     left = iota((16, 128), 1) < 64
     zero = jnp.zeros((16, 128), F32)
@@ -614,12 +617,22 @@
     return lax.ppermute(x, ALL, pairs)
 
 
-def around_ring(x, stride, step):
-    pairs = []
-    for s in range(SLABS):
+def around_chips(x):
+    return [x] + [lax.ppermute(x, "bottom", [(i, (i + d) % 4) for i in range(4)]) for d in range(1, 4)]
+
+
+def both_cores(boxes):
+    return boxes + [swap_cores(box) for box in boxes]
+
+
+def ring_sums(x, stride):
+    def moved(s, step):
         at = s // stride % 4
-        pairs.append((s, s + ((at + step) % 4 - at) * stride))
-    return lax.ppermute(x, "slab", pairs)
+        return s + ((at + step) % 4 - at) * stride
+
+    beside = [(8 * s + m, 8 * moved(s, 1 if m < 4 else 3) + m) for s in range(SLABS) for m in range(8)]
+    across = [(s, moved(s, 2)) for s in range(SLABS)]
+    return lax.ppermute(x, ALL, beside), lax.ppermute(x, "slab", across)
 
 
 def among(x):
@@ -630,46 +643,56 @@
     meta = jnp.stack([lax.axis_index("slab"), lax.axis_index(LB)]).astype(jnp.int32)
     smem = [meta, brick_map]
     fine = (26, 40, 256)
-    packed = run(
-        first_kernel, [(8, SENT, 8, 128)], smem, [u_init, source, coeffs], [(8, 32, 128)],
+    packed, ac = run(
+        first_kernel, [(8, SENT, 8, 128), (8, 16, 128)], smem, [u_init, source, coeffs],
+        [(8, 32, 128), (16, 32, 128), (256, 128)],
     )
     got = among(packed)
     leaving = run(cross_kernel, [(4, FACE + 4, 8, 128)], smem, [got])
+    leaving, ac = lax.optimization_barrier((leaving, ac))
     cross = to_slabs(leaving, False)
+    cross, *ac_boxes = lax.optimization_barrier((cross, *around_chips(ac)))
     sent, coef = run(
         mid_kernel, [(8, GOT, 8, 128), (2, 8, 2, 8, 128)], smem, [got, cross], [(12, FACE, 8, 128)],
     )
     coef_other = swap_cores(coef)
     halo = among(sent)
+    faces = (4, 5, 16, 128)
+    coarse = (28, 32, 128)
+    held = [(8, 8, 16, 128), faces, faces]
+    ac_boxes = both_cores(ac_boxes)
+    ac_cross = to_slabs(run(faces_kernel, [faces], smem, ac_boxes, held[:1]), True)
+    ac_other = swap_cores(ac_cross)
+    halo, ac_cross, ac_other, coef_other = lax.optimization_barrier((halo, ac_cross, ac_other, coef_other))
+    rc, u_b, f_r, f_b, i_r, i_b = run(
+        fine_down_kernel, [(8, 16, 128)] + [fine] * 5, smem, [u_init, source, coeffs, halo],
+        [fine, (16, 32, 128), (256, 128)],
+    )
+    boxes = both_cores(around_chips(rc))
+    leaving = run(faces_kernel, [faces], smem, boxes, held[:1])
+    leaving, ac_cross, ac_other, coef = lax.optimization_barrier((leaving, ac_cross, ac_other, coef))
+    cross = to_slabs(leaving, True)
     weights = run(
         weights_kernel, [(16, 16, 128)], [meta], [coef, coef_other],
         [(26, 16, 128)] * 6 + [(8, 2, 8, 128)] * 2,
     )
-    halo, weights = lax.optimization_barrier((halo, weights))
-    rc, u_b, f_r, f_b, i_r, i_b = run(
-        fine_down_kernel, [(2, 8, 16, 128)] + [fine] * 5, smem, [u_init, source, coeffs, halo],
-        [fine, (2, 16, 32, 128), (256, 128)],
-    )
-    boxes = [rc] + [
-        lax.ppermute(rc, "bottom", [(i, (i + d) % 4) for i in range(4)]) for d in range(1, 4)
-    ]
-    boxes = boxes + [swap_cores(box) for box in boxes]
-    leaving = run(faces_kernel, [(4, 2, 5, 16, 128)], smem, boxes, [(8, 2, 8, 16, 128)])
-    cross = to_slabs(leaving, True)
+    ca_r, ci_r, ci_b, ab = run(
+        coarse_coef_kernel, [coarse] * 3 + [(22, 16, 128)], smem, ac_boxes + [ac_cross, ac_other],
+        held + [coarse, (22, 32, 128), (352, 128)],
+    )
+    cross, weights, ca_r, ci_r, ci_b, ab = lax.optimization_barrier((cross, weights, ca_r, ci_r, ci_b, ab))
+    rb, rb_send, part, ec_b, r_r, r_b = run(
+        coarse_down_kernel, [(22, 16, 128), (18, 16, 128), (8, 128)] + [coarse] * 3, smem,
+        boxes + [cross, swap_cores(cross), weights, ca_r, ci_r, ci_b, ab],
+        held + [coarse, (22, 32, 128), (352, 128)],
+    )
+    cross = to_slabs(rb_send, True)
+    near, far = ring_sums(part, 1)
+    cross, near, far = lax.optimization_barrier((cross, near, far))
     other = swap_cores(cross)
-    coarse = (28, 32, 128)
-    faces = (4, 2, 5, 16, 128)
-    rb, rb_send, part, ec_b, r_r, r_b, ci_r, ci_b = run(
-        coarse_down_kernel, [(22, 16, 128), (18, 16, 128), (8, 128)] + [coarse] * 5, smem,
-        boxes + [cross, other, weights],
-        [(8, 2, 8, 16, 128), faces, faces, coarse, coarse, coarse, (2, 22, 32, 128), (352, 128)],
-    )
-    cross = to_slabs(rb_send, True)
-    rows = [around_ring(part, 1, d) for d in range(1, 4)]
-    cross, *rows = lax.optimization_barrier((cross, *rows))
-    other = swap_cores(cross)
-    part = (part + rows[0]) + (rows[1] + rows[2])
-    sums = [part] + [around_ring(part, 4, d) for d in range(1, 4)]
+    part = (part + swap_cores(near)) + (near + far)
+    near, far = ring_sums(part, 4)
+    sums = [part, near, far, swap_cores(near)]
     bottom = (28, 16, 128)
     es = run(
         bottom_kernel, [(22, 16, 128)], [meta], [rb, cross, other],

time: 118 us -> 116 us (0.983)
  waiting for transfers between devices: 31.1 us -> 22.5 us
  starting transfers between devices: 36.8 us -> 41.1 us
  Pallas kernels: 23.5 us -> 24.9 us
  local copies, waits for them, and re-layouts: 4.91 us -> 6.23 us
    all_to_all x1, waiting for transfers between devices: 11.7 us -> 3.66 us  [among(): return lax.all_to_all(x, LB, split_axis=0, concat_axis=0, tiled=True)]
    ppermute x7 -> x14, starting transfers between devices: 10.5 us -> 16.6 us  [swap_cores(): return lax.ppermute(x, 'level', [(0, 1), (1, 0)])]
    ppermute x3 -> x4, waiting for transfers between devices: 10.7 us -> 6.03 us  [to_slabs(): return lax.ppermute(x, ALL, pairs)]
    ppermute x9 -> x10, waiting for transfers between devices: 5.31 us -> 7.82 us  [the longest x6 5.78 us: around_chips(): lax.ppermute(x, 'bottom', [(i, (i + d) % 4) for i in range(4)])]
    all_to_all x1, starting transfers between devices: 5.82 us -> 4.01 us  [among(): return lax.all_to_all(x, LB, split_axis=0, concat_axis=0, tiled=True)]
    ppermute x7 -> x14, waiting for transfers between devices: 3.42 us -> 4.95 us  [swap_cores(): return lax.ppermute(x, 'level', [(0, 1), (1, 0)])]
    pallas_call x9 -> x11, Pallas kernels: 23.5 us -> 24.9 us  [run(): pl.pallas_call(kernel, out_shape=shapes[0] if single else shapes, in_spec...]
    ppermute x9 -> x10, starting transfers between devices: 14.8 us -> 13.5 us  [the longest x4 8.61 us: ring_sums(): return (lax.ppermute(x, ALL, beside), lax.ppermute(x, 'slab', across))]
  transfers between devices with their start and end apart: 20 -> 29, of which waited for: 10 -> 18; matrix products, arithmetic and copies ran while one was open for 0% -> 0% of each run, Pallas kernels for 5% -> 7%
where the time goes in v5:
time: 116 us
  starting transfers between devices  41.1 us (35%)
  Pallas kernels  24.9 us (21%)
  waiting for transfers between devices  22.5 us (19%)
  blocking collectives  20.8 us (18%)
  local copies, waits for them, and re-layouts  6.23 us (5%)
    pallas_call x11, Pallas kernels, run(): pl.pallas_call(kernel, out_shape=shapes[0] if single else shapes, in_spec...  24.9 us
    all_to_all x1, blocking collectives, among(): return lax.all_to_all(x, LB, split_axis=0, concat_axis=0, tiled=True)  20.8 us
    ppermute x14, starting transfers between devices, swap_cores(): return lax.ppermute(x, 'level', [(0, 1), (1, 0)])  16.6 us
    ppermute x4, starting transfers between devices, ring_sums(): return (lax.ppermute(x, ALL, beside), lax.ppermute(x, 'slab', across))  8.61 us
    ppermute x4, starting transfers between devices, to_slabs(): return lax.ppermute(x, ALL, pairs)  7.01 us
    unnamed x23, local copies, waits for them, and re-layouts  6.23 us
    ppermute x4, waiting for transfers between devices, to_slabs(): return lax.ppermute(x, ALL, pairs)  6.03 us
    ppermute x6, waiting for transfers between devices, around_chips(): lax.ppermute(x, 'bottom', [(i, (i + d) % 4) for i in range(4)])  5.78 us
  transfers between devices with their start and end apart: 29, of which 18 were waited for; matrix products, arithmetic and copies ran while one was open for 0% of the time, Pallas kernels for 7%

profile of v5, /device:TPU:1, one launch (start us, length us, event | category | flops | bytes accessed | tf_op | source)
XLA Modules:
  0.0 115.7 jit_solution(11175740053621121309)
XLA Ops:
  0.0 0.8 copy.13.bricks
  0.8 0.1 pad_add_fusion.meta
  0.8 1.0 copy-done
  1.9 1.0 copy-done.2
  2.9 1.0 copy-done.4
  4.0 1.7 %shard_map.46 = (f32[8,32,8,128]{3,2,1,0:T(8,128)S(1)}, f32[8,16,128]{2,1,0:T(8,128)S(1)}) custom-call(s32[2]{0:T(128)S(1)} %pad_add_fusion.meta, s32[16,8]{1,0:T(8,128)S(1)} %copy.13.bricks, f32[1,32,32,128]{3,2,1,0:T(8,128)S(1)} %copy-done, f32[1,32,32,128]{3,2,1,0:T(8,128)S(1)} %copy-done.2, f32[1,32,32,128]{3,2,1,0:T(8,128)S(1)} %copy-done.4), custom_call_target="tpu_custom_call" | custom-call | tf_op jit(solution)/shard_map/pallas_call | solution.py:21
  5.7 20.8 %all_to_all.10.recv = f32[8,32,8,128]{3,2,1,0:T(8,128)S(1)} all-to-all(f32[8,32,8,128]{3,2,1,0:T(8,128)S(1)} %get-tuple-element.49), channel_id=1, replica_groups=mesh['slab'=16,'level'=2,'bottom'=4] {'level','bottom'}, dimensions={0} | all-to-all | bytes 2097152 | tf_op jit(solution)/shard_map/all_to_all | solution.py:639
  26.4 0.7 shard_map.47
  27.1 3.1 %collective-permute-start = (f32[4,21,8,128]{3,2,1,0:T(8,128)S(1)}, f32[4,21,8,128]{3,2,1,0:T(8,128)S(1)}, u32[]{:S(2)}, u32[]{:S(2)}) collective-permute-start(f32[4,21,8,128]{3,2,1,0:T(8,128)S(1)} %shard_map.47), channel_id=1, source_target_pairs={{8,0},{9,1},{10,2},{11,3},{4,12},{5,13},{6,14},{7,15},{16,8},{17,9... | collective-permute-start | bytes 1032200 | tf_op jit(solution)/shard_map/ppermute | solution.py:617
  30.3 0.9 collective-permute-start.3
  31.2 1.5 %collective-permute-start.2 = (f32[8,16,128]{2,1,0:T(8,128)S(1)}, f32[8,16,128]{2,1,0:T(8,128)S(1)}, u32[]{:S(2)}, u32[]{:S(2)}) collective-permute-start(f32[8,16,128]{2,1,0:T(8,128)S(1)} %get-tuple-element.55.refs_0_), channel_id=1, source_target_pairs={{0,2},{1,3},{2,0},{3,1},{4,6},{5,7},{6,4},{7,5},{8,10},{9,11},{10,... | collective-permute-start | bytes 196616 | tf_op jit(solution)/shard_map/ppermute | solution.py:621
  32.7 1.4 %collective-permute-done.3.refs_3_ = f32[8,16,128]{2,1,0:T(8,128)S(1)} collective-permute-done((f32[8,16,128]{2,1,0:T(8,128)S(1)}, f32[8,16,128]{2,1,0:T(8,128)S(1)}, u32[]{:S(2)}, u32[]{:S(2)}) %collective-permute-start.3) | collective-permute-done | bytes 65568 | tf_op jit(solution)/shard_map/ppermute | solution.py:621
  34.2 2.5 %collective-permute-done.2.refs_2_ = f32[8,16,128]{2,1,0:T(8,128)S(1)} collective-permute-done((f32[8,16,128]{2,1,0:T(8,128)S(1)}, f32[8,16,128]{2,1,0:T(8,128)S(1)}, u32[]{:S(2)}, u32[]{:S(2)}) %collective-permute-start.2) | collective-permute-done | bytes 65568 | tf_op jit(solution)/shard_map/ppermute | solution.py:621
  36.7 1.4 %collective-permute-done.1.refs_1_ = f32[8,16,128]{2,1,0:T(8,128)S(1)} collective-permute-done((f32[8,16,128]{2,1,0:T(8,128)S(1)}, f32[8,16,128]{2,1,0:T(8,128)S(1)}, u32[]{:S(2)}, u32[]{:S(2)}) %collective-permute-start.1) | collective-permute-done | bytes 65568 | tf_op jit(solution)/shard_map/ppermute | solution.py:621
  38.1 1.3 %shard_map.48 = (f32[8,35,8,128]{3,2,1,0:T(8,128)S(1)}, f32[2,8,2,8,128]{4,3,2,1,0:T(8,128)S(1)}) custom-call(s32[2]{0:T(128)S(1)} %pad_add_fusion.meta, s32[16,8]{1,0:T(8,128)S(1)} %copy.13.bricks, f32[8,32,8,128]{3,2,1,0:T(8,128)S(1)} %all_to_all.10.recv, f32[4,21,8,128]{3,2,1,0:T(8,128)S(1)} %collective-permute-done.cross), custom_call_target="tpu_custom_call" | custom-call | tf_op jit(solution)/shard_map/pallas_call | solution.py:21
  39.4 1.0 copy-done.6
  40.5 4.0 %all-to-all-start.1 = ((f32[8,35,8,128]{3,2,1,0:T(8,128)}), f32[8,35,8,128]{3,2,1,0:T(8,128)S(1)}, u32[]{:S(2)}, u32[]{:S(2)}) async-start(f32[8,35,8,128]{3,2,1,0:T(8,128)} %copy-done.6), calls=%async_computation.1 | async-start | bytes 2293760 | tf_op jit(solution)/shard_map/all_to_all | solution.py:639
  44.5 0.2 collective-permute-start.4
  44.6 0.3 collective-permute-start.5
  45.0 0.2 collective-permute-start.6
  45.1 0.3 collective-permute-start.7
  45.5 0.2 collective-permute-done.4.refs_4_
  45.7 0.2 collective-permute-done.5.refs_5_
  45.9 0.3 collective-permute-done.6.refs_6_
  46.2 0.2 collective-permute-done.7.refs_7_
  46.4 0.7 shard_map.49
  47.1 1.3 %collective-permute-start.8 = (f32[4,5,16,128]{3,2,1,0:T(8,128)S(1)}, f32[4,5,16,128]{3,2,1,0:T(8,128)S(1)}, u32[]{:S(2)}, u32[]{:S(2)}) collective-permute-start(f32[4,5,16,128]{3,2,1,0:T(8,128)S(1)} %shard_map.49), channel_id=1, source_target_pairs={{0,8},{1,9},{2,10},{3,11},{12,4},{13,5},{14,6},{15,7},{8,16},{9,17... | collective-permute-start | bytes 491528 | tf_op jit(solution)/shard_map/ppermute | solution.py:617
  48.4 5.3 %collective-permute-done.8.refs_8_ = f32[4,5,16,128]{3,2,1,0:T(8,128)S(1)} collective-permute-done((f32[4,5,16,128]{3,2,1,0:T(8,128)S(1)}, f32[4,5,16,128]{3,2,1,0:T(8,128)S(1)}, u32[]{:S(2)}, u32[]{:S(2)}) %collective-permute-start.8) | collective-permute-done | bytes 163872 | tf_op jit(solution)/shard_map/ppermute | solution.py:617
  53.7 0.5 collective-permute-start.9
  54.2 0.1 collective-permute-start.10
  54.2 1.3 %collective-permute-done.10.there = f32[2,8,2,8,128]{4,3,2,1,0:T(8,128)S(1)} collective-permute-done((f32[2,8,2,8,128]{4,3,2,1,0:T(8,128)S(1)}, f32[2,8,2,8,128]{4,3,2,1,0:T(8,128)S(1)}, u32[]{:S(2)}, u32[]{:S(2)}) %collective-permute-start.10) | collective-permute-done | bytes 131104 | tf_op jit(solution)/shard_map/ppermute | solution.py:608
  55.5 0.6 copy-done.9
  56.2 0.7 copy-done.7
  56.9 3.7 %all-to-all-done.1.recv = f32[8,35,8,128]{3,2,1,0:T(8,128)S(1)} async-done(((f32[8,35,8,128]{3,2,1,0:T(8,128)}), f32[8,35,8,128]{3,2,1,0:T(8,128)S(1)}, u32[]{:S(2)}, u32[]{:S(2)}) %all-to-all-start.1) | async-done | bytes 1146912 | tf_op jit(solution)/shard_map/all_to_all | solution.py:639
  60.5 4.5 %shard_map.50 = (f32[8,16,128]{2,1,0:T(8,128)S(1)}, f32[26,40,256]{2,1,0:T(8,128)S(1)}, f32[26,40,256]{2,1,0:T(8,128)S(1)}, f32[26,40,256]{2,1,0:T(8,128)S(1)}, ...) custom-call(s32[2]{0:T(128)S(1)} %pad_add_fusion.meta, s32[16,8]{1,0:T(8,128)S(1)} %copy.13.bricks, ...), custom_call_target="tpu_custom_call" | custom-call | tf_op jit(solution)/shard_map/pallas_call | solution.py:21
  65.1 1.1 collective-permute-start.13
  66.2 1.4 %collective-permute-start.12 = (f32[8,16,128]{2,1,0:T(8,128)S(1)}, f32[8,16,128]{2,1,0:T(8,128)S(1)}, u32[]{:S(2)}, u32[]{:S(2)}) collective-permute-start(f32[8,16,128]{2,1,0:T(8,128)S(1)} %get-tuple-element.61.refs_0_), channel_id=1, source_target_pairs={{0,2},{1,3},{2,0},{3,1},{4,6},{5,7},{6,4},{7,5},{8,10},{9,11},{10,... | collective-permute-start | bytes 196616 | tf_op jit(solution)/shard_map/ppermute | solution.py:621
  67.5 0.8 collective-permute-start.14
  68.3 2.1 %collective-permute-start.17 = (f32[8,16,128]{2,1,0:T(8,128)S(1)}, f32[8,16,128]{2,1,0:T(8,128)S(1)}, u32[]{:S(2)}, u32[]{:S(2)}) collective-permute-start(f32[8,16,128]{2,1,0:T(8,128)S(1)} %collective-permute-done.13.refs_3_), channel_id=1, source_target_pairs={{0,4},{4,0},{1,5},{5,1},{2,6},{6,2},{3,7},{7,3},{8,12},{12,8},{9,1... | collective-permute-start | bytes 196616 | tf_op jit(solution)/shard_map/ppermute | solution.py:608
  70.4 0.4 collective-permute-done.12.refs_2_
  70.8 2.5 %collective-permute-start.16 = (f32[8,16,128]{2,1,0:T(8,128)S(1)}, f32[8,16,128]{2,1,0:T(8,128)S(1)}, u32[]{:S(2)}, u32[]{:S(2)}) collective-permute-start(f32[8,16,128]{2,1,0:T(8,128)S(1)} %collective-permute-done.12.refs_2_), channel_id=1, source_target_pairs={{0,4},{4,0},{1,5},{5,1},{2,6},{6,2},{3,7},{7,3},{8,12},{12,8},{9,1... | collective-permute-start | bytes 196616 | tf_op jit(solution)/shard_map/ppermute | solution.py:608
  73.3 0.7 collective-permute-start.15
  74.0 0.2 collective-permute-done.16.refs_6_
  74.2 0.7 collective-permute-done.15.refs_5_
  74.9 0.7 shard_map.51
  75.6 1.3 %collective-permute-start.18 = (f32[4,5,16,128]{3,2,1,0:T(8,128)S(1)}, f32[4,5,16,128]{3,2,1,0:T(8,128)S(1)}, u32[]{:S(2)}, u32[]{:S(2)}) collective-permute-start(f32[4,5,16,128]{3,2,1,0:T(8,128)S(1)} %shard_map.51), channel_id=1, source_target_pairs={{0,8},{1,9},{2,10},{3,11},{12,4},{13,5},{14,6},{15,7},{8,16},{9,17... | collective-permute-start | bytes 491528 | tf_op jit(solution)/shard_map/ppermute | solution.py:617
  76.9 3.0 %shard_map.52.refs_10_ = f32[16,16,128]{2,1,0:T(8,128)S(1)} custom-call(s32[2]{0:T(128)S(1)} %pad_add_fusion.meta, f32[2,8,2,8,128]{4,3,2,1,0:T(8,128)S(1)} %get-tuple-element.65.here, f32[2,8,2,8,128]{4,3,2,1,0:T(8,128)S(1)} %copy-done.10), custom_call_target="tpu_custom_call" | custom-call | tf_op jit(solution)/shard_map/pallas_call | solution.py:21
  79.9 1.3 %shard_map.53 = (f32[28,32,128]{2,1,0:T(8,128)S(1)}, f32[28,32,128]{2,1,0:T(8,128)S(1)}, f32[28,32,128]{2,1,0:T(8,128)S(1)}, f32[22,16,128]{2,1,0:T(8,128)S(1)}) custom-call(s32[2]{0:T(128)S(1)} %pad_add_fusion.meta, s32[16,8]{1,0:T(8,128)S(1)} %copy.13.bricks, f32[8,16,128]{2,1,0:T(8,128)S(1)} %get-tuple-element.55.refs_0_, ...), custom_call_target="tpu_custom_call" | custom-call | tf_op jit(solution)/shard_map/pallas_call | solution.py:21
  81.2 0.7 collective-permute-done.18.refs_8_
  81.9 2.3 %collective-permute-start.19 = (f32[4,5,16,128]{3,2,1,0:T(8,128)S(1)}, f32[4,5,16,128]{3,2,1,0:T(8,128)S(1)}, u32[]{:S(2)}, u32[]{:S(2)}) collective-permute-start(f32[4,5,16,128]{3,2,1,0:T(8,128)S(1)} %collective-permute-done.18.refs_8_), channel_id=1, source_target_pairs={{0,4},{4,0},{1,5},{5,1},{2,6},{6,2},{3,7},{7,3},{8,12},{12,8},{9,1... | collective-permute-start | bytes 491528 | tf_op jit(solution)/shard_map/ppermute | solution.py:608
  84.2 1.0 collective-permute-done.19.refs_9_
  85.3 2.5 %shard_map.54 = (f32[22,16,128]{2,1,0:T(8,128)S(1)}, f32[18,16,128]{2,1,0:T(8,128)S(1)}, f32[8,128]{1,0:T(8,128)S(1)}, f32[28,32,128]{2,1,0:T(8,128)S(1)}, f32[2...) custom-call(s32[2]{0:T(128)S(1)} %pad_add_fusion.meta, s32[16,8]{1,0:T(8,128)S(1)} %copy.13.bricks, ...), custom_call_target="tpu_custom_call" | custom-call | tf_op jit(solution)/shard_map/pallas_call | solution.py:21
  87.8 1.3 %collective-permute-start.20 = (f32[18,16,128]{2,1,0:T(8,128)S(1)}, f32[18,16,128]{2,1,0:T(8,128)S(1)}, u32[]{:S(2)}, u32[]{:S(2)}) collective-permute-start(f32[18,16,128]{2,1,0:T(8,128)S(1)} %get-tuple-element.80), channel_id=1, source_target_pairs={{0,8},{1,9},{2,10},{3,11},{12,4},{13,5},{14,6},{15,7},{8,16},{9,17... | collective-permute-start | bytes 442376 | tf_op jit(solution)/shard_map/ppermute | solution.py:617
  89.1 3.5 %collective-permute-start.22 = (f32[8,128]{1,0:T(8,128)S(1)}, f32[8,128]{1,0:T(8,128)S(1)}, u32[]{:S(2)}, u32[]{:S(2)}) collective-permute-start(f32[8,128]{1,0:T(8,128)S(1)} %get-tuple-element.79), channel_id=1, source_target_pairs={{0,16},{8,24},{16,0},{24,8},{32,48},{40,56},{48,32},{56,40},{64,80... | collective-permute-start | bytes 12296 | tf_op jit(solution)/shard_map/ppermute | solution.py:635
  92.6 1.4 %collective-permute-start.21 = (f32[8,128]{1,0:T(8,128)S(1)}, f32[8,128]{1,0:T(8,128)S(1)}, u32[]{:S(2)}, u32[]{:S(2)}) collective-permute-start(f32[8,128]{1,0:T(8,128)S(1)} %get-tuple-element.79), channel_id=1, source_target_pairs={{0,8},{1,9},{2,10},{3,11},{4,28},{5,29},{6,30},{7,31},{8,16},{9,17... | collective-permute-start | bytes 12296 | tf_op jit(solution)/shard_map/ppermute | solution.py:635
  94.1 1.5 %collective-permute-done.21 = f32[8,128]{1,0:T(8,128)S(1)} collective-permute-done((f32[8,128]{1,0:T(8,128)S(1)}, f32[8,128]{1,0:T(8,128)S(1)}, u32[]{:S(2)}, u32[]{:S(2)}) %collective-permute-start.21) | collective-permute-done | bytes 4128 | tf_op jit(solution)/shard_map/ppermute | solution.py:635
  95.6 5.3 %collective-permute-start.23 = (f32[8,128]{1,0:T(8,128)S(1)}, f32[8,128]{1,0:T(8,128)S(1)}, u32[]{:S(2)}, u32[]{:S(2)}) collective-permute-start(f32[8,128]{1,0:T(8,128)S(1)} %collective-permute-done.21), channel_id=1, source_target_pairs={{0,4},{4,0},{1,5},{5,1},{2,6},{6,2},{3,7},{7,3},{8,12},{12,8},{9,1... | collective-permute-start | bytes 12296 | tf_op jit(solution)/shard_map/ppermute | solution.py:608
  100.9 0.8 collective-permute-done.23
  101.7 3.4 %collective-permute-start.24 = (f32[8,128]{1,0:T(8,128)S(1)}, f32[8,128]{1,0:T(8,128)S(1)}, u32[]{:S(2)}, u32[]{:S(2)}) collective-permute-start(f32[8,128]{1,0:T(8,128)S(1)} %add_add_fusion.sum_0), channel_id=1, source_target_pairs={{0,32},{1,33},{2,34},{3,35},{4,100},{5,101},{6,102},{7,103},{8,40}... | collective-permute-start | bytes 12296 | tf_op jit(solution)/shard_map/ppermute | solution.py:635
  105.1 0.2 collective-permute-start.25
  105.4 0.5 collective-permute-done.24.sum_1
  105.9 1.5 %collective-permute-start.26 = (f32[8,128]{1,0:T(8,128)S(1)}, f32[8,128]{1,0:T(8,128)S(1)}, u32[]{:S(2)}, u32[]{:S(2)}) collective-permute-start(f32[8,128]{1,0:T(8,128)S(1)} %collective-permute-done.24.sum_1), channel_id=1, source_target_pairs={{0,4},{4,0},{1,5},{5,1},{2,6},{6,2},{3,7},{7,3},{8,12},{12,8},{9,1... | collective-permute-start | bytes 12296 | tf_op jit(solution)/shard_map/ppermute | solution.py:608
  107.3 2.9 %shard_map.55.es = f32[22,16,128]{2,1,0:T(8,128)S(1)} custom-call(s32[2]{0:T(128)S(1)} %pad_add_fusion.meta, f32[22,16,128]{2,1,0:T(8,128)S(1)} %get-tuple-element.83.rb, f32[18,16,128]{2,1,0:T(8,128)S(1)} %collective-permute-done.20.one, f32[18,16,128]{2,1,0:T(8,128)S(1)} %collective-permute-done.27.two), custom_call_target="tpu_custom_call" | custom-call | tf_op jit(solution)/shard_map/pallas_call | solution.py:21
  110.3 5.4 %shard_map.56 = f32[1,32,32,128]{3,2,1,0:T(8,128)} custom-call(s32[2]{0:T(128)S(1)} %pad_add_fusion.meta, s32[16,8]{1,0:T(8,128)S(1)} %copy.13.bricks, f32[8,128]{1,0:T(8,128)S(1)} %add_add_fusion.sum_0, f32[8,128]{1,0:T(8,128)S(1)} %collective-permute-done.24.sum_1, f32[8,128]{1,0:T(8,128)S(1)} %collective-permute-done.25.sum_2, ...), custom_call_target="tpu_custom_call" | custom-call | tf_op jit(solution)/shard_map/pallas_call | solution.py:21
  (31 shorter events, 0.1 us)
Async XLA Ops:
  0.8 1.0 copy-start
  1.9 1.0 copy-start.2
  2.9 1.0 copy-start.4
  27.1 11.0 %collective-permute-start = (f32[4,21,8,128]{3,2,1,0:T(8,128)S(1)}, f32[4,21,8,128]{3,2,1,0:T(8,128)S(1)}, u32[]{:S(2)}, u32[]{:S(2)}) collective-permute-start(f32[4,21,8,128]{3,2,1,0:T(8,128)S(1)} %shard_map.47), channel_id=1, source_target_pairs={{8,0},{9,1},{10,2},{11,3},{4,12},{5,13},{6,14},{7,15},{16,8},{17,9... | collective-permute-start | bytes 1032200 | tf_op jit(solution)/shard_map/ppermute | solution.py:617
  30.3 3.9 %collective-permute-start.3 = (f32[8,16,128]{2,1,0:T(8,128)S(1)}, f32[8,16,128]{2,1,0:T(8,128)S(1)}, u32[]{:S(2)}, u32[]{:S(2)}) collective-permute-start(f32[8,16,128]{2,1,0:T(8,128)S(1)} %get-tuple-element.55.refs_0_), channel_id=1, source_target_pairs={{0,3},{1,0},{2,1},{3,2},{4,7},{5,4},{6,5},{7,6},{8,11},{9,8},{10,9... | collective-permute-start | bytes 196616 | tf_op jit(solution)/shard_map/ppermute | solution.py:621
  31.2 5.5 %collective-permute-start.2 = (f32[8,16,128]{2,1,0:T(8,128)S(1)}, f32[8,16,128]{2,1,0:T(8,128)S(1)}, u32[]{:S(2)}, u32[]{:S(2)}) collective-permute-start(f32[8,16,128]{2,1,0:T(8,128)S(1)} %get-tuple-element.55.refs_0_), channel_id=1, source_target_pairs={{0,2},{1,3},{2,0},{3,1},{4,6},{5,7},{6,4},{7,5},{8,10},{9,11},{10,... | collective-permute-start | bytes 196616 | tf_op jit(solution)/shard_map/ppermute | solution.py:621
  32.7 5.4 %collective-permute-start.1 = (f32[8,16,128]{2,1,0:T(8,128)S(1)}, f32[8,16,128]{2,1,0:T(8,128)S(1)}, u32[]{:S(2)}, u32[]{:S(2)}) collective-permute-start(f32[8,16,128]{2,1,0:T(8,128)S(1)} %get-tuple-element.55.refs_0_), channel_id=1, source_target_pairs={{0,1},{1,2},{2,3},{3,0},{4,5},{5,6},{6,7},{7,4},{8,9},{9,10},{10,1... | collective-permute-start | bytes 196616 | tf_op jit(solution)/shard_map/ppermute | solution.py:621
  39.4 1.0 copy-start.6
  40.5 20.1 %copy-start.1 = (f32[1,32,32,128]{3,2,1,0:T(8,128)S(1)}, f32[1,32,32,128]{3,2,1,0:T(8,128)}, u32[]{:S(2)}) copy-start(f32[1,32,32,128]{3,2,1,0:T(8,128)} %u.3) | copy-start | bytes 1572868
  40.5 20.1 %copy-start.3 = (f32[1,32,32,128]{3,2,1,0:T(8,128)S(1)}, f32[1,32,32,128]{3,2,1,0:T(8,128)}, u32[]{:S(2)}) copy-start(f32[1,32,32,128]{3,2,1,0:T(8,128)} %f.3) | copy-start | bytes 1572868
  40.5 20.1 %copy-start.5 = (f32[1,32,32,128]{3,2,1,0:T(8,128)S(1)}, f32[1,32,32,128]{3,2,1,0:T(8,128)}, u32[]{:S(2)}) copy-start(f32[1,32,32,128]{3,2,1,0:T(8,128)} %a.3) | copy-start | bytes 1572868
  40.5 20.1 %all-to-all-start.1 = ((f32[8,35,8,128]{3,2,1,0:T(8,128)}), f32[8,35,8,128]{3,2,1,0:T(8,128)S(1)}, u32[]{:S(2)}, u32[]{:S(2)}) async-start(f32[8,35,8,128]{3,2,1,0:T(8,128)} %copy-done.6), calls=%async_computation.1 | async-start | bytes 2293760 | tf_op jit(solution)/shard_map/all_to_all | solution.py:639
  44.5 1.3 %collective-permute-start.4 = (f32[8,16,128]{2,1,0:T(8,128)S(1)}, f32[8,16,128]{2,1,0:T(8,128)S(1)}, u32[]{:S(2)}, u32[]{:S(2)}) collective-permute-start(f32[8,16,128]{2,1,0:T(8,128)S(1)} %get-tuple-element.55.refs_0_), channel_id=1, source_target_pairs={{0,4},{4,0},{1,5},{5,1},{2,6},{6,2},{3,7},{7,3},{8,12},{12,8},{9,1... | collective-permute-start | bytes 196616 | tf_op jit(solution)/shard_map/ppermute | solution.py:608
  44.6 1.3 %collective-permute-start.5 = (f32[8,16,128]{2,1,0:T(8,128)S(1)}, f32[8,16,128]{2,1,0:T(8,128)S(1)}, u32[]{:S(2)}, u32[]{:S(2)}) collective-permute-start(f32[8,16,128]{2,1,0:T(8,128)S(1)} %collective-permute-done.1.refs_1_), channel_id=1, source_target_pairs={{0,4},{4,0},{1,5},{5,1},{2,6},{6,2},{3,7},{7,3},{8,12},{12,8},{9,1... | collective-permute-start | bytes 196616 | tf_op jit(solution)/shard_map/ppermute | solution.py:608
  45.0 1.3 %collective-permute-start.6 = (f32[8,16,128]{2,1,0:T(8,128)S(1)}, f32[8,16,128]{2,1,0:T(8,128)S(1)}, u32[]{:S(2)}, u32[]{:S(2)}) collective-permute-start(f32[8,16,128]{2,1,0:T(8,128)S(1)} %collective-permute-done.2.refs_2_), channel_id=1, source_target_pairs={{0,4},{4,0},{1,5},{5,1},{2,6},{6,2},{3,7},{7,3},{8,12},{12,8},{9,1... | collective-permute-start | bytes 196616 | tf_op jit(solution)/shard_map/ppermute | solution.py:608
  45.1 1.3 %collective-permute-start.7 = (f32[8,16,128]{2,1,0:T(8,128)S(1)}, f32[8,16,128]{2,1,0:T(8,128)S(1)}, u32[]{:S(2)}, u32[]{:S(2)}) collective-permute-start(f32[8,16,128]{2,1,0:T(8,128)S(1)} %collective-permute-done.3.refs_3_), channel_id=1, source_target_pairs={{0,4},{4,0},{1,5},{5,1},{2,6},{6,2},{3,7},{7,3},{8,12},{12,8},{9,1... | collective-permute-start | bytes 196616 | tf_op jit(solution)/shard_map/ppermute | solution.py:608
  47.1 6.6 %collective-permute-start.8 = (f32[4,5,16,128]{3,2,1,0:T(8,128)S(1)}, f32[4,5,16,128]{3,2,1,0:T(8,128)S(1)}, u32[]{:S(2)}, u32[]{:S(2)}) collective-permute-start(f32[4,5,16,128]{3,2,1,0:T(8,128)S(1)} %shard_map.49), channel_id=1, source_target_pairs={{0,8},{1,9},{2,10},{3,11},{12,4},{13,5},{14,6},{15,7},{8,16},{9,17... | collective-permute-start | bytes 491528 | tf_op jit(solution)/shard_map/ppermute | solution.py:617
  53.7 2.5 %collective-permute-start.9 = (f32[4,5,16,128]{3,2,1,0:T(8,128)S(1)}, f32[4,5,16,128]{3,2,1,0:T(8,128)S(1)}, u32[]{:S(2)}, u32[]{:S(2)}) collective-permute-start(f32[4,5,16,128]{3,2,1,0:T(8,128)S(1)} %collective-permute-done.8.refs_8_), channel_id=1, source_target_pairs={{0,4},{4,0},{1,5},{5,1},{2,6},{6,2},{3,7},{7,3},{8,12},{12,8},{9,1... | collective-permute-start | bytes 491528 | tf_op jit(solution)/shard_map/ppermute | solution.py:608
  54.2 1.3 %collective-permute-start.10 = (f32[2,8,2,8,128]{4,3,2,1,0:T(8,128)S(1)}, f32[2,8,2,8,128]{4,3,2,1,0:T(8,128)S(1)}, u32[]{:S(2)}, u32[]{:S(2)}) collective-permute-start(f32[2,8,2,8,128]{4,3,2,1,0:T(8,128)S(1)} %get-tuple-element.65.here), channel_id=1, source_target_pairs={{0,4},{4,0},{1,5},{5,1},{2,6},{6,2},{3,7},{7,3},{8,12},{12,8},{9,1... | collective-permute-start | bytes 393224 | tf_op jit(solution)/shard_map/ppermute | solution.py:608
  55.5 0.7 copy-start.9
  56.2 0.7 copy-start.7
  60.5 16.4 %copy-start.10 = (f32[2,8,2,8,128]{4,3,2,1,0:T(8,128)S(1)}, f32[2,8,2,8,128]{4,3,2,1,0:T(8,128)}, u32[]{:S(2)}) copy-start(f32[2,8,2,8,128]{4,3,2,1,0:T(8,128)} %copy-done.9) | copy-start | bytes 393220
  65.1 14.8 %copy-start.8 = (f32[4,5,16,128]{3,2,1,0:T(8,128)S(1)}, f32[4,5,16,128]{3,2,1,0:T(8,128)}, u32[]{:S(2)}) copy-start(f32[4,5,16,128]{3,2,1,0:T(8,128)} %copy-done.7) | copy-start | bytes 491524
  65.1 3.2 %collective-permute-start.13 = (f32[8,16,128]{2,1,0:T(8,128)S(1)}, f32[8,16,128]{2,1,0:T(8,128)S(1)}, u32[]{:S(2)}, u32[]{:S(2)}) collective-permute-start(f32[8,16,128]{2,1,0:T(8,128)S(1)} %get-tuple-element.61.refs_0_), channel_id=1, source_target_pairs={{0,3},{1,0},{2,1},{3,2},{4,7},{5,4},{6,5},{7,6},{8,11},{9,8},{10,9... | collective-permute-start | bytes 196616 | tf_op jit(solution)/shard_map/ppermute | solution.py:621
  66.2 4.6 %collective-permute-start.12 = (f32[8,16,128]{2,1,0:T(8,128)S(1)}, f32[8,16,128]{2,1,0:T(8,128)S(1)}, u32[]{:S(2)}, u32[]{:S(2)}) collective-permute-start(f32[8,16,128]{2,1,0:T(8,128)S(1)} %get-tuple-element.61.refs_0_), channel_id=1, source_target_pairs={{0,2},{1,3},{2,0},{3,1},{4,6},{5,7},{6,4},{7,5},{8,10},{9,11},{10,... | collective-permute-start | bytes 196616 | tf_op jit(solution)/shard_map/ppermute | solution.py:621
  67.5 5.7 %collective-permute-start.11 = (f32[8,16,128]{2,1,0:T(8,128)S(1)}, f32[8,16,128]{2,1,0:T(8,128)S(1)}, u32[]{:S(2)}, u32[]{:S(2)}) collective-permute-start(f32[8,16,128]{2,1,0:T(8,128)S(1)} %get-tuple-element.61.refs_0_), channel_id=1, source_target_pairs={{0,1},{1,2},{2,3},{3,0},{4,5},{5,6},{6,7},{7,4},{8,9},{9,10},{10,1... | collective-permute-start | bytes 196616 | tf_op jit(solution)/shard_map/ppermute | solution.py:621
  67.5 6.4 %collective-permute-start.14 = (f32[8,16,128]{2,1,0:T(8,128)S(1)}, f32[8,16,128]{2,1,0:T(8,128)S(1)}, u32[]{:S(2)}, u32[]{:S(2)}) collective-permute-start(f32[8,16,128]{2,1,0:T(8,128)S(1)} %get-tuple-element.61.refs_0_), channel_id=1, source_target_pairs={{0,4},{4,0},{1,5},{5,1},{2,6},{6,2},{3,7},{7,3},{8,12},{12,8},{9,1... | collective-permute-start | bytes 196616 | tf_op jit(solution)/shard_map/ppermute | solution.py:608
  68.3 5.6 %collective-permute-start.17 = (f32[8,16,128]{2,1,0:T(8,128)S(1)}, f32[8,16,128]{2,1,0:T(8,128)S(1)}, u32[]{:S(2)}, u32[]{:S(2)}) collective-permute-start(f32[8,16,128]{2,1,0:T(8,128)S(1)} %collective-permute-done.13.refs_3_), channel_id=1, source_target_pairs={{0,4},{4,0},{1,5},{5,1},{2,6},{6,2},{3,7},{7,3},{8,12},{12,8},{9,1... | collective-permute-start | bytes 196616 | tf_op jit(solution)/shard_map/ppermute | solution.py:608
  70.8 3.4 %collective-permute-start.16 = (f32[8,16,128]{2,1,0:T(8,128)S(1)}, f32[8,16,128]{2,1,0:T(8,128)S(1)}, u32[]{:S(2)}, u32[]{:S(2)}) collective-permute-start(f32[8,16,128]{2,1,0:T(8,128)S(1)} %collective-permute-done.12.refs_2_), channel_id=1, source_target_pairs={{0,4},{4,0},{1,5},{5,1},{2,6},{6,2},{3,7},{7,3},{8,12},{12,8},{9,1... | collective-permute-start | bytes 196616 | tf_op jit(solution)/shard_map/ppermute | solution.py:608
  73.3 1.6 %collective-permute-start.15 = (f32[8,16,128]{2,1,0:T(8,128)S(1)}, f32[8,16,128]{2,1,0:T(8,128)S(1)}, u32[]{:S(2)}, u32[]{:S(2)}) collective-permute-start(f32[8,16,128]{2,1,0:T(8,128)S(1)} %collective-permute-done.11.refs_1_), channel_id=1, source_target_pairs={{0,4},{4,0},{1,5},{5,1},{2,6},{6,2},{3,7},{7,3},{8,12},{12,8},{9,1... | collective-permute-start | bytes 196616 | tf_op jit(solution)/shard_map/ppermute | solution.py:608
  75.6 6.3 %collective-permute-start.18 = (f32[4,5,16,128]{3,2,1,0:T(8,128)S(1)}, f32[4,5,16,128]{3,2,1,0:T(8,128)S(1)}, u32[]{:S(2)}, u32[]{:S(2)}) collective-permute-start(f32[4,5,16,128]{3,2,1,0:T(8,128)S(1)} %shard_map.51), channel_id=1, source_target_pairs={{0,8},{1,9},{2,10},{3,11},{12,4},{13,5},{14,6},{15,7},{8,16},{9,17... | collective-permute-start | bytes 491528 | tf_op jit(solution)/shard_map/ppermute | solution.py:617
  81.9 3.4 %collective-permute-start.19 = (f32[4,5,16,128]{3,2,1,0:T(8,128)S(1)}, f32[4,5,16,128]{3,2,1,0:T(8,128)S(1)}, u32[]{:S(2)}, u32[]{:S(2)}) collective-permute-start(f32[4,5,16,128]{3,2,1,0:T(8,128)S(1)} %collective-permute-done.18.refs_8_), channel_id=1, source_target_pairs={{0,4},{4,0},{1,5},{5,1},{2,6},{6,2},{3,7},{7,3},{8,12},{12,8},{9,1... | collective-permute-start | bytes 491528 | tf_op jit(solution)/shard_map/ppermute | solution.py:608
  87.8 7.8 %collective-permute-start.20 = (f32[18,16,128]{2,1,0:T(8,128)S(1)}, f32[18,16,128]{2,1,0:T(8,128)S(1)}, u32[]{:S(2)}, u32[]{:S(2)}) collective-permute-start(f32[18,16,128]{2,1,0:T(8,128)S(1)} %get-tuple-element.80), channel_id=1, source_target_pairs={{0,8},{1,9},{2,10},{3,11},{12,4},{13,5},{14,6},{15,7},{8,16},{9,17... | collective-permute-start | bytes 442376 | tf_op jit(solution)/shard_map/ppermute | solution.py:617
  89.1 5.0 %collective-permute-start.22 = (f32[8,128]{1,0:T(8,128)S(1)}, f32[8,128]{1,0:T(8,128)S(1)}, u32[]{:S(2)}, u32[]{:S(2)}) collective-permute-start(f32[8,128]{1,0:T(8,128)S(1)} %get-tuple-element.79), channel_id=1, source_target_pairs={{0,16},{8,24},{16,0},{24,8},{32,48},{40,56},{48,32},{56,40},{64,80... | collective-permute-start | bytes 12296 | tf_op jit(solution)/shard_map/ppermute | solution.py:635
  92.6 3.0 %collective-permute-start.21 = (f32[8,128]{1,0:T(8,128)S(1)}, f32[8,128]{1,0:T(8,128)S(1)}, u32[]{:S(2)}, u32[]{:S(2)}) collective-permute-start(f32[8,128]{1,0:T(8,128)S(1)} %get-tuple-element.79), channel_id=1, source_target_pairs={{0,8},{1,9},{2,10},{3,11},{4,28},{5,29},{6,30},{7,31},{8,16},{9,17... | collective-permute-start | bytes 12296 | tf_op jit(solution)/shard_map/ppermute | solution.py:635
  95.6 6.1 %collective-permute-start.23 = (f32[8,128]{1,0:T(8,128)S(1)}, f32[8,128]{1,0:T(8,128)S(1)}, u32[]{:S(2)}, u32[]{:S(2)}) collective-permute-start(f32[8,128]{1,0:T(8,128)S(1)} %collective-permute-done.21), channel_id=1, source_target_pairs={{0,4},{4,0},{1,5},{5,1},{2,6},{6,2},{3,7},{7,3},{8,12},{12,8},{9,1... | collective-permute-start | bytes 12296 | tf_op jit(solution)/shard_map/ppermute | solution.py:608
  100.9 6.4 %collective-permute-start.27 = (f32[18,16,128]{2,1,0:T(8,128)S(1)}, f32[18,16,128]{2,1,0:T(8,128)S(1)}, u32[]{:S(2)}, u32[]{:S(2)}) collective-permute-start(f32[18,16,128]{2,1,0:T(8,128)S(1)} %collective-permute-done.20.one), channel_id=1, source_target_pairs={{0,4},{4,0},{1,5},{5,1},{2,6},{6,2},{3,7},{7,3},{8,12},{12,8},{9,1... | collective-permute-start | bytes 442376 | tf_op jit(solution)/shard_map/ppermute | solution.py:608
  101.7 4.1 %collective-permute-start.24 = (f32[8,128]{1,0:T(8,128)S(1)}, f32[8,128]{1,0:T(8,128)S(1)}, u32[]{:S(2)}, u32[]{:S(2)}) collective-permute-start(f32[8,128]{1,0:T(8,128)S(1)} %add_add_fusion.sum_0), channel_id=1, source_target_pairs={{0,32},{1,33},{2,34},{3,35},{4,100},{5,101},{6,102},{7,103},{8,40}... | collective-permute-start | bytes 12296 | tf_op jit(solution)/shard_map/ppermute | solution.py:635
  105.1 5.1 %collective-permute-start.25 = (f32[8,128]{1,0:T(8,128)S(1)}, f32[8,128]{1,0:T(8,128)S(1)}, u32[]{:S(2)}, u32[]{:S(2)}) collective-permute-start(f32[8,128]{1,0:T(8,128)S(1)} %add_add_fusion.sum_0), channel_id=1, source_target_pairs={{0,64},{8,72},{16,80},{24,88},{32,96},{40,104},{48,112},{56,120},{... | collective-permute-start | bytes 12296 | tf_op jit(solution)/shard_map/ppermute | solution.py:635
  105.9 4.4 %collective-permute-start.26 = (f32[8,128]{1,0:T(8,128)S(1)}, f32[8,128]{1,0:T(8,128)S(1)}, u32[]{:S(2)}, u32[]{:S(2)}) collective-permute-start(f32[8,128]{1,0:T(8,128)S(1)} %collective-permute-done.24.sum_1), channel_id=1, source_target_pairs={{0,4},{4,0},{1,5},{5,1},{2,6},{6,2},{3,7},{7,3},{8,12},{12,8},{9,1... | collective-permute-start | bytes 12296 | tf_op jit(solution)/shard_map/ppermute | solution.py:608

commit v6 on v5

--- a/solution.py
+++ b/solution.py
@@ -152,6 +152,11 @@
     in_x = (x0 & (lane < 8)) | (jnp.logical_not(x0) & (lane >= 120))
     five = (y0 & (row < 5)) | (jnp.logical_not(y0) & (row >= 3))
     three = (y0 & (row < 3)) | (jnp.logical_not(y0) & (row >= 5))
+    seven = (y0 & (row != 7)) | (jnp.logical_not(y0) & (row != 0))
+    mask = odd(8, 128)
+
+    def cut(c, tile):
+        return jnp.where(seven, tile, 0.0) if c >= 3 else tile
 
     def strip(tile, pos):
         shift = (jnp.where(bit_x == 0, 0, 120) + 128 - 8 * pos) % 128
@@ -171,11 +176,13 @@
             for g in range(4):
                 grids[c][at, 8 * g : 8 * g + 8, 0:128] = recv[k, 4 * i + g]
                 grids[c][at, 8 * g : 8 * g + 8, 128:256] = strip(recv[k, GOT_STRIPS], 4 * i + g)
-            grids[c][at, 32:40, 0:128] = rows[i]
-            grids[c][at, 32:40, 128:256] = sides[i]
+            grids[c][at, 32:40, 0:128] = cut(c, rows[i])
+            grids[c][at, 32:40, 128:256] = cut(c, sides[i])
         at = 1 if high else 24
         both = recv[k, 16]
-        for c, cells in ((1, both), (3, swap_lanes(both))):
+        other = swap_lanes(both)
+        other = jnp.where(mask, other, 0.0) if high else jnp.where(mask, 0.0, other)
+        for c, cells in ((1, both), (3, other)):
             grids[c][at, 8 * j : 8 * j + 8, 0:128] = cells
             grids[c][at, 8 * j : 8 * j + 8, 128:256] = jnp.zeros((8, 128), F32)
             grids[c][at, 32:40] = jnp.zeros((8, 256), F32)
@@ -183,8 +190,8 @@
             for c in range(ARRAYS):
                 i = tl * ARRAYS + c
                 at = OWN + 2 * k + tl
-                grids[c][at, 32:40, 0:128] = recv[k, GOT_Y + i]
-                grids[c][at, 32:40, 128:256] = strip(recv[k, GOT_STRIPS + 1], 3 + i)
+                grids[c][at, 32:40, 0:128] = cut(c, recv[k, GOT_Y + i])
+                grids[c][at, 32:40, 128:256] = cut(c, strip(recv[k, GOT_STRIPS + 1], 3 + i))
                 for g in range(4):
                     n = 4 * i + g
                     side = strip(recv[k, GOT_X + n // 16], n % 16)
@@ -227,10 +234,11 @@
         out[j] = jnp.where(even, summed[2 * j], summed[2 * j + 1])
 
 
-def first_kernel(meta, bricks, u, f, a, out, ac, small, planes, rows):
+def first_kernel(meta, bricks, u, f, a, out, ac, small, planes, rows, inverse):
     _, _, bit_x, bit_y, _ = place_of(meta, bricks)
     mask = odd(32, 128)
-    sources = ((u, False), (f, True), (f, False), (a, True), (a, False))
+    inverse[...] = 1.0 / (a[...] + 6.0)
+    sources = ((u, False), (f, True), (f, False), (inverse, True), (inverse, False))
 
     def get(c, t):
         return pair_of(sources[c][0], t, sources[c][1], mask)
@@ -270,19 +278,29 @@
     lax.fori_loop(lo, hi, step, 0, unroll=True)
 
 
+def select_dot(cells, chosen):
+    half, total = chosen.astype(jnp.bfloat16), None
+    for _ in range(3):
+        part = cells.astype(jnp.bfloat16)
+        cells = cells - part.astype(F32)
+        moved = jnp.dot(part, half, preferred_element_type=F32)
+        total = moved if total is None else total + moved
+    return total
+
+
 def pick(rows, cols, keep):
     return jnp.where(keep(iota((rows, cols), 0), iota((rows, cols), 1)), 1.0, 0.0).astype(F32)
 
 
 def fine_down_kernel(meta, bricks, u, f, a, recv, rc, u_b, f_r, f_b, i_r, i_b, u_r, resid, small):
-    slab, _, bit_x, bit_y, bit_z = place_of(meta, bricks)
+    _, _, bit_x, bit_y, _ = place_of(meta, bricks)
     own = odd(32, 128)
-    grids = (u_b, f_r, f_b, i_r, i_b)
-    sources = ((u, False), (f, True), (f, False), (a, True), (a, False))
     for t in range(16):
-        for grid, (cells, red) in zip(grids, sources):
-            grid[OWN + t, 0:32, 0:128] = pair_of(cells, t, red, own)
-    unpack_shell(recv, grids, bit_x, bit_y)
+        here = (OWN + t, slice(0, 32), slice(0, 128))
+        u_b[here] = pair_of(u, t, False, own)
+        f_r[here], f_b[here] = pair_of(f, t, True, own), pair_of(f, t, False, own)
+        i_r[here], i_b[here] = 1.0 / (pair_of(a, t, True, own) + 6.0), 1.0 / (pair_of(a, t, False, own) + 6.0)
+    unpack_shell(recv, (u_b, f_r, f_b, i_r, i_b), bit_x, bit_y)
     zero = jnp.zeros((40, 256), F32)
     for k in (0, 25):
         u_r[k] = zero
@@ -290,26 +308,9 @@
     for k in (1, 24):
         f_b[k] = zero
         i_b[k] = zero
-    row, lane = iota((40, 256), 0), iota((40, 256), 1)
-    x0, y0 = is_zero(bit_x, (40, 256)), is_zero(bit_y, (40, 256))
-    x1, y1 = jnp.logical_not(x0), jnp.logical_not(y0)
-    inside = (row < 32) | (y0 & (row < 39)) | (y1 & (row >= 33))
-    inside = inside & ((lane < 128) | (x0 & (lane < 136)) | (x1 & (lane >= 248)))
-    no_low = (slab == 0) & (bit_z == 0)
-    no_high = (slab == SLABS - 1) & (bit_z == 1)
-
-    mask_int = (row + lane) & 1
-
-    def invert(k, carry):
-        gone = jnp.where((no_low & (k < OWN)) | (no_high & (k >= OWN + 16)), 1, 0)
-        keep = inside & is_zero(gone, (40, 256))
-        far = jnp.where(k == 1, mask_int, jnp.where(k == 24, 1 - mask_int, 1)) == 1
-        i_r[k] = jnp.where(keep & far, 1.0 / (i_r[k] + 6.0), 0.0)
-        ends = jnp.where((k == 1) | (k == 24), 1, 0)
-        i_b[k] = jnp.where(keep & is_zero(ends, (40, 256)), 1.0 / (i_b[k] + 6.0), 0.0)
-        return carry
-
-    lax.fori_loop(1, 25, invert, 0, unroll=4)
+    row = iota((40, 256), 0)
+    y0 = is_zero(bit_y, (40, 256))
+    y1 = jnp.logical_not(y0)
     mask = odd(40, 256)
     cut = (y0 & (row == 0), y1 & (row == 31))
     half_sweep(u_r, u_b, f_r, i_r, 1, 25, True, mask, 1.0, 0, cut)
@@ -319,7 +320,8 @@
     for t in range(16):
         total = around(u_b, OWN + t, True, mask, 0)[0:32, 0:128]
         diag = pair_of(a, t, True, own) + 6.0
-        resid[t] = pair_of(f, t, True, own) + total - diag * u_r[OWN + t, 0:32, 0:128]
+        here = (OWN + t, slice(0, 32), slice(0, 128))
+        resid[t] = f_r[here] + total - diag * u_r[here]
     pack_coarse(resid, small, rc)
 
 
@@ -538,40 +540,44 @@
     slab, _, bit_x, bit_y, bit_z = place_of(meta, bricks)
     total = (sum_0[...] + sum_1[...]) + (sum_2[...] + sum_3[...])
     mean = jnp.sum(total) * (1.0 / (SLABS * 16 * 16 * 64))
-    for i in range(22):
-        shifted = es[i] - mean
-        if i < 3:
-            shifted = jnp.where(is_zero(slab, (16, 128)), 0.0, shifted)
-        if i >= 19:
-            shifted = jnp.where(is_zero(slab - (SLABS - 1), (16, 128)), 0.0, shifted)
-        small[16 * i : 16 * i + 16] = shifted
+    base = 8 * bit_z
+    no_low = jnp.where((slab == 0) & (bit_z == 0), 0, 1)
+    no_high = jnp.where((slab == SLABS - 1) & (bit_z == 1), 0, 1)
+    for j in range(14):
+        shifted = es[base + j] - mean
+        if j < 3:
+            shifted = jnp.where(is_zero(no_low, (16, 128)), 0.0, shifted)
+        if j >= 11:
+            shifted = jnp.where(is_zero(no_high, (16, 128)), 0.0, shifted)
+        small[16 * j : 16 * j + 16] = shifted
     spread = pick(128, 128, lambda r, c: r == (c >> 1))
-    small[...] = jnp.dot(small[...], spread, precision=EXACT, preferred_element_type=F32)
-    for i in range(22):
-        rows = small[16 * i : 16 * i + 16]
-        wide[i, pl.ds(0, 16, stride=2), :] = rows
-        wide[i, pl.ds(1, 16, stride=2), :] = rows
-    for k in (0, 1, 2, 25, 26, 27):
+    small[...] = select_dot(small[...], spread)
+    for j in range(14):
+        rows = small[16 * j : 16 * j + 16]
+        wide[j, pl.ds(0, 16, stride=2), :] = rows
+        wide[j, pl.ds(1, 16, stride=2), :] = rows
+    for k in (0, 15):
         e_r[k] = jnp.zeros((32, 128), F32)
         e_b[k] = jnp.zeros((32, 128), F32)
-    for i in range(22):
-        e_b[3 + i] = ec_b[3 + i] + wide[i]
+    for j in range(14):
+        e_b[1 + j] = ec_b[base + 3 + j] + wide[j]
     coarse = odd(32, 128)
-    for _ in range(2):
-        half_sweep(e_r, e_b, r_r, ci_r, 3, 25, True, coarse, 0.25, 2)
-        half_sweep(e_b, e_r, r_b, ci_b, 3, 25, False, coarse, 0.25, 2)
+    r_r, r_b, ci_r, ci_b = (grid.at[pl.ds(base + 2, 16)] for grid in (r_r, r_b, ci_r, ci_b))
+    half_sweep(e_r, e_b, r_r, ci_r, 1, 15, True, coarse, 0.25, 2)
+    half_sweep(e_b, e_r, r_b, ci_b, 2, 14, False, coarse, 0.25, 2)
+    half_sweep(e_r, e_b, r_r, ci_r, 2, 14, True, coarse, 0.25, 2)
+    half_sweep(e_b, e_r, r_b, ci_b, 3, 13, False, coarse, 0.25, 2)
     for n in range(20):
-        z = n - 2
-        k = 8 * bit_z + (z // 2 + 6)
+        k, upper = n // 2 + 3, n % 2
         red, black = e_r[k], e_b[k]
-        planes[32 * n : 32 * n + 32] = jnp.where(coarse, red, black) if z % 2 else jnp.where(coarse, black, red)
+        planes[32 * n : 32 * n + 32] = jnp.where(coarse, red, black) if upper else jnp.where(coarse, black, red)
 
     lane = iota((128, 256), 1)
     x0 = is_zero(bit_x, (128, 256))
     start = jnp.where(lane < 128, 64 * bit_x + (lane >> 1), (lane >> 1) + jnp.where(x0, 0, -64))
     usable = (lane < 128) | (x0 & (lane < 136)) | (jnp.logical_not(x0) & (lane >= 248))
     spread = jnp.where(usable & (iota((128, 256), 0) == start), 1.0, 0.0).astype(F32)
-    tall_rows = jnp.dot(planes[...], spread, precision=EXACT, preferred_element_type=F32)
+    tall_rows = select_dot(planes[...], spread)
     for n in range(20):
         rows = tall_rows[32 * n : 32 * n + 32]
         for h in range(2):
@@ -645,7 +651,7 @@
     fine = (26, 40, 256)
     packed, ac = run(
         first_kernel, [(8, SENT, 8, 128), (8, 16, 128)], smem, [u_init, source, coeffs],
-        [(8, 32, 128), (16, 32, 128), (256, 128)],
+        [(8, 32, 128), (16, 32, 128), (256, 128), (1, 32, 32, 128)],
     )
     got = among(packed)
     leaving = run(cross_kernel, [(4, FACE + 4, 8, 128)], smem, [got])
@@ -701,7 +707,7 @@
     return run(
         up_kernel, [(1, 32, 32, 128)], smem,
         sums + [es, ec_b, r_r, r_b, ci_r, ci_b, u_b, f_r, f_b, i_r, i_b],
-        [coarse, coarse, (352, 128), (22, 32, 128), (640, 128), (20, 2, 64, 128), (22, 40, 256), (22, 40, 256)],
+        [(16, 32, 128)] * 2 + [(224, 128), (14, 32, 128), (640, 128), (20, 2, 64, 128), (22, 40, 256), (22, 40, 256)],
     )
 
 

time: 116 us -> 115 us (level)
  Pallas kernels: 24.9 us -> 23.7 us
where the time goes in v6:
time: 115 us
  starting transfers between devices  41.3 us (36%)
  Pallas kernels  23.7 us (21%)
  waiting for transfers between devices  22.3 us (19%)
  blocking collectives  20.8 us (18%)
  local copies, waits for them, and re-layouts  6.23 us (5%)
    pallas_call x11, Pallas kernels, run(): pl.pallas_call(kernel, out_shape=shapes[0] if single else shapes, in_spec...  23.7 us
    all_to_all x1, blocking collectives, among(): return lax.all_to_all(x, LB, split_axis=0, concat_axis=0, tiled=True)  20.8 us
    ppermute x14, starting transfers between devices, swap_cores(): return lax.ppermute(x, 'level', [(0, 1), (1, 0)])  16.8 us
    ppermute x4, starting transfers between devices, ring_sums(): return (lax.ppermute(x, ALL, beside), lax.ppermute(x, 'slab', across))  8.61 us
    ppermute x4, starting transfers between devices, to_slabs(): return lax.ppermute(x, ALL, pairs)  7.01 us
    unnamed x23, local copies, waits for them, and re-layouts  6.23 us
    ppermute x4, waiting for transfers between devices, to_slabs(): return lax.ppermute(x, ALL, pairs)  6.03 us
    ppermute x6, waiting for transfers between devices, around_chips(): lax.ppermute(x, 'bottom', [(i, (i + d) % 4) for i in range(4)])  5.78 us
  transfers between devices with their start and end apart: 29, of which 18 were waited for; matrix products, arithmetic and copies ran while one was open for 0% of the time, Pallas kernels for 7%

profile of v6, /device:TPU:1, one launch (start us, length us, event | category | flops | bytes accessed | tf_op | source)
XLA Modules:
  0.0 114.6 jit_solution(5450559887381973988)
XLA Ops:
  0.0 0.8 copy.13.bricks
  0.8 0.1 pad_add_fusion.meta
  0.8 1.0 copy-done
  1.9 1.0 copy-done.2
  2.9 1.0 copy-done.4
  4.0 1.7 %shard_map.46 = (f32[8,32,8,128]{3,2,1,0:T(8,128)S(1)}, f32[8,16,128]{2,1,0:T(8,128)S(1)}) custom-call(s32[2]{0:T(128)S(1)} %pad_add_fusion.meta, s32[16,8]{1,0:T(8,128)S(1)} %copy.13.bricks, f32[1,32,32,128]{3,2,1,0:T(8,128)S(1)} %copy-done, f32[1,32,32,128]{3,2,1,0:T(8,128)S(1)} %copy-done.2, f32[1,32,32,128]{3,2,1,0:T(8,128)S(1)} %copy-done.4), custom_call_target="tpu_custom_call" | custom-call | tf_op jit(solution)/shard_map/pallas_call | solution.py:21
  5.7 20.8 %all_to_all.10.recv = f32[8,32,8,128]{3,2,1,0:T(8,128)S(1)} all-to-all(f32[8,32,8,128]{3,2,1,0:T(8,128)S(1)} %get-tuple-element.49), channel_id=1, replica_groups=mesh['slab'=16,'level'=2,'bottom'=4] {'level','bottom'}, dimensions={0} | all-to-all | bytes 2097152 | tf_op jit(solution)/shard_map/all_to_all | solution.py:645
  26.4 0.7 shard_map.47
  27.1 3.1 %collective-permute-start = (f32[4,21,8,128]{3,2,1,0:T(8,128)S(1)}, f32[4,21,8,128]{3,2,1,0:T(8,128)S(1)}, u32[]{:S(2)}, u32[]{:S(2)}) collective-permute-start(f32[4,21,8,128]{3,2,1,0:T(8,128)S(1)} %shard_map.47), channel_id=1, source_target_pairs={{8,0},{9,1},{10,2},{11,3},{4,12},{5,13},{6,14},{7,15},{16,8},{17,9... | collective-permute-start | bytes 1032200 | tf_op jit(solution)/shard_map/ppermute | solution.py:623
  30.3 0.9 collective-permute-start.3
  31.2 1.5 %collective-permute-start.2 = (f32[8,16,128]{2,1,0:T(8,128)S(1)}, f32[8,16,128]{2,1,0:T(8,128)S(1)}, u32[]{:S(2)}, u32[]{:S(2)}) collective-permute-start(f32[8,16,128]{2,1,0:T(8,128)S(1)} %get-tuple-element.55.refs_0_), channel_id=1, source_target_pairs={{0,2},{1,3},{2,0},{3,1},{4,6},{5,7},{6,4},{7,5},{8,10},{9,11},{10,... | collective-permute-start | bytes 196616 | tf_op jit(solution)/shard_map/ppermute | solution.py:627
  32.7 1.4 %collective-permute-done.3.refs_3_ = f32[8,16,128]{2,1,0:T(8,128)S(1)} collective-permute-done((f32[8,16,128]{2,1,0:T(8,128)S(1)}, f32[8,16,128]{2,1,0:T(8,128)S(1)}, u32[]{:S(2)}, u32[]{:S(2)}) %collective-permute-start.3) | collective-permute-done | bytes 65568 | tf_op jit(solution)/shard_map/ppermute | solution.py:627
  34.2 2.5 %collective-permute-done.2.refs_2_ = f32[8,16,128]{2,1,0:T(8,128)S(1)} collective-permute-done((f32[8,16,128]{2,1,0:T(8,128)S(1)}, f32[8,16,128]{2,1,0:T(8,128)S(1)}, u32[]{:S(2)}, u32[]{:S(2)}) %collective-permute-start.2) | collective-permute-done | bytes 65568 | tf_op jit(solution)/shard_map/ppermute | solution.py:627
  36.7 1.4 %collective-permute-done.1.refs_1_ = f32[8,16,128]{2,1,0:T(8,128)S(1)} collective-permute-done((f32[8,16,128]{2,1,0:T(8,128)S(1)}, f32[8,16,128]{2,1,0:T(8,128)S(1)}, u32[]{:S(2)}, u32[]{:S(2)}) %collective-permute-start.1) | collective-permute-done | bytes 65568 | tf_op jit(solution)/shard_map/ppermute | solution.py:627
  38.1 1.3 %shard_map.48 = (f32[8,35,8,128]{3,2,1,0:T(8,128)S(1)}, f32[2,8,2,8,128]{4,3,2,1,0:T(8,128)S(1)}) custom-call(s32[2]{0:T(128)S(1)} %pad_add_fusion.meta, s32[16,8]{1,0:T(8,128)S(1)} %copy.13.bricks, f32[8,32,8,128]{3,2,1,0:T(8,128)S(1)} %all_to_all.10.recv, f32[4,21,8,128]{3,2,1,0:T(8,128)S(1)} %collective-permute-done.cross), custom_call_target="tpu_custom_call" | custom-call | tf_op jit(solution)/shard_map/pallas_call | solution.py:21
  39.4 1.0 copy-done.6
  40.5 4.0 %all-to-all-start.1 = ((f32[8,35,8,128]{3,2,1,0:T(8,128)}), f32[8,35,8,128]{3,2,1,0:T(8,128)S(1)}, u32[]{:S(2)}, u32[]{:S(2)}) async-start(f32[8,35,8,128]{3,2,1,0:T(8,128)} %copy-done.6), calls=%async_computation.1 | async-start | bytes 2293760 | tf_op jit(solution)/shard_map/all_to_all | solution.py:645
  44.5 0.2 collective-permute-start.4
  44.6 0.3 collective-permute-start.5
  45.0 0.2 collective-permute-start.6
  45.1 0.3 collective-permute-start.7
  45.5 0.2 collective-permute-done.4.refs_4_
  45.7 0.2 collective-permute-done.5.refs_5_
  45.9 0.3 collective-permute-done.6.refs_6_
  46.2 0.2 collective-permute-done.7.refs_7_
  46.4 0.7 shard_map.49
  47.1 1.3 %collective-permute-start.8 = (f32[4,5,16,128]{3,2,1,0:T(8,128)S(1)}, f32[4,5,16,128]{3,2,1,0:T(8,128)S(1)}, u32[]{:S(2)}, u32[]{:S(2)}) collective-permute-start(f32[4,5,16,128]{3,2,1,0:T(8,128)S(1)} %shard_map.49), channel_id=1, source_target_pairs={{0,8},{1,9},{2,10},{3,11},{12,4},{13,5},{14,6},{15,7},{8,16},{9,17... | collective-permute-start | bytes 491528 | tf_op jit(solution)/shard_map/ppermute | solution.py:623
  48.4 5.3 %collective-permute-done.8.refs_8_ = f32[4,5,16,128]{3,2,1,0:T(8,128)S(1)} collective-permute-done((f32[4,5,16,128]{3,2,1,0:T(8,128)S(1)}, f32[4,5,16,128]{3,2,1,0:T(8,128)S(1)}, u32[]{:S(2)}, u32[]{:S(2)}) %collective-permute-start.8) | collective-permute-done | bytes 163872 | tf_op jit(solution)/shard_map/ppermute | solution.py:623
  53.7 0.5 collective-permute-start.9
  54.2 0.1 collective-permute-start.10
  54.2 1.3 %collective-permute-done.10.there = f32[2,8,2,8,128]{4,3,2,1,0:T(8,128)S(1)} collective-permute-done((f32[2,8,2,8,128]{4,3,2,1,0:T(8,128)S(1)}, f32[2,8,2,8,128]{4,3,2,1,0:T(8,128)S(1)}, u32[]{:S(2)}, u32[]{:S(2)}) %collective-permute-start.10) | collective-permute-done | bytes 131104 | tf_op jit(solution)/shard_map/ppermute | solution.py:614
  55.5 0.6 copy-done.9
  56.2 0.7 copy-done.7
  56.9 3.7 %all-to-all-done.1.recv = f32[8,35,8,128]{3,2,1,0:T(8,128)S(1)} async-done(((f32[8,35,8,128]{3,2,1,0:T(8,128)}), f32[8,35,8,128]{3,2,1,0:T(8,128)S(1)}, u32[]{:S(2)}, u32[]{:S(2)}) %all-to-all-start.1) | async-done | bytes 1146912 | tf_op jit(solution)/shard_map/all_to_all | solution.py:645
  60.5 4.6 %shard_map.50 = (f32[8,16,128]{2,1,0:T(8,128)S(1)}, f32[26,40,256]{2,1,0:T(8,128)S(1)}, f32[26,40,256]{2,1,0:T(8,128)S(1)}, f32[26,40,256]{2,1,0:T(8,128)S(1)}, ...) custom-call(s32[2]{0:T(128)S(1)} %pad_add_fusion.meta, s32[16,8]{1,0:T(8,128)S(1)} %copy.13.bricks, ...), custom_call_target="tpu_custom_call" | custom-call | tf_op jit(solution)/shard_map/pallas_call | solution.py:21
  65.1 1.1 collective-permute-start.13
  66.2 1.4 %collective-permute-start.12 = (f32[8,16,128]{2,1,0:T(8,128)S(1)}, f32[8,16,128]{2,1,0:T(8,128)S(1)}, u32[]{:S(2)}, u32[]{:S(2)}) collective-permute-start(f32[8,16,128]{2,1,0:T(8,128)S(1)} %get-tuple-element.61.refs_0_), channel_id=1, source_target_pairs={{0,2},{1,3},{2,0},{3,1},{4,6},{5,7},{6,4},{7,5},{8,10},{9,11},{10,... | collective-permute-start | bytes 196616 | tf_op jit(solution)/shard_map/ppermute | solution.py:627
  67.6 0.8 collective-permute-start.14
  68.3 2.1 %collective-permute-start.17 = (f32[8,16,128]{2,1,0:T(8,128)S(1)}, f32[8,16,128]{2,1,0:T(8,128)S(1)}, u32[]{:S(2)}, u32[]{:S(2)}) collective-permute-start(f32[8,16,128]{2,1,0:T(8,128)S(1)} %collective-permute-done.13.refs_3_), channel_id=1, source_target_pairs={{0,4},{4,0},{1,5},{5,1},{2,6},{6,2},{3,7},{7,3},{8,12},{12,8},{9,1... | collective-permute-start | bytes 196616 | tf_op jit(solution)/shard_map/ppermute | solution.py:614
  70.4 0.4 collective-permute-done.12.refs_2_
  70.8 2.5 %collective-permute-start.16 = (f32[8,16,128]{2,1,0:T(8,128)S(1)}, f32[8,16,128]{2,1,0:T(8,128)S(1)}, u32[]{:S(2)}, u32[]{:S(2)}) collective-permute-start(f32[8,16,128]{2,1,0:T(8,128)S(1)} %collective-permute-done.12.refs_2_), channel_id=1, source_target_pairs={{0,4},{4,0},{1,5},{5,1},{2,6},{6,2},{3,7},{7,3},{8,12},{12,8},{9,1... | collective-permute-start | bytes 196616 | tf_op jit(solution)/shard_map/ppermute | solution.py:614
  73.3 0.7 collective-permute-start.15
  74.0 0.2 collective-permute-done.16.refs_6_
  74.2 0.7 collective-permute-done.15.refs_5_
  74.9 0.7 shard_map.51
  75.6 1.3 %collective-permute-start.18 = (f32[4,5,16,128]{3,2,1,0:T(8,128)S(1)}, f32[4,5,16,128]{3,2,1,0:T(8,128)S(1)}, u32[]{:S(2)}, u32[]{:S(2)}) collective-permute-start(f32[4,5,16,128]{3,2,1,0:T(8,128)S(1)} %shard_map.51), channel_id=1, source_target_pairs={{0,8},{1,9},{2,10},{3,11},{12,4},{13,5},{14,6},{15,7},{8,16},{9,17... | collective-permute-start | bytes 491528 | tf_op jit(solution)/shard_map/ppermute | solution.py:623
  76.9 3.0 %shard_map.52.refs_10_ = f32[16,16,128]{2,1,0:T(8,128)S(1)} custom-call(s32[2]{0:T(128)S(1)} %pad_add_fusion.meta, f32[2,8,2,8,128]{4,3,2,1,0:T(8,128)S(1)} %get-tuple-element.65.here, f32[2,8,2,8,128]{4,3,2,1,0:T(8,128)S(1)} %copy-done.10), custom_call_target="tpu_custom_call" | custom-call | tf_op jit(solution)/shard_map/pallas_call | solution.py:21
  79.9 1.3 %shard_map.53 = (f32[28,32,128]{2,1,0:T(8,128)S(1)}, f32[28,32,128]{2,1,0:T(8,128)S(1)}, f32[28,32,128]{2,1,0:T(8,128)S(1)}, f32[22,16,128]{2,1,0:T(8,128)S(1)}) custom-call(s32[2]{0:T(128)S(1)} %pad_add_fusion.meta, s32[16,8]{1,0:T(8,128)S(1)} %copy.13.bricks, f32[8,16,128]{2,1,0:T(8,128)S(1)} %get-tuple-element.55.refs_0_, ...), custom_call_target="tpu_custom_call" | custom-call | tf_op jit(solution)/shard_map/pallas_call | solution.py:21
  81.2 0.7 collective-permute-done.18.refs_8_
  81.9 2.5 %collective-permute-start.19 = (f32[4,5,16,128]{3,2,1,0:T(8,128)S(1)}, f32[4,5,16,128]{3,2,1,0:T(8,128)S(1)}, u32[]{:S(2)}, u32[]{:S(2)}) collective-permute-start(f32[4,5,16,128]{3,2,1,0:T(8,128)S(1)} %collective-permute-done.18.refs_8_), channel_id=1, source_target_pairs={{0,4},{4,0},{1,5},{5,1},{2,6},{6,2},{3,7},{7,3},{8,12},{12,8},{9,1... | collective-permute-start | bytes 491528 | tf_op jit(solution)/shard_map/ppermute | solution.py:614
  84.4 1.0 collective-permute-done.19.refs_9_
  85.5 2.4 %shard_map.54 = (f32[22,16,128]{2,1,0:T(8,128)S(1)}, f32[18,16,128]{2,1,0:T(8,128)S(1)}, f32[8,128]{1,0:T(8,128)S(1)}, f32[28,32,128]{2,1,0:T(8,128)S(1)}, f32[2...) custom-call(s32[2]{0:T(128)S(1)} %pad_add_fusion.meta, s32[16,8]{1,0:T(8,128)S(1)} %copy.13.bricks, ...), custom_call_target="tpu_custom_call" | custom-call | tf_op jit(solution)/shard_map/pallas_call | solution.py:21
  87.8 1.3 %collective-permute-start.20 = (f32[18,16,128]{2,1,0:T(8,128)S(1)}, f32[18,16,128]{2,1,0:T(8,128)S(1)}, u32[]{:S(2)}, u32[]{:S(2)}) collective-permute-start(f32[18,16,128]{2,1,0:T(8,128)S(1)} %get-tuple-element.80), channel_id=1, source_target_pairs={{0,8},{1,9},{2,10},{3,11},{12,4},{13,5},{14,6},{15,7},{8,16},{9,17... | collective-permute-start | bytes 442376 | tf_op jit(solution)/shard_map/ppermute | solution.py:623
  89.1 3.5 %collective-permute-start.22 = (f32[8,128]{1,0:T(8,128)S(1)}, f32[8,128]{1,0:T(8,128)S(1)}, u32[]{:S(2)}, u32[]{:S(2)}) collective-permute-start(f32[8,128]{1,0:T(8,128)S(1)} %get-tuple-element.79), channel_id=1, source_target_pairs={{0,16},{8,24},{16,0},{24,8},{32,48},{40,56},{48,32},{56,40},{64,80... | collective-permute-start | bytes 12296 | tf_op jit(solution)/shard_map/ppermute | solution.py:641
  92.6 1.4 %collective-permute-start.21 = (f32[8,128]{1,0:T(8,128)S(1)}, f32[8,128]{1,0:T(8,128)S(1)}, u32[]{:S(2)}, u32[]{:S(2)}) collective-permute-start(f32[8,128]{1,0:T(8,128)S(1)} %get-tuple-element.79), channel_id=1, source_target_pairs={{0,8},{1,9},{2,10},{3,11},{4,28},{5,29},{6,30},{7,31},{8,16},{9,17... | collective-permute-start | bytes 12296 | tf_op jit(solution)/shard_map/ppermute | solution.py:641
  94.1 1.5 %collective-permute-done.21 = f32[8,128]{1,0:T(8,128)S(1)} collective-permute-done((f32[8,128]{1,0:T(8,128)S(1)}, f32[8,128]{1,0:T(8,128)S(1)}, u32[]{:S(2)}, u32[]{:S(2)}) %collective-permute-start.21) | collective-permute-done | bytes 4128 | tf_op jit(solution)/shard_map/ppermute | solution.py:641
  95.6 5.3 %collective-permute-start.23 = (f32[8,128]{1,0:T(8,128)S(1)}, f32[8,128]{1,0:T(8,128)S(1)}, u32[]{:S(2)}, u32[]{:S(2)}) collective-permute-start(f32[8,128]{1,0:T(8,128)S(1)} %collective-permute-done.21), channel_id=1, source_target_pairs={{0,4},{4,0},{1,5},{5,1},{2,6},{6,2},{3,7},{7,3},{8,12},{12,8},{9,1... | collective-permute-start | bytes 12296 | tf_op jit(solution)/shard_map/ppermute | solution.py:614
  100.9 0.8 collective-permute-done.23
  101.8 3.2 %collective-permute-start.24 = (f32[8,128]{1,0:T(8,128)S(1)}, f32[8,128]{1,0:T(8,128)S(1)}, u32[]{:S(2)}, u32[]{:S(2)}) collective-permute-start(f32[8,128]{1,0:T(8,128)S(1)} %add_add_fusion.sum_0), channel_id=1, source_target_pairs={{0,32},{1,33},{2,34},{3,35},{4,100},{5,101},{6,102},{7,103},{8,40}... | collective-permute-start | bytes 12296 | tf_op jit(solution)/shard_map/ppermute | solution.py:641
  105.0 0.4 collective-permute-start.25
  105.4 0.3 collective-permute-done.24.sum_1
  105.7 1.5 %collective-permute-start.26 = (f32[8,128]{1,0:T(8,128)S(1)}, f32[8,128]{1,0:T(8,128)S(1)}, u32[]{:S(2)}, u32[]{:S(2)}) collective-permute-start(f32[8,128]{1,0:T(8,128)S(1)} %collective-permute-done.24.sum_1), channel_id=1, source_target_pairs={{0,4},{4,0},{1,5},{5,1},{2,6},{6,2},{3,7},{7,3},{8,12},{12,8},{9,1... | collective-permute-start | bytes 12296 | tf_op jit(solution)/shard_map/ppermute | solution.py:614
  107.2 2.9 %shard_map.55.es = f32[22,16,128]{2,1,0:T(8,128)S(1)} custom-call(s32[2]{0:T(128)S(1)} %pad_add_fusion.meta, f32[22,16,128]{2,1,0:T(8,128)S(1)} %get-tuple-element.83.rb, f32[18,16,128]{2,1,0:T(8,128)S(1)} %collective-permute-done.20.one, f32[18,16,128]{2,1,0:T(8,128)S(1)} %collective-permute-done.27.two), custom_call_target="tpu_custom_call" | custom-call | tf_op jit(solution)/shard_map/pallas_call | solution.py:21
  110.1 4.5 %shard_map.56 = f32[1,32,32,128]{3,2,1,0:T(8,128)} custom-call(s32[2]{0:T(128)S(1)} %pad_add_fusion.meta, s32[16,8]{1,0:T(8,128)S(1)} %copy.13.bricks, f32[8,128]{1,0:T(8,128)S(1)} %add_add_fusion.sum_0, f32[8,128]{1,0:T(8,128)S(1)} %collective-permute-done.24.sum_1, f32[8,128]{1,0:T(8,128)S(1)} %collective-permute-done.25.sum_2, ...), custom_call_target="tpu_custom_call" | custom-call | tf_op jit(solution)/shard_map/pallas_call | solution.py:21
  (31 shorter events, 0.1 us)
Async XLA Ops:
  0.8 1.0 copy-start
  1.9 1.0 copy-start.2
  2.9 1.0 copy-start.4
  27.1 11.0 %collective-permute-start = (f32[4,21,8,128]{3,2,1,0:T(8,128)S(1)}, f32[4,21,8,128]{3,2,1,0:T(8,128)S(1)}, u32[]{:S(2)}, u32[]{:S(2)}) collective-permute-start(f32[4,21,8,128]{3,2,1,0:T(8,128)S(1)} %shard_map.47), channel_id=1, source_target_pairs={{8,0},{9,1},{10,2},{11,3},{4,12},{5,13},{6,14},{7,15},{16,8},{17,9... | collective-permute-start | bytes 1032200 | tf_op jit(solution)/shard_map/ppermute | solution.py:623
  30.3 3.9 %collective-permute-start.3 = (f32[8,16,128]{2,1,0:T(8,128)S(1)}, f32[8,16,128]{2,1,0:T(8,128)S(1)}, u32[]{:S(2)}, u32[]{:S(2)}) collective-permute-start(f32[8,16,128]{2,1,0:T(8,128)S(1)} %get-tuple-element.55.refs_0_), channel_id=1, source_target_pairs={{0,3},{1,0},{2,1},{3,2},{4,7},{5,4},{6,5},{7,6},{8,11},{9,8},{10,9... | collective-permute-start | bytes 196616 | tf_op jit(solution)/shard_map/ppermute | solution.py:627
  31.2 5.5 %collective-permute-start.2 = (f32[8,16,128]{2,1,0:T(8,128)S(1)}, f32[8,16,128]{2,1,0:T(8,128)S(1)}, u32[]{:S(2)}, u32[]{:S(2)}) collective-permute-start(f32[8,16,128]{2,1,0:T(8,128)S(1)} %get-tuple-element.55.refs_0_), channel_id=1, source_target_pairs={{0,2},{1,3},{2,0},{3,1},{4,6},{5,7},{6,4},{7,5},{8,10},{9,11},{10,... | collective-permute-start | bytes 196616 | tf_op jit(solution)/shard_map/ppermute | solution.py:627
  32.7 5.4 %collective-permute-start.1 = (f32[8,16,128]{2,1,0:T(8,128)S(1)}, f32[8,16,128]{2,1,0:T(8,128)S(1)}, u32[]{:S(2)}, u32[]{:S(2)}) collective-permute-start(f32[8,16,128]{2,1,0:T(8,128)S(1)} %get-tuple-element.55.refs_0_), channel_id=1, source_target_pairs={{0,1},{1,2},{2,3},{3,0},{4,5},{5,6},{6,7},{7,4},{8,9},{9,10},{10,1... | collective-permute-start | bytes 196616 | tf_op jit(solution)/shard_map/ppermute | solution.py:627
  39.4 1.0 copy-start.6
  40.5 20.1 %copy-start.1 = (f32[1,32,32,128]{3,2,1,0:T(8,128)S(1)}, f32[1,32,32,128]{3,2,1,0:T(8,128)}, u32[]{:S(2)}) copy-start(f32[1,32,32,128]{3,2,1,0:T(8,128)} %u.3) | copy-start | bytes 1572868
  40.5 20.1 %copy-start.3 = (f32[1,32,32,128]{3,2,1,0:T(8,128)S(1)}, f32[1,32,32,128]{3,2,1,0:T(8,128)}, u32[]{:S(2)}) copy-start(f32[1,32,32,128]{3,2,1,0:T(8,128)} %f.3) | copy-start | bytes 1572868
  40.5 20.1 %copy-start.5 = (f32[1,32,32,128]{3,2,1,0:T(8,128)S(1)}, f32[1,32,32,128]{3,2,1,0:T(8,128)}, u32[]{:S(2)}) copy-start(f32[1,32,32,128]{3,2,1,0:T(8,128)} %a.3) | copy-start | bytes 1572868
  40.5 20.1 %all-to-all-start.1 = ((f32[8,35,8,128]{3,2,1,0:T(8,128)}), f32[8,35,8,128]{3,2,1,0:T(8,128)S(1)}, u32[]{:S(2)}, u32[]{:S(2)}) async-start(f32[8,35,8,128]{3,2,1,0:T(8,128)} %copy-done.6), calls=%async_computation.1 | async-start | bytes 2293760 | tf_op jit(solution)/shard_map/all_to_all | solution.py:645
  44.5 1.3 %collective-permute-start.4 = (f32[8,16,128]{2,1,0:T(8,128)S(1)}, f32[8,16,128]{2,1,0:T(8,128)S(1)}, u32[]{:S(2)}, u32[]{:S(2)}) collective-permute-start(f32[8,16,128]{2,1,0:T(8,128)S(1)} %get-tuple-element.55.refs_0_), channel_id=1, source_target_pairs={{0,4},{4,0},{1,5},{5,1},{2,6},{6,2},{3,7},{7,3},{8,12},{12,8},{9,1... | collective-permute-start | bytes 196616 | tf_op jit(solution)/shard_map/ppermute | solution.py:614
  44.6 1.3 %collective-permute-start.5 = (f32[8,16,128]{2,1,0:T(8,128)S(1)}, f32[8,16,128]{2,1,0:T(8,128)S(1)}, u32[]{:S(2)}, u32[]{:S(2)}) collective-permute-start(f32[8,16,128]{2,1,0:T(8,128)S(1)} %collective-permute-done.1.refs_1_), channel_id=1, source_target_pairs={{0,4},{4,0},{1,5},{5,1},{2,6},{6,2},{3,7},{7,3},{8,12},{12,8},{9,1... | collective-permute-start | bytes 196616 | tf_op jit(solution)/shard_map/ppermute | solution.py:614
  45.0 1.3 %collective-permute-start.6 = (f32[8,16,128]{2,1,0:T(8,128)S(1)}, f32[8,16,128]{2,1,0:T(8,128)S(1)}, u32[]{:S(2)}, u32[]{:S(2)}) collective-permute-start(f32[8,16,128]{2,1,0:T(8,128)S(1)} %collective-permute-done.2.refs_2_), channel_id=1, source_target_pairs={{0,4},{4,0},{1,5},{5,1},{2,6},{6,2},{3,7},{7,3},{8,12},{12,8},{9,1... | collective-permute-start | bytes 196616 | tf_op jit(solution)/shard_map/ppermute | solution.py:614
  45.1 1.3 %collective-permute-start.7 = (f32[8,16,128]{2,1,0:T(8,128)S(1)}, f32[8,16,128]{2,1,0:T(8,128)S(1)}, u32[]{:S(2)}, u32[]{:S(2)}) collective-permute-start(f32[8,16,128]{2,1,0:T(8,128)S(1)} %collective-permute-done.3.refs_3_), channel_id=1, source_target_pairs={{0,4},{4,0},{1,5},{5,1},{2,6},{6,2},{3,7},{7,3},{8,12},{12,8},{9,1... | collective-permute-start | bytes 196616 | tf_op jit(solution)/shard_map/ppermute | solution.py:614
  47.1 6.6 %collective-permute-start.8 = (f32[4,5,16,128]{3,2,1,0:T(8,128)S(1)}, f32[4,5,16,128]{3,2,1,0:T(8,128)S(1)}, u32[]{:S(2)}, u32[]{:S(2)}) collective-permute-start(f32[4,5,16,128]{3,2,1,0:T(8,128)S(1)} %shard_map.49), channel_id=1, source_target_pairs={{0,8},{1,9},{2,10},{3,11},{12,4},{13,5},{14,6},{15,7},{8,16},{9,17... | collective-permute-start | bytes 491528 | tf_op jit(solution)/shard_map/ppermute | solution.py:623
  53.7 2.5 %collective-permute-start.9 = (f32[4,5,16,128]{3,2,1,0:T(8,128)S(1)}, f32[4,5,16,128]{3,2,1,0:T(8,128)S(1)}, u32[]{:S(2)}, u32[]{:S(2)}) collective-permute-start(f32[4,5,16,128]{3,2,1,0:T(8,128)S(1)} %collective-permute-done.8.refs_8_), channel_id=1, source_target_pairs={{0,4},{4,0},{1,5},{5,1},{2,6},{6,2},{3,7},{7,3},{8,12},{12,8},{9,1... | collective-permute-start | bytes 491528 | tf_op jit(solution)/shard_map/ppermute | solution.py:614
  54.2 1.3 %collective-permute-start.10 = (f32[2,8,2,8,128]{4,3,2,1,0:T(8,128)S(1)}, f32[2,8,2,8,128]{4,3,2,1,0:T(8,128)S(1)}, u32[]{:S(2)}, u32[]{:S(2)}) collective-permute-start(f32[2,8,2,8,128]{4,3,2,1,0:T(8,128)S(1)} %get-tuple-element.65.here), channel_id=1, source_target_pairs={{0,4},{4,0},{1,5},{5,1},{2,6},{6,2},{3,7},{7,3},{8,12},{12,8},{9,1... | collective-permute-start | bytes 393224 | tf_op jit(solution)/shard_map/ppermute | solution.py:614
  55.5 0.7 copy-start.9
  56.2 0.7 copy-start.7
  60.5 16.4 %copy-start.10 = (f32[2,8,2,8,128]{4,3,2,1,0:T(8,128)S(1)}, f32[2,8,2,8,128]{4,3,2,1,0:T(8,128)}, u32[]{:S(2)}) copy-start(f32[2,8,2,8,128]{4,3,2,1,0:T(8,128)} %copy-done.9) | copy-start | bytes 393220
  65.1 14.8 %copy-start.8 = (f32[4,5,16,128]{3,2,1,0:T(8,128)S(1)}, f32[4,5,16,128]{3,2,1,0:T(8,128)}, u32[]{:S(2)}) copy-start(f32[4,5,16,128]{3,2,1,0:T(8,128)} %copy-done.7) | copy-start | bytes 491524
  65.1 3.2 %collective-permute-start.13 = (f32[8,16,128]{2,1,0:T(8,128)S(1)}, f32[8,16,128]{2,1,0:T(8,128)S(1)}, u32[]{:S(2)}, u32[]{:S(2)}) collective-permute-start(f32[8,16,128]{2,1,0:T(8,128)S(1)} %get-tuple-element.61.refs_0_), channel_id=1, source_target_pairs={{0,3},{1,0},{2,1},{3,2},{4,7},{5,4},{6,5},{7,6},{8,11},{9,8},{10,9... | collective-permute-start | bytes 196616 | tf_op jit(solution)/shard_map/ppermute | solution.py:627
  66.2 4.6 %collective-permute-start.12 = (f32[8,16,128]{2,1,0:T(8,128)S(1)}, f32[8,16,128]{2,1,0:T(8,128)S(1)}, u32[]{:S(2)}, u32[]{:S(2)}) collective-permute-start(f32[8,16,128]{2,1,0:T(8,128)S(1)} %get-tuple-element.61.refs_0_), channel_id=1, source_target_pairs={{0,2},{1,3},{2,0},{3,1},{4,6},{5,7},{6,4},{7,5},{8,10},{9,11},{10,... | collective-permute-start | bytes 196616 | tf_op jit(solution)/shard_map/ppermute | solution.py:627
  67.6 5.7 %collective-permute-start.11 = (f32[8,16,128]{2,1,0:T(8,128)S(1)}, f32[8,16,128]{2,1,0:T(8,128)S(1)}, u32[]{:S(2)}, u32[]{:S(2)}) collective-permute-start(f32[8,16,128]{2,1,0:T(8,128)S(1)} %get-tuple-element.61.refs_0_), channel_id=1, source_target_pairs={{0,1},{1,2},{2,3},{3,0},{4,5},{5,6},{6,7},{7,4},{8,9},{9,10},{10,1... | collective-permute-start | bytes 196616 | tf_op jit(solution)/shard_map/ppermute | solution.py:627
  67.6 6.4 %collective-permute-start.14 = (f32[8,16,128]{2,1,0:T(8,128)S(1)}, f32[8,16,128]{2,1,0:T(8,128)S(1)}, u32[]{:S(2)}, u32[]{:S(2)}) collective-permute-start(f32[8,16,128]{2,1,0:T(8,128)S(1)} %get-tuple-element.61.refs_0_), channel_id=1, source_target_pairs={{0,4},{4,0},{1,5},{5,1},{2,6},{6,2},{3,7},{7,3},{8,12},{12,8},{9,1... | collective-permute-start | bytes 196616 | tf_op jit(solution)/shard_map/ppermute | solution.py:614
  68.3 5.6 %collective-permute-start.17 = (f32[8,16,128]{2,1,0:T(8,128)S(1)}, f32[8,16,128]{2,1,0:T(8,128)S(1)}, u32[]{:S(2)}, u32[]{:S(2)}) collective-permute-start(f32[8,16,128]{2,1,0:T(8,128)S(1)} %collective-permute-done.13.refs_3_), channel_id=1, source_target_pairs={{0,4},{4,0},{1,5},{5,1},{2,6},{6,2},{3,7},{7,3},{8,12},{12,8},{9,1... | collective-permute-start | bytes 196616 | tf_op jit(solution)/shard_map/ppermute | solution.py:614
  70.8 3.4 %collective-permute-start.16 = (f32[8,16,128]{2,1,0:T(8,128)S(1)}, f32[8,16,128]{2,1,0:T(8,128)S(1)}, u32[]{:S(2)}, u32[]{:S(2)}) collective-permute-start(f32[8,16,128]{2,1,0:T(8,128)S(1)} %collective-permute-done.12.refs_2_), channel_id=1, source_target_pairs={{0,4},{4,0},{1,5},{5,1},{2,6},{6,2},{3,7},{7,3},{8,12},{12,8},{9,1... | collective-permute-start | bytes 196616 | tf_op jit(solution)/shard_map/ppermute | solution.py:614
  73.3 1.6 %collective-permute-start.15 = (f32[8,16,128]{2,1,0:T(8,128)S(1)}, f32[8,16,128]{2,1,0:T(8,128)S(1)}, u32[]{:S(2)}, u32[]{:S(2)}) collective-permute-start(f32[8,16,128]{2,1,0:T(8,128)S(1)} %collective-permute-done.11.refs_1_), channel_id=1, source_target_pairs={{0,4},{4,0},{1,5},{5,1},{2,6},{6,2},{3,7},{7,3},{8,12},{12,8},{9,1... | collective-permute-start | bytes 196616 | tf_op jit(solution)/shard_map/ppermute | solution.py:614
  75.6 6.3 %collective-permute-start.18 = (f32[4,5,16,128]{3,2,1,0:T(8,128)S(1)}, f32[4,5,16,128]{3,2,1,0:T(8,128)S(1)}, u32[]{:S(2)}, u32[]{:S(2)}) collective-permute-start(f32[4,5,16,128]{3,2,1,0:T(8,128)S(1)} %shard_map.51), channel_id=1, source_target_pairs={{0,8},{1,9},{2,10},{3,11},{12,4},{13,5},{14,6},{15,7},{8,16},{9,17... | collective-permute-start | bytes 491528 | tf_op jit(solution)/shard_map/ppermute | solution.py:623
  81.9 3.5 %collective-permute-start.19 = (f32[4,5,16,128]{3,2,1,0:T(8,128)S(1)}, f32[4,5,16,128]{3,2,1,0:T(8,128)S(1)}, u32[]{:S(2)}, u32[]{:S(2)}) collective-permute-start(f32[4,5,16,128]{3,2,1,0:T(8,128)S(1)} %collective-permute-done.18.refs_8_), channel_id=1, source_target_pairs={{0,4},{4,0},{1,5},{5,1},{2,6},{6,2},{3,7},{7,3},{8,12},{12,8},{9,1... | collective-permute-start | bytes 491528 | tf_op jit(solution)/shard_map/ppermute | solution.py:614
  87.8 7.8 %collective-permute-start.20 = (f32[18,16,128]{2,1,0:T(8,128)S(1)}, f32[18,16,128]{2,1,0:T(8,128)S(1)}, u32[]{:S(2)}, u32[]{:S(2)}) collective-permute-start(f32[18,16,128]{2,1,0:T(8,128)S(1)} %get-tuple-element.80), channel_id=1, source_target_pairs={{0,8},{1,9},{2,10},{3,11},{12,4},{13,5},{14,6},{15,7},{8,16},{9,17... | collective-permute-start | bytes 442376 | tf_op jit(solution)/shard_map/ppermute | solution.py:623
  89.1 5.0 %collective-permute-start.22 = (f32[8,128]{1,0:T(8,128)S(1)}, f32[8,128]{1,0:T(8,128)S(1)}, u32[]{:S(2)}, u32[]{:S(2)}) collective-permute-start(f32[8,128]{1,0:T(8,128)S(1)} %get-tuple-element.79), channel_id=1, source_target_pairs={{0,16},{8,24},{16,0},{24,8},{32,48},{40,56},{48,32},{56,40},{64,80... | collective-permute-start | bytes 12296 | tf_op jit(solution)/shard_map/ppermute | solution.py:641
  92.6 3.0 %collective-permute-start.21 = (f32[8,128]{1,0:T(8,128)S(1)}, f32[8,128]{1,0:T(8,128)S(1)}, u32[]{:S(2)}, u32[]{:S(2)}) collective-permute-start(f32[8,128]{1,0:T(8,128)S(1)} %get-tuple-element.79), channel_id=1, source_target_pairs={{0,8},{1,9},{2,10},{3,11},{4,28},{5,29},{6,30},{7,31},{8,16},{9,17... | collective-permute-start | bytes 12296 | tf_op jit(solution)/shard_map/ppermute | solution.py:641
  95.6 6.1 %collective-permute-start.23 = (f32[8,128]{1,0:T(8,128)S(1)}, f32[8,128]{1,0:T(8,128)S(1)}, u32[]{:S(2)}, u32[]{:S(2)}) collective-permute-start(f32[8,128]{1,0:T(8,128)S(1)} %collective-permute-done.21), channel_id=1, source_target_pairs={{0,4},{4,0},{1,5},{5,1},{2,6},{6,2},{3,7},{7,3},{8,12},{12,8},{9,1... | collective-permute-start | bytes 12296 | tf_op jit(solution)/shard_map/ppermute | solution.py:614
  100.9 6.3 %collective-permute-start.27 = (f32[18,16,128]{2,1,0:T(8,128)S(1)}, f32[18,16,128]{2,1,0:T(8,128)S(1)}, u32[]{:S(2)}, u32[]{:S(2)}) collective-permute-start(f32[18,16,128]{2,1,0:T(8,128)S(1)} %collective-permute-done.20.one), channel_id=1, source_target_pairs={{0,4},{4,0},{1,5},{5,1},{2,6},{6,2},{3,7},{7,3},{8,12},{12,8},{9,1... | collective-permute-start | bytes 442376 | tf_op jit(solution)/shard_map/ppermute | solution.py:614
  101.8 4.0 %collective-permute-start.24 = (f32[8,128]{1,0:T(8,128)S(1)}, f32[8,128]{1,0:T(8,128)S(1)}, u32[]{:S(2)}, u32[]{:S(2)}) collective-permute-start(f32[8,128]{1,0:T(8,128)S(1)} %add_add_fusion.sum_0), channel_id=1, source_target_pairs={{0,32},{1,33},{2,34},{3,35},{4,100},{5,101},{6,102},{7,103},{8,40}... | collective-permute-start | bytes 12296 | tf_op jit(solution)/shard_map/ppermute | solution.py:641
  105.0 5.1 %collective-permute-start.25 = (f32[8,128]{1,0:T(8,128)S(1)}, f32[8,128]{1,0:T(8,128)S(1)}, u32[]{:S(2)}, u32[]{:S(2)}) collective-permute-start(f32[8,128]{1,0:T(8,128)S(1)} %add_add_fusion.sum_0), channel_id=1, source_target_pairs={{0,64},{8,72},{16,80},{24,88},{32,96},{40,104},{48,112},{56,120},{... | collective-permute-start | bytes 12296 | tf_op jit(solution)/shard_map/ppermute | solution.py:641
  105.7 4.4 %collective-permute-start.26 = (f32[8,128]{1,0:T(8,128)S(1)}, f32[8,128]{1,0:T(8,128)S(1)}, u32[]{:S(2)}, u32[]{:S(2)}) collective-permute-start(f32[8,128]{1,0:T(8,128)S(1)} %collective-permute-done.24.sum_1), channel_id=1, source_target_pairs={{0,4},{4,0},{1,5},{5,1},{2,6},{6,2},{3,7},{7,3},{8,12},{12,8},{9,1... | collective-permute-start | bytes 12296 | tf_op jit(solution)/shard_map/ppermute | solution.py:614

commit v7 on v6

--- a/solution.py
+++ b/solution.py
@@ -657,11 +657,12 @@
     leaving = run(cross_kernel, [(4, FACE + 4, 8, 128)], smem, [got])
     leaving, ac = lax.optimization_barrier((leaving, ac))
     cross = to_slabs(leaving, False)
-    cross, *ac_boxes = lax.optimization_barrier((cross, *around_chips(ac)))
+    ac_boxes = around_chips(ac)
     sent, coef = run(
         mid_kernel, [(8, GOT, 8, 128), (2, 8, 2, 8, 128)], smem, [got, cross], [(12, FACE, 8, 128)],
     )
     coef_other = swap_cores(coef)
+    sent, *ac_boxes = lax.optimization_barrier((sent, *ac_boxes))
     halo = among(sent)
     faces = (4, 5, 16, 128)
     coarse = (28, 32, 128)

time: 115 us -> 113 us (0.983)
  waiting for transfers between devices: 22.3 us -> 19.9 us
    ppermute x6, waiting for transfers between devices: 5.78 us -> 1.71 us  [around_chips(): lax.ppermute(x, 'bottom', [(i, (i + d) % 4) for i in range(4)])]
    ppermute x4, waiting for transfers between devices: 6.03 us -> 7.25 us  [to_slabs(): return lax.ppermute(x, ALL, pairs)]
  transfers between devices with their start and end apart: 29 -> 29, of which waited for: 18 -> 17; matrix products, arithmetic and copies ran while one was open for 0% -> 0% of each run, Pallas kernels for 7% -> 8%
where the time goes in v7:
time: 113 us; the launch traced here: 112 us
  starting transfers between devices  41.5 us (37%)
  Pallas kernels  23.7 us (21%)
  blocking collectives  20.8 us (18%)
  waiting for transfers between devices  19.9 us (18%)
  local copies, waits for them, and re-layouts  6.23 us (6%)
    pallas_call x11, Pallas kernels, run(): pl.pallas_call(kernel, out_shape=shapes[0] if single else shapes, in_spec...  23.7 us
    all_to_all x1, blocking collectives, among(): return lax.all_to_all(x, LB, split_axis=0, concat_axis=0, tiled=True)  20.8 us
    ppermute x14, starting transfers between devices, swap_cores(): return lax.ppermute(x, 'level', [(0, 1), (1, 0)])  15.8 us
    ppermute x4, starting transfers between devices, ring_sums(): return (lax.ppermute(x, ALL, beside), lax.ppermute(x, 'slab', across))  9.25 us
    ppermute x4, waiting for transfers between devices, to_slabs(): return lax.ppermute(x, ALL, pairs)  7.25 us
    ppermute x4, starting transfers between devices, to_slabs(): return lax.ppermute(x, ALL, pairs)  7.01 us
    unnamed x23, local copies, waits for them, and re-layouts  6.23 us
    ppermute x6, starting transfers between devices, around_chips(): lax.ppermute(x, 'bottom', [(i, (i + d) % 4) for i in range(4)])  4.87 us
  transfers between devices with their start and end apart: 29, of which 17 were waited for; matrix products, arithmetic and copies ran while one was open for 0% of the time, Pallas kernels for 8%

profile of v7, /device:TPU:1, one launch (start us, length us, event | category | flops | bytes accessed | tf_op | source)
XLA Modules:
  0.0 112.4 jit_solution(12638882781198515304)
XLA Ops:
  0.0 0.8 copy.13.bricks
  0.8 0.1 pad_add_fusion.meta
  0.8 1.0 copy-done
  1.9 1.0 copy-done.2
  2.9 1.0 copy-done.4
  4.0 1.7 %shard_map.46 = (f32[8,32,8,128]{3,2,1,0:T(8,128)S(1)}, f32[8,16,128]{2,1,0:T(8,128)S(1)}) custom-call(s32[2]{0:T(128)S(1)} %pad_add_fusion.meta, s32[16,8]{1,0:T(8,128)S(1)} %copy.13.bricks, f32[1,32,32,128]{3,2,1,0:T(8,128)S(1)} %copy-done, f32[1,32,32,128]{3,2,1,0:T(8,128)S(1)} %copy-done.2, f32[1,32,32,128]{3,2,1,0:T(8,128)S(1)} %copy-done.4), custom_call_target="tpu_custom_call" | custom-call | tf_op jit(solution)/shard_map/pallas_call | solution.py:21
  5.7 20.8 %all_to_all.10.recv = f32[8,32,8,128]{3,2,1,0:T(8,128)S(1)} all-to-all(f32[8,32,8,128]{3,2,1,0:T(8,128)S(1)} %get-tuple-element.49), channel_id=1, replica_groups=mesh['slab'=16,'level'=2,'bottom'=4] {'level','bottom'}, dimensions={0} | all-to-all | bytes 2097152 | tf_op jit(solution)/shard_map/all_to_all | solution.py:645
  26.4 0.7 shard_map.47
  27.1 3.1 %collective-permute-start = (f32[4,21,8,128]{3,2,1,0:T(8,128)S(1)}, f32[4,21,8,128]{3,2,1,0:T(8,128)S(1)}, u32[]{:S(2)}, u32[]{:S(2)}) collective-permute-start(f32[4,21,8,128]{3,2,1,0:T(8,128)S(1)} %shard_map.47), channel_id=1, source_target_pairs={{8,0},{9,1},{10,2},{11,3},{4,12},{5,13},{6,14},{7,15},{16,8},{17,9... | collective-permute-start | bytes 1032200 | tf_op jit(solution)/shard_map/ppermute | solution.py:623
  30.3 0.9 collective-permute-start.3
  31.2 1.5 %collective-permute-start.2 = (f32[8,16,128]{2,1,0:T(8,128)S(1)}, f32[8,16,128]{2,1,0:T(8,128)S(1)}, u32[]{:S(2)}, u32[]{:S(2)}) collective-permute-start(f32[8,16,128]{2,1,0:T(8,128)S(1)} %get-tuple-element.55.refs_0_), channel_id=1, source_target_pairs={{0,2},{1,3},{2,0},{3,1},{4,6},{5,7},{6,4},{7,5},{8,10},{9,11},{10,... | collective-permute-start | bytes 196616 | tf_op jit(solution)/shard_map/ppermute | solution.py:627
  32.7 1.7 %collective-permute-done.cross = f32[4,21,8,128]{3,2,1,0:T(8,128)S(1)} collective-permute-done((f32[4,21,8,128]{3,2,1,0:T(8,128)S(1)}, f32[4,21,8,128]{3,2,1,0:T(8,128)S(1)}, u32[]{:S(2)}, u32[]{:S(2)}) %collective-permute-start) | collective-permute-done | bytes 344096 | tf_op jit(solution)/shard_map/ppermute | solution.py:623
  34.4 1.3 %shard_map.48 = (f32[8,35,8,128]{3,2,1,0:T(8,128)S(1)}, f32[2,8,2,8,128]{4,3,2,1,0:T(8,128)S(1)}) custom-call(s32[2]{0:T(128)S(1)} %pad_add_fusion.meta, s32[16,8]{1,0:T(8,128)S(1)} %copy.13.bricks, f32[8,32,8,128]{3,2,1,0:T(8,128)S(1)} %all_to_all.10.recv, f32[4,21,8,128]{3,2,1,0:T(8,128)S(1)} %collective-permute-done.cross), custom_call_target="tpu_custom_call" | custom-call | tf_op jit(solution)/shard_map/pallas_call | solution.py:21
  35.8 1.0 copy-done.6
  36.8 1.3 %collective-permute-done.1.refs_1_ = f32[8,16,128]{2,1,0:T(8,128)S(1)} collective-permute-done((f32[8,16,128]{2,1,0:T(8,128)S(1)}, f32[8,16,128]{2,1,0:T(8,128)S(1)}, u32[]{:S(2)}, u32[]{:S(2)}) %collective-permute-start.1) | collective-permute-done | bytes 65568 | tf_op jit(solution)/shard_map/ppermute | solution.py:627
  38.1 4.6 %all-to-all-start.1 = ((f32[8,35,8,128]{3,2,1,0:T(8,128)}), f32[8,35,8,128]{3,2,1,0:T(8,128)S(1)}, u32[]{:S(2)}, u32[]{:S(2)}) async-start(f32[8,35,8,128]{3,2,1,0:T(8,128)} %copy-done.6), calls=%async_computation.1 | async-start | bytes 2293760 | tf_op jit(solution)/shard_map/all_to_all | solution.py:645
  42.7 0.2 collective-permute-start.4
  42.8 0.3 collective-permute-start.5
  43.2 0.2 collective-permute-start.6
  43.3 0.3 collective-permute-start.7
  43.7 0.2 collective-permute-done.4.refs_4_
  43.9 0.2 collective-permute-done.5.refs_5_
  44.1 0.3 collective-permute-done.6.refs_6_
  44.4 0.2 collective-permute-done.7.refs_7_
  44.6 0.7 shard_map.49
  45.3 1.3 %collective-permute-start.8 = (f32[4,5,16,128]{3,2,1,0:T(8,128)S(1)}, f32[4,5,16,128]{3,2,1,0:T(8,128)S(1)}, u32[]{:S(2)}, u32[]{:S(2)}) collective-permute-start(f32[4,5,16,128]{3,2,1,0:T(8,128)S(1)} %shard_map.49), channel_id=1, source_target_pairs={{0,8},{1,9},{2,10},{3,11},{12,4},{13,5},{14,6},{15,7},{8,16},{9,17... | collective-permute-start | bytes 491528 | tf_op jit(solution)/shard_map/ppermute | solution.py:623
  46.6 5.1 %collective-permute-done.8.refs_8_ = f32[4,5,16,128]{3,2,1,0:T(8,128)S(1)} collective-permute-done((f32[4,5,16,128]{3,2,1,0:T(8,128)S(1)}, f32[4,5,16,128]{3,2,1,0:T(8,128)S(1)}, u32[]{:S(2)}, u32[]{:S(2)}) %collective-permute-start.8) | collective-permute-done | bytes 163872 | tf_op jit(solution)/shard_map/ppermute | solution.py:623
  51.7 0.2 collective-permute-start.9
  51.9 0.3 collective-permute-start.10
  52.2 1.1 collective-permute-done.10.there
  53.3 0.6 copy-done.9
  53.9 0.7 copy-done.7
  54.6 4.1 %all-to-all-done.1.recv = f32[8,35,8,128]{3,2,1,0:T(8,128)S(1)} async-done(((f32[8,35,8,128]{3,2,1,0:T(8,128)}), f32[8,35,8,128]{3,2,1,0:T(8,128)S(1)}, u32[]{:S(2)}, u32[]{:S(2)}) %all-to-all-start.1) | async-done | bytes 1146912 | tf_op jit(solution)/shard_map/all_to_all | solution.py:645
  58.7 4.6 %shard_map.50 = (f32[8,16,128]{2,1,0:T(8,128)S(1)}, f32[26,40,256]{2,1,0:T(8,128)S(1)}, f32[26,40,256]{2,1,0:T(8,128)S(1)}, f32[26,40,256]{2,1,0:T(8,128)S(1)}, ...) custom-call(s32[2]{0:T(128)S(1)} %pad_add_fusion.meta, s32[16,8]{1,0:T(8,128)S(1)} %copy.13.bricks, ...), custom_call_target="tpu_custom_call" | custom-call | tf_op jit(solution)/shard_map/pallas_call | solution.py:21
  63.3 0.0 copy-start.8
  63.3 1.1 collective-permute-start.13
  64.4 1.4 %collective-permute-start.12 = (f32[8,16,128]{2,1,0:T(8,128)S(1)}, f32[8,16,128]{2,1,0:T(8,128)S(1)}, u32[]{:S(2)}, u32[]{:S(2)}) collective-permute-start(f32[8,16,128]{2,1,0:T(8,128)S(1)} %get-tuple-element.61.refs_0_), channel_id=1, source_target_pairs={{0,2},{1,3},{2,0},{3,1},{4,6},{5,7},{6,4},{7,5},{8,10},{9,11},{10,... | collective-permute-start | bytes 196616 | tf_op jit(solution)/shard_map/ppermute | solution.py:627
  65.8 0.8 collective-permute-start.14
  66.5 2.1 %collective-permute-start.17 = (f32[8,16,128]{2,1,0:T(8,128)S(1)}, f32[8,16,128]{2,1,0:T(8,128)S(1)}, u32[]{:S(2)}, u32[]{:S(2)}) collective-permute-start(f32[8,16,128]{2,1,0:T(8,128)S(1)} %collective-permute-done.13.refs_3_), channel_id=1, source_target_pairs={{0,4},{4,0},{1,5},{5,1},{2,6},{6,2},{3,7},{7,3},{8,12},{12,8},{9,1... | collective-permute-start | bytes 196616 | tf_op jit(solution)/shard_map/ppermute | solution.py:614
  68.6 0.4 collective-permute-done.12.refs_2_
  69.0 2.5 %collective-permute-start.16 = (f32[8,16,128]{2,1,0:T(8,128)S(1)}, f32[8,16,128]{2,1,0:T(8,128)S(1)}, u32[]{:S(2)}, u32[]{:S(2)}) collective-permute-start(f32[8,16,128]{2,1,0:T(8,128)S(1)} %collective-permute-done.12.refs_2_), channel_id=1, source_target_pairs={{0,4},{4,0},{1,5},{5,1},{2,6},{6,2},{3,7},{7,3},{8,12},{12,8},{9,1... | collective-permute-start | bytes 196616 | tf_op jit(solution)/shard_map/ppermute | solution.py:614
  71.5 0.7 collective-permute-start.15
  72.2 0.2 collective-permute-done.16.refs_6_
  72.4 0.7 collective-permute-done.15.refs_5_
  73.1 0.7 shard_map.51
  73.8 1.3 %collective-permute-start.18 = (f32[4,5,16,128]{3,2,1,0:T(8,128)S(1)}, f32[4,5,16,128]{3,2,1,0:T(8,128)S(1)}, u32[]{:S(2)}, u32[]{:S(2)}) collective-permute-start(f32[4,5,16,128]{3,2,1,0:T(8,128)S(1)} %shard_map.51), channel_id=1, source_target_pairs={{0,8},{1,9},{2,10},{3,11},{12,4},{13,5},{14,6},{15,7},{8,16},{9,17... | collective-permute-start | bytes 491528 | tf_op jit(solution)/shard_map/ppermute | solution.py:623
  75.1 3.0 %shard_map.52.refs_10_ = f32[16,16,128]{2,1,0:T(8,128)S(1)} custom-call(s32[2]{0:T(128)S(1)} %pad_add_fusion.meta, f32[2,8,2,8,128]{4,3,2,1,0:T(8,128)S(1)} %get-tuple-element.65.here, f32[2,8,2,8,128]{4,3,2,1,0:T(8,128)S(1)} %copy-done.10), custom_call_target="tpu_custom_call" | custom-call | tf_op jit(solution)/shard_map/pallas_call | solution.py:21
  78.1 1.3 %shard_map.53 = (f32[28,32,128]{2,1,0:T(8,128)S(1)}, f32[28,32,128]{2,1,0:T(8,128)S(1)}, f32[28,32,128]{2,1,0:T(8,128)S(1)}, f32[22,16,128]{2,1,0:T(8,128)S(1)}) custom-call(s32[2]{0:T(128)S(1)} %pad_add_fusion.meta, s32[16,8]{1,0:T(8,128)S(1)} %copy.13.bricks, f32[8,16,128]{2,1,0:T(8,128)S(1)} %get-tuple-element.55.refs_0_, ...), custom_call_target="tpu_custom_call" | custom-call | tf_op jit(solution)/shard_map/pallas_call | solution.py:21
  79.4 0.5 collective-permute-done.18.refs_8_
  79.9 2.3 %collective-permute-start.19 = (f32[4,5,16,128]{3,2,1,0:T(8,128)S(1)}, f32[4,5,16,128]{3,2,1,0:T(8,128)S(1)}, u32[]{:S(2)}, u32[]{:S(2)}) collective-permute-start(f32[4,5,16,128]{3,2,1,0:T(8,128)S(1)} %collective-permute-done.18.refs_8_), channel_id=1, source_target_pairs={{0,4},{4,0},{1,5},{5,1},{2,6},{6,2},{3,7},{7,3},{8,12},{12,8},{9,1... | collective-permute-start | bytes 491528 | tf_op jit(solution)/shard_map/ppermute | solution.py:614
  82.1 1.0 collective-permute-done.19.refs_9_
  83.2 2.4 %shard_map.54 = (f32[22,16,128]{2,1,0:T(8,128)S(1)}, f32[18,16,128]{2,1,0:T(8,128)S(1)}, f32[8,128]{1,0:T(8,128)S(1)}, f32[28,32,128]{2,1,0:T(8,128)S(1)}, f32[2...) custom-call(s32[2]{0:T(128)S(1)} %pad_add_fusion.meta, s32[16,8]{1,0:T(8,128)S(1)} %copy.13.bricks, ...), custom_call_target="tpu_custom_call" | custom-call | tf_op jit(solution)/shard_map/pallas_call | solution.py:21
  85.5 1.3 %collective-permute-start.20 = (f32[18,16,128]{2,1,0:T(8,128)S(1)}, f32[18,16,128]{2,1,0:T(8,128)S(1)}, u32[]{:S(2)}, u32[]{:S(2)}) collective-permute-start(f32[18,16,128]{2,1,0:T(8,128)S(1)} %get-tuple-element.80), channel_id=1, source_target_pairs={{0,8},{1,9},{2,10},{3,11},{12,4},{13,5},{14,6},{15,7},{8,16},{9,17... | collective-permute-start | bytes 442376 | tf_op jit(solution)/shard_map/ppermute | solution.py:623
  86.8 5.3 %collective-permute-start.22 = (f32[8,128]{1,0:T(8,128)S(1)}, f32[8,128]{1,0:T(8,128)S(1)}, u32[]{:S(2)}, u32[]{:S(2)}) collective-permute-start(f32[8,128]{1,0:T(8,128)S(1)} %get-tuple-element.79), channel_id=1, source_target_pairs={{0,16},{8,24},{16,0},{24,8},{32,48},{40,56},{48,32},{56,40},{64,80... | collective-permute-start | bytes 12296 | tf_op jit(solution)/shard_map/ppermute | solution.py:641
  92.1 0.4 collective-permute-start.21
  92.4 0.6 collective-permute-done.22
  93.1 1.5 %collective-permute-done.21 = f32[8,128]{1,0:T(8,128)S(1)} collective-permute-done((f32[8,128]{1,0:T(8,128)S(1)}, f32[8,128]{1,0:T(8,128)S(1)}, u32[]{:S(2)}, u32[]{:S(2)}) %collective-permute-start.21) | collective-permute-done | bytes 4128 | tf_op jit(solution)/shard_map/ppermute | solution.py:641
  94.5 4.5 %collective-permute-start.23 = (f32[8,128]{1,0:T(8,128)S(1)}, f32[8,128]{1,0:T(8,128)S(1)}, u32[]{:S(2)}, u32[]{:S(2)}) collective-permute-start(f32[8,128]{1,0:T(8,128)S(1)} %collective-permute-done.21), channel_id=1, source_target_pairs={{0,4},{4,0},{1,5},{5,1},{2,6},{6,2},{3,7},{7,3},{8,12},{12,8},{9,1... | collective-permute-start | bytes 12296 | tf_op jit(solution)/shard_map/ppermute | solution.py:614
  99.0 0.8 collective-permute-done.23
  99.9 2.8 %collective-permute-start.24 = (f32[8,128]{1,0:T(8,128)S(1)}, f32[8,128]{1,0:T(8,128)S(1)}, u32[]{:S(2)}, u32[]{:S(2)}) collective-permute-start(f32[8,128]{1,0:T(8,128)S(1)} %add_add_fusion.sum_0), channel_id=1, source_target_pairs={{0,32},{1,33},{2,34},{3,35},{4,100},{5,101},{6,102},{7,103},{8,40}... | collective-permute-start | bytes 12296 | tf_op jit(solution)/shard_map/ppermute | solution.py:641
  102.6 0.9 collective-permute-start.25
  103.5 1.5 %collective-permute-start.26 = (f32[8,128]{1,0:T(8,128)S(1)}, f32[8,128]{1,0:T(8,128)S(1)}, u32[]{:S(2)}, u32[]{:S(2)}) collective-permute-start(f32[8,128]{1,0:T(8,128)S(1)} %collective-permute-done.24.sum_1), channel_id=1, source_target_pairs={{0,4},{4,0},{1,5},{5,1},{2,6},{6,2},{3,7},{7,3},{8,12},{12,8},{9,1... | collective-permute-start | bytes 12296 | tf_op jit(solution)/shard_map/ppermute | solution.py:614
  105.0 2.9 %shard_map.55.es = f32[22,16,128]{2,1,0:T(8,128)S(1)} custom-call(s32[2]{0:T(128)S(1)} %pad_add_fusion.meta, f32[22,16,128]{2,1,0:T(8,128)S(1)} %get-tuple-element.83.rb, f32[18,16,128]{2,1,0:T(8,128)S(1)} %collective-permute-done.20.one, f32[18,16,128]{2,1,0:T(8,128)S(1)} %collective-permute-done.27.two), custom_call_target="tpu_custom_call" | custom-call | tf_op jit(solution)/shard_map/pallas_call | solution.py:21
  108.0 4.5 %shard_map.56 = f32[1,32,32,128]{3,2,1,0:T(8,128)} custom-call(s32[2]{0:T(128)S(1)} %pad_add_fusion.meta, s32[16,8]{1,0:T(8,128)S(1)} %copy.13.bricks, f32[8,128]{1,0:T(8,128)S(1)} %add_add_fusion.sum_0, f32[8,128]{1,0:T(8,128)S(1)} %collective-permute-done.24.sum_1, f32[8,128]{1,0:T(8,128)S(1)} %collective-permute-done.25.sum_2, ...), custom_call_target="tpu_custom_call" | custom-call | tf_op jit(solution)/shard_map/pallas_call | solution.py:21
  (31 shorter events, 0.1 us)
Async XLA Ops:
  0.8 1.0 copy-start
  1.9 1.0 copy-start.2
  2.9 1.0 copy-start.4
  27.1 7.3 %collective-permute-start = (f32[4,21,8,128]{3,2,1,0:T(8,128)S(1)}, f32[4,21,8,128]{3,2,1,0:T(8,128)S(1)}, u32[]{:S(2)}, u32[]{:S(2)}) collective-permute-start(f32[4,21,8,128]{3,2,1,0:T(8,128)S(1)} %shard_map.47), channel_id=1, source_target_pairs={{8,0},{9,1},{10,2},{11,3},{4,12},{5,13},{6,14},{7,15},{16,8},{17,9... | collective-permute-start | bytes 1032200 | tf_op jit(solution)/shard_map/ppermute | solution.py:623
  30.3 6.5 %collective-permute-start.3 = (f32[8,16,128]{2,1,0:T(8,128)S(1)}, f32[8,16,128]{2,1,0:T(8,128)S(1)}, u32[]{:S(2)}, u32[]{:S(2)}) collective-permute-start(f32[8,16,128]{2,1,0:T(8,128)S(1)} %get-tuple-element.55.refs_0_), channel_id=1, source_target_pairs={{0,3},{1,0},{2,1},{3,2},{4,7},{5,4},{6,5},{7,6},{8,11},{9,8},{10,9... | collective-permute-start | bytes 196616 | tf_op jit(solution)/shard_map/ppermute | solution.py:627
  31.2 5.6 %collective-permute-start.2 = (f32[8,16,128]{2,1,0:T(8,128)S(1)}, f32[8,16,128]{2,1,0:T(8,128)S(1)}, u32[]{:S(2)}, u32[]{:S(2)}) collective-permute-start(f32[8,16,128]{2,1,0:T(8,128)S(1)} %get-tuple-element.55.refs_0_), channel_id=1, source_target_pairs={{0,2},{1,3},{2,0},{3,1},{4,6},{5,7},{6,4},{7,5},{8,10},{9,11},{10,... | collective-permute-start | bytes 196616 | tf_op jit(solution)/shard_map/ppermute | solution.py:627
  32.7 5.4 %collective-permute-start.1 = (f32[8,16,128]{2,1,0:T(8,128)S(1)}, f32[8,16,128]{2,1,0:T(8,128)S(1)}, u32[]{:S(2)}, u32[]{:S(2)}) collective-permute-start(f32[8,16,128]{2,1,0:T(8,128)S(1)} %get-tuple-element.55.refs_0_), channel_id=1, source_target_pairs={{0,1},{1,2},{2,3},{3,0},{4,5},{5,6},{6,7},{7,4},{8,9},{9,10},{10,1... | collective-permute-start | bytes 196616 | tf_op jit(solution)/shard_map/ppermute | solution.py:627
  35.8 1.0 copy-start.6
  38.1 20.6 %copy-start.1 = (f32[1,32,32,128]{3,2,1,0:T(8,128)S(1)}, f32[1,32,32,128]{3,2,1,0:T(8,128)}, u32[]{:S(2)}) copy-start(f32[1,32,32,128]{3,2,1,0:T(8,128)} %u.3) | copy-start | bytes 1572868
  38.1 20.6 %copy-start.3 = (f32[1,32,32,128]{3,2,1,0:T(8,128)S(1)}, f32[1,32,32,128]{3,2,1,0:T(8,128)}, u32[]{:S(2)}) copy-start(f32[1,32,32,128]{3,2,1,0:T(8,128)} %f.3) | copy-start | bytes 1572868
  38.1 20.6 %copy-start.5 = (f32[1,32,32,128]{3,2,1,0:T(8,128)S(1)}, f32[1,32,32,128]{3,2,1,0:T(8,128)}, u32[]{:S(2)}) copy-start(f32[1,32,32,128]{3,2,1,0:T(8,128)} %a.3) | copy-start | bytes 1572868
  38.1 20.6 %all-to-all-start.1 = ((f32[8,35,8,128]{3,2,1,0:T(8,128)}), f32[8,35,8,128]{3,2,1,0:T(8,128)S(1)}, u32[]{:S(2)}, u32[]{:S(2)}) async-start(f32[8,35,8,128]{3,2,1,0:T(8,128)} %copy-done.6), calls=%async_computation.1 | async-start | bytes 2293760 | tf_op jit(solution)/shard_map/all_to_all | solution.py:645
  42.7 1.3 %collective-permute-start.4 = (f32[8,16,128]{2,1,0:T(8,128)S(1)}, f32[8,16,128]{2,1,0:T(8,128)S(1)}, u32[]{:S(2)}, u32[]{:S(2)}) collective-permute-start(f32[8,16,128]{2,1,0:T(8,128)S(1)} %get-tuple-element.55.refs_0_), channel_id=1, source_target_pairs={{0,4},{4,0},{1,5},{5,1},{2,6},{6,2},{3,7},{7,3},{8,12},{12,8},{9,1... | collective-permute-start | bytes 196616 | tf_op jit(solution)/shard_map/ppermute | solution.py:614
  42.8 1.3 %collective-permute-start.5 = (f32[8,16,128]{2,1,0:T(8,128)S(1)}, f32[8,16,128]{2,1,0:T(8,128)S(1)}, u32[]{:S(2)}, u32[]{:S(2)}) collective-permute-start(f32[8,16,128]{2,1,0:T(8,128)S(1)} %collective-permute-done.1.refs_1_), channel_id=1, source_target_pairs={{0,4},{4,0},{1,5},{5,1},{2,6},{6,2},{3,7},{7,3},{8,12},{12,8},{9,1... | collective-permute-start | bytes 196616 | tf_op jit(solution)/shard_map/ppermute | solution.py:614
  43.2 1.3 %collective-permute-start.6 = (f32[8,16,128]{2,1,0:T(8,128)S(1)}, f32[8,16,128]{2,1,0:T(8,128)S(1)}, u32[]{:S(2)}, u32[]{:S(2)}) collective-permute-start(f32[8,16,128]{2,1,0:T(8,128)S(1)} %collective-permute-done.2.refs_2_), channel_id=1, source_target_pairs={{0,4},{4,0},{1,5},{5,1},{2,6},{6,2},{3,7},{7,3},{8,12},{12,8},{9,1... | collective-permute-start | bytes 196616 | tf_op jit(solution)/shard_map/ppermute | solution.py:614
  43.3 1.3 %collective-permute-start.7 = (f32[8,16,128]{2,1,0:T(8,128)S(1)}, f32[8,16,128]{2,1,0:T(8,128)S(1)}, u32[]{:S(2)}, u32[]{:S(2)}) collective-permute-start(f32[8,16,128]{2,1,0:T(8,128)S(1)} %collective-permute-done.3.refs_3_), channel_id=1, source_target_pairs={{0,4},{4,0},{1,5},{5,1},{2,6},{6,2},{3,7},{7,3},{8,12},{12,8},{9,1... | collective-permute-start | bytes 196616 | tf_op jit(solution)/shard_map/ppermute | solution.py:614
  45.3 6.4 %collective-permute-start.8 = (f32[4,5,16,128]{3,2,1,0:T(8,128)S(1)}, f32[4,5,16,128]{3,2,1,0:T(8,128)S(1)}, u32[]{:S(2)}, u32[]{:S(2)}) collective-permute-start(f32[4,5,16,128]{3,2,1,0:T(8,128)S(1)} %shard_map.49), channel_id=1, source_target_pairs={{0,8},{1,9},{2,10},{3,11},{12,4},{13,5},{14,6},{15,7},{8,16},{9,17... | collective-permute-start | bytes 491528 | tf_op jit(solution)/shard_map/ppermute | solution.py:623
  51.7 2.2 %collective-permute-start.9 = (f32[4,5,16,128]{3,2,1,0:T(8,128)S(1)}, f32[4,5,16,128]{3,2,1,0:T(8,128)S(1)}, u32[]{:S(2)}, u32[]{:S(2)}) collective-permute-start(f32[4,5,16,128]{3,2,1,0:T(8,128)S(1)} %collective-permute-done.8.refs_8_), channel_id=1, source_target_pairs={{0,4},{4,0},{1,5},{5,1},{2,6},{6,2},{3,7},{7,3},{8,12},{12,8},{9,1... | collective-permute-start | bytes 491528 | tf_op jit(solution)/shard_map/ppermute | solution.py:614
  51.9 1.4 %collective-permute-start.10 = (f32[2,8,2,8,128]{4,3,2,1,0:T(8,128)S(1)}, f32[2,8,2,8,128]{4,3,2,1,0:T(8,128)S(1)}, u32[]{:S(2)}, u32[]{:S(2)}) collective-permute-start(f32[2,8,2,8,128]{4,3,2,1,0:T(8,128)S(1)} %get-tuple-element.65.here), channel_id=1, source_target_pairs={{0,4},{4,0},{1,5},{5,1},{2,6},{6,2},{3,7},{7,3},{8,12},{12,8},{9,1... | collective-permute-start | bytes 393224 | tf_op jit(solution)/shard_map/ppermute | solution.py:614
  53.3 0.7 copy-start.9
  53.9 0.7 copy-start.7
  58.7 16.4 %copy-start.10 = (f32[2,8,2,8,128]{4,3,2,1,0:T(8,128)S(1)}, f32[2,8,2,8,128]{4,3,2,1,0:T(8,128)}, u32[]{:S(2)}) copy-start(f32[2,8,2,8,128]{4,3,2,1,0:T(8,128)} %copy-done.9) | copy-start | bytes 393220
  63.3 14.8 %copy-start.8 = (f32[4,5,16,128]{3,2,1,0:T(8,128)S(1)}, f32[4,5,16,128]{3,2,1,0:T(8,128)}, u32[]{:S(2)}) copy-start(f32[4,5,16,128]{3,2,1,0:T(8,128)} %copy-done.7) | copy-start | bytes 491524
  63.3 3.2 %collective-permute-start.13 = (f32[8,16,128]{2,1,0:T(8,128)S(1)}, f32[8,16,128]{2,1,0:T(8,128)S(1)}, u32[]{:S(2)}, u32[]{:S(2)}) collective-permute-start(f32[8,16,128]{2,1,0:T(8,128)S(1)} %get-tuple-element.61.refs_0_), channel_id=1, source_target_pairs={{0,3},{1,0},{2,1},{3,2},{4,7},{5,4},{6,5},{7,6},{8,11},{9,8},{10,9... | collective-permute-start | bytes 196616 | tf_op jit(solution)/shard_map/ppermute | solution.py:627
  64.4 4.6 %collective-permute-start.12 = (f32[8,16,128]{2,1,0:T(8,128)S(1)}, f32[8,16,128]{2,1,0:T(8,128)S(1)}, u32[]{:S(2)}, u32[]{:S(2)}) collective-permute-start(f32[8,16,128]{2,1,0:T(8,128)S(1)} %get-tuple-element.61.refs_0_), channel_id=1, source_target_pairs={{0,2},{1,3},{2,0},{3,1},{4,6},{5,7},{6,4},{7,5},{8,10},{9,11},{10,... | collective-permute-start | bytes 196616 | tf_op jit(solution)/shard_map/ppermute | solution.py:627
  65.8 5.7 %collective-permute-start.11 = (f32[8,16,128]{2,1,0:T(8,128)S(1)}, f32[8,16,128]{2,1,0:T(8,128)S(1)}, u32[]{:S(2)}, u32[]{:S(2)}) collective-permute-start(f32[8,16,128]{2,1,0:T(8,128)S(1)} %get-tuple-element.61.refs_0_), channel_id=1, source_target_pairs={{0,1},{1,2},{2,3},{3,0},{4,5},{5,6},{6,7},{7,4},{8,9},{9,10},{10,1... | collective-permute-start | bytes 196616 | tf_op jit(solution)/shard_map/ppermute | solution.py:627
  65.8 6.4 %collective-permute-start.14 = (f32[8,16,128]{2,1,0:T(8,128)S(1)}, f32[8,16,128]{2,1,0:T(8,128)S(1)}, u32[]{:S(2)}, u32[]{:S(2)}) collective-permute-start(f32[8,16,128]{2,1,0:T(8,128)S(1)} %get-tuple-element.61.refs_0_), channel_id=1, source_target_pairs={{0,4},{4,0},{1,5},{5,1},{2,6},{6,2},{3,7},{7,3},{8,12},{12,8},{9,1... | collective-permute-start | bytes 196616 | tf_op jit(solution)/shard_map/ppermute | solution.py:614
  66.5 5.6 %collective-permute-start.17 = (f32[8,16,128]{2,1,0:T(8,128)S(1)}, f32[8,16,128]{2,1,0:T(8,128)S(1)}, u32[]{:S(2)}, u32[]{:S(2)}) collective-permute-start(f32[8,16,128]{2,1,0:T(8,128)S(1)} %collective-permute-done.13.refs_3_), channel_id=1, source_target_pairs={{0,4},{4,0},{1,5},{5,1},{2,6},{6,2},{3,7},{7,3},{8,12},{12,8},{9,1... | collective-permute-start | bytes 196616 | tf_op jit(solution)/shard_map/ppermute | solution.py:614
  69.0 3.4 %collective-permute-start.16 = (f32[8,16,128]{2,1,0:T(8,128)S(1)}, f32[8,16,128]{2,1,0:T(8,128)S(1)}, u32[]{:S(2)}, u32[]{:S(2)}) collective-permute-start(f32[8,16,128]{2,1,0:T(8,128)S(1)} %collective-permute-done.12.refs_2_), channel_id=1, source_target_pairs={{0,4},{4,0},{1,5},{5,1},{2,6},{6,2},{3,7},{7,3},{8,12},{12,8},{9,1... | collective-permute-start | bytes 196616 | tf_op jit(solution)/shard_map/ppermute | solution.py:614
  71.5 1.6 %collective-permute-start.15 = (f32[8,16,128]{2,1,0:T(8,128)S(1)}, f32[8,16,128]{2,1,0:T(8,128)S(1)}, u32[]{:S(2)}, u32[]{:S(2)}) collective-permute-start(f32[8,16,128]{2,1,0:T(8,128)S(1)} %collective-permute-done.11.refs_1_), channel_id=1, source_target_pairs={{0,4},{4,0},{1,5},{5,1},{2,6},{6,2},{3,7},{7,3},{8,12},{12,8},{9,1... | collective-permute-start | bytes 196616 | tf_op jit(solution)/shard_map/ppermute | solution.py:614
  73.8 6.1 %collective-permute-start.18 = (f32[4,5,16,128]{3,2,1,0:T(8,128)S(1)}, f32[4,5,16,128]{3,2,1,0:T(8,128)S(1)}, u32[]{:S(2)}, u32[]{:S(2)}) collective-permute-start(f32[4,5,16,128]{3,2,1,0:T(8,128)S(1)} %shard_map.51), channel_id=1, source_target_pairs={{0,8},{1,9},{2,10},{3,11},{12,4},{13,5},{14,6},{15,7},{8,16},{9,17... | collective-permute-start | bytes 491528 | tf_op jit(solution)/shard_map/ppermute | solution.py:623
  79.9 3.3 %collective-permute-start.19 = (f32[4,5,16,128]{3,2,1,0:T(8,128)S(1)}, f32[4,5,16,128]{3,2,1,0:T(8,128)S(1)}, u32[]{:S(2)}, u32[]{:S(2)}) collective-permute-start(f32[4,5,16,128]{3,2,1,0:T(8,128)S(1)} %collective-permute-done.18.refs_8_), channel_id=1, source_target_pairs={{0,4},{4,0},{1,5},{5,1},{2,6},{6,2},{3,7},{7,3},{8,12},{12,8},{9,1... | collective-permute-start | bytes 491528 | tf_op jit(solution)/shard_map/ppermute | solution.py:614
  85.5 9.0 %collective-permute-start.20 = (f32[18,16,128]{2,1,0:T(8,128)S(1)}, f32[18,16,128]{2,1,0:T(8,128)S(1)}, u32[]{:S(2)}, u32[]{:S(2)}) collective-permute-start(f32[18,16,128]{2,1,0:T(8,128)S(1)} %get-tuple-element.80), channel_id=1, source_target_pairs={{0,8},{1,9},{2,10},{3,11},{12,4},{13,5},{14,6},{15,7},{8,16},{9,17... | collective-permute-start | bytes 442376 | tf_op jit(solution)/shard_map/ppermute | solution.py:623
  86.8 6.3 %collective-permute-start.22 = (f32[8,128]{1,0:T(8,128)S(1)}, f32[8,128]{1,0:T(8,128)S(1)}, u32[]{:S(2)}, u32[]{:S(2)}) collective-permute-start(f32[8,128]{1,0:T(8,128)S(1)} %get-tuple-element.79), channel_id=1, source_target_pairs={{0,16},{8,24},{16,0},{24,8},{32,48},{40,56},{48,32},{56,40},{64,80... | collective-permute-start | bytes 12296 | tf_op jit(solution)/shard_map/ppermute | solution.py:641
  92.1 2.5 %collective-permute-start.21 = (f32[8,128]{1,0:T(8,128)S(1)}, f32[8,128]{1,0:T(8,128)S(1)}, u32[]{:S(2)}, u32[]{:S(2)}) collective-permute-start(f32[8,128]{1,0:T(8,128)S(1)} %get-tuple-element.79), channel_id=1, source_target_pairs={{0,8},{1,9},{2,10},{3,11},{4,28},{5,29},{6,30},{7,31},{8,16},{9,17... | collective-permute-start | bytes 12296 | tf_op jit(solution)/shard_map/ppermute | solution.py:641
  94.5 5.3 %collective-permute-start.23 = (f32[8,128]{1,0:T(8,128)S(1)}, f32[8,128]{1,0:T(8,128)S(1)}, u32[]{:S(2)}, u32[]{:S(2)}) collective-permute-start(f32[8,128]{1,0:T(8,128)S(1)} %collective-permute-done.21), channel_id=1, source_target_pairs={{0,4},{4,0},{1,5},{5,1},{2,6},{6,2},{3,7},{7,3},{8,12},{12,8},{9,1... | collective-permute-start | bytes 12296 | tf_op jit(solution)/shard_map/ppermute | solution.py:614
  99.0 6.0 %collective-permute-start.27 = (f32[18,16,128]{2,1,0:T(8,128)S(1)}, f32[18,16,128]{2,1,0:T(8,128)S(1)}, u32[]{:S(2)}, u32[]{:S(2)}) collective-permute-start(f32[18,16,128]{2,1,0:T(8,128)S(1)} %collective-permute-done.20.one), channel_id=1, source_target_pairs={{0,4},{4,0},{1,5},{5,1},{2,6},{6,2},{3,7},{7,3},{8,12},{12,8},{9,1... | collective-permute-start | bytes 442376 | tf_op jit(solution)/shard_map/ppermute | solution.py:614
  99.9 3.6 %collective-permute-start.24 = (f32[8,128]{1,0:T(8,128)S(1)}, f32[8,128]{1,0:T(8,128)S(1)}, u32[]{:S(2)}, u32[]{:S(2)}) collective-permute-start(f32[8,128]{1,0:T(8,128)S(1)} %add_add_fusion.sum_0), channel_id=1, source_target_pairs={{0,32},{1,33},{2,34},{3,35},{4,100},{5,101},{6,102},{7,103},{8,40}... | collective-permute-start | bytes 12296 | tf_op jit(solution)/shard_map/ppermute | solution.py:641
  102.6 5.3 %collective-permute-start.25 = (f32[8,128]{1,0:T(8,128)S(1)}, f32[8,128]{1,0:T(8,128)S(1)}, u32[]{:S(2)}, u32[]{:S(2)}) collective-permute-start(f32[8,128]{1,0:T(8,128)S(1)} %add_add_fusion.sum_0), channel_id=1, source_target_pairs={{0,64},{8,72},{16,80},{24,88},{32,96},{40,104},{48,112},{56,120},{... | collective-permute-start | bytes 12296 | tf_op jit(solution)/shard_map/ppermute | solution.py:641
  103.5 4.5 %collective-permute-start.26 = (f32[8,128]{1,0:T(8,128)S(1)}, f32[8,128]{1,0:T(8,128)S(1)}, u32[]{:S(2)}, u32[]{:S(2)}) collective-permute-start(f32[8,128]{1,0:T(8,128)S(1)} %collective-permute-done.24.sum_1), channel_id=1, source_target_pairs={{0,4},{4,0},{1,5},{5,1},{2,6},{6,2},{3,7},{7,3},{8,12},{12,8},{9,1... | collective-permute-start | bytes 12296 | tf_op jit(solution)/shard_map/ppermute | solution.py:614

commit v8 on v7

--- a/solution.py
+++ b/solution.py
@@ -421,11 +421,14 @@
         total = 0.25 * around(e_b, k, True, mask, 2)
         resid[n] = r_r[k] + total - (a_r[k] + 1.5) * e_r[k]
     rb[...] = to_bottom(resid, small, 0) + ab[...]
-    rb_send[...] = rb[pl.ds(jnp.where(me < 4, 1, 3), 18)]
+    rb_send[0:18] = rb[pl.ds(jnp.where(me < 4, 1, 3), 18)]
     total = jnp.zeros((16, 128), F32)
     for i in range(16):
         total = total + rb[3 + i] * weights[i]
-    part[...] = total[0:8] + total[8:16]
+    total = total[0:8] + total[8:16]
+    part[...] = total
+    rb_send[18, 0:8] = total
+    rb_send[18, 8:16] = total
 
 
 def bottom_kernel(meta, rb, one, two, es, e_r, e_b, g_r, g_b, i_r, i_b, low, high):
@@ -614,11 +617,11 @@
     return lax.ppermute(x, "level", [(0, 1), (1, 0)])
 
 
-def to_slabs(x, up_first):
+def to_slabs(x, up_first, wrap=False):
     pairs = []
-    for s in range(SLABS - 1):
+    for s in range(SLABS if wrap else SLABS - 1):
         for m in range(8):
-            low, high = s * 8 + m, (s + 1) * 8 + m
+            low, high = s * 8 + m, (s + 1) % SLABS * 8 + m
             pairs.append((low, high) if (m < 4) == up_first else (high, low))
     return lax.ppermute(x, ALL, pairs)
 
@@ -631,13 +634,9 @@
     return boxes + [swap_cores(box) for box in boxes]
 
 
-def ring_sums(x, stride):
-    def moved(s, step):
-        at = s // stride % 4
-        return s + ((at + step) % 4 - at) * stride
-
-    beside = [(8 * s + m, 8 * moved(s, 1 if m < 4 else 3) + m) for s in range(SLABS) for m in range(8)]
-    across = [(s, moved(s, 2)) for s in range(SLABS)]
+def fours_apart(x):
+    beside = [(8 * s + m, 8 * ((s + (4 if m < 4 else 12)) % SLABS) + m) for s in range(SLABS) for m in range(8)]
+    across = [(s, (s + 8) % SLABS) for s in range(SLABS)]
     return lax.ppermute(x, ALL, beside), lax.ppermute(x, "slab", across)
 
 
@@ -689,21 +688,21 @@
     )
     cross, weights, ca_r, ci_r, ci_b, ab = lax.optimization_barrier((cross, weights, ca_r, ci_r, ci_b, ab))
     rb, rb_send, part, ec_b, r_r, r_b = run(
-        coarse_down_kernel, [(22, 16, 128), (18, 16, 128), (8, 128)] + [coarse] * 3, smem,
+        coarse_down_kernel, [(22, 16, 128), (19, 16, 128), (8, 128)] + [coarse] * 3, smem,
         boxes + [cross, swap_cores(cross), weights, ca_r, ci_r, ci_b, ab],
         held + [coarse, (22, 32, 128), (352, 128)],
     )
-    cross = to_slabs(rb_send, True)
-    near, far = ring_sums(part, 1)
-    cross, near, far = lax.optimization_barrier((cross, near, far))
+    cross = to_slabs(rb_send, True, wrap=True)
+    far = lax.ppermute(part, "slab", [(s, (s - 2) % SLABS) for s in range(SLABS)])
+    cross, far = lax.optimization_barrier((cross, far))
     other = swap_cores(cross)
-    part = (part + swap_cores(near)) + (near + far)
-    near, far = ring_sums(part, 4)
+    part = (part + far) + (cross[18, 0:8] + other[18, 0:8])
+    near, far = fours_apart(part)
     sums = [part, near, far, swap_cores(near)]
     bottom = (28, 16, 128)
     es = run(
         bottom_kernel, [(22, 16, 128)], [meta], [rb, cross, other],
-        [bottom] * 6 + [(18, 16, 128)] * 2,
+        [bottom] * 6 + [(19, 16, 128)] * 2,
     )
     return run(
         up_kernel, [(1, 32, 32, 128)], smem,

time: 113 us -> 111 us (0.982)
  starting transfers between devices: 41.5 us -> 38.7 us
    ppermute x4, starting transfers between devices: 7.01 us -> 10.8 us  [to_slabs(): return lax.ppermute(x, ALL, pairs)]
    ppermute x14 -> x13, starting transfers between devices: 15.8 us -> 12.3 us  [swap_cores(): return lax.ppermute(x, 'level', [(0, 1), (1, 0)])]
    ppermute x4 -> x3, starting transfers between devices: 9.25 us -> 6.18 us  [the longest x2 4.37 us: fours_apart(): return (lax.ppermute(x, ALL, beside), lax.ppermute(x, 'slab', across))]
    ppermute x4 -> x3, waiting for transfers between devices: 2.11 us -> 3 us  [the longest x1 2.25 us: body(): lax.ppermute(part, 'slab', [(s, (s - 2) % SLABS) for s in range(SLABS)])]
    ppermute x14 -> x13, waiting for transfers between devices: 4.74 us -> 4.93 us  [swap_cores(): return lax.ppermute(x, 'level', [(0, 1), (1, 0)])]
  transfers between devices with their start and end apart: 29 -> 27, of which waited for: 17 -> 17; matrix products, arithmetic and copies ran while one was open for 0% -> 0% of each run, Pallas kernels for 8% -> 8%
where the time goes in v8:
time: 111 us
  starting transfers between devices  38.7 us (35%)
  Pallas kernels  23.8 us (21%)
  waiting for transfers between devices  21 us (19%)
  blocking collectives  20.8 us (19%)
  local copies, waits for them, and re-layouts  6.23 us (6%)
    pallas_call x11, Pallas kernels, run(): pl.pallas_call(kernel, out_shape=shapes[0] if single else shapes, in_spec...  23.8 us
    all_to_all x1, blocking collectives, among(): return lax.all_to_all(x, LB, split_axis=0, concat_axis=0, tiled=True)  20.8 us
    ppermute x13, starting transfers between devices, swap_cores(): return lax.ppermute(x, 'level', [(0, 1), (1, 0)])  12.3 us
    ppermute x4, starting transfers between devices, to_slabs(): return lax.ppermute(x, ALL, pairs)  10.8 us
    ppermute x4, waiting for transfers between devices, to_slabs(): return lax.ppermute(x, ALL, pairs)  7.25 us
    unnamed x23, local copies, waits for them, and re-layouts  6.23 us
    ppermute x13, waiting for transfers between devices, swap_cores(): return lax.ppermute(x, 'level', [(0, 1), (1, 0)])  4.93 us
    ppermute x6, starting transfers between devices, around_chips(): lax.ppermute(x, 'bottom', [(i, (i + d) % 4) for i in range(4)])  4.87 us
  transfers between devices with their start and end apart: 27, of which 17 were waited for; matrix products, arithmetic and copies ran while one was open for 0% of the time, Pallas kernels for 8%

profile of v8, /device:TPU:1, one launch (start us, length us, event | category | flops | bytes accessed | tf_op | source)
XLA Modules:
  0.0 110.8 jit_solution(7635257026628577583)
XLA Ops:
  0.0 0.8 copy.13.bricks
  0.8 0.1 pad_add_fusion.meta
  0.8 1.0 copy-done
  1.9 1.0 copy-done.2
  2.9 1.0 copy-done.4
  4.0 1.7 %shard_map.46 = (f32[8,32,8,128]{3,2,1,0:T(8,128)S(1)}, f32[8,16,128]{2,1,0:T(8,128)S(1)}) custom-call(s32[2]{0:T(128)S(1)} %pad_add_fusion.meta, s32[16,8]{1,0:T(8,128)S(1)} %copy.13.bricks, f32[1,32,32,128]{3,2,1,0:T(8,128)S(1)} %copy-done, f32[1,32,32,128]{3,2,1,0:T(8,128)S(1)} %copy-done.2, f32[1,32,32,128]{3,2,1,0:T(8,128)S(1)} %copy-done.4), custom_call_target="tpu_custom_call" | custom-call | tf_op jit(solution)/shard_map/pallas_call | solution.py:21
  5.7 20.8 %all_to_all.10.recv = f32[8,32,8,128]{3,2,1,0:T(8,128)S(1)} all-to-all(f32[8,32,8,128]{3,2,1,0:T(8,128)S(1)} %get-tuple-element.48), channel_id=1, replica_groups=mesh['slab'=16,'level'=2,'bottom'=4] {'level','bottom'}, dimensions={0} | all-to-all | bytes 2097152 | tf_op jit(solution)/shard_map/all_to_all | solution.py:644
  26.4 0.7 shard_map.47
  27.1 3.1 %collective-permute-start = (f32[4,21,8,128]{3,2,1,0:T(8,128)S(1)}, f32[4,21,8,128]{3,2,1,0:T(8,128)S(1)}, u32[]{:S(2)}, u32[]{:S(2)}) collective-permute-start(f32[4,21,8,128]{3,2,1,0:T(8,128)S(1)} %shard_map.47), channel_id=1, source_target_pairs={{8,0},{9,1},{10,2},{11,3},{4,12},{5,13},{6,14},{7,15},{16,8},{17,9... | collective-permute-start | bytes 1032200 | tf_op jit(solution)/shard_map/ppermute | solution.py:626
  30.3 0.9 collective-permute-start.3
  31.2 1.5 %collective-permute-start.2 = (f32[8,16,128]{2,1,0:T(8,128)S(1)}, f32[8,16,128]{2,1,0:T(8,128)S(1)}, u32[]{:S(2)}, u32[]{:S(2)}) collective-permute-start(f32[8,16,128]{2,1,0:T(8,128)S(1)} %get-tuple-element.54.refs_0_), channel_id=1, source_target_pairs={{0,2},{1,3},{2,0},{3,1},{4,6},{5,7},{6,4},{7,5},{8,10},{9,11},{10,... | collective-permute-start | bytes 196616 | tf_op jit(solution)/shard_map/ppermute | solution.py:630
  32.7 1.7 %collective-permute-done.cross = f32[4,21,8,128]{3,2,1,0:T(8,128)S(1)} collective-permute-done((f32[4,21,8,128]{3,2,1,0:T(8,128)S(1)}, f32[4,21,8,128]{3,2,1,0:T(8,128)S(1)}, u32[]{:S(2)}, u32[]{:S(2)}) %collective-permute-start) | collective-permute-done | bytes 344096 | tf_op jit(solution)/shard_map/ppermute | solution.py:626
  34.4 1.3 %shard_map.48 = (f32[8,35,8,128]{3,2,1,0:T(8,128)S(1)}, f32[2,8,2,8,128]{4,3,2,1,0:T(8,128)S(1)}) custom-call(s32[2]{0:T(128)S(1)} %pad_add_fusion.meta, s32[16,8]{1,0:T(8,128)S(1)} %copy.13.bricks, f32[8,32,8,128]{3,2,1,0:T(8,128)S(1)} %all_to_all.10.recv, f32[4,21,8,128]{3,2,1,0:T(8,128)S(1)} %collective-permute-done.cross), custom_call_target="tpu_custom_call" | custom-call | tf_op jit(solution)/shard_map/pallas_call | solution.py:21
  35.8 1.0 copy-done.6
  36.8 0.0 collective-permute-done.3.refs_3_
  36.8 1.3 %collective-permute-done.1.refs_1_ = f32[8,16,128]{2,1,0:T(8,128)S(1)} collective-permute-done((f32[8,16,128]{2,1,0:T(8,128)S(1)}, f32[8,16,128]{2,1,0:T(8,128)S(1)}, u32[]{:S(2)}, u32[]{:S(2)}) %collective-permute-start.1) | collective-permute-done | bytes 65568 | tf_op jit(solution)/shard_map/ppermute | solution.py:630
  38.1 4.6 %all-to-all-start.1 = ((f32[8,35,8,128]{3,2,1,0:T(8,128)}), f32[8,35,8,128]{3,2,1,0:T(8,128)S(1)}, u32[]{:S(2)}, u32[]{:S(2)}) async-start(f32[8,35,8,128]{3,2,1,0:T(8,128)} %copy-done.6), calls=%async_computation.1 | async-start | bytes 2293760 | tf_op jit(solution)/shard_map/all_to_all | solution.py:644
  42.7 0.2 collective-permute-start.4
  42.8 0.3 collective-permute-start.5
  43.2 0.2 collective-permute-start.6
  43.4 0.3 collective-permute-start.7
  43.7 0.2 collective-permute-done.4.refs_4_
  43.9 0.2 collective-permute-done.5.refs_5_
  44.1 0.3 collective-permute-done.6.refs_6_
  44.4 0.2 collective-permute-done.7.refs_7_
  44.6 0.7 shard_map.49
  45.3 1.3 %collective-permute-start.8 = (f32[4,5,16,128]{3,2,1,0:T(8,128)S(1)}, f32[4,5,16,128]{3,2,1,0:T(8,128)S(1)}, u32[]{:S(2)}, u32[]{:S(2)}) collective-permute-start(f32[4,5,16,128]{3,2,1,0:T(8,128)S(1)} %shard_map.49), channel_id=1, source_target_pairs={{0,8},{1,9},{2,10},{3,11},{12,4},{13,5},{14,6},{15,7},{8,16},{9,17... | collective-permute-start | bytes 491528 | tf_op jit(solution)/shard_map/ppermute | solution.py:626
  46.6 5.1 %collective-permute-done.8.refs_8_ = f32[4,5,16,128]{3,2,1,0:T(8,128)S(1)} collective-permute-done((f32[4,5,16,128]{3,2,1,0:T(8,128)S(1)}, f32[4,5,16,128]{3,2,1,0:T(8,128)S(1)}, u32[]{:S(2)}, u32[]{:S(2)}) %collective-permute-start.8) | collective-permute-done | bytes 163872 | tf_op jit(solution)/shard_map/ppermute | solution.py:626
  51.7 0.2 collective-permute-start.9
  51.9 0.3 collective-permute-start.10
  52.2 1.1 collective-permute-done.10.there
  53.3 0.6 copy-done.9
  53.9 0.0 collective-permute-done.9.refs_9_
  53.9 0.7 copy-done.7
  54.6 4.1 %all-to-all-done.1.recv = f32[8,35,8,128]{3,2,1,0:T(8,128)S(1)} async-done(((f32[8,35,8,128]{3,2,1,0:T(8,128)}), f32[8,35,8,128]{3,2,1,0:T(8,128)S(1)}, u32[]{:S(2)}, u32[]{:S(2)}) %all-to-all-start.1) | async-done | bytes 1146912 | tf_op jit(solution)/shard_map/all_to_all | solution.py:644
  58.7 4.6 %shard_map.50 = (f32[8,16,128]{2,1,0:T(8,128)S(1)}, f32[26,40,256]{2,1,0:T(8,128)S(1)}, f32[26,40,256]{2,1,0:T(8,128)S(1)}, f32[26,40,256]{2,1,0:T(8,128)S(1)}, ...) custom-call(s32[2]{0:T(128)S(1)} %pad_add_fusion.meta, s32[16,8]{1,0:T(8,128)S(1)} %copy.13.bricks, ...), custom_call_target="tpu_custom_call" | custom-call | tf_op jit(solution)/shard_map/pallas_call | solution.py:21
  63.3 0.0 copy-start.8
  63.3 1.1 collective-permute-start.13
  64.4 1.4 %collective-permute-start.12 = (f32[8,16,128]{2,1,0:T(8,128)S(1)}, f32[8,16,128]{2,1,0:T(8,128)S(1)}, u32[]{:S(2)}, u32[]{:S(2)}) collective-permute-start(f32[8,16,128]{2,1,0:T(8,128)S(1)} %get-tuple-element.60.refs_0_), channel_id=1, source_target_pairs={{0,2},{1,3},{2,0},{3,1},{4,6},{5,7},{6,4},{7,5},{8,10},{9,11},{10,... | collective-permute-start | bytes 196616 | tf_op jit(solution)/shard_map/ppermute | solution.py:630
  65.8 0.8 collective-permute-start.14
  66.6 2.1 %collective-permute-start.17 = (f32[8,16,128]{2,1,0:T(8,128)S(1)}, f32[8,16,128]{2,1,0:T(8,128)S(1)}, u32[]{:S(2)}, u32[]{:S(2)}) collective-permute-start(f32[8,16,128]{2,1,0:T(8,128)S(1)} %collective-permute-done.13.refs_3_), channel_id=1, source_target_pairs={{0,4},{4,0},{1,5},{5,1},{2,6},{6,2},{3,7},{7,3},{8,12},{12,8},{9,1... | collective-permute-start | bytes 196616 | tf_op jit(solution)/shard_map/ppermute | solution.py:617
  68.6 0.4 collective-permute-done.12.refs_2_
  69.0 2.5 %collective-permute-start.16 = (f32[8,16,128]{2,1,0:T(8,128)S(1)}, f32[8,16,128]{2,1,0:T(8,128)S(1)}, u32[]{:S(2)}, u32[]{:S(2)}) collective-permute-start(f32[8,16,128]{2,1,0:T(8,128)S(1)} %collective-permute-done.12.refs_2_), channel_id=1, source_target_pairs={{0,4},{4,0},{1,5},{5,1},{2,6},{6,2},{3,7},{7,3},{8,12},{12,8},{9,1... | collective-permute-start | bytes 196616 | tf_op jit(solution)/shard_map/ppermute | solution.py:617
  71.5 0.7 collective-permute-start.15
  72.2 0.2 collective-permute-done.16.refs_6_
  72.4 0.7 collective-permute-done.15.refs_5_
  73.1 0.7 shard_map.51
  73.8 1.3 %collective-permute-start.18 = (f32[4,5,16,128]{3,2,1,0:T(8,128)S(1)}, f32[4,5,16,128]{3,2,1,0:T(8,128)S(1)}, u32[]{:S(2)}, u32[]{:S(2)}) collective-permute-start(f32[4,5,16,128]{3,2,1,0:T(8,128)S(1)} %shard_map.51), channel_id=1, source_target_pairs={{0,8},{1,9},{2,10},{3,11},{12,4},{13,5},{14,6},{15,7},{8,16},{9,17... | collective-permute-start | bytes 491528 | tf_op jit(solution)/shard_map/ppermute | solution.py:626
  75.1 3.0 %shard_map.52.refs_10_ = f32[16,16,128]{2,1,0:T(8,128)S(1)} custom-call(s32[2]{0:T(128)S(1)} %pad_add_fusion.meta, f32[2,8,2,8,128]{4,3,2,1,0:T(8,128)S(1)} %get-tuple-element.64.here, f32[2,8,2,8,128]{4,3,2,1,0:T(8,128)S(1)} %copy-done.10), custom_call_target="tpu_custom_call" | custom-call | tf_op jit(solution)/shard_map/pallas_call | solution.py:21
  78.1 1.3 %shard_map.53 = (f32[28,32,128]{2,1,0:T(8,128)S(1)}, f32[28,32,128]{2,1,0:T(8,128)S(1)}, f32[28,32,128]{2,1,0:T(8,128)S(1)}, f32[22,16,128]{2,1,0:T(8,128)S(1)}) custom-call(s32[2]{0:T(128)S(1)} %pad_add_fusion.meta, s32[16,8]{1,0:T(8,128)S(1)} %copy.13.bricks, f32[8,16,128]{2,1,0:T(8,128)S(1)} %get-tuple-element.54.refs_0_, ...), custom_call_target="tpu_custom_call" | custom-call | tf_op jit(solution)/shard_map/pallas_call | solution.py:21
  79.4 0.5 collective-permute-done.18.refs_8_
  79.9 2.3 %collective-permute-start.19 = (f32[4,5,16,128]{3,2,1,0:T(8,128)S(1)}, f32[4,5,16,128]{3,2,1,0:T(8,128)S(1)}, u32[]{:S(2)}, u32[]{:S(2)}) collective-permute-start(f32[4,5,16,128]{3,2,1,0:T(8,128)S(1)} %collective-permute-done.18.refs_8_), channel_id=1, source_target_pairs={{0,4},{4,0},{1,5},{5,1},{2,6},{6,2},{3,7},{7,3},{8,12},{12,8},{9,1... | collective-permute-start | bytes 491528 | tf_op jit(solution)/shard_map/ppermute | solution.py:617
  82.2 1.0 collective-permute-done.19.refs_9_
  83.2 2.4 %shard_map.54 = (f32[22,16,128]{2,1,0:T(8,128)S(1)}, f32[19,16,128]{2,1,0:T(8,128)S(1)}, f32[8,128]{1,0:T(8,128)S(1)}, f32[28,32,128]{2,1,0:T(8,128)S(1)}, f32[2...) custom-call(s32[2]{0:T(128)S(1)} %pad_add_fusion.meta, s32[16,8]{1,0:T(8,128)S(1)} %copy.13.bricks, ...), custom_call_target="tpu_custom_call" | custom-call | tf_op jit(solution)/shard_map/pallas_call | solution.py:21
  85.6 5.1 %collective-permute-start.20 = (f32[19,16,128]{2,1,0:T(8,128)S(1)}, f32[19,16,128]{2,1,0:T(8,128)S(1)}, u32[]{:S(2)}, u32[]{:S(2)}) collective-permute-start(f32[19,16,128]{2,1,0:T(8,128)S(1)} %get-tuple-element.79), channel_id=1, source_target_pairs={{0,8},{1,9},{2,10},{3,11},{12,4},{13,5},{14,6},{15,7},{8,16},{9,17... | collective-permute-start | bytes 466952 | tf_op jit(solution)/shard_map/ppermute | solution.py:626
  90.7 1.8 %collective-permute-start.21 = (f32[8,128]{1,0:T(8,128)S(1)}, f32[8,128]{1,0:T(8,128)S(1)}, u32[]{:S(2)}, u32[]{:S(2)}) collective-permute-start(f32[8,128]{1,0:T(8,128)S(1)} %get-tuple-element.78), channel_id=1, source_target_pairs={{0,112},{8,120},{16,0},{24,8},{32,16},{40,24},{48,32},{56,40},{64,... | collective-permute-start | bytes 12296 | tf_op jit(solution)/shard_map/ppermute | solution.py:696
  92.5 2.2 %collective-permute-done.21 = f32[8,128]{1,0:T(8,128)S(1)} collective-permute-done((f32[8,128]{1,0:T(8,128)S(1)}, f32[8,128]{1,0:T(8,128)S(1)}, u32[]{:S(2)}, u32[]{:S(2)}) %collective-permute-start.21) | collective-permute-done | bytes 4128 | tf_op jit(solution)/shard_map/ppermute | solution.py:696
  94.7 1.0 collective-permute-start.22
  95.7 1.0 collective-permute-done.22.two
  96.7 4.4 %collective-permute-start.23 = (f32[8,128]{1,0:T(8,128)S(1)}, f32[8,128]{1,0:T(8,128)S(1)}, u32[]{:S(2)}, u32[]{:S(2)}) collective-permute-start(f32[8,128]{1,0:T(8,128)S(1)} %fusion.1.sum_0), channel_id=1, source_target_pairs={{0,32},{1,33},{2,34},{3,35},{4,100},{5,101},{6,102},{7,103},{8,40}... | collective-permute-start | bytes 12296 | tf_op jit(solution)/shard_map/ppermute | solution.py:640
  101.1 0.8 collective-permute-done.23.sum_1
  101.9 1.5 %collective-permute-start.25 = (f32[8,128]{1,0:T(8,128)S(1)}, f32[8,128]{1,0:T(8,128)S(1)}, u32[]{:S(2)}, u32[]{:S(2)}) collective-permute-start(f32[8,128]{1,0:T(8,128)S(1)} %collective-permute-done.23.sum_1), channel_id=1, source_target_pairs={{0,4},{4,0},{1,5},{5,1},{2,6},{6,2},{3,7},{7,3},{8,12},{12,8},{9,1... | collective-permute-start | bytes 12296 | tf_op jit(solution)/shard_map/ppermute | solution.py:617
  103.3 2.9 %shard_map.55.es = f32[22,16,128]{2,1,0:T(8,128)S(1)} custom-call(s32[2]{0:T(128)S(1)} %pad_add_fusion.meta, f32[22,16,128]{2,1,0:T(8,128)S(1)} %get-tuple-element.82.rb, f32[19,16,128]{2,1,0:T(8,128)S(1)} %collective-permute-done.20.one, f32[19,16,128]{2,1,0:T(8,128)S(1)} %collective-permute-done.22.two), custom_call_target="tpu_custom_call" | custom-call | tf_op jit(solution)/shard_map/pallas_call | solution.py:21
  106.3 4.5 %shard_map.56 = f32[1,32,32,128]{3,2,1,0:T(8,128)} custom-call(s32[2]{0:T(128)S(1)} %pad_add_fusion.meta, s32[16,8]{1,0:T(8,128)S(1)} %copy.13.bricks, f32[8,128]{1,0:T(8,128)S(1)} %fusion.1.sum_0, f32[8,128]{1,0:T(8,128)S(1)} %collective-permute-done.23.sum_1, f32[8,128]{1,0:T(8,128)S(1)} %collective-permute-done.24.sum_2, ...), custom_call_target="tpu_custom_call" | custom-call | tf_op jit(solution)/shard_map/pallas_call | solution.py:21
  (27 shorter events, 0.1 us)
Async XLA Ops:
  0.8 1.0 copy-start
  1.9 1.0 copy-start.2
  2.9 1.0 copy-start.4
  27.1 7.3 %collective-permute-start = (f32[4,21,8,128]{3,2,1,0:T(8,128)S(1)}, f32[4,21,8,128]{3,2,1,0:T(8,128)S(1)}, u32[]{:S(2)}, u32[]{:S(2)}) collective-permute-start(f32[4,21,8,128]{3,2,1,0:T(8,128)S(1)} %shard_map.47), channel_id=1, source_target_pairs={{8,0},{9,1},{10,2},{11,3},{4,12},{5,13},{6,14},{7,15},{16,8},{17,9... | collective-permute-start | bytes 1032200 | tf_op jit(solution)/shard_map/ppermute | solution.py:626
  30.3 6.5 %collective-permute-start.3 = (f32[8,16,128]{2,1,0:T(8,128)S(1)}, f32[8,16,128]{2,1,0:T(8,128)S(1)}, u32[]{:S(2)}, u32[]{:S(2)}) collective-permute-start(f32[8,16,128]{2,1,0:T(8,128)S(1)} %get-tuple-element.54.refs_0_), channel_id=1, source_target_pairs={{0,3},{1,0},{2,1},{3,2},{4,7},{5,4},{6,5},{7,6},{8,11},{9,8},{10,9... | collective-permute-start | bytes 196616 | tf_op jit(solution)/shard_map/ppermute | solution.py:630
  31.2 5.6 %collective-permute-start.2 = (f32[8,16,128]{2,1,0:T(8,128)S(1)}, f32[8,16,128]{2,1,0:T(8,128)S(1)}, u32[]{:S(2)}, u32[]{:S(2)}) collective-permute-start(f32[8,16,128]{2,1,0:T(8,128)S(1)} %get-tuple-element.54.refs_0_), channel_id=1, source_target_pairs={{0,2},{1,3},{2,0},{3,1},{4,6},{5,7},{6,4},{7,5},{8,10},{9,11},{10,... | collective-permute-start | bytes 196616 | tf_op jit(solution)/shard_map/ppermute | solution.py:630
  32.7 5.4 %collective-permute-start.1 = (f32[8,16,128]{2,1,0:T(8,128)S(1)}, f32[8,16,128]{2,1,0:T(8,128)S(1)}, u32[]{:S(2)}, u32[]{:S(2)}) collective-permute-start(f32[8,16,128]{2,1,0:T(8,128)S(1)} %get-tuple-element.54.refs_0_), channel_id=1, source_target_pairs={{0,1},{1,2},{2,3},{3,0},{4,5},{5,6},{6,7},{7,4},{8,9},{9,10},{10,1... | collective-permute-start | bytes 196616 | tf_op jit(solution)/shard_map/ppermute | solution.py:630
  35.8 1.0 copy-start.6
  38.1 20.6 %copy-start.1 = (f32[1,32,32,128]{3,2,1,0:T(8,128)S(1)}, f32[1,32,32,128]{3,2,1,0:T(8,128)}, u32[]{:S(2)}) copy-start(f32[1,32,32,128]{3,2,1,0:T(8,128)} %u.3) | copy-start | bytes 1572868
  38.1 20.6 %copy-start.3 = (f32[1,32,32,128]{3,2,1,0:T(8,128)S(1)}, f32[1,32,32,128]{3,2,1,0:T(8,128)}, u32[]{:S(2)}) copy-start(f32[1,32,32,128]{3,2,1,0:T(8,128)} %f.3) | copy-start | bytes 1572868
  38.1 20.6 %copy-start.5 = (f32[1,32,32,128]{3,2,1,0:T(8,128)S(1)}, f32[1,32,32,128]{3,2,1,0:T(8,128)}, u32[]{:S(2)}) copy-start(f32[1,32,32,128]{3,2,1,0:T(8,128)} %a.3) | copy-start | bytes 1572868
  38.1 20.6 %all-to-all-start.1 = ((f32[8,35,8,128]{3,2,1,0:T(8,128)}), f32[8,35,8,128]{3,2,1,0:T(8,128)S(1)}, u32[]{:S(2)}, u32[]{:S(2)}) async-start(f32[8,35,8,128]{3,2,1,0:T(8,128)} %copy-done.6), calls=%async_computation.1 | async-start | bytes 2293760 | tf_op jit(solution)/shard_map/all_to_all | solution.py:644
  42.7 1.3 %collective-permute-start.4 = (f32[8,16,128]{2,1,0:T(8,128)S(1)}, f32[8,16,128]{2,1,0:T(8,128)S(1)}, u32[]{:S(2)}, u32[]{:S(2)}) collective-permute-start(f32[8,16,128]{2,1,0:T(8,128)S(1)} %get-tuple-element.54.refs_0_), channel_id=1, source_target_pairs={{0,4},{4,0},{1,5},{5,1},{2,6},{6,2},{3,7},{7,3},{8,12},{12,8},{9,1... | collective-permute-start | bytes 196616 | tf_op jit(solution)/shard_map/ppermute | solution.py:617
  42.8 1.3 %collective-permute-start.5 = (f32[8,16,128]{2,1,0:T(8,128)S(1)}, f32[8,16,128]{2,1,0:T(8,128)S(1)}, u32[]{:S(2)}, u32[]{:S(2)}) collective-permute-start(f32[8,16,128]{2,1,0:T(8,128)S(1)} %collective-permute-done.1.refs_1_), channel_id=1, source_target_pairs={{0,4},{4,0},{1,5},{5,1},{2,6},{6,2},{3,7},{7,3},{8,12},{12,8},{9,1... | collective-permute-start | bytes 196616 | tf_op jit(solution)/shard_map/ppermute | solution.py:617
  43.2 1.3 %collective-permute-start.6 = (f32[8,16,128]{2,1,0:T(8,128)S(1)}, f32[8,16,128]{2,1,0:T(8,128)S(1)}, u32[]{:S(2)}, u32[]{:S(2)}) collective-permute-start(f32[8,16,128]{2,1,0:T(8,128)S(1)} %collective-permute-done.2.refs_2_), channel_id=1, source_target_pairs={{0,4},{4,0},{1,5},{5,1},{2,6},{6,2},{3,7},{7,3},{8,12},{12,8},{9,1... | collective-permute-start | bytes 196616 | tf_op jit(solution)/shard_map/ppermute | solution.py:617
  43.4 1.3 %collective-permute-start.7 = (f32[8,16,128]{2,1,0:T(8,128)S(1)}, f32[8,16,128]{2,1,0:T(8,128)S(1)}, u32[]{:S(2)}, u32[]{:S(2)}) collective-permute-start(f32[8,16,128]{2,1,0:T(8,128)S(1)} %collective-permute-done.3.refs_3_), channel_id=1, source_target_pairs={{0,4},{4,0},{1,5},{5,1},{2,6},{6,2},{3,7},{7,3},{8,12},{12,8},{9,1... | collective-permute-start | bytes 196616 | tf_op jit(solution)/shard_map/ppermute | solution.py:617
  45.3 6.4 %collective-permute-start.8 = (f32[4,5,16,128]{3,2,1,0:T(8,128)S(1)}, f32[4,5,16,128]{3,2,1,0:T(8,128)S(1)}, u32[]{:S(2)}, u32[]{:S(2)}) collective-permute-start(f32[4,5,16,128]{3,2,1,0:T(8,128)S(1)} %shard_map.49), channel_id=1, source_target_pairs={{0,8},{1,9},{2,10},{3,11},{12,4},{13,5},{14,6},{15,7},{8,16},{9,17... | collective-permute-start | bytes 491528 | tf_op jit(solution)/shard_map/ppermute | solution.py:626
  51.7 2.2 %collective-permute-start.9 = (f32[4,5,16,128]{3,2,1,0:T(8,128)S(1)}, f32[4,5,16,128]{3,2,1,0:T(8,128)S(1)}, u32[]{:S(2)}, u32[]{:S(2)}) collective-permute-start(f32[4,5,16,128]{3,2,1,0:T(8,128)S(1)} %collective-permute-done.8.refs_8_), channel_id=1, source_target_pairs={{0,4},{4,0},{1,5},{5,1},{2,6},{6,2},{3,7},{7,3},{8,12},{12,8},{9,1... | collective-permute-start | bytes 491528 | tf_op jit(solution)/shard_map/ppermute | solution.py:617
  51.9 1.4 %collective-permute-start.10 = (f32[2,8,2,8,128]{4,3,2,1,0:T(8,128)S(1)}, f32[2,8,2,8,128]{4,3,2,1,0:T(8,128)S(1)}, u32[]{:S(2)}, u32[]{:S(2)}) collective-permute-start(f32[2,8,2,8,128]{4,3,2,1,0:T(8,128)S(1)} %get-tuple-element.64.here), channel_id=1, source_target_pairs={{0,4},{4,0},{1,5},{5,1},{2,6},{6,2},{3,7},{7,3},{8,12},{12,8},{9,1... | collective-permute-start | bytes 393224 | tf_op jit(solution)/shard_map/ppermute | solution.py:617
  53.3 0.6 copy-start.9
  53.9 0.7 copy-start.7
  58.7 16.4 %copy-start.10 = (f32[2,8,2,8,128]{4,3,2,1,0:T(8,128)S(1)}, f32[2,8,2,8,128]{4,3,2,1,0:T(8,128)}, u32[]{:S(2)}) copy-start(f32[2,8,2,8,128]{4,3,2,1,0:T(8,128)} %copy-done.9) | copy-start | bytes 393220
  63.3 14.8 %copy-start.8 = (f32[4,5,16,128]{3,2,1,0:T(8,128)S(1)}, f32[4,5,16,128]{3,2,1,0:T(8,128)}, u32[]{:S(2)}) copy-start(f32[4,5,16,128]{3,2,1,0:T(8,128)} %copy-done.7) | copy-start | bytes 491524
  63.3 3.2 %collective-permute-start.13 = (f32[8,16,128]{2,1,0:T(8,128)S(1)}, f32[8,16,128]{2,1,0:T(8,128)S(1)}, u32[]{:S(2)}, u32[]{:S(2)}) collective-permute-start(f32[8,16,128]{2,1,0:T(8,128)S(1)} %get-tuple-element.60.refs_0_), channel_id=1, source_target_pairs={{0,3},{1,0},{2,1},{3,2},{4,7},{5,4},{6,5},{7,6},{8,11},{9,8},{10,9... | collective-permute-start | bytes 196616 | tf_op jit(solution)/shard_map/ppermute | solution.py:630
  64.4 4.6 %collective-permute-start.12 = (f32[8,16,128]{2,1,0:T(8,128)S(1)}, f32[8,16,128]{2,1,0:T(8,128)S(1)}, u32[]{:S(2)}, u32[]{:S(2)}) collective-permute-start(f32[8,16,128]{2,1,0:T(8,128)S(1)} %get-tuple-element.60.refs_0_), channel_id=1, source_target_pairs={{0,2},{1,3},{2,0},{3,1},{4,6},{5,7},{6,4},{7,5},{8,10},{9,11},{10,... | collective-permute-start | bytes 196616 | tf_op jit(solution)/shard_map/ppermute | solution.py:630
  65.8 5.7 %collective-permute-start.11 = (f32[8,16,128]{2,1,0:T(8,128)S(1)}, f32[8,16,128]{2,1,0:T(8,128)S(1)}, u32[]{:S(2)}, u32[]{:S(2)}) collective-permute-start(f32[8,16,128]{2,1,0:T(8,128)S(1)} %get-tuple-element.60.refs_0_), channel_id=1, source_target_pairs={{0,1},{1,2},{2,3},{3,0},{4,5},{5,6},{6,7},{7,4},{8,9},{9,10},{10,1... | collective-permute-start | bytes 196616 | tf_op jit(solution)/shard_map/ppermute | solution.py:630
  65.8 6.4 %collective-permute-start.14 = (f32[8,16,128]{2,1,0:T(8,128)S(1)}, f32[8,16,128]{2,1,0:T(8,128)S(1)}, u32[]{:S(2)}, u32[]{:S(2)}) collective-permute-start(f32[8,16,128]{2,1,0:T(8,128)S(1)} %get-tuple-element.60.refs_0_), channel_id=1, source_target_pairs={{0,4},{4,0},{1,5},{5,1},{2,6},{6,2},{3,7},{7,3},{8,12},{12,8},{9,1... | collective-permute-start | bytes 196616 | tf_op jit(solution)/shard_map/ppermute | solution.py:617
  66.6 5.6 %collective-permute-start.17 = (f32[8,16,128]{2,1,0:T(8,128)S(1)}, f32[8,16,128]{2,1,0:T(8,128)S(1)}, u32[]{:S(2)}, u32[]{:S(2)}) collective-permute-start(f32[8,16,128]{2,1,0:T(8,128)S(1)} %collective-permute-done.13.refs_3_), channel_id=1, source_target_pairs={{0,4},{4,0},{1,5},{5,1},{2,6},{6,2},{3,7},{7,3},{8,12},{12,8},{9,1... | collective-permute-start | bytes 196616 | tf_op jit(solution)/shard_map/ppermute | solution.py:617
  69.0 3.4 %collective-permute-start.16 = (f32[8,16,128]{2,1,0:T(8,128)S(1)}, f32[8,16,128]{2,1,0:T(8,128)S(1)}, u32[]{:S(2)}, u32[]{:S(2)}) collective-permute-start(f32[8,16,128]{2,1,0:T(8,128)S(1)} %collective-permute-done.12.refs_2_), channel_id=1, source_target_pairs={{0,4},{4,0},{1,5},{5,1},{2,6},{6,2},{3,7},{7,3},{8,12},{12,8},{9,1... | collective-permute-start | bytes 196616 | tf_op jit(solution)/shard_map/ppermute | solution.py:617
  71.5 1.6 %collective-permute-start.15 = (f32[8,16,128]{2,1,0:T(8,128)S(1)}, f32[8,16,128]{2,1,0:T(8,128)S(1)}, u32[]{:S(2)}, u32[]{:S(2)}) collective-permute-start(f32[8,16,128]{2,1,0:T(8,128)S(1)} %collective-permute-done.11.refs_1_), channel_id=1, source_target_pairs={{0,4},{4,0},{1,5},{5,1},{2,6},{6,2},{3,7},{7,3},{8,12},{12,8},{9,1... | collective-permute-start | bytes 196616 | tf_op jit(solution)/shard_map/ppermute | solution.py:617
  73.8 6.1 %collective-permute-start.18 = (f32[4,5,16,128]{3,2,1,0:T(8,128)S(1)}, f32[4,5,16,128]{3,2,1,0:T(8,128)S(1)}, u32[]{:S(2)}, u32[]{:S(2)}) collective-permute-start(f32[4,5,16,128]{3,2,1,0:T(8,128)S(1)} %shard_map.51), channel_id=1, source_target_pairs={{0,8},{1,9},{2,10},{3,11},{12,4},{13,5},{14,6},{15,7},{8,16},{9,17... | collective-permute-start | bytes 491528 | tf_op jit(solution)/shard_map/ppermute | solution.py:626
  79.9 3.3 %collective-permute-start.19 = (f32[4,5,16,128]{3,2,1,0:T(8,128)S(1)}, f32[4,5,16,128]{3,2,1,0:T(8,128)S(1)}, u32[]{:S(2)}, u32[]{:S(2)}) collective-permute-start(f32[4,5,16,128]{3,2,1,0:T(8,128)S(1)} %collective-permute-done.18.refs_8_), channel_id=1, source_target_pairs={{0,4},{4,0},{1,5},{5,1},{2,6},{6,2},{3,7},{7,3},{8,12},{12,8},{9,1... | collective-permute-start | bytes 491528 | tf_op jit(solution)/shard_map/ppermute | solution.py:617
  85.6 9.1 %collective-permute-start.20 = (f32[19,16,128]{2,1,0:T(8,128)S(1)}, f32[19,16,128]{2,1,0:T(8,128)S(1)}, u32[]{:S(2)}, u32[]{:S(2)}) collective-permute-start(f32[19,16,128]{2,1,0:T(8,128)S(1)} %get-tuple-element.79), channel_id=1, source_target_pairs={{0,8},{1,9},{2,10},{3,11},{12,4},{13,5},{14,6},{15,7},{8,16},{9,17... | collective-permute-start | bytes 466952 | tf_op jit(solution)/shard_map/ppermute | solution.py:626
  90.7 4.1 %collective-permute-start.21 = (f32[8,128]{1,0:T(8,128)S(1)}, f32[8,128]{1,0:T(8,128)S(1)}, u32[]{:S(2)}, u32[]{:S(2)}) collective-permute-start(f32[8,128]{1,0:T(8,128)S(1)} %get-tuple-element.78), channel_id=1, source_target_pairs={{0,112},{8,120},{16,0},{24,8},{32,16},{40,24},{48,32},{56,40},{64,... | collective-permute-start | bytes 12296 | tf_op jit(solution)/shard_map/ppermute | solution.py:696
  94.7 2.0 %collective-permute-start.22 = (f32[19,16,128]{2,1,0:T(8,128)S(1)}, f32[19,16,128]{2,1,0:T(8,128)S(1)}, u32[]{:S(2)}, u32[]{:S(2)}) collective-permute-start(f32[19,16,128]{2,1,0:T(8,128)S(1)} %collective-permute-done.20.one), channel_id=1, source_target_pairs={{0,4},{4,0},{1,5},{5,1},{2,6},{6,2},{3,7},{7,3},{8,12},{12,8},{9,1... | collective-permute-start | bytes 466952 | tf_op jit(solution)/shard_map/ppermute | solution.py:617
  96.7 5.1 %collective-permute-start.23 = (f32[8,128]{1,0:T(8,128)S(1)}, f32[8,128]{1,0:T(8,128)S(1)}, u32[]{:S(2)}, u32[]{:S(2)}) collective-permute-start(f32[8,128]{1,0:T(8,128)S(1)} %fusion.1.sum_0), channel_id=1, source_target_pairs={{0,32},{1,33},{2,34},{3,35},{4,100},{5,101},{6,102},{7,103},{8,40}... | collective-permute-start | bytes 12296 | tf_op jit(solution)/shard_map/ppermute | solution.py:640
  101.1 5.1 %collective-permute-start.24 = (f32[8,128]{1,0:T(8,128)S(1)}, f32[8,128]{1,0:T(8,128)S(1)}, u32[]{:S(2)}, u32[]{:S(2)}) collective-permute-start(f32[8,128]{1,0:T(8,128)S(1)} %fusion.1.sum_0), channel_id=1, source_target_pairs={{0,64},{8,72},{16,80},{24,88},{32,96},{40,104},{48,112},{56,120},{... | collective-permute-start | bytes 12296 | tf_op jit(solution)/shard_map/ppermute | solution.py:640
  101.9 4.4 %collective-permute-start.25 = (f32[8,128]{1,0:T(8,128)S(1)}, f32[8,128]{1,0:T(8,128)S(1)}, u32[]{:S(2)}, u32[]{:S(2)}) collective-permute-start(f32[8,128]{1,0:T(8,128)S(1)} %collective-permute-done.23.sum_1), channel_id=1, source_target_pairs={{0,4},{4,0},{1,5},{5,1},{2,6},{6,2},{3,7},{7,3},{8,12},{12,8},{9,1... | collective-permute-start | bytes 12296 | tf_op jit(solution)/shard_map/ppermute | solution.py:617

commit v9 on v8

--- a/solution.py
+++ b/solution.py
@@ -50,7 +50,7 @@
 
 ARRAYS = 5
 FACE = 17
-SENT_Y, SENT_X, SENT_COEF, SENT = 17, 27, 30, 32
+SENT_Y, SENT_X, SENT = 17, 27, 30
 GOT_ROWS, GOT_STRIPS, GOT_Y, GOT_X, GOT = 17, 20, 22, 32, 35
 
 
@@ -99,20 +99,13 @@
     slab, me = meta[0], meta[1]
     for i in range(4):
         src = jnp.where(me >= 4, bricks[slab, 4 + i], bricks[slab, i])
-        out[i, 0:FACE] = recv[src, 0:FACE]
-        for j in range(2):
-            coef = recv[bricks[slab, 2 * i + j], SENT_COEF:SENT]
-            out[i, FACE + 2 * j : FACE + 2 * j + 2] = coef
-
-
-def mid_kernel(meta, bricks, recv, cross, out, coef, faces):
+        out[i] = recv[src, 0:FACE]
+
+
+def mid_kernel(meta, bricks, recv, cross, out, faces):
     slab, me = meta[0], meta[1]
     faces[0:8] = recv[:, 0:FACE]
-    faces[8:12] = cross[:, 0:FACE]
-    for p in range(8):
-        coef[0, p] = recv[bricks[slab, p], SENT_COEF:SENT]
-        j = FACE + 2 * (p & 1)
-        coef[1, p] = cross[p >> 1, j : j + 2]
+    faces[8:12] = cross[...]
     row = iota((8, 128), 0)
     for p in range(8):
         bx, by, bz = p & 1, (p >> 1) & 1, p >> 2
@@ -143,7 +136,7 @@
         for i in range(2):
             out[dest, GOT_STRIPS + i] = merge_strips(list(enumerate(strips[16 * i : 16 * i + 16])))
         out[dest, GOT_Y:GOT_X] = recv[from_y, SENT_Y:SENT_X]
-        out[dest, GOT_X:GOT] = recv[from_x, SENT_X:SENT_COEF]
+        out[dest, GOT_X:GOT] = recv[from_x, SENT_X:SENT]
 
 
 def unpack_shell(recv, grids, bit_x, bit_y):
@@ -203,7 +196,7 @@
     return jnp.where(mask, high, low) if red else jnp.where(mask, low, high)
 
 
-def pack_bottom_coef(a, out, small):
+def pack_bottom_coef(a, ac, small):
     for i in range(8):
         planes = (a[0, 4 * i] + a[0, 4 * i + 1]) + (a[0, 4 * i + 2] + a[0, 4 * i + 3])
         small[i] = planes
@@ -218,8 +211,7 @@
         tile = cells[32 * h : 32 * h + 8]
         for j in range(1, 4):
             tile = jnp.where(group == j, cells[32 * h + 8 * j : 32 * h + 8 * j + 8], tile)
-        for k in range(8):
-            out[k, SENT_COEF + h] = tile
+        ac[8, 8 * h : 8 * h + 8] = tile
 
 
 def pack_coarse(planes, small, out):
@@ -244,7 +236,7 @@
         return pair_of(sources[c][0], t, sources[c][1], mask)
 
     pack_shell(get, out, bit_x, bit_y)
-    pack_bottom_coef(a, out, small)
+    pack_bottom_coef(a, ac, small)
     for t in range(16):
         planes[t] = a[0, 2 * t] + a[0, 2 * t + 1]
     pack_coarse(planes, rows, ac)
@@ -337,7 +329,9 @@
     start = jnp.where(me < 4, 3, 0)
     for i in range(4):
         member = jnp.where(me < 4, bricks[slab, 4 + i], bricks[slab, i])
-        out[i] = held[slot_of(member, me), pl.ds(start, 5)]
+        out[i, 0:5] = held[slot_of(member, me), pl.ds(start, 5)]
+        for j in range(5, out.shape[1]):
+            out[i, j] = held[slot_of(bricks[slab, 2 * i + j - 5], me), 8]
 
 
 def sort_sides(me, one, two, low, high):
@@ -384,10 +378,14 @@
 
 def coarse_coef_kernel(meta, bricks, *refs):
     boxes, (one, two) = refs[:8], refs[8:10]
-    a_r, i_r, i_b, ab = refs[10:14]
-    held, low, high, a_b, planes, small = refs[14:]
-    slab = meta[0]
+    a_r, i_r, i_b, ab, coef = refs[10:15]
+    held, low, high, a_b, planes, small = refs[15:]
+    slab, me = meta[0], meta[1]
     assemble(meta, bricks, boxes, one, two, a_r, a_b, held, low, high)
+    for p in range(8):
+        coef[0, p] = low[p >> 1, 5 + (p & 1)]
+        coef[1, p] = held[slot_of(bricks[slab, p], me), 8]
+        coef[2, p] = high[p >> 1, 5 + (p & 1)]
     for k in range(1, 27):
         keep = jnp.full((32, 128), 0, jnp.int32) == 0
         if k < 6:
@@ -470,31 +468,20 @@
         es[i] = jnp.where(mask, e_r[k], e_b[k]) if upper else jnp.where(mask, e_b[k], e_r[k])
 
 
-def weights_kernel(meta, here, there, out, t_r, t_b, w_r, w_b, i_r, i_b, low, high):
-    slab, me = meta[0], meta[1]
-
-    @pl.when(me < 4)
-    def _():
-        low[...] = there[1]
-        high[...] = here[1]
-
-    @pl.when(me >= 4)
-    def _():
-        low[...] = here[1]
-        high[...] = there[1]
-
+def weights_kernel(meta, coef, out, t_r, t_b, w_r, w_b, i_r, i_b):
+    slab = meta[0]
     lane = iota((8, 128), 1)
 
-    def plane(boxes, z):
+    def plane(part, z):
         rows = []
         for by in range(2):
             place, shift = 4 * (z >> 3) + 2 * by, 32 * (z & 3)
-            west = pltpu.roll(boxes(place, (z & 7) >> 2), (128 - shift) % 128, 1)
-            east = pltpu.roll(boxes(place + 1, (z & 7) >> 2), (160 - shift) % 128, 1)
+            here = slice(8 * ((z & 7) >> 2), 8 * ((z & 7) >> 2) + 8)
+            west = pltpu.roll(coef[part, place, here], (128 - shift) % 128, 1)
+            east = pltpu.roll(coef[part, place + 1, here], (160 - shift) % 128, 1)
             rows.append(jnp.where(lane < 32, west, east))
         return jnp.concatenate(rows, 0)
 
-    parts = (lambda p, h: low[p, h], lambda p, h: here[0, p, h], lambda p, h: high[p, h])
     mask = odd(16, 128)
     left = iota((16, 128), 1) < 64
     zero = jnp.zeros((16, 128), F32)
@@ -502,7 +489,7 @@
         t_r[k] = zero
         t_b[k] = zero
     for j in range(24):
-        lower, upper = (plane(parts[(2 * j + i) // 16], (2 * j + i) % 16) for i in range(2))
+        lower, upper = (plane((2 * j + i) // 16, (2 * j + i) % 16) for i in range(2))
         keep = left
         if j < 8:
             keep = left & jnp.logical_not(is_zero(slab, (16, 128)))
@@ -649,43 +636,38 @@
     smem = [meta, brick_map]
     fine = (26, 40, 256)
     packed, ac = run(
-        first_kernel, [(8, SENT, 8, 128), (8, 16, 128)], smem, [u_init, source, coeffs],
+        first_kernel, [(8, SENT, 8, 128), (9, 16, 128)], smem, [u_init, source, coeffs],
         [(8, 32, 128), (16, 32, 128), (256, 128), (1, 32, 32, 128)],
     )
     got = among(packed)
-    leaving = run(cross_kernel, [(4, FACE + 4, 8, 128)], smem, [got])
+    leaving = run(cross_kernel, [(4, FACE, 8, 128)], smem, [got])
     leaving, ac = lax.optimization_barrier((leaving, ac))
     cross = to_slabs(leaving, False)
     ac_boxes = around_chips(ac)
-    sent, coef = run(
-        mid_kernel, [(8, GOT, 8, 128), (2, 8, 2, 8, 128)], smem, [got, cross], [(12, FACE, 8, 128)],
-    )
-    coef_other = swap_cores(coef)
+    sent = run(mid_kernel, [(8, GOT, 8, 128)], smem, [got, cross], [(12, FACE, 8, 128)])
     sent, *ac_boxes = lax.optimization_barrier((sent, *ac_boxes))
     halo = among(sent)
     faces = (4, 5, 16, 128)
     coarse = (28, 32, 128)
     held = [(8, 8, 16, 128), faces, faces]
     ac_boxes = both_cores(ac_boxes)
-    ac_cross = to_slabs(run(faces_kernel, [faces], smem, ac_boxes, held[:1]), True)
+    ac_held = [(8, 9, 16, 128), (4, 7, 16, 128), (4, 7, 16, 128)]
+    ac_cross = to_slabs(run(faces_kernel, ac_held[1:2], smem, ac_boxes, ac_held[:1]), True)
     ac_other = swap_cores(ac_cross)
-    halo, ac_cross, ac_other, coef_other = lax.optimization_barrier((halo, ac_cross, ac_other, coef_other))
+    halo, ac_cross, ac_other = lax.optimization_barrier((halo, ac_cross, ac_other))
     rc, u_b, f_r, f_b, i_r, i_b = run(
         fine_down_kernel, [(8, 16, 128)] + [fine] * 5, smem, [u_init, source, coeffs, halo],
         [fine, (16, 32, 128), (256, 128)],
     )
     boxes = both_cores(around_chips(rc))
     leaving = run(faces_kernel, [faces], smem, boxes, held[:1])
-    leaving, ac_cross, ac_other, coef = lax.optimization_barrier((leaving, ac_cross, ac_other, coef))
+    leaving, ac_cross, ac_other = lax.optimization_barrier((leaving, ac_cross, ac_other))
     cross = to_slabs(leaving, True)
-    weights = run(
-        weights_kernel, [(16, 16, 128)], [meta], [coef, coef_other],
-        [(26, 16, 128)] * 6 + [(8, 2, 8, 128)] * 2,
+    ca_r, ci_r, ci_b, ab, coef = run(
+        coarse_coef_kernel, [coarse] * 3 + [(22, 16, 128), (3, 8, 16, 128)], smem, ac_boxes + [ac_cross, ac_other],
+        ac_held + [coarse, (22, 32, 128), (352, 128)],
     )
-    ca_r, ci_r, ci_b, ab = run(
-        coarse_coef_kernel, [coarse] * 3 + [(22, 16, 128)], smem, ac_boxes + [ac_cross, ac_other],
-        held + [coarse, (22, 32, 128), (352, 128)],
-    )
+    weights = run(weights_kernel, [(16, 16, 128)], [meta], [coef], [(26, 16, 128)] * 6)
     cross, weights, ca_r, ci_r, ci_b, ab = lax.optimization_barrier((cross, weights, ca_r, ci_r, ci_b, ab))
     rb, rb_send, part, ec_b, r_r, r_b = run(
         coarse_down_kernel, [(22, 16, 128), (19, 16, 128), (8, 128)] + [coarse] * 3, smem,

time: 111 us -> 111 us (level)
  local copies, waits for them, and re-layouts: 6.23 us -> 4.58 us
  Pallas kernels: 23.8 us -> 25.1 us
  waiting for transfers between devices: 21 us -> 22.3 us
    unnamed x23 -> x17, local copies, waits for them, and re-layouts: 6.23 us -> 4.58 us
    pallas_call x11, Pallas kernels: 23.8 us -> 25.1 us  [run(): pl.pallas_call(kernel, out_shape=shapes[0] if single else shapes, in_spec...]
    ppermute x13 -> x12, starting transfers between devices: 12.3 us -> 11.8 us  [swap_cores(): return lax.ppermute(x, 'level', [(0, 1), (1, 0)])]
    ppermute x13 -> x12, waiting for transfers between devices: 4.93 us -> 4.98 us  [swap_cores(): return lax.ppermute(x, 'level', [(0, 1), (1, 0)])]
  transfers between devices with their start and end apart: 27 -> 26, of which waited for: 17 -> 18; matrix products, arithmetic and copies ran while one was open for 0% -> 0% of each run, Pallas kernels for 8% -> 9%
where the time goes in v9:
time: 111 us; the launch traced here: 110 us
  starting transfers between devices  38 us (34%)
  Pallas kernels  25.1 us (23%)
  waiting for transfers between devices  22.3 us (20%)
  blocking collectives  20.1 us (18%)
  local copies, waits for them, and re-layouts  4.58 us (4%)
    pallas_call x11, Pallas kernels, run(): pl.pallas_call(kernel, out_shape=shapes[0] if single else shapes, in_spec...  25.1 us
    all_to_all x1, blocking collectives, among(): return lax.all_to_all(x, LB, split_axis=0, concat_axis=0, tiled=True)  20.1 us
    ppermute x12, starting transfers between devices, swap_cores(): return lax.ppermute(x, 'level', [(0, 1), (1, 0)])  11.8 us
    ppermute x4, starting transfers between devices, to_slabs(): return lax.ppermute(x, ALL, pairs)  10.8 us
    ppermute x4, waiting for transfers between devices, to_slabs(): return lax.ppermute(x, ALL, pairs)  7.58 us
    ppermute x12, waiting for transfers between devices, swap_cores(): return lax.ppermute(x, 'level', [(0, 1), (1, 0)])  4.98 us
    ppermute x2, starting transfers between devices, fours_apart(): return (lax.ppermute(x, ALL, beside), lax.ppermute(x, 'slab', across))  4.98 us
    ppermute x6, starting transfers between devices, around_chips(): lax.ppermute(x, 'bottom', [(i, (i + d) % 4) for i in range(4)])  4.87 us
  transfers between devices with their start and end apart: 26, of which 18 were waited for; matrix products, arithmetic and copies ran while one was open for 0% of the time, Pallas kernels for 9%

profile of v9, /device:TPU:1, one launch (start us, length us, event | category | flops | bytes accessed | tf_op | source)
XLA Modules:
  0.0 110.2 jit_solution(14861092371146755223)
XLA Ops:
  0.0 0.8 copy.13.bricks
  0.8 0.1 pad_add_fusion.meta
  0.8 1.0 copy-done
  1.9 1.0 copy-done.2
  2.9 1.0 copy-done.4
  4.0 1.7 %shard_map.46 = (f32[8,30,8,128]{3,2,1,0:T(8,128)S(1)}, f32[9,16,128]{2,1,0:T(8,128)S(1)}) custom-call(s32[2]{0:T(128)S(1)} %pad_add_fusion.meta, s32[16,8]{1,0:T(8,128)S(1)} %copy.13.bricks, f32[1,32,32,128]{3,2,1,0:T(8,128)S(1)} %copy-done, f32[1,32,32,128]{3,2,1,0:T(8,128)S(1)} %copy-done.2, f32[1,32,32,128]{3,2,1,0:T(8,128)S(1)} %copy-done.4), custom_call_target="tpu_custom_call" | custom-call | tf_op jit(solution)/shard_map/pallas_call | solution.py:21
  5.7 20.1 %all_to_all.10.recv = f32[8,30,8,128]{3,2,1,0:T(8,128)S(1)} all-to-all(f32[8,30,8,128]{3,2,1,0:T(8,128)S(1)} %get-tuple-element.45), channel_id=1, replica_groups=mesh['slab'=16,'level'=2,'bottom'=4] {'level','bottom'}, dimensions={0} | all-to-all | bytes 1966080 | tf_op jit(solution)/shard_map/all_to_all | solution.py:631
  25.8 0.7 shard_map.47
  26.5 3.1 %collective-permute-start = (f32[4,17,8,128]{3,2,1,0:T(8,128)S(1)}, f32[4,17,8,128]{3,2,1,0:T(8,128)S(1)}, u32[]{:S(2)}, u32[]{:S(2)}) collective-permute-start(f32[4,17,8,128]{3,2,1,0:T(8,128)S(1)} %shard_map.47), channel_id=1, source_target_pairs={{8,0},{9,1},{10,2},{11,3},{4,12},{5,13},{6,14},{7,15},{16,8},{17,9... | collective-permute-start | bytes 835592 | tf_op jit(solution)/shard_map/ppermute | solution.py:613
  29.6 1.0 collective-permute-start.3
  30.6 1.5 %collective-permute-start.2 = (f32[9,16,128]{2,1,0:T(8,128)S(1)}, f32[9,16,128]{2,1,0:T(8,128)S(1)}, u32[]{:S(2)}, u32[]{:S(2)}) collective-permute-start(f32[9,16,128]{2,1,0:T(8,128)S(1)} %get-tuple-element.50.refs_0_), channel_id=1, source_target_pairs={{0,2},{1,3},{2,0},{3,1},{4,6},{5,7},{6,4},{7,5},{8,10},{9,11},{10,... | collective-permute-start | bytes 221192 | tf_op jit(solution)/shard_map/ppermute | solution.py:617
  32.1 0.0 collective-permute-start.1
  32.1 1.0 collective-permute-done.cross
  33.1 2.3 %shard_map.48 = f32[8,35,8,128]{3,2,1,0:T(8,128)} custom-call(s32[2]{0:T(128)S(1)} %pad_add_fusion.meta, s32[16,8]{1,0:T(8,128)S(1)} %copy.13.bricks, f32[8,30,8,128]{3,2,1,0:T(8,128)S(1)} %all_to_all.10.recv, f32[4,17,8,128]{3,2,1,0:T(8,128)S(1)} %collective-permute-done.cross), custom_call_target="tpu_custom_call" | custom-call | tf_op jit(solution)/shard_map/pallas_call | solution.py:21
  35.4 0.6 collective-permute-done.2.refs_2_
  36.1 1.7 %collective-permute-done.1.refs_1_ = f32[9,16,128]{2,1,0:T(8,128)S(1)} collective-permute-done((f32[9,16,128]{2,1,0:T(8,128)S(1)}, f32[9,16,128]{2,1,0:T(8,128)S(1)}, u32[]{:S(2)}, u32[]{:S(2)}) %collective-permute-start.1) | collective-permute-done | bytes 73760 | tf_op jit(solution)/shard_map/ppermute | solution.py:617
  37.8 3.9 %all-to-all-start.1 = ((f32[8,35,8,128]{3,2,1,0:T(8,128)}), f32[8,35,8,128]{3,2,1,0:T(8,128)S(1)}, u32[]{:S(2)}, u32[]{:S(2)}) async-start(f32[8,35,8,128]{3,2,1,0:T(8,128)} %shard_map.48), calls=%async_computation.1 | async-start | bytes 2293760 | tf_op jit(solution)/shard_map/all_to_all | solution.py:631
  41.6 0.2 collective-permute-start.4
  41.8 0.3 collective-permute-start.5
  42.2 0.2 collective-permute-start.6
  42.3 0.3 collective-permute-start.7
  42.7 0.2 collective-permute-done.4.refs_4_
  42.9 0.2 collective-permute-done.5.refs_5_
  43.1 0.3 collective-permute-done.6.refs_6_
  43.4 0.2 collective-permute-done.7.refs_7_
  43.6 0.7 shard_map.49
  44.3 1.3 %collective-permute-start.8 = (f32[4,7,16,128]{3,2,1,0:T(8,128)S(1)}, f32[4,7,16,128]{3,2,1,0:T(8,128)S(1)}, u32[]{:S(2)}, u32[]{:S(2)}) collective-permute-start(f32[4,7,16,128]{3,2,1,0:T(8,128)S(1)} %shard_map.49), channel_id=1, source_target_pairs={{0,8},{1,9},{2,10},{3,11},{12,4},{13,5},{14,6},{15,7},{8,16},{9,17... | collective-permute-start | bytes 688136 | tf_op jit(solution)/shard_map/ppermute | solution.py:613
  45.6 5.9 %collective-permute-done.8.refs_8_ = f32[4,7,16,128]{3,2,1,0:T(8,128)S(1)} collective-permute-done((f32[4,7,16,128]{3,2,1,0:T(8,128)S(1)}, f32[4,7,16,128]{3,2,1,0:T(8,128)S(1)}, u32[]{:S(2)}, u32[]{:S(2)}) %collective-permute-start.8) | collective-permute-done | bytes 229408 | tf_op jit(solution)/shard_map/ppermute | solution.py:613
  51.5 0.5 collective-permute-start.9
  52.0 1.1 %collective-permute-done.9.refs_9_ = f32[4,7,16,128]{3,2,1,0:T(8,128)S(1)} collective-permute-done((f32[4,7,16,128]{3,2,1,0:T(8,128)S(1)}, f32[4,7,16,128]{3,2,1,0:T(8,128)S(1)}, u32[]{:S(2)}, u32[]{:S(2)}) %collective-permute-start.9) | collective-permute-done | bytes 229408 | tf_op jit(solution)/shard_map/ppermute | solution.py:604
  53.1 0.7 copy-done.6
  53.8 3.9 %all-to-all-done.1.recv = f32[8,35,8,128]{3,2,1,0:T(8,128)S(1)} async-done(((f32[8,35,8,128]{3,2,1,0:T(8,128)}), f32[8,35,8,128]{3,2,1,0:T(8,128)S(1)}, u32[]{:S(2)}, u32[]{:S(2)}) %all-to-all-start.1) | async-done | bytes 1146912 | tf_op jit(solution)/shard_map/all_to_all | solution.py:631
  57.7 4.6 %shard_map.50 = (f32[8,16,128]{2,1,0:T(8,128)S(1)}, f32[26,40,256]{2,1,0:T(8,128)S(1)}, f32[26,40,256]{2,1,0:T(8,128)S(1)}, f32[26,40,256]{2,1,0:T(8,128)S(1)}, ...) custom-call(s32[2]{0:T(128)S(1)} %pad_add_fusion.meta, s32[16,8]{1,0:T(8,128)S(1)} %copy.13.bricks, ...), custom_call_target="tpu_custom_call" | custom-call | tf_op jit(solution)/shard_map/pallas_call | solution.py:21
  62.3 1.1 collective-permute-start.12
  63.4 1.4 %collective-permute-start.11 = (f32[8,16,128]{2,1,0:T(8,128)S(1)}, f32[8,16,128]{2,1,0:T(8,128)S(1)}, u32[]{:S(2)}, u32[]{:S(2)}) collective-permute-start(f32[8,16,128]{2,1,0:T(8,128)S(1)} %get-tuple-element.55.refs_0_), channel_id=1, source_target_pairs={{0,2},{1,3},{2,0},{3,1},{4,6},{5,7},{6,4},{7,5},{8,10},{9,11},{10,... | collective-permute-start | bytes 196616 | tf_op jit(solution)/shard_map/ppermute | solution.py:617
  64.8 0.8 collective-permute-start.13
  65.5 2.1 %collective-permute-start.16 = (f32[8,16,128]{2,1,0:T(8,128)S(1)}, f32[8,16,128]{2,1,0:T(8,128)S(1)}, u32[]{:S(2)}, u32[]{:S(2)}) collective-permute-start(f32[8,16,128]{2,1,0:T(8,128)S(1)} %collective-permute-done.12.refs_3_), channel_id=1, source_target_pairs={{0,4},{4,0},{1,5},{5,1},{2,6},{6,2},{3,7},{7,3},{8,12},{12,8},{9,1... | collective-permute-start | bytes 196616 | tf_op jit(solution)/shard_map/ppermute | solution.py:604
  67.6 0.4 collective-permute-done.11.refs_2_
  68.0 2.5 %collective-permute-start.15 = (f32[8,16,128]{2,1,0:T(8,128)S(1)}, f32[8,16,128]{2,1,0:T(8,128)S(1)}, u32[]{:S(2)}, u32[]{:S(2)}) collective-permute-start(f32[8,16,128]{2,1,0:T(8,128)S(1)} %collective-permute-done.11.refs_2_), channel_id=1, source_target_pairs={{0,4},{4,0},{1,5},{5,1},{2,6},{6,2},{3,7},{7,3},{8,12},{12,8},{9,1... | collective-permute-start | bytes 196616 | tf_op jit(solution)/shard_map/ppermute | solution.py:604
  70.5 0.0 collective-permute-done.10.refs_1_
  70.5 0.7 collective-permute-start.14
  71.2 0.2 collective-permute-done.15.refs_6_
  71.4 0.7 collective-permute-done.14.refs_5_
  72.1 0.7 shard_map.51
  72.8 1.3 %collective-permute-start.17 = (f32[4,5,16,128]{3,2,1,0:T(8,128)S(1)}, f32[4,5,16,128]{3,2,1,0:T(8,128)S(1)}, u32[]{:S(2)}, u32[]{:S(2)}) collective-permute-start(f32[4,5,16,128]{3,2,1,0:T(8,128)S(1)} %shard_map.51), channel_id=1, source_target_pairs={{0,8},{1,9},{2,10},{3,11},{12,4},{13,5},{14,6},{15,7},{8,16},{9,17... | collective-permute-start | bytes 491528 | tf_op jit(solution)/shard_map/ppermute | solution.py:613
  74.1 1.3 %shard_map.52 = (f32[28,32,128]{2,1,0:T(8,128)S(1)}, f32[28,32,128]{2,1,0:T(8,128)S(1)}, f32[28,32,128]{2,1,0:T(8,128)S(1)}, f32[22,16,128]{2,1,0:T(8,128)S(1)}, f32[3,8,16,128]{3,2,1,0:T(8,128)S(1)}) custom-call(s32[2]{0:T(128)S(1)} %pad_add_fusion.meta, s32[16,8]{1,0:T(8,128)S(1)} %copy.13.bricks, f32[9,16,128]{2,1,0:T(8,128)S(1)} %get-tuple-element.50.refs_0_, ...), custom_call_target="tpu_custom_call" | custom-call | tf_op jit(solution)/shard_map/pallas_call | solution.py:21
  75.4 3.0 %shard_map.53.refs_10_ = f32[16,16,128]{2,1,0:T(8,128)S(1)} custom-call(s32[2]{0:T(128)S(1)} %pad_add_fusion.meta, f32[3,8,16,128]{3,2,1,0:T(8,128)S(1)} %get-tuple-element.61.coef), custom_call_target="tpu_custom_call" | custom-call | tf_op jit(solution)/shard_map/pallas_call | solution.py:21
  78.4 0.6 collective-permute-done.17.refs_8_
  79.0 2.3 %collective-permute-start.18 = (f32[4,5,16,128]{3,2,1,0:T(8,128)S(1)}, f32[4,5,16,128]{3,2,1,0:T(8,128)S(1)}, u32[]{:S(2)}, u32[]{:S(2)}) collective-permute-start(f32[4,5,16,128]{3,2,1,0:T(8,128)S(1)} %collective-permute-done.17.refs_8_), channel_id=1, source_target_pairs={{0,4},{4,0},{1,5},{5,1},{2,6},{6,2},{3,7},{7,3},{8,12},{12,8},{9,1... | collective-permute-start | bytes 491528 | tf_op jit(solution)/shard_map/ppermute | solution.py:604
  81.3 1.0 collective-permute-done.18.refs_9_
  82.4 2.6 %shard_map.54 = (f32[22,16,128]{2,1,0:T(8,128)S(1)}, f32[19,16,128]{2,1,0:T(8,128)S(1)}, f32[8,128]{1,0:T(8,128)S(1)}, f32[28,32,128]{2,1,0:T(8,128)S(1)}, f32[2...) custom-call(s32[2]{0:T(128)S(1)} %pad_add_fusion.meta, s32[16,8]{1,0:T(8,128)S(1)} %copy.13.bricks, ...), custom_call_target="tpu_custom_call" | custom-call | tf_op jit(solution)/shard_map/pallas_call | solution.py:21
  84.9 5.1 %collective-permute-start.19 = (f32[19,16,128]{2,1,0:T(8,128)S(1)}, f32[19,16,128]{2,1,0:T(8,128)S(1)}, u32[]{:S(2)}, u32[]{:S(2)}) collective-permute-start(f32[19,16,128]{2,1,0:T(8,128)S(1)} %get-tuple-element.73), channel_id=1, source_target_pairs={{0,8},{1,9},{2,10},{3,11},{12,4},{13,5},{14,6},{15,7},{8,16},{9,17... | collective-permute-start | bytes 466952 | tf_op jit(solution)/shard_map/ppermute | solution.py:613
  90.0 1.7 %collective-permute-start.20 = (f32[8,128]{1,0:T(8,128)S(1)}, f32[8,128]{1,0:T(8,128)S(1)}, u32[]{:S(2)}, u32[]{:S(2)}) collective-permute-start(f32[8,128]{1,0:T(8,128)S(1)} %get-tuple-element.72), channel_id=1, source_target_pairs={{0,112},{8,120},{16,0},{24,8},{32,16},{40,24},{48,32},{56,40},{64,... | collective-permute-start | bytes 12296 | tf_op jit(solution)/shard_map/ppermute | solution.py:678
  91.7 2.3 %collective-permute-done.20 = f32[8,128]{1,0:T(8,128)S(1)} collective-permute-done((f32[8,128]{1,0:T(8,128)S(1)}, f32[8,128]{1,0:T(8,128)S(1)}, u32[]{:S(2)}, u32[]{:S(2)}) %collective-permute-start.20) | collective-permute-done | bytes 4128 | tf_op jit(solution)/shard_map/ppermute | solution.py:678
  94.0 0.5 collective-permute-start.21
  94.5 1.0 collective-permute-done.21.two
  95.6 5.0 %collective-permute-start.22 = (f32[8,128]{1,0:T(8,128)S(1)}, f32[8,128]{1,0:T(8,128)S(1)}, u32[]{:S(2)}, u32[]{:S(2)}) collective-permute-start(f32[8,128]{1,0:T(8,128)S(1)} %fusion.1.sum_0), channel_id=1, source_target_pairs={{0,32},{1,33},{2,34},{3,35},{4,100},{5,101},{6,102},{7,103},{8,40}... | collective-permute-start | bytes 12296 | tf_op jit(solution)/shard_map/ppermute | solution.py:627
  100.5 0.0 collective-permute-start.23
  100.5 0.8 collective-permute-done.22.sum_1
  101.3 1.5 %collective-permute-start.24 = (f32[8,128]{1,0:T(8,128)S(1)}, f32[8,128]{1,0:T(8,128)S(1)}, u32[]{:S(2)}, u32[]{:S(2)}) collective-permute-start(f32[8,128]{1,0:T(8,128)S(1)} %collective-permute-done.22.sum_1), channel_id=1, source_target_pairs={{0,4},{4,0},{1,5},{5,1},{2,6},{6,2},{3,7},{7,3},{8,12},{12,8},{9,1... | collective-permute-start | bytes 12296 | tf_op jit(solution)/shard_map/ppermute | solution.py:604
  102.8 2.9 %shard_map.55.es = f32[22,16,128]{2,1,0:T(8,128)S(1)} custom-call(s32[2]{0:T(128)S(1)} %pad_add_fusion.meta, f32[22,16,128]{2,1,0:T(8,128)S(1)} %get-tuple-element.76.rb, f32[19,16,128]{2,1,0:T(8,128)S(1)} %collective-permute-done.19.one, f32[19,16,128]{2,1,0:T(8,128)S(1)} %collective-permute-done.21.two), custom_call_target="tpu_custom_call" | custom-call | tf_op jit(solution)/shard_map/pallas_call | solution.py:21
  105.7 0.0 collective-permute-done.23.sum_2
  105.7 0.0 collective-permute-done.24.sum_3
  105.7 4.5 %shard_map.56 = f32[1,32,32,128]{3,2,1,0:T(8,128)} custom-call(s32[2]{0:T(128)S(1)} %pad_add_fusion.meta, s32[16,8]{1,0:T(8,128)S(1)} %copy.13.bricks, f32[8,128]{1,0:T(8,128)S(1)} %fusion.1.sum_0, f32[8,128]{1,0:T(8,128)S(1)} %collective-permute-done.22.sum_1, f32[8,128]{1,0:T(8,128)S(1)} %collective-permute-done.23.sum_2, ...), custom_call_target="tpu_custom_call" | custom-call | tf_op jit(solution)/shard_map/pallas_call | solution.py:21
  (19 shorter events, 0.0 us)
Async XLA Ops:
  0.8 1.0 copy-start
  1.9 1.0 copy-start.2
  2.9 1.0 copy-start.4
  26.5 6.6 %collective-permute-start = (f32[4,17,8,128]{3,2,1,0:T(8,128)S(1)}, f32[4,17,8,128]{3,2,1,0:T(8,128)S(1)}, u32[]{:S(2)}, u32[]{:S(2)}) collective-permute-start(f32[4,17,8,128]{3,2,1,0:T(8,128)S(1)} %shard_map.47), channel_id=1, source_target_pairs={{8,0},{9,1},{10,2},{11,3},{4,12},{5,13},{6,14},{7,15},{16,8},{17,9... | collective-permute-start | bytes 835592 | tf_op jit(solution)/shard_map/ppermute | solution.py:613
  29.6 5.8 %collective-permute-start.3 = (f32[9,16,128]{2,1,0:T(8,128)S(1)}, f32[9,16,128]{2,1,0:T(8,128)S(1)}, u32[]{:S(2)}, u32[]{:S(2)}) collective-permute-start(f32[9,16,128]{2,1,0:T(8,128)S(1)} %get-tuple-element.50.refs_0_), channel_id=1, source_target_pairs={{0,3},{1,0},{2,1},{3,2},{4,7},{5,4},{6,5},{7,6},{8,11},{9,8},{10,9... | collective-permute-start | bytes 221192 | tf_op jit(solution)/shard_map/ppermute | solution.py:617
  30.6 5.5 %collective-permute-start.2 = (f32[9,16,128]{2,1,0:T(8,128)S(1)}, f32[9,16,128]{2,1,0:T(8,128)S(1)}, u32[]{:S(2)}, u32[]{:S(2)}) collective-permute-start(f32[9,16,128]{2,1,0:T(8,128)S(1)} %get-tuple-element.50.refs_0_), channel_id=1, source_target_pairs={{0,2},{1,3},{2,0},{3,1},{4,6},{5,7},{6,4},{7,5},{8,10},{9,11},{10,... | collective-permute-start | bytes 221192 | tf_op jit(solution)/shard_map/ppermute | solution.py:617
  32.1 5.7 %collective-permute-start.1 = (f32[9,16,128]{2,1,0:T(8,128)S(1)}, f32[9,16,128]{2,1,0:T(8,128)S(1)}, u32[]{:S(2)}, u32[]{:S(2)}) collective-permute-start(f32[9,16,128]{2,1,0:T(8,128)S(1)} %get-tuple-element.50.refs_0_), channel_id=1, source_target_pairs={{0,1},{1,2},{2,3},{3,0},{4,5},{5,6},{6,7},{7,4},{8,9},{9,10},{10,1... | collective-permute-start | bytes 221192 | tf_op jit(solution)/shard_map/ppermute | solution.py:617
  35.4 22.3 %copy-start.1 = (f32[1,32,32,128]{3,2,1,0:T(8,128)S(1)}, f32[1,32,32,128]{3,2,1,0:T(8,128)}, u32[]{:S(2)}) copy-start(f32[1,32,32,128]{3,2,1,0:T(8,128)} %u.3) | copy-start | bytes 1572868
  35.4 22.3 %copy-start.3 = (f32[1,32,32,128]{3,2,1,0:T(8,128)S(1)}, f32[1,32,32,128]{3,2,1,0:T(8,128)}, u32[]{:S(2)}) copy-start(f32[1,32,32,128]{3,2,1,0:T(8,128)} %f.3) | copy-start | bytes 1572868
  35.4 22.3 %copy-start.5 = (f32[1,32,32,128]{3,2,1,0:T(8,128)S(1)}, f32[1,32,32,128]{3,2,1,0:T(8,128)}, u32[]{:S(2)}) copy-start(f32[1,32,32,128]{3,2,1,0:T(8,128)} %a.3) | copy-start | bytes 1572868
  37.8 19.9 %all-to-all-start.1 = ((f32[8,35,8,128]{3,2,1,0:T(8,128)}), f32[8,35,8,128]{3,2,1,0:T(8,128)S(1)}, u32[]{:S(2)}, u32[]{:S(2)}) async-start(f32[8,35,8,128]{3,2,1,0:T(8,128)} %shard_map.48), calls=%async_computation.1 | async-start | bytes 2293760 | tf_op jit(solution)/shard_map/all_to_all | solution.py:631
  41.6 1.3 %collective-permute-start.4 = (f32[9,16,128]{2,1,0:T(8,128)S(1)}, f32[9,16,128]{2,1,0:T(8,128)S(1)}, u32[]{:S(2)}, u32[]{:S(2)}) collective-permute-start(f32[9,16,128]{2,1,0:T(8,128)S(1)} %get-tuple-element.50.refs_0_), channel_id=1, source_target_pairs={{0,4},{4,0},{1,5},{5,1},{2,6},{6,2},{3,7},{7,3},{8,12},{12,8},{9,1... | collective-permute-start | bytes 221192 | tf_op jit(solution)/shard_map/ppermute | solution.py:604
  41.8 1.3 %collective-permute-start.5 = (f32[9,16,128]{2,1,0:T(8,128)S(1)}, f32[9,16,128]{2,1,0:T(8,128)S(1)}, u32[]{:S(2)}, u32[]{:S(2)}) collective-permute-start(f32[9,16,128]{2,1,0:T(8,128)S(1)} %collective-permute-done.1.refs_1_), channel_id=1, source_target_pairs={{0,4},{4,0},{1,5},{5,1},{2,6},{6,2},{3,7},{7,3},{8,12},{12,8},{9,1... | collective-permute-start | bytes 221192 | tf_op jit(solution)/shard_map/ppermute | solution.py:604
  42.2 1.3 %collective-permute-start.6 = (f32[9,16,128]{2,1,0:T(8,128)S(1)}, f32[9,16,128]{2,1,0:T(8,128)S(1)}, u32[]{:S(2)}, u32[]{:S(2)}) collective-permute-start(f32[9,16,128]{2,1,0:T(8,128)S(1)} %collective-permute-done.2.refs_2_), channel_id=1, source_target_pairs={{0,4},{4,0},{1,5},{5,1},{2,6},{6,2},{3,7},{7,3},{8,12},{12,8},{9,1... | collective-permute-start | bytes 221192 | tf_op jit(solution)/shard_map/ppermute | solution.py:604
  42.3 1.3 %collective-permute-start.7 = (f32[9,16,128]{2,1,0:T(8,128)S(1)}, f32[9,16,128]{2,1,0:T(8,128)S(1)}, u32[]{:S(2)}, u32[]{:S(2)}) collective-permute-start(f32[9,16,128]{2,1,0:T(8,128)S(1)} %collective-permute-done.3.refs_3_), channel_id=1, source_target_pairs={{0,4},{4,0},{1,5},{5,1},{2,6},{6,2},{3,7},{7,3},{8,12},{12,8},{9,1... | collective-permute-start | bytes 221192 | tf_op jit(solution)/shard_map/ppermute | solution.py:604
  44.3 7.2 %collective-permute-start.8 = (f32[4,7,16,128]{3,2,1,0:T(8,128)S(1)}, f32[4,7,16,128]{3,2,1,0:T(8,128)S(1)}, u32[]{:S(2)}, u32[]{:S(2)}) collective-permute-start(f32[4,7,16,128]{3,2,1,0:T(8,128)S(1)} %shard_map.49), channel_id=1, source_target_pairs={{0,8},{1,9},{2,10},{3,11},{12,4},{13,5},{14,6},{15,7},{8,16},{9,17... | collective-permute-start | bytes 688136 | tf_op jit(solution)/shard_map/ppermute | solution.py:613
  51.5 1.6 %collective-permute-start.9 = (f32[4,7,16,128]{3,2,1,0:T(8,128)S(1)}, f32[4,7,16,128]{3,2,1,0:T(8,128)S(1)}, u32[]{:S(2)}, u32[]{:S(2)}) collective-permute-start(f32[4,7,16,128]{3,2,1,0:T(8,128)S(1)} %collective-permute-done.8.refs_8_), channel_id=1, source_target_pairs={{0,4},{4,0},{1,5},{5,1},{2,6},{6,2},{3,7},{7,3},{8,12},{12,8},{9,1... | collective-permute-start | bytes 688136 | tf_op jit(solution)/shard_map/ppermute | solution.py:604
  53.1 0.7 copy-start.6
  57.7 16.4 %copy-start.7 = (f32[4,7,16,128]{3,2,1,0:T(8,128)S(1)}, f32[4,7,16,128]{3,2,1,0:T(8,128)}, u32[]{:S(2)}) copy-start(f32[4,7,16,128]{3,2,1,0:T(8,128)} %copy-done.6) | copy-start | bytes 688132
  62.3 3.2 %collective-permute-start.12 = (f32[8,16,128]{2,1,0:T(8,128)S(1)}, f32[8,16,128]{2,1,0:T(8,128)S(1)}, u32[]{:S(2)}, u32[]{:S(2)}) collective-permute-start(f32[8,16,128]{2,1,0:T(8,128)S(1)} %get-tuple-element.55.refs_0_), channel_id=1, source_target_pairs={{0,3},{1,0},{2,1},{3,2},{4,7},{5,4},{6,5},{7,6},{8,11},{9,8},{10,9... | collective-permute-start | bytes 196616 | tf_op jit(solution)/shard_map/ppermute | solution.py:617
  63.4 4.6 %collective-permute-start.11 = (f32[8,16,128]{2,1,0:T(8,128)S(1)}, f32[8,16,128]{2,1,0:T(8,128)S(1)}, u32[]{:S(2)}, u32[]{:S(2)}) collective-permute-start(f32[8,16,128]{2,1,0:T(8,128)S(1)} %get-tuple-element.55.refs_0_), channel_id=1, source_target_pairs={{0,2},{1,3},{2,0},{3,1},{4,6},{5,7},{6,4},{7,5},{8,10},{9,11},{10,... | collective-permute-start | bytes 196616 | tf_op jit(solution)/shard_map/ppermute | solution.py:617
  64.8 5.7 %collective-permute-start.10 = (f32[8,16,128]{2,1,0:T(8,128)S(1)}, f32[8,16,128]{2,1,0:T(8,128)S(1)}, u32[]{:S(2)}, u32[]{:S(2)}) collective-permute-start(f32[8,16,128]{2,1,0:T(8,128)S(1)} %get-tuple-element.55.refs_0_), channel_id=1, source_target_pairs={{0,1},{1,2},{2,3},{3,0},{4,5},{5,6},{6,7},{7,4},{8,9},{9,10},{10,1... | collective-permute-start | bytes 196616 | tf_op jit(solution)/shard_map/ppermute | solution.py:617
  64.8 6.4 %collective-permute-start.13 = (f32[8,16,128]{2,1,0:T(8,128)S(1)}, f32[8,16,128]{2,1,0:T(8,128)S(1)}, u32[]{:S(2)}, u32[]{:S(2)}) collective-permute-start(f32[8,16,128]{2,1,0:T(8,128)S(1)} %get-tuple-element.55.refs_0_), channel_id=1, source_target_pairs={{0,4},{4,0},{1,5},{5,1},{2,6},{6,2},{3,7},{7,3},{8,12},{12,8},{9,1... | collective-permute-start | bytes 196616 | tf_op jit(solution)/shard_map/ppermute | solution.py:604
  65.5 5.6 %collective-permute-start.16 = (f32[8,16,128]{2,1,0:T(8,128)S(1)}, f32[8,16,128]{2,1,0:T(8,128)S(1)}, u32[]{:S(2)}, u32[]{:S(2)}) collective-permute-start(f32[8,16,128]{2,1,0:T(8,128)S(1)} %collective-permute-done.12.refs_3_), channel_id=1, source_target_pairs={{0,4},{4,0},{1,5},{5,1},{2,6},{6,2},{3,7},{7,3},{8,12},{12,8},{9,1... | collective-permute-start | bytes 196616 | tf_op jit(solution)/shard_map/ppermute | solution.py:604
  68.0 3.4 %collective-permute-start.15 = (f32[8,16,128]{2,1,0:T(8,128)S(1)}, f32[8,16,128]{2,1,0:T(8,128)S(1)}, u32[]{:S(2)}, u32[]{:S(2)}) collective-permute-start(f32[8,16,128]{2,1,0:T(8,128)S(1)} %collective-permute-done.11.refs_2_), channel_id=1, source_target_pairs={{0,4},{4,0},{1,5},{5,1},{2,6},{6,2},{3,7},{7,3},{8,12},{12,8},{9,1... | collective-permute-start | bytes 196616 | tf_op jit(solution)/shard_map/ppermute | solution.py:604
  70.5 1.6 %collective-permute-start.14 = (f32[8,16,128]{2,1,0:T(8,128)S(1)}, f32[8,16,128]{2,1,0:T(8,128)S(1)}, u32[]{:S(2)}, u32[]{:S(2)}) collective-permute-start(f32[8,16,128]{2,1,0:T(8,128)S(1)} %collective-permute-done.10.refs_1_), channel_id=1, source_target_pairs={{0,4},{4,0},{1,5},{5,1},{2,6},{6,2},{3,7},{7,3},{8,12},{12,8},{9,1... | collective-permute-start | bytes 196616 | tf_op jit(solution)/shard_map/ppermute | solution.py:604
  72.8 6.2 %collective-permute-start.17 = (f32[4,5,16,128]{3,2,1,0:T(8,128)S(1)}, f32[4,5,16,128]{3,2,1,0:T(8,128)S(1)}, u32[]{:S(2)}, u32[]{:S(2)}) collective-permute-start(f32[4,5,16,128]{3,2,1,0:T(8,128)S(1)} %shard_map.51), channel_id=1, source_target_pairs={{0,8},{1,9},{2,10},{3,11},{12,4},{13,5},{14,6},{15,7},{8,16},{9,17... | collective-permute-start | bytes 491528 | tf_op jit(solution)/shard_map/ppermute | solution.py:613
  79.0 3.3 %collective-permute-start.18 = (f32[4,5,16,128]{3,2,1,0:T(8,128)S(1)}, f32[4,5,16,128]{3,2,1,0:T(8,128)S(1)}, u32[]{:S(2)}, u32[]{:S(2)}) collective-permute-start(f32[4,5,16,128]{3,2,1,0:T(8,128)S(1)} %collective-permute-done.17.refs_8_), channel_id=1, source_target_pairs={{0,4},{4,0},{1,5},{5,1},{2,6},{6,2},{3,7},{7,3},{8,12},{12,8},{9,1... | collective-permute-start | bytes 491528 | tf_op jit(solution)/shard_map/ppermute | solution.py:604
  84.9 9.1 %collective-permute-start.19 = (f32[19,16,128]{2,1,0:T(8,128)S(1)}, f32[19,16,128]{2,1,0:T(8,128)S(1)}, u32[]{:S(2)}, u32[]{:S(2)}) collective-permute-start(f32[19,16,128]{2,1,0:T(8,128)S(1)} %get-tuple-element.73), channel_id=1, source_target_pairs={{0,8},{1,9},{2,10},{3,11},{12,4},{13,5},{14,6},{15,7},{8,16},{9,17... | collective-permute-start | bytes 466952 | tf_op jit(solution)/shard_map/ppermute | solution.py:613
  90.0 4.0 %collective-permute-start.20 = (f32[8,128]{1,0:T(8,128)S(1)}, f32[8,128]{1,0:T(8,128)S(1)}, u32[]{:S(2)}, u32[]{:S(2)}) collective-permute-start(f32[8,128]{1,0:T(8,128)S(1)} %get-tuple-element.72), channel_id=1, source_target_pairs={{0,112},{8,120},{16,0},{24,8},{32,16},{40,24},{48,32},{56,40},{64,... | collective-permute-start | bytes 12296 | tf_op jit(solution)/shard_map/ppermute | solution.py:678
  94.0 1.5 %collective-permute-start.21 = (f32[19,16,128]{2,1,0:T(8,128)S(1)}, f32[19,16,128]{2,1,0:T(8,128)S(1)}, u32[]{:S(2)}, u32[]{:S(2)}) collective-permute-start(f32[19,16,128]{2,1,0:T(8,128)S(1)} %collective-permute-done.19.one), channel_id=1, source_target_pairs={{0,4},{4,0},{1,5},{5,1},{2,6},{6,2},{3,7},{7,3},{8,12},{12,8},{9,1... | collective-permute-start | bytes 466952 | tf_op jit(solution)/shard_map/ppermute | solution.py:604
  95.6 5.7 %collective-permute-start.22 = (f32[8,128]{1,0:T(8,128)S(1)}, f32[8,128]{1,0:T(8,128)S(1)}, u32[]{:S(2)}, u32[]{:S(2)}) collective-permute-start(f32[8,128]{1,0:T(8,128)S(1)} %fusion.1.sum_0), channel_id=1, source_target_pairs={{0,32},{1,33},{2,34},{3,35},{4,100},{5,101},{6,102},{7,103},{8,40}... | collective-permute-start | bytes 12296 | tf_op jit(solution)/shard_map/ppermute | solution.py:627
  100.5 5.1 %collective-permute-start.23 = (f32[8,128]{1,0:T(8,128)S(1)}, f32[8,128]{1,0:T(8,128)S(1)}, u32[]{:S(2)}, u32[]{:S(2)}) collective-permute-start(f32[8,128]{1,0:T(8,128)S(1)} %fusion.1.sum_0), channel_id=1, source_target_pairs={{0,64},{8,72},{16,80},{24,88},{32,96},{40,104},{48,112},{56,120},{... | collective-permute-start | bytes 12296 | tf_op jit(solution)/shard_map/ppermute | solution.py:627
  101.3 4.4 %collective-permute-start.24 = (f32[8,128]{1,0:T(8,128)S(1)}, f32[8,128]{1,0:T(8,128)S(1)}, u32[]{:S(2)}, u32[]{:S(2)}) collective-permute-start(f32[8,128]{1,0:T(8,128)S(1)} %collective-permute-done.22.sum_1), channel_id=1, source_target_pairs={{0,4},{4,0},{1,5},{5,1},{2,6},{6,2},{3,7},{7,3},{8,12},{12,8},{9,1... | collective-permute-start | bytes 12296 | tf_op jit(solution)/shard_map/ppermute | solution.py:604

commit v10 on v9

--- a/solution.py
+++ b/solution.py
@@ -50,8 +50,9 @@
 
 ARRAYS = 5
 FACE = 17
-SENT_Y, SENT_X, SENT = 17, 27, 30
-GOT_ROWS, GOT_STRIPS, GOT_Y, GOT_X, GOT = 17, 20, 22, 32, 35
+SENT_Y, SENT_X, SENT = 17, 26, 29
+GOT_ROWS, GOT_STRIPS, GOT_Y, GOT_X, GOT = 17, 20, 22, 31, 34
+ROOM = (2, 4, 7)
 
 
 def face_planes(j):
@@ -75,6 +76,8 @@
 def pack_shell(get, out, bit_x, bit_y):
     x0, y0 = is_zero(bit_x), is_zero(bit_y)
     mask = odd(32, 128)
+    row = iota((8, 128), 0)
+    free = (y0 & (row < 2)) | (jnp.logical_not(y0) & (row >= 6))
     for k in range(8):
         high, j = k >= 4, k % 4
         for i, (c, far) in enumerate(face_planes(j)):
@@ -83,14 +86,19 @@
         one, two = get(1, t), swap_lanes(get(3, t))
         both = jnp.where(mask, one, two) if high else jnp.where(mask, two, one)
         out[k, 16] = both[8 * j : 8 * j + 8]
-        strips = []
+        strips, rows = [], []
         for tl in range(2):
             for c in range(ARRAYS):
                 v = get(c, 2 * k + tl)
-                out[k, SENT_Y + tl * ARRAYS + c] = jnp.where(y0, v[24:32], v[0:8])
+                rows.append(jnp.where(y0, v[24:32], v[0:8]))
                 for g in range(4):
                     tile = v[8 * g : 8 * g + 8]
                     strips.append(jnp.where(x0, pltpu.roll(tile, 8, 1), tile))
+        last = rows.pop()
+        for i, at in enumerate(ROOM):
+            rows[at] = jnp.where(free, pltpu.roll(last, 6 - 2 * i, 0), rows[at])
+        for i, tile in enumerate(rows):
+            out[k, SENT_Y + i] = tile
         for i in range(3):
             out[k, SENT_X + i] = merge_strips(list(enumerate(strips[16 * i : 16 * i + 16])))
 
@@ -132,7 +140,7 @@
             out[dest, GOT_ROWS + i] = tile
         strips = [strip_of(faces[at_x, i]) for i in range(16)] + [strip_of(tile) for tile in rows_of(at_xy)]
         from_y, from_x, from_xy = bricks[slab, p ^ 2], bricks[slab, p ^ 1], bricks[slab, p ^ 3]
-        strips += [strip_of(recv[from_xy, SENT_Y + i]) for i in range(2 * ARRAYS)]
+        strips += [strip_of(recv[from_xy, SENT_Y + i]) for i in range(SENT_X - SENT_Y)]
         for i in range(2):
             out[dest, GOT_STRIPS + i] = merge_strips(list(enumerate(strips[16 * i : 16 * i + 16])))
         out[dest, GOT_Y:GOT_X] = recv[from_y, SENT_Y:SENT_X]
@@ -159,6 +167,13 @@
         one, shared, last = tiles
         moved = jnp.where(y0, pltpu.roll(shared, 3, 0), pltpu.roll(shared, 5, 0))
         return [one, jnp.where(five, shared, 0.0), jnp.where(three, moved, 0.0), last]
+
+    def with_last(tiles):
+        pair = jnp.where(y0, row >> 1, (row >> 1) - 1)
+        last = jnp.zeros((8, 128), F32)
+        for i, at in enumerate(ROOM):
+            last = jnp.where(pair == i, pltpu.roll(tiles[at], 2 + 2 * i, 0), last)
+        return tiles + [last]
 
     for k in range(8):
         high, j = k >= 4, k % 4
@@ -179,12 +194,14 @@
             grids[c][at, 8 * j : 8 * j + 8, 0:128] = cells
             grids[c][at, 8 * j : 8 * j + 8, 128:256] = jnp.zeros((8, 128), F32)
             grids[c][at, 32:40] = jnp.zeros((8, 256), F32)
+        rows = with_last([recv[k, GOT_Y + i] for i in range(GOT_X - GOT_Y)])
+        sides = with_last([strip(recv[k, GOT_STRIPS + 1], 3 + i) for i in range(GOT_X - GOT_Y)])
         for tl in range(2):
             for c in range(ARRAYS):
                 i = tl * ARRAYS + c
                 at = OWN + 2 * k + tl
-                grids[c][at, 32:40, 0:128] = cut(c, recv[k, GOT_Y + i])
-                grids[c][at, 32:40, 128:256] = cut(c, strip(recv[k, GOT_STRIPS + 1], 3 + i))
+                grids[c][at, 32:40, 0:128] = cut(c, rows[i])
+                grids[c][at, 32:40, 128:256] = cut(c, sides[i])
                 for g in range(4):
                     n = 4 * i + g
                     side = strip(recv[k, GOT_X + n // 16], n % 16)

time: 111 us -> 110 us (level)
  no operation moved by 1% of the time
where the time goes in v10:
time: 110 us
  starting transfers between devices  38.5 us (35%)
  Pallas kernels  24.9 us (23%)
  waiting for transfers between devices  21.8 us (20%)
  blocking collectives  19.7 us (18%)
  local copies, waits for them, and re-layouts  4.58 us (4%)
    pallas_call x11, Pallas kernels, run(): pl.pallas_call(kernel, out_shape=shapes[0] if single else shapes, in_spec...  24.9 us
    all_to_all x1, blocking collectives, among(): return lax.all_to_all(x, LB, split_axis=0, concat_axis=0, tiled=True)  19.7 us
    ppermute x12, starting transfers between devices, swap_cores(): return lax.ppermute(x, 'level', [(0, 1), (1, 0)])  11.8 us
    ppermute x4, starting transfers between devices, to_slabs(): return lax.ppermute(x, ALL, pairs)  10.8 us
    ppermute x4, waiting for transfers between devices, to_slabs(): return lax.ppermute(x, ALL, pairs)  7.53 us
    ppermute x2, starting transfers between devices, fours_apart(): return (lax.ppermute(x, ALL, beside), lax.ppermute(x, 'slab', across))  5.06 us
    ppermute x12, waiting for transfers between devices, swap_cores(): return lax.ppermute(x, 'level', [(0, 1), (1, 0)])  4.98 us
    ppermute x6, starting transfers between devices, around_chips(): lax.ppermute(x, 'bottom', [(i, (i + d) % 4) for i in range(4)])  4.94 us
  transfers between devices with their start and end apart: 26, of which 18 were waited for; matrix products, arithmetic and copies ran while one was open for 0% of the time, Pallas kernels for 9%

profile of v10, /device:TPU:1, one launch (start us, length us, event | category | flops | bytes accessed | tf_op | source)
XLA Modules:
  0.0 109.8 jit_solution(6396697474261005027)
XLA Ops:
  0.0 0.8 copy.13.bricks
  0.8 0.1 pad_add_fusion.meta
  0.8 1.0 copy-done
  1.9 1.0 copy-done.2
  2.9 1.0 copy-done.4
  4.0 1.7 %shard_map.46 = (f32[8,29,8,128]{3,2,1,0:T(8,128)S(1)}, f32[9,16,128]{2,1,0:T(8,128)S(1)}) custom-call(s32[2]{0:T(128)S(1)} %pad_add_fusion.meta, s32[16,8]{1,0:T(8,128)S(1)} %copy.13.bricks, f32[1,32,32,128]{3,2,1,0:T(8,128)S(1)} %copy-done, f32[1,32,32,128]{3,2,1,0:T(8,128)S(1)} %copy-done.2, f32[1,32,32,128]{3,2,1,0:T(8,128)S(1)} %copy-done.4), custom_call_target="tpu_custom_call" | custom-call | tf_op jit(solution)/shard_map/pallas_call | solution.py:21
  5.7 19.7 %all_to_all.10.recv = f32[8,29,8,128]{3,2,1,0:T(8,128)S(1)} all-to-all(f32[8,29,8,128]{3,2,1,0:T(8,128)S(1)} %get-tuple-element.45), channel_id=1, replica_groups=mesh['slab'=16,'level'=2,'bottom'=4] {'level','bottom'}, dimensions={0} | all-to-all | bytes 1900544 | tf_op jit(solution)/shard_map/all_to_all | solution.py:648
  25.4 0.7 shard_map.47
  26.1 3.1 %collective-permute-start = (f32[4,17,8,128]{3,2,1,0:T(8,128)S(1)}, f32[4,17,8,128]{3,2,1,0:T(8,128)S(1)}, u32[]{:S(2)}, u32[]{:S(2)}) collective-permute-start(f32[4,17,8,128]{3,2,1,0:T(8,128)S(1)} %shard_map.47), channel_id=1, source_target_pairs={{8,0},{9,1},{10,2},{11,3},{4,12},{5,13},{6,14},{7,15},{16,8},{17,9... | collective-permute-start | bytes 835592 | tf_op jit(solution)/shard_map/ppermute | solution.py:630
  29.2 1.0 collective-permute-start.3
  30.3 1.5 %collective-permute-start.2 = (f32[9,16,128]{2,1,0:T(8,128)S(1)}, f32[9,16,128]{2,1,0:T(8,128)S(1)}, u32[]{:S(2)}, u32[]{:S(2)}) collective-permute-start(f32[9,16,128]{2,1,0:T(8,128)S(1)} %get-tuple-element.50.refs_0_), channel_id=1, source_target_pairs={{0,2},{1,3},{2,0},{3,1},{4,6},{5,7},{6,4},{7,5},{8,10},{9,11},{10,... | collective-permute-start | bytes 221192 | tf_op jit(solution)/shard_map/ppermute | solution.py:634
  31.7 0.0 collective-permute-start.1
  31.7 0.9 collective-permute-done.cross
  32.7 2.3 %shard_map.48 = f32[8,34,8,128]{3,2,1,0:T(8,128)} custom-call(s32[2]{0:T(128)S(1)} %pad_add_fusion.meta, s32[16,8]{1,0:T(8,128)S(1)} %copy.13.bricks, f32[8,29,8,128]{3,2,1,0:T(8,128)S(1)} %all_to_all.10.recv, f32[4,17,8,128]{3,2,1,0:T(8,128)S(1)} %collective-permute-done.cross), custom_call_target="tpu_custom_call" | custom-call | tf_op jit(solution)/shard_map/pallas_call | solution.py:21
  35.0 0.7 collective-permute-done.2.refs_2_
  35.8 1.6 %collective-permute-done.1.refs_1_ = f32[9,16,128]{2,1,0:T(8,128)S(1)} collective-permute-done((f32[9,16,128]{2,1,0:T(8,128)S(1)}, f32[9,16,128]{2,1,0:T(8,128)S(1)}, u32[]{:S(2)}, u32[]{:S(2)}) %collective-permute-start.1) | collective-permute-done | bytes 73760 | tf_op jit(solution)/shard_map/ppermute | solution.py:634
  37.4 3.9 %all-to-all-start.1 = ((f32[8,34,8,128]{3,2,1,0:T(8,128)}), f32[8,34,8,128]{3,2,1,0:T(8,128)S(1)}, u32[]{:S(2)}, u32[]{:S(2)}) async-start(f32[8,34,8,128]{3,2,1,0:T(8,128)} %shard_map.48), calls=%async_computation.1 | async-start | bytes 2228224 | tf_op jit(solution)/shard_map/all_to_all | solution.py:648
  41.3 0.2 collective-permute-start.4
  41.5 0.3 collective-permute-start.5
  41.8 0.2 collective-permute-start.6
  42.0 0.3 collective-permute-start.7
  42.3 0.2 collective-permute-done.4.refs_4_
  42.6 0.2 collective-permute-done.5.refs_5_
  42.7 0.3 collective-permute-done.6.refs_6_
  43.1 0.2 collective-permute-done.7.refs_7_
  43.2 0.7 shard_map.49
  44.0 1.3 %collective-permute-start.8 = (f32[4,7,16,128]{3,2,1,0:T(8,128)S(1)}, f32[4,7,16,128]{3,2,1,0:T(8,128)S(1)}, u32[]{:S(2)}, u32[]{:S(2)}) collective-permute-start(f32[4,7,16,128]{3,2,1,0:T(8,128)S(1)} %shard_map.49), channel_id=1, source_target_pairs={{0,8},{1,9},{2,10},{3,11},{12,4},{13,5},{14,6},{15,7},{8,16},{9,17... | collective-permute-start | bytes 688136 | tf_op jit(solution)/shard_map/ppermute | solution.py:630
  45.3 5.9 %collective-permute-done.8.refs_8_ = f32[4,7,16,128]{3,2,1,0:T(8,128)S(1)} collective-permute-done((f32[4,7,16,128]{3,2,1,0:T(8,128)S(1)}, f32[4,7,16,128]{3,2,1,0:T(8,128)S(1)}, u32[]{:S(2)}, u32[]{:S(2)}) %collective-permute-start.8) | collective-permute-done | bytes 229408 | tf_op jit(solution)/shard_map/ppermute | solution.py:630
  51.2 0.5 collective-permute-start.9
  51.7 1.1 %collective-permute-done.9.refs_9_ = f32[4,7,16,128]{3,2,1,0:T(8,128)S(1)} collective-permute-done((f32[4,7,16,128]{3,2,1,0:T(8,128)S(1)}, f32[4,7,16,128]{3,2,1,0:T(8,128)S(1)}, u32[]{:S(2)}, u32[]{:S(2)}) %collective-permute-start.9) | collective-permute-done | bytes 229408 | tf_op jit(solution)/shard_map/ppermute | solution.py:621
  52.8 0.7 copy-done.6
  53.5 3.5 %all-to-all-done.1.recv = f32[8,34,8,128]{3,2,1,0:T(8,128)S(1)} async-done(((f32[8,34,8,128]{3,2,1,0:T(8,128)}), f32[8,34,8,128]{3,2,1,0:T(8,128)S(1)}, u32[]{:S(2)}, u32[]{:S(2)}) %all-to-all-start.1) | async-done | bytes 1114144 | tf_op jit(solution)/shard_map/all_to_all | solution.py:648
  57.0 4.5 %shard_map.50 = (f32[8,16,128]{2,1,0:T(8,128)S(1)}, f32[26,40,256]{2,1,0:T(8,128)S(1)}, f32[26,40,256]{2,1,0:T(8,128)S(1)}, f32[26,40,256]{2,1,0:T(8,128)S(1)}, ...) custom-call(s32[2]{0:T(128)S(1)} %pad_add_fusion.meta, s32[16,8]{1,0:T(8,128)S(1)} %copy.13.bricks, ...), custom_call_target="tpu_custom_call" | custom-call | tf_op jit(solution)/shard_map/pallas_call | solution.py:21
  61.5 1.1 collective-permute-start.12
  62.6 1.4 %collective-permute-start.11 = (f32[8,16,128]{2,1,0:T(8,128)S(1)}, f32[8,16,128]{2,1,0:T(8,128)S(1)}, u32[]{:S(2)}, u32[]{:S(2)}) collective-permute-start(f32[8,16,128]{2,1,0:T(8,128)S(1)} %get-tuple-element.55.refs_0_), channel_id=1, source_target_pairs={{0,2},{1,3},{2,0},{3,1},{4,6},{5,7},{6,4},{7,5},{8,10},{9,11},{10,... | collective-permute-start | bytes 196616 | tf_op jit(solution)/shard_map/ppermute | solution.py:634
  63.9 0.0 collective-permute-start.10
  63.9 0.8 collective-permute-start.13
  64.7 0.0 collective-permute-done.12.refs_3_
  64.7 2.1 %collective-permute-start.16 = (f32[8,16,128]{2,1,0:T(8,128)S(1)}, f32[8,16,128]{2,1,0:T(8,128)S(1)}, u32[]{:S(2)}, u32[]{:S(2)}) collective-permute-start(f32[8,16,128]{2,1,0:T(8,128)S(1)} %collective-permute-done.12.refs_3_), channel_id=1, source_target_pairs={{0,4},{4,0},{1,5},{5,1},{2,6},{6,2},{3,7},{7,3},{8,12},{12,8},{9,1... | collective-permute-start | bytes 196616 | tf_op jit(solution)/shard_map/ppermute | solution.py:621
  66.8 0.4 collective-permute-done.11.refs_2_
  67.2 2.5 %collective-permute-start.15 = (f32[8,16,128]{2,1,0:T(8,128)S(1)}, f32[8,16,128]{2,1,0:T(8,128)S(1)}, u32[]{:S(2)}, u32[]{:S(2)}) collective-permute-start(f32[8,16,128]{2,1,0:T(8,128)S(1)} %collective-permute-done.11.refs_2_), channel_id=1, source_target_pairs={{0,4},{4,0},{1,5},{5,1},{2,6},{6,2},{3,7},{7,3},{8,12},{12,8},{9,1... | collective-permute-start | bytes 196616 | tf_op jit(solution)/shard_map/ppermute | solution.py:621
  69.7 0.7 collective-permute-start.14
  70.4 0.0 collective-permute-done.13.refs_4_
  70.4 0.0 collective-permute-done.16.refs_7_
  70.4 0.2 collective-permute-done.15.refs_6_
  70.6 0.7 collective-permute-done.14.refs_5_
  71.3 0.7 shard_map.51
  72.0 1.3 %collective-permute-start.17 = (f32[4,5,16,128]{3,2,1,0:T(8,128)S(1)}, f32[4,5,16,128]{3,2,1,0:T(8,128)S(1)}, u32[]{:S(2)}, u32[]{:S(2)}) collective-permute-start(f32[4,5,16,128]{3,2,1,0:T(8,128)S(1)} %shard_map.51), channel_id=1, source_target_pairs={{0,8},{1,9},{2,10},{3,11},{12,4},{13,5},{14,6},{15,7},{8,16},{9,17... | collective-permute-start | bytes 491528 | tf_op jit(solution)/shard_map/ppermute | solution.py:630
  73.3 1.3 %shard_map.52 = (f32[28,32,128]{2,1,0:T(8,128)S(1)}, f32[28,32,128]{2,1,0:T(8,128)S(1)}, f32[28,32,128]{2,1,0:T(8,128)S(1)}, f32[22,16,128]{2,1,0:T(8,128)S(1)}, f32[3,8,16,128]{3,2,1,0:T(8,128)S(1)}) custom-call(s32[2]{0:T(128)S(1)} %pad_add_fusion.meta, s32[16,8]{1,0:T(8,128)S(1)} %copy.13.bricks, f32[9,16,128]{2,1,0:T(8,128)S(1)} %get-tuple-element.50.refs_0_, ...), custom_call_target="tpu_custom_call" | custom-call | tf_op jit(solution)/shard_map/pallas_call | solution.py:21
  74.6 3.0 %shard_map.53.refs_10_ = f32[16,16,128]{2,1,0:T(8,128)S(1)} custom-call(s32[2]{0:T(128)S(1)} %pad_add_fusion.meta, f32[3,8,16,128]{3,2,1,0:T(8,128)S(1)} %get-tuple-element.61.coef), custom_call_target="tpu_custom_call" | custom-call | tf_op jit(solution)/shard_map/pallas_call | solution.py:21
  77.6 0.7 collective-permute-done.17.refs_8_
  78.2 2.3 %collective-permute-start.18 = (f32[4,5,16,128]{3,2,1,0:T(8,128)S(1)}, f32[4,5,16,128]{3,2,1,0:T(8,128)S(1)}, u32[]{:S(2)}, u32[]{:S(2)}) collective-permute-start(f32[4,5,16,128]{3,2,1,0:T(8,128)S(1)} %collective-permute-done.17.refs_8_), channel_id=1, source_target_pairs={{0,4},{4,0},{1,5},{5,1},{2,6},{6,2},{3,7},{7,3},{8,12},{12,8},{9,1... | collective-permute-start | bytes 491528 | tf_op jit(solution)/shard_map/ppermute | solution.py:621
  80.6 1.0 collective-permute-done.18.refs_9_
  81.6 2.6 %shard_map.54 = (f32[22,16,128]{2,1,0:T(8,128)S(1)}, f32[19,16,128]{2,1,0:T(8,128)S(1)}, f32[8,128]{1,0:T(8,128)S(1)}, f32[28,32,128]{2,1,0:T(8,128)S(1)}, f32[2...) custom-call(s32[2]{0:T(128)S(1)} %pad_add_fusion.meta, s32[16,8]{1,0:T(8,128)S(1)} %copy.13.bricks, ...), custom_call_target="tpu_custom_call" | custom-call | tf_op jit(solution)/shard_map/pallas_call | solution.py:21
  84.2 5.1 %collective-permute-start.19 = (f32[19,16,128]{2,1,0:T(8,128)S(1)}, f32[19,16,128]{2,1,0:T(8,128)S(1)}, u32[]{:S(2)}, u32[]{:S(2)}) collective-permute-start(f32[19,16,128]{2,1,0:T(8,128)S(1)} %get-tuple-element.73), channel_id=1, source_target_pairs={{0,8},{1,9},{2,10},{3,11},{12,4},{13,5},{14,6},{15,7},{8,16},{9,17... | collective-permute-start | bytes 466952 | tf_op jit(solution)/shard_map/ppermute | solution.py:630
  89.3 2.0 %collective-permute-start.20 = (f32[8,128]{1,0:T(8,128)S(1)}, f32[8,128]{1,0:T(8,128)S(1)}, u32[]{:S(2)}, u32[]{:S(2)}) collective-permute-start(f32[8,128]{1,0:T(8,128)S(1)} %get-tuple-element.72), channel_id=1, source_target_pairs={{0,112},{8,120},{16,0},{24,8},{32,16},{40,24},{48,32},{56,40},{64,... | collective-permute-start | bytes 12296 | tf_op jit(solution)/shard_map/ppermute | solution.py:695
  91.3 2.2 %collective-permute-done.20 = f32[8,128]{1,0:T(8,128)S(1)} collective-permute-done((f32[8,128]{1,0:T(8,128)S(1)}, f32[8,128]{1,0:T(8,128)S(1)}, u32[]{:S(2)}, u32[]{:S(2)}) %collective-permute-start.20) | collective-permute-done | bytes 4128 | tf_op jit(solution)/shard_map/ppermute | solution.py:695
  93.5 0.5 collective-permute-start.21
  94.0 1.0 collective-permute-done.21.two
  95.0 5.1 %collective-permute-start.22 = (f32[8,128]{1,0:T(8,128)S(1)}, f32[8,128]{1,0:T(8,128)S(1)}, u32[]{:S(2)}, u32[]{:S(2)}) collective-permute-start(f32[8,128]{1,0:T(8,128)S(1)} %fusion.1.sum_0), channel_id=1, source_target_pairs={{0,32},{1,33},{2,34},{3,35},{4,100},{5,101},{6,102},{7,103},{8,40}... | collective-permute-start | bytes 12296 | tf_op jit(solution)/shard_map/ppermute | solution.py:644
  100.1 0.8 collective-permute-done.22.sum_1
  100.9 1.5 %collective-permute-start.24 = (f32[8,128]{1,0:T(8,128)S(1)}, f32[8,128]{1,0:T(8,128)S(1)}, u32[]{:S(2)}, u32[]{:S(2)}) collective-permute-start(f32[8,128]{1,0:T(8,128)S(1)} %collective-permute-done.22.sum_1), channel_id=1, source_target_pairs={{0,4},{4,0},{1,5},{5,1},{2,6},{6,2},{3,7},{7,3},{8,12},{12,8},{9,1... | collective-permute-start | bytes 12296 | tf_op jit(solution)/shard_map/ppermute | solution.py:621
  102.3 2.9 %shard_map.55.es = f32[22,16,128]{2,1,0:T(8,128)S(1)} custom-call(s32[2]{0:T(128)S(1)} %pad_add_fusion.meta, f32[22,16,128]{2,1,0:T(8,128)S(1)} %get-tuple-element.76.rb, f32[19,16,128]{2,1,0:T(8,128)S(1)} %collective-permute-done.19.one, f32[19,16,128]{2,1,0:T(8,128)S(1)} %collective-permute-done.21.two), custom_call_target="tpu_custom_call" | custom-call | tf_op jit(solution)/shard_map/pallas_call | solution.py:21
  105.3 4.5 %shard_map.56 = f32[1,32,32,128]{3,2,1,0:T(8,128)} custom-call(s32[2]{0:T(128)S(1)} %pad_add_fusion.meta, s32[16,8]{1,0:T(8,128)S(1)} %copy.13.bricks, f32[8,128]{1,0:T(8,128)S(1)} %fusion.1.sum_0, f32[8,128]{1,0:T(8,128)S(1)} %collective-permute-done.22.sum_1, f32[8,128]{1,0:T(8,128)S(1)} %collective-permute-done.23.sum_2, ...), custom_call_target="tpu_custom_call" | custom-call | tf_op jit(solution)/shard_map/pallas_call | solution.py:21
  (19 shorter events, 0.0 us)
Async XLA Ops:
  0.8 1.0 copy-start
  1.9 1.0 copy-start.2
  2.9 1.0 copy-start.4
  26.1 6.6 %collective-permute-start = (f32[4,17,8,128]{3,2,1,0:T(8,128)S(1)}, f32[4,17,8,128]{3,2,1,0:T(8,128)S(1)}, u32[]{:S(2)}, u32[]{:S(2)}) collective-permute-start(f32[4,17,8,128]{3,2,1,0:T(8,128)S(1)} %shard_map.47), channel_id=1, source_target_pairs={{8,0},{9,1},{10,2},{11,3},{4,12},{5,13},{6,14},{7,15},{16,8},{17,9... | collective-permute-start | bytes 835592 | tf_op jit(solution)/shard_map/ppermute | solution.py:630
  29.2 5.8 %collective-permute-start.3 = (f32[9,16,128]{2,1,0:T(8,128)S(1)}, f32[9,16,128]{2,1,0:T(8,128)S(1)}, u32[]{:S(2)}, u32[]{:S(2)}) collective-permute-start(f32[9,16,128]{2,1,0:T(8,128)S(1)} %get-tuple-element.50.refs_0_), channel_id=1, source_target_pairs={{0,3},{1,0},{2,1},{3,2},{4,7},{5,4},{6,5},{7,6},{8,11},{9,8},{10,9... | collective-permute-start | bytes 221192 | tf_op jit(solution)/shard_map/ppermute | solution.py:634
  30.3 5.5 %collective-permute-start.2 = (f32[9,16,128]{2,1,0:T(8,128)S(1)}, f32[9,16,128]{2,1,0:T(8,128)S(1)}, u32[]{:S(2)}, u32[]{:S(2)}) collective-permute-start(f32[9,16,128]{2,1,0:T(8,128)S(1)} %get-tuple-element.50.refs_0_), channel_id=1, source_target_pairs={{0,2},{1,3},{2,0},{3,1},{4,6},{5,7},{6,4},{7,5},{8,10},{9,11},{10,... | collective-permute-start | bytes 221192 | tf_op jit(solution)/shard_map/ppermute | solution.py:634
  31.7 5.7 %collective-permute-start.1 = (f32[9,16,128]{2,1,0:T(8,128)S(1)}, f32[9,16,128]{2,1,0:T(8,128)S(1)}, u32[]{:S(2)}, u32[]{:S(2)}) collective-permute-start(f32[9,16,128]{2,1,0:T(8,128)S(1)} %get-tuple-element.50.refs_0_), channel_id=1, source_target_pairs={{0,1},{1,2},{2,3},{3,0},{4,5},{5,6},{6,7},{7,4},{8,9},{9,10},{10,1... | collective-permute-start | bytes 221192 | tf_op jit(solution)/shard_map/ppermute | solution.py:634
  35.0 22.0 %copy-start.1 = (f32[1,32,32,128]{3,2,1,0:T(8,128)S(1)}, f32[1,32,32,128]{3,2,1,0:T(8,128)}, u32[]{:S(2)}) copy-start(f32[1,32,32,128]{3,2,1,0:T(8,128)} %u.3) | copy-start | bytes 1572868
  35.0 22.0 %copy-start.3 = (f32[1,32,32,128]{3,2,1,0:T(8,128)S(1)}, f32[1,32,32,128]{3,2,1,0:T(8,128)}, u32[]{:S(2)}) copy-start(f32[1,32,32,128]{3,2,1,0:T(8,128)} %f.3) | copy-start | bytes 1572868
  35.0 22.0 %copy-start.5 = (f32[1,32,32,128]{3,2,1,0:T(8,128)S(1)}, f32[1,32,32,128]{3,2,1,0:T(8,128)}, u32[]{:S(2)}) copy-start(f32[1,32,32,128]{3,2,1,0:T(8,128)} %a.3) | copy-start | bytes 1572868
  37.4 19.6 %all-to-all-start.1 = ((f32[8,34,8,128]{3,2,1,0:T(8,128)}), f32[8,34,8,128]{3,2,1,0:T(8,128)S(1)}, u32[]{:S(2)}, u32[]{:S(2)}) async-start(f32[8,34,8,128]{3,2,1,0:T(8,128)} %shard_map.48), calls=%async_computation.1 | async-start | bytes 2228224 | tf_op jit(solution)/shard_map/all_to_all | solution.py:648
  41.3 1.3 %collective-permute-start.4 = (f32[9,16,128]{2,1,0:T(8,128)S(1)}, f32[9,16,128]{2,1,0:T(8,128)S(1)}, u32[]{:S(2)}, u32[]{:S(2)}) collective-permute-start(f32[9,16,128]{2,1,0:T(8,128)S(1)} %get-tuple-element.50.refs_0_), channel_id=1, source_target_pairs={{0,4},{4,0},{1,5},{5,1},{2,6},{6,2},{3,7},{7,3},{8,12},{12,8},{9,1... | collective-permute-start | bytes 221192 | tf_op jit(solution)/shard_map/ppermute | solution.py:621
  41.5 1.3 %collective-permute-start.5 = (f32[9,16,128]{2,1,0:T(8,128)S(1)}, f32[9,16,128]{2,1,0:T(8,128)S(1)}, u32[]{:S(2)}, u32[]{:S(2)}) collective-permute-start(f32[9,16,128]{2,1,0:T(8,128)S(1)} %collective-permute-done.1.refs_1_), channel_id=1, source_target_pairs={{0,4},{4,0},{1,5},{5,1},{2,6},{6,2},{3,7},{7,3},{8,12},{12,8},{9,1... | collective-permute-start | bytes 221192 | tf_op jit(solution)/shard_map/ppermute | solution.py:621
  41.8 1.3 %collective-permute-start.6 = (f32[9,16,128]{2,1,0:T(8,128)S(1)}, f32[9,16,128]{2,1,0:T(8,128)S(1)}, u32[]{:S(2)}, u32[]{:S(2)}) collective-permute-start(f32[9,16,128]{2,1,0:T(8,128)S(1)} %collective-permute-done.2.refs_2_), channel_id=1, source_target_pairs={{0,4},{4,0},{1,5},{5,1},{2,6},{6,2},{3,7},{7,3},{8,12},{12,8},{9,1... | collective-permute-start | bytes 221192 | tf_op jit(solution)/shard_map/ppermute | solution.py:621
  42.0 1.3 %collective-permute-start.7 = (f32[9,16,128]{2,1,0:T(8,128)S(1)}, f32[9,16,128]{2,1,0:T(8,128)S(1)}, u32[]{:S(2)}, u32[]{:S(2)}) collective-permute-start(f32[9,16,128]{2,1,0:T(8,128)S(1)} %collective-permute-done.3.refs_3_), channel_id=1, source_target_pairs={{0,4},{4,0},{1,5},{5,1},{2,6},{6,2},{3,7},{7,3},{8,12},{12,8},{9,1... | collective-permute-start | bytes 221192 | tf_op jit(solution)/shard_map/ppermute | solution.py:621
  44.0 7.2 %collective-permute-start.8 = (f32[4,7,16,128]{3,2,1,0:T(8,128)S(1)}, f32[4,7,16,128]{3,2,1,0:T(8,128)S(1)}, u32[]{:S(2)}, u32[]{:S(2)}) collective-permute-start(f32[4,7,16,128]{3,2,1,0:T(8,128)S(1)} %shard_map.49), channel_id=1, source_target_pairs={{0,8},{1,9},{2,10},{3,11},{12,4},{13,5},{14,6},{15,7},{8,16},{9,17... | collective-permute-start | bytes 688136 | tf_op jit(solution)/shard_map/ppermute | solution.py:630
  51.2 1.6 %collective-permute-start.9 = (f32[4,7,16,128]{3,2,1,0:T(8,128)S(1)}, f32[4,7,16,128]{3,2,1,0:T(8,128)S(1)}, u32[]{:S(2)}, u32[]{:S(2)}) collective-permute-start(f32[4,7,16,128]{3,2,1,0:T(8,128)S(1)} %collective-permute-done.8.refs_8_), channel_id=1, source_target_pairs={{0,4},{4,0},{1,5},{5,1},{2,6},{6,2},{3,7},{7,3},{8,12},{12,8},{9,1... | collective-permute-start | bytes 688136 | tf_op jit(solution)/shard_map/ppermute | solution.py:621
  52.8 0.7 copy-start.6
  57.0 16.3 %copy-start.7 = (f32[4,7,16,128]{3,2,1,0:T(8,128)S(1)}, f32[4,7,16,128]{3,2,1,0:T(8,128)}, u32[]{:S(2)}) copy-start(f32[4,7,16,128]{3,2,1,0:T(8,128)} %copy-done.6) | copy-start | bytes 688132
  61.5 3.2 %collective-permute-start.12 = (f32[8,16,128]{2,1,0:T(8,128)S(1)}, f32[8,16,128]{2,1,0:T(8,128)S(1)}, u32[]{:S(2)}, u32[]{:S(2)}) collective-permute-start(f32[8,16,128]{2,1,0:T(8,128)S(1)} %get-tuple-element.55.refs_0_), channel_id=1, source_target_pairs={{0,3},{1,0},{2,1},{3,2},{4,7},{5,4},{6,5},{7,6},{8,11},{9,8},{10,9... | collective-permute-start | bytes 196616 | tf_op jit(solution)/shard_map/ppermute | solution.py:634
  62.6 4.6 %collective-permute-start.11 = (f32[8,16,128]{2,1,0:T(8,128)S(1)}, f32[8,16,128]{2,1,0:T(8,128)S(1)}, u32[]{:S(2)}, u32[]{:S(2)}) collective-permute-start(f32[8,16,128]{2,1,0:T(8,128)S(1)} %get-tuple-element.55.refs_0_), channel_id=1, source_target_pairs={{0,2},{1,3},{2,0},{3,1},{4,6},{5,7},{6,4},{7,5},{8,10},{9,11},{10,... | collective-permute-start | bytes 196616 | tf_op jit(solution)/shard_map/ppermute | solution.py:634
  63.9 5.7 %collective-permute-start.10 = (f32[8,16,128]{2,1,0:T(8,128)S(1)}, f32[8,16,128]{2,1,0:T(8,128)S(1)}, u32[]{:S(2)}, u32[]{:S(2)}) collective-permute-start(f32[8,16,128]{2,1,0:T(8,128)S(1)} %get-tuple-element.55.refs_0_), channel_id=1, source_target_pairs={{0,1},{1,2},{2,3},{3,0},{4,5},{5,6},{6,7},{7,4},{8,9},{9,10},{10,1... | collective-permute-start | bytes 196616 | tf_op jit(solution)/shard_map/ppermute | solution.py:634
  63.9 6.4 %collective-permute-start.13 = (f32[8,16,128]{2,1,0:T(8,128)S(1)}, f32[8,16,128]{2,1,0:T(8,128)S(1)}, u32[]{:S(2)}, u32[]{:S(2)}) collective-permute-start(f32[8,16,128]{2,1,0:T(8,128)S(1)} %get-tuple-element.55.refs_0_), channel_id=1, source_target_pairs={{0,4},{4,0},{1,5},{5,1},{2,6},{6,2},{3,7},{7,3},{8,12},{12,8},{9,1... | collective-permute-start | bytes 196616 | tf_op jit(solution)/shard_map/ppermute | solution.py:621
  64.7 5.6 %collective-permute-start.16 = (f32[8,16,128]{2,1,0:T(8,128)S(1)}, f32[8,16,128]{2,1,0:T(8,128)S(1)}, u32[]{:S(2)}, u32[]{:S(2)}) collective-permute-start(f32[8,16,128]{2,1,0:T(8,128)S(1)} %collective-permute-done.12.refs_3_), channel_id=1, source_target_pairs={{0,4},{4,0},{1,5},{5,1},{2,6},{6,2},{3,7},{7,3},{8,12},{12,8},{9,1... | collective-permute-start | bytes 196616 | tf_op jit(solution)/shard_map/ppermute | solution.py:621
  67.2 3.4 %collective-permute-start.15 = (f32[8,16,128]{2,1,0:T(8,128)S(1)}, f32[8,16,128]{2,1,0:T(8,128)S(1)}, u32[]{:S(2)}, u32[]{:S(2)}) collective-permute-start(f32[8,16,128]{2,1,0:T(8,128)S(1)} %collective-permute-done.11.refs_2_), channel_id=1, source_target_pairs={{0,4},{4,0},{1,5},{5,1},{2,6},{6,2},{3,7},{7,3},{8,12},{12,8},{9,1... | collective-permute-start | bytes 196616 | tf_op jit(solution)/shard_map/ppermute | solution.py:621
  69.7 1.6 %collective-permute-start.14 = (f32[8,16,128]{2,1,0:T(8,128)S(1)}, f32[8,16,128]{2,1,0:T(8,128)S(1)}, u32[]{:S(2)}, u32[]{:S(2)}) collective-permute-start(f32[8,16,128]{2,1,0:T(8,128)S(1)} %collective-permute-done.10.refs_1_), channel_id=1, source_target_pairs={{0,4},{4,0},{1,5},{5,1},{2,6},{6,2},{3,7},{7,3},{8,12},{12,8},{9,1... | collective-permute-start | bytes 196616 | tf_op jit(solution)/shard_map/ppermute | solution.py:621
  72.0 6.3 %collective-permute-start.17 = (f32[4,5,16,128]{3,2,1,0:T(8,128)S(1)}, f32[4,5,16,128]{3,2,1,0:T(8,128)S(1)}, u32[]{:S(2)}, u32[]{:S(2)}) collective-permute-start(f32[4,5,16,128]{3,2,1,0:T(8,128)S(1)} %shard_map.51), channel_id=1, source_target_pairs={{0,8},{1,9},{2,10},{3,11},{12,4},{13,5},{14,6},{15,7},{8,16},{9,17... | collective-permute-start | bytes 491528 | tf_op jit(solution)/shard_map/ppermute | solution.py:630
  78.2 3.3 %collective-permute-start.18 = (f32[4,5,16,128]{3,2,1,0:T(8,128)S(1)}, f32[4,5,16,128]{3,2,1,0:T(8,128)S(1)}, u32[]{:S(2)}, u32[]{:S(2)}) collective-permute-start(f32[4,5,16,128]{3,2,1,0:T(8,128)S(1)} %collective-permute-done.17.refs_8_), channel_id=1, source_target_pairs={{0,4},{4,0},{1,5},{5,1},{2,6},{6,2},{3,7},{7,3},{8,12},{12,8},{9,1... | collective-permute-start | bytes 491528 | tf_op jit(solution)/shard_map/ppermute | solution.py:621
  84.2 9.4 %collective-permute-start.19 = (f32[19,16,128]{2,1,0:T(8,128)S(1)}, f32[19,16,128]{2,1,0:T(8,128)S(1)}, u32[]{:S(2)}, u32[]{:S(2)}) collective-permute-start(f32[19,16,128]{2,1,0:T(8,128)S(1)} %get-tuple-element.73), channel_id=1, source_target_pairs={{0,8},{1,9},{2,10},{3,11},{12,4},{13,5},{14,6},{15,7},{8,16},{9,17... | collective-permute-start | bytes 466952 | tf_op jit(solution)/shard_map/ppermute | solution.py:630
  89.3 4.3 %collective-permute-start.20 = (f32[8,128]{1,0:T(8,128)S(1)}, f32[8,128]{1,0:T(8,128)S(1)}, u32[]{:S(2)}, u32[]{:S(2)}) collective-permute-start(f32[8,128]{1,0:T(8,128)S(1)} %get-tuple-element.72), channel_id=1, source_target_pairs={{0,112},{8,120},{16,0},{24,8},{32,16},{40,24},{48,32},{56,40},{64,... | collective-permute-start | bytes 12296 | tf_op jit(solution)/shard_map/ppermute | solution.py:695
  93.5 1.5 %collective-permute-start.21 = (f32[19,16,128]{2,1,0:T(8,128)S(1)}, f32[19,16,128]{2,1,0:T(8,128)S(1)}, u32[]{:S(2)}, u32[]{:S(2)}) collective-permute-start(f32[19,16,128]{2,1,0:T(8,128)S(1)} %collective-permute-done.19.one), channel_id=1, source_target_pairs={{0,4},{4,0},{1,5},{5,1},{2,6},{6,2},{3,7},{7,3},{8,12},{12,8},{9,1... | collective-permute-start | bytes 466952 | tf_op jit(solution)/shard_map/ppermute | solution.py:621
  95.0 5.8 %collective-permute-start.22 = (f32[8,128]{1,0:T(8,128)S(1)}, f32[8,128]{1,0:T(8,128)S(1)}, u32[]{:S(2)}, u32[]{:S(2)}) collective-permute-start(f32[8,128]{1,0:T(8,128)S(1)} %fusion.1.sum_0), channel_id=1, source_target_pairs={{0,32},{1,33},{2,34},{3,35},{4,100},{5,101},{6,102},{7,103},{8,40}... | collective-permute-start | bytes 12296 | tf_op jit(solution)/shard_map/ppermute | solution.py:644
  100.1 5.1 %collective-permute-start.23 = (f32[8,128]{1,0:T(8,128)S(1)}, f32[8,128]{1,0:T(8,128)S(1)}, u32[]{:S(2)}, u32[]{:S(2)}) collective-permute-start(f32[8,128]{1,0:T(8,128)S(1)} %fusion.1.sum_0), channel_id=1, source_target_pairs={{0,64},{8,72},{16,80},{24,88},{32,96},{40,104},{48,112},{56,120},{... | collective-permute-start | bytes 12296 | tf_op jit(solution)/shard_map/ppermute | solution.py:644
  100.9 4.4 %collective-permute-start.24 = (f32[8,128]{1,0:T(8,128)S(1)}, f32[8,128]{1,0:T(8,128)S(1)}, u32[]{:S(2)}, u32[]{:S(2)}) collective-permute-start(f32[8,128]{1,0:T(8,128)S(1)} %collective-permute-done.22.sum_1), channel_id=1, source_target_pairs={{0,4},{4,0},{1,5},{5,1},{2,6},{6,2},{3,7},{7,3},{8,12},{12,8},{9,1... | collective-permute-start | bytes 12296 | tf_op jit(solution)/shard_map/ppermute | solution.py:621

commit v11 on v10

--- a/solution.py
+++ b/solution.py
@@ -472,14 +472,12 @@
                 g_r[1 + j], i_r[1 + j], e_r[1 + j] = force, inverse, force * inverse
             else:
                 g_b[1 + j], i_b[1 + j] = force, inverse
-    half_sweep(e_b, e_r, g_b, i_b, 1, 27, False, mask, 0.0625, 1)
-
-    def sweep(n, carry):
-        half_sweep(e_r, e_b, g_r, i_r, 1, 27, True, mask, 0.0625, 1)
-        half_sweep(e_b, e_r, g_b, i_b, 1, 27, False, mask, 0.0625, 1)
-        return carry
-
-    lax.fori_loop(0, 7, sweep, 0)
+    for n in range(2, 17):
+        far = (20 - n) // 2
+        if n % 2:
+            half_sweep(e_r, e_b, g_r, i_r, 10 - far, 18 + far, True, mask, 0.0625, 1)
+        else:
+            half_sweep(e_b, e_r, g_b, i_b, 10 - far, 18 + far, False, mask, 0.0625, 1)
     for i in range(22):
         k, upper = (15 + i) // 2 + 1, (15 + i) % 2
         es[i] = jnp.where(mask, e_r[k], e_b[k]) if upper else jnp.where(mask, e_b[k], e_r[k])

time: 110 us -> 109 us (level)
  no operation moved by 1% of the time
where the time goes in v11:
time: 109 us
  starting transfers between devices  38.5 us (35%)
  Pallas kernels  24.1 us (22%)
  waiting for transfers between devices  21.8 us (20%)
  blocking collectives  19.7 us (18%)
  local copies, waits for them, and re-layouts  4.58 us (4%)
    pallas_call x11, Pallas kernels, run(): pl.pallas_call(kernel, out_shape=shapes[0] if single else shapes, in_spec...  24.1 us
    all_to_all x1, blocking collectives, among(): return lax.all_to_all(x, LB, split_axis=0, concat_axis=0, tiled=True)  19.7 us
    ppermute x12, starting transfers between devices, swap_cores(): return lax.ppermute(x, 'level', [(0, 1), (1, 0)])  11.8 us
    ppermute x4, starting transfers between devices, to_slabs(): return lax.ppermute(x, ALL, pairs)  10.8 us
    ppermute x4, waiting for transfers between devices, to_slabs(): return lax.ppermute(x, ALL, pairs)  7.52 us
    ppermute x2, starting transfers between devices, fours_apart(): return (lax.ppermute(x, ALL, beside), lax.ppermute(x, 'slab', across))  5.06 us
    ppermute x12, waiting for transfers between devices, swap_cores(): return lax.ppermute(x, 'level', [(0, 1), (1, 0)])  4.98 us
    ppermute x6, starting transfers between devices, around_chips(): lax.ppermute(x, 'bottom', [(i, (i + d) % 4) for i in range(4)])  4.94 us
  transfers between devices with their start and end apart: 26, of which 18 were waited for; matrix products, arithmetic and copies ran while one was open for 0% of the time, Pallas kernels for 9%

profile of v11, /device:TPU:1, one launch (start us, length us, event | category | flops | bytes accessed | tf_op | source)
XLA Modules:
  0.0 108.9 jit_solution(5734108452238313756)
XLA Ops:
  0.0 0.8 copy.13.bricks
  0.8 0.1 pad_add_fusion.meta
  0.8 1.0 copy-done
  1.9 1.0 copy-done.2
  2.9 1.0 copy-done.4
  4.0 1.7 %shard_map.46 = (f32[8,29,8,128]{3,2,1,0:T(8,128)S(1)}, f32[9,16,128]{2,1,0:T(8,128)S(1)}) custom-call(s32[2]{0:T(128)S(1)} %pad_add_fusion.meta, s32[16,8]{1,0:T(8,128)S(1)} %copy.13.bricks, f32[1,32,32,128]{3,2,1,0:T(8,128)S(1)} %copy-done, f32[1,32,32,128]{3,2,1,0:T(8,128)S(1)} %copy-done.2, f32[1,32,32,128]{3,2,1,0:T(8,128)S(1)} %copy-done.4), custom_call_target="tpu_custom_call" | custom-call | tf_op jit(solution)/shard_map/pallas_call | solution.py:21
  5.7 19.7 %all_to_all.10.recv = f32[8,29,8,128]{3,2,1,0:T(8,128)S(1)} all-to-all(f32[8,29,8,128]{3,2,1,0:T(8,128)S(1)} %get-tuple-element.45), channel_id=1, replica_groups=mesh['slab'=16,'level'=2,'bottom'=4] {'level','bottom'}, dimensions={0} | all-to-all | bytes 1900544 | tf_op jit(solution)/shard_map/all_to_all | solution.py:646
  25.4 0.7 shard_map.47
  26.1 3.1 %collective-permute-start = (f32[4,17,8,128]{3,2,1,0:T(8,128)S(1)}, f32[4,17,8,128]{3,2,1,0:T(8,128)S(1)}, u32[]{:S(2)}, u32[]{:S(2)}) collective-permute-start(f32[4,17,8,128]{3,2,1,0:T(8,128)S(1)} %shard_map.47), channel_id=1, source_target_pairs={{8,0},{9,1},{10,2},{11,3},{4,12},{5,13},{6,14},{7,15},{16,8},{17,9... | collective-permute-start | bytes 835592 | tf_op jit(solution)/shard_map/ppermute | solution.py:628
  29.2 1.0 collective-permute-start.3
  30.3 1.5 %collective-permute-start.2 = (f32[9,16,128]{2,1,0:T(8,128)S(1)}, f32[9,16,128]{2,1,0:T(8,128)S(1)}, u32[]{:S(2)}, u32[]{:S(2)}) collective-permute-start(f32[9,16,128]{2,1,0:T(8,128)S(1)} %get-tuple-element.50.refs_0_), channel_id=1, source_target_pairs={{0,2},{1,3},{2,0},{3,1},{4,6},{5,7},{6,4},{7,5},{8,10},{9,11},{10,... | collective-permute-start | bytes 221192 | tf_op jit(solution)/shard_map/ppermute | solution.py:632
  31.7 0.0 collective-permute-start.1
  31.7 0.9 collective-permute-done.cross
  32.7 2.3 %shard_map.48 = f32[8,34,8,128]{3,2,1,0:T(8,128)} custom-call(s32[2]{0:T(128)S(1)} %pad_add_fusion.meta, s32[16,8]{1,0:T(8,128)S(1)} %copy.13.bricks, f32[8,29,8,128]{3,2,1,0:T(8,128)S(1)} %all_to_all.10.recv, f32[4,17,8,128]{3,2,1,0:T(8,128)S(1)} %collective-permute-done.cross), custom_call_target="tpu_custom_call" | custom-call | tf_op jit(solution)/shard_map/pallas_call | solution.py:21
  35.0 0.7 collective-permute-done.2.refs_2_
  35.8 1.6 %collective-permute-done.1.refs_1_ = f32[9,16,128]{2,1,0:T(8,128)S(1)} collective-permute-done((f32[9,16,128]{2,1,0:T(8,128)S(1)}, f32[9,16,128]{2,1,0:T(8,128)S(1)}, u32[]{:S(2)}, u32[]{:S(2)}) %collective-permute-start.1) | collective-permute-done | bytes 73760 | tf_op jit(solution)/shard_map/ppermute | solution.py:632
  37.4 3.9 %all-to-all-start.1 = ((f32[8,34,8,128]{3,2,1,0:T(8,128)}), f32[8,34,8,128]{3,2,1,0:T(8,128)S(1)}, u32[]{:S(2)}, u32[]{:S(2)}) async-start(f32[8,34,8,128]{3,2,1,0:T(8,128)} %shard_map.48), calls=%async_computation.1 | async-start | bytes 2228224 | tf_op jit(solution)/shard_map/all_to_all | solution.py:646
  41.3 0.2 collective-permute-start.4
  41.5 0.3 collective-permute-start.5
  41.8 0.2 collective-permute-start.6
  42.0 0.3 collective-permute-start.7
  42.3 0.2 collective-permute-done.4.refs_4_
  42.6 0.2 collective-permute-done.5.refs_5_
  42.7 0.3 collective-permute-done.6.refs_6_
  43.1 0.2 collective-permute-done.7.refs_7_
  43.2 0.7 shard_map.49
  44.0 1.3 %collective-permute-start.8 = (f32[4,7,16,128]{3,2,1,0:T(8,128)S(1)}, f32[4,7,16,128]{3,2,1,0:T(8,128)S(1)}, u32[]{:S(2)}, u32[]{:S(2)}) collective-permute-start(f32[4,7,16,128]{3,2,1,0:T(8,128)S(1)} %shard_map.49), channel_id=1, source_target_pairs={{0,8},{1,9},{2,10},{3,11},{12,4},{13,5},{14,6},{15,7},{8,16},{9,17... | collective-permute-start | bytes 688136 | tf_op jit(solution)/shard_map/ppermute | solution.py:628
  45.3 5.9 %collective-permute-done.8.refs_8_ = f32[4,7,16,128]{3,2,1,0:T(8,128)S(1)} collective-permute-done((f32[4,7,16,128]{3,2,1,0:T(8,128)S(1)}, f32[4,7,16,128]{3,2,1,0:T(8,128)S(1)}, u32[]{:S(2)}, u32[]{:S(2)}) %collective-permute-start.8) | collective-permute-done | bytes 229408 | tf_op jit(solution)/shard_map/ppermute | solution.py:628
  51.2 0.5 collective-permute-start.9
  51.7 1.1 %collective-permute-done.9.refs_9_ = f32[4,7,16,128]{3,2,1,0:T(8,128)S(1)} collective-permute-done((f32[4,7,16,128]{3,2,1,0:T(8,128)S(1)}, f32[4,7,16,128]{3,2,1,0:T(8,128)S(1)}, u32[]{:S(2)}, u32[]{:S(2)}) %collective-permute-start.9) | collective-permute-done | bytes 229408 | tf_op jit(solution)/shard_map/ppermute | solution.py:619
  52.8 0.7 copy-done.6
  53.5 3.5 %all-to-all-done.1.recv = f32[8,34,8,128]{3,2,1,0:T(8,128)S(1)} async-done(((f32[8,34,8,128]{3,2,1,0:T(8,128)}), f32[8,34,8,128]{3,2,1,0:T(8,128)S(1)}, u32[]{:S(2)}, u32[]{:S(2)}) %all-to-all-start.1) | async-done | bytes 1114144 | tf_op jit(solution)/shard_map/all_to_all | solution.py:646
  57.0 4.5 %shard_map.50 = (f32[8,16,128]{2,1,0:T(8,128)S(1)}, f32[26,40,256]{2,1,0:T(8,128)S(1)}, f32[26,40,256]{2,1,0:T(8,128)S(1)}, f32[26,40,256]{2,1,0:T(8,128)S(1)}, ...) custom-call(s32[2]{0:T(128)S(1)} %pad_add_fusion.meta, s32[16,8]{1,0:T(8,128)S(1)} %copy.13.bricks, ...), custom_call_target="tpu_custom_call" | custom-call | tf_op jit(solution)/shard_map/pallas_call | solution.py:21
  61.5 1.1 collective-permute-start.12
  62.6 1.4 %collective-permute-start.11 = (f32[8,16,128]{2,1,0:T(8,128)S(1)}, f32[8,16,128]{2,1,0:T(8,128)S(1)}, u32[]{:S(2)}, u32[]{:S(2)}) collective-permute-start(f32[8,16,128]{2,1,0:T(8,128)S(1)} %get-tuple-element.55.refs_0_), channel_id=1, source_target_pairs={{0,2},{1,3},{2,0},{3,1},{4,6},{5,7},{6,4},{7,5},{8,10},{9,11},{10,... | collective-permute-start | bytes 196616 | tf_op jit(solution)/shard_map/ppermute | solution.py:632
  63.9 0.0 collective-permute-start.10
  63.9 0.8 collective-permute-start.13
  64.7 0.0 collective-permute-done.12.refs_3_
  64.7 2.1 %collective-permute-start.16 = (f32[8,16,128]{2,1,0:T(8,128)S(1)}, f32[8,16,128]{2,1,0:T(8,128)S(1)}, u32[]{:S(2)}, u32[]{:S(2)}) collective-permute-start(f32[8,16,128]{2,1,0:T(8,128)S(1)} %collective-permute-done.12.refs_3_), channel_id=1, source_target_pairs={{0,4},{4,0},{1,5},{5,1},{2,6},{6,2},{3,7},{7,3},{8,12},{12,8},{9,1... | collective-permute-start | bytes 196616 | tf_op jit(solution)/shard_map/ppermute | solution.py:619
  66.8 0.4 collective-permute-done.11.refs_2_
  67.2 2.5 %collective-permute-start.15 = (f32[8,16,128]{2,1,0:T(8,128)S(1)}, f32[8,16,128]{2,1,0:T(8,128)S(1)}, u32[]{:S(2)}, u32[]{:S(2)}) collective-permute-start(f32[8,16,128]{2,1,0:T(8,128)S(1)} %collective-permute-done.11.refs_2_), channel_id=1, source_target_pairs={{0,4},{4,0},{1,5},{5,1},{2,6},{6,2},{3,7},{7,3},{8,12},{12,8},{9,1... | collective-permute-start | bytes 196616 | tf_op jit(solution)/shard_map/ppermute | solution.py:619
  69.7 0.7 collective-permute-start.14
  70.4 0.0 collective-permute-done.13.refs_4_
  70.4 0.0 collective-permute-done.16.refs_7_
  70.4 0.2 collective-permute-done.15.refs_6_
  70.6 0.7 collective-permute-done.14.refs_5_
  71.3 0.7 shard_map.51
  72.0 1.3 %collective-permute-start.17 = (f32[4,5,16,128]{3,2,1,0:T(8,128)S(1)}, f32[4,5,16,128]{3,2,1,0:T(8,128)S(1)}, u32[]{:S(2)}, u32[]{:S(2)}) collective-permute-start(f32[4,5,16,128]{3,2,1,0:T(8,128)S(1)} %shard_map.51), channel_id=1, source_target_pairs={{0,8},{1,9},{2,10},{3,11},{12,4},{13,5},{14,6},{15,7},{8,16},{9,17... | collective-permute-start | bytes 491528 | tf_op jit(solution)/shard_map/ppermute | solution.py:628
  73.3 1.3 %shard_map.52 = (f32[28,32,128]{2,1,0:T(8,128)S(1)}, f32[28,32,128]{2,1,0:T(8,128)S(1)}, f32[28,32,128]{2,1,0:T(8,128)S(1)}, f32[22,16,128]{2,1,0:T(8,128)S(1)}, f32[3,8,16,128]{3,2,1,0:T(8,128)S(1)}) custom-call(s32[2]{0:T(128)S(1)} %pad_add_fusion.meta, s32[16,8]{1,0:T(8,128)S(1)} %copy.13.bricks, f32[9,16,128]{2,1,0:T(8,128)S(1)} %get-tuple-element.50.refs_0_, ...), custom_call_target="tpu_custom_call" | custom-call | tf_op jit(solution)/shard_map/pallas_call | solution.py:21
  74.6 3.0 %shard_map.53.refs_10_ = f32[16,16,128]{2,1,0:T(8,128)S(1)} custom-call(s32[2]{0:T(128)S(1)} %pad_add_fusion.meta, f32[3,8,16,128]{3,2,1,0:T(8,128)S(1)} %get-tuple-element.61.coef), custom_call_target="tpu_custom_call" | custom-call | tf_op jit(solution)/shard_map/pallas_call | solution.py:21
  77.6 0.7 collective-permute-done.17.refs_8_
  78.2 2.3 %collective-permute-start.18 = (f32[4,5,16,128]{3,2,1,0:T(8,128)S(1)}, f32[4,5,16,128]{3,2,1,0:T(8,128)S(1)}, u32[]{:S(2)}, u32[]{:S(2)}) collective-permute-start(f32[4,5,16,128]{3,2,1,0:T(8,128)S(1)} %collective-permute-done.17.refs_8_), channel_id=1, source_target_pairs={{0,4},{4,0},{1,5},{5,1},{2,6},{6,2},{3,7},{7,3},{8,12},{12,8},{9,1... | collective-permute-start | bytes 491528 | tf_op jit(solution)/shard_map/ppermute | solution.py:619
  80.6 1.0 collective-permute-done.18.refs_9_
  81.6 2.6 %shard_map.54 = (f32[22,16,128]{2,1,0:T(8,128)S(1)}, f32[19,16,128]{2,1,0:T(8,128)S(1)}, f32[8,128]{1,0:T(8,128)S(1)}, f32[28,32,128]{2,1,0:T(8,128)S(1)}, f32[2...) custom-call(s32[2]{0:T(128)S(1)} %pad_add_fusion.meta, s32[16,8]{1,0:T(8,128)S(1)} %copy.13.bricks, ...), custom_call_target="tpu_custom_call" | custom-call | tf_op jit(solution)/shard_map/pallas_call | solution.py:21
  84.2 5.1 %collective-permute-start.19 = (f32[19,16,128]{2,1,0:T(8,128)S(1)}, f32[19,16,128]{2,1,0:T(8,128)S(1)}, u32[]{:S(2)}, u32[]{:S(2)}) collective-permute-start(f32[19,16,128]{2,1,0:T(8,128)S(1)} %get-tuple-element.73), channel_id=1, source_target_pairs={{0,8},{1,9},{2,10},{3,11},{12,4},{13,5},{14,6},{15,7},{8,16},{9,17... | collective-permute-start | bytes 466952 | tf_op jit(solution)/shard_map/ppermute | solution.py:628
  89.3 2.0 %collective-permute-start.20 = (f32[8,128]{1,0:T(8,128)S(1)}, f32[8,128]{1,0:T(8,128)S(1)}, u32[]{:S(2)}, u32[]{:S(2)}) collective-permute-start(f32[8,128]{1,0:T(8,128)S(1)} %get-tuple-element.72), channel_id=1, source_target_pairs={{0,112},{8,120},{16,0},{24,8},{32,16},{40,24},{48,32},{56,40},{64,... | collective-permute-start | bytes 12296 | tf_op jit(solution)/shard_map/ppermute | solution.py:693
  91.3 2.2 %collective-permute-done.20 = f32[8,128]{1,0:T(8,128)S(1)} collective-permute-done((f32[8,128]{1,0:T(8,128)S(1)}, f32[8,128]{1,0:T(8,128)S(1)}, u32[]{:S(2)}, u32[]{:S(2)}) %collective-permute-start.20) | collective-permute-done | bytes 4128 | tf_op jit(solution)/shard_map/ppermute | solution.py:693
  93.5 0.5 collective-permute-start.21
  94.0 1.0 collective-permute-done.21.two
  95.0 5.1 %collective-permute-start.22 = (f32[8,128]{1,0:T(8,128)S(1)}, f32[8,128]{1,0:T(8,128)S(1)}, u32[]{:S(2)}, u32[]{:S(2)}) collective-permute-start(f32[8,128]{1,0:T(8,128)S(1)} %fusion.1.sum_0), channel_id=1, source_target_pairs={{0,32},{1,33},{2,34},{3,35},{4,100},{5,101},{6,102},{7,103},{8,40}... | collective-permute-start | bytes 12296 | tf_op jit(solution)/shard_map/ppermute | solution.py:642
  100.1 0.8 collective-permute-done.22.sum_1
  100.9 1.5 %collective-permute-start.24 = (f32[8,128]{1,0:T(8,128)S(1)}, f32[8,128]{1,0:T(8,128)S(1)}, u32[]{:S(2)}, u32[]{:S(2)}) collective-permute-start(f32[8,128]{1,0:T(8,128)S(1)} %collective-permute-done.22.sum_1), channel_id=1, source_target_pairs={{0,4},{4,0},{1,5},{5,1},{2,6},{6,2},{3,7},{7,3},{8,12},{12,8},{9,1... | collective-permute-start | bytes 12296 | tf_op jit(solution)/shard_map/ppermute | solution.py:619
  102.3 2.0 %shard_map.55.es = f32[22,16,128]{2,1,0:T(8,128)S(1)} custom-call(s32[2]{0:T(128)S(1)} %pad_add_fusion.meta, f32[22,16,128]{2,1,0:T(8,128)S(1)} %get-tuple-element.76.rb, f32[19,16,128]{2,1,0:T(8,128)S(1)} %collective-permute-done.19.one, f32[19,16,128]{2,1,0:T(8,128)S(1)} %collective-permute-done.21.two), custom_call_target="tpu_custom_call" | custom-call | tf_op jit(solution)/shard_map/pallas_call | solution.py:21
  104.4 4.5 %shard_map.56 = f32[1,32,32,128]{3,2,1,0:T(8,128)} custom-call(s32[2]{0:T(128)S(1)} %pad_add_fusion.meta, s32[16,8]{1,0:T(8,128)S(1)} %copy.13.bricks, f32[8,128]{1,0:T(8,128)S(1)} %fusion.1.sum_0, f32[8,128]{1,0:T(8,128)S(1)} %collective-permute-done.22.sum_1, f32[8,128]{1,0:T(8,128)S(1)} %collective-permute-done.23.sum_2, ...), custom_call_target="tpu_custom_call" | custom-call | tf_op jit(solution)/shard_map/pallas_call | solution.py:21
  (19 shorter events, 0.0 us)
Async XLA Ops:
  0.8 1.0 copy-start
  1.9 1.0 copy-start.2
  2.9 1.0 copy-start.4
  26.1 6.6 %collective-permute-start = (f32[4,17,8,128]{3,2,1,0:T(8,128)S(1)}, f32[4,17,8,128]{3,2,1,0:T(8,128)S(1)}, u32[]{:S(2)}, u32[]{:S(2)}) collective-permute-start(f32[4,17,8,128]{3,2,1,0:T(8,128)S(1)} %shard_map.47), channel_id=1, source_target_pairs={{8,0},{9,1},{10,2},{11,3},{4,12},{5,13},{6,14},{7,15},{16,8},{17,9... | collective-permute-start | bytes 835592 | tf_op jit(solution)/shard_map/ppermute | solution.py:628
  29.2 5.8 %collective-permute-start.3 = (f32[9,16,128]{2,1,0:T(8,128)S(1)}, f32[9,16,128]{2,1,0:T(8,128)S(1)}, u32[]{:S(2)}, u32[]{:S(2)}) collective-permute-start(f32[9,16,128]{2,1,0:T(8,128)S(1)} %get-tuple-element.50.refs_0_), channel_id=1, source_target_pairs={{0,3},{1,0},{2,1},{3,2},{4,7},{5,4},{6,5},{7,6},{8,11},{9,8},{10,9... | collective-permute-start | bytes 221192 | tf_op jit(solution)/shard_map/ppermute | solution.py:632
  30.3 5.5 %collective-permute-start.2 = (f32[9,16,128]{2,1,0:T(8,128)S(1)}, f32[9,16,128]{2,1,0:T(8,128)S(1)}, u32[]{:S(2)}, u32[]{:S(2)}) collective-permute-start(f32[9,16,128]{2,1,0:T(8,128)S(1)} %get-tuple-element.50.refs_0_), channel_id=1, source_target_pairs={{0,2},{1,3},{2,0},{3,1},{4,6},{5,7},{6,4},{7,5},{8,10},{9,11},{10,... | collective-permute-start | bytes 221192 | tf_op jit(solution)/shard_map/ppermute | solution.py:632
  31.7 5.7 %collective-permute-start.1 = (f32[9,16,128]{2,1,0:T(8,128)S(1)}, f32[9,16,128]{2,1,0:T(8,128)S(1)}, u32[]{:S(2)}, u32[]{:S(2)}) collective-permute-start(f32[9,16,128]{2,1,0:T(8,128)S(1)} %get-tuple-element.50.refs_0_), channel_id=1, source_target_pairs={{0,1},{1,2},{2,3},{3,0},{4,5},{5,6},{6,7},{7,4},{8,9},{9,10},{10,1... | collective-permute-start | bytes 221192 | tf_op jit(solution)/shard_map/ppermute | solution.py:632
  35.0 22.0 %copy-start.1 = (f32[1,32,32,128]{3,2,1,0:T(8,128)S(1)}, f32[1,32,32,128]{3,2,1,0:T(8,128)}, u32[]{:S(2)}) copy-start(f32[1,32,32,128]{3,2,1,0:T(8,128)} %u.3) | copy-start | bytes 1572868
  35.0 22.0 %copy-start.3 = (f32[1,32,32,128]{3,2,1,0:T(8,128)S(1)}, f32[1,32,32,128]{3,2,1,0:T(8,128)}, u32[]{:S(2)}) copy-start(f32[1,32,32,128]{3,2,1,0:T(8,128)} %f.3) | copy-start | bytes 1572868
  35.0 22.0 %copy-start.5 = (f32[1,32,32,128]{3,2,1,0:T(8,128)S(1)}, f32[1,32,32,128]{3,2,1,0:T(8,128)}, u32[]{:S(2)}) copy-start(f32[1,32,32,128]{3,2,1,0:T(8,128)} %a.3) | copy-start | bytes 1572868
  37.4 19.6 %all-to-all-start.1 = ((f32[8,34,8,128]{3,2,1,0:T(8,128)}), f32[8,34,8,128]{3,2,1,0:T(8,128)S(1)}, u32[]{:S(2)}, u32[]{:S(2)}) async-start(f32[8,34,8,128]{3,2,1,0:T(8,128)} %shard_map.48), calls=%async_computation.1 | async-start | bytes 2228224 | tf_op jit(solution)/shard_map/all_to_all | solution.py:646
  41.3 1.3 %collective-permute-start.4 = (f32[9,16,128]{2,1,0:T(8,128)S(1)}, f32[9,16,128]{2,1,0:T(8,128)S(1)}, u32[]{:S(2)}, u32[]{:S(2)}) collective-permute-start(f32[9,16,128]{2,1,0:T(8,128)S(1)} %get-tuple-element.50.refs_0_), channel_id=1, source_target_pairs={{0,4},{4,0},{1,5},{5,1},{2,6},{6,2},{3,7},{7,3},{8,12},{12,8},{9,1... | collective-permute-start | bytes 221192 | tf_op jit(solution)/shard_map/ppermute | solution.py:619
  41.5 1.3 %collective-permute-start.5 = (f32[9,16,128]{2,1,0:T(8,128)S(1)}, f32[9,16,128]{2,1,0:T(8,128)S(1)}, u32[]{:S(2)}, u32[]{:S(2)}) collective-permute-start(f32[9,16,128]{2,1,0:T(8,128)S(1)} %collective-permute-done.1.refs_1_), channel_id=1, source_target_pairs={{0,4},{4,0},{1,5},{5,1},{2,6},{6,2},{3,7},{7,3},{8,12},{12,8},{9,1... | collective-permute-start | bytes 221192 | tf_op jit(solution)/shard_map/ppermute | solution.py:619
  41.8 1.3 %collective-permute-start.6 = (f32[9,16,128]{2,1,0:T(8,128)S(1)}, f32[9,16,128]{2,1,0:T(8,128)S(1)}, u32[]{:S(2)}, u32[]{:S(2)}) collective-permute-start(f32[9,16,128]{2,1,0:T(8,128)S(1)} %collective-permute-done.2.refs_2_), channel_id=1, source_target_pairs={{0,4},{4,0},{1,5},{5,1},{2,6},{6,2},{3,7},{7,3},{8,12},{12,8},{9,1... | collective-permute-start | bytes 221192 | tf_op jit(solution)/shard_map/ppermute | solution.py:619
  42.0 1.3 %collective-permute-start.7 = (f32[9,16,128]{2,1,0:T(8,128)S(1)}, f32[9,16,128]{2,1,0:T(8,128)S(1)}, u32[]{:S(2)}, u32[]{:S(2)}) collective-permute-start(f32[9,16,128]{2,1,0:T(8,128)S(1)} %collective-permute-done.3.refs_3_), channel_id=1, source_target_pairs={{0,4},{4,0},{1,5},{5,1},{2,6},{6,2},{3,7},{7,3},{8,12},{12,8},{9,1... | collective-permute-start | bytes 221192 | tf_op jit(solution)/shard_map/ppermute | solution.py:619
  44.0 7.2 %collective-permute-start.8 = (f32[4,7,16,128]{3,2,1,0:T(8,128)S(1)}, f32[4,7,16,128]{3,2,1,0:T(8,128)S(1)}, u32[]{:S(2)}, u32[]{:S(2)}) collective-permute-start(f32[4,7,16,128]{3,2,1,0:T(8,128)S(1)} %shard_map.49), channel_id=1, source_target_pairs={{0,8},{1,9},{2,10},{3,11},{12,4},{13,5},{14,6},{15,7},{8,16},{9,17... | collective-permute-start | bytes 688136 | tf_op jit(solution)/shard_map/ppermute | solution.py:628
  51.2 1.6 %collective-permute-start.9 = (f32[4,7,16,128]{3,2,1,0:T(8,128)S(1)}, f32[4,7,16,128]{3,2,1,0:T(8,128)S(1)}, u32[]{:S(2)}, u32[]{:S(2)}) collective-permute-start(f32[4,7,16,128]{3,2,1,0:T(8,128)S(1)} %collective-permute-done.8.refs_8_), channel_id=1, source_target_pairs={{0,4},{4,0},{1,5},{5,1},{2,6},{6,2},{3,7},{7,3},{8,12},{12,8},{9,1... | collective-permute-start | bytes 688136 | tf_op jit(solution)/shard_map/ppermute | solution.py:619
  52.8 0.7 copy-start.6
  57.0 16.3 %copy-start.7 = (f32[4,7,16,128]{3,2,1,0:T(8,128)S(1)}, f32[4,7,16,128]{3,2,1,0:T(8,128)}, u32[]{:S(2)}) copy-start(f32[4,7,16,128]{3,2,1,0:T(8,128)} %copy-done.6) | copy-start | bytes 688132
  61.5 3.2 %collective-permute-start.12 = (f32[8,16,128]{2,1,0:T(8,128)S(1)}, f32[8,16,128]{2,1,0:T(8,128)S(1)}, u32[]{:S(2)}, u32[]{:S(2)}) collective-permute-start(f32[8,16,128]{2,1,0:T(8,128)S(1)} %get-tuple-element.55.refs_0_), channel_id=1, source_target_pairs={{0,3},{1,0},{2,1},{3,2},{4,7},{5,4},{6,5},{7,6},{8,11},{9,8},{10,9... | collective-permute-start | bytes 196616 | tf_op jit(solution)/shard_map/ppermute | solution.py:632
  62.6 4.6 %collective-permute-start.11 = (f32[8,16,128]{2,1,0:T(8,128)S(1)}, f32[8,16,128]{2,1,0:T(8,128)S(1)}, u32[]{:S(2)}, u32[]{:S(2)}) collective-permute-start(f32[8,16,128]{2,1,0:T(8,128)S(1)} %get-tuple-element.55.refs_0_), channel_id=1, source_target_pairs={{0,2},{1,3},{2,0},{3,1},{4,6},{5,7},{6,4},{7,5},{8,10},{9,11},{10,... | collective-permute-start | bytes 196616 | tf_op jit(solution)/shard_map/ppermute | solution.py:632
  63.9 5.7 %collective-permute-start.10 = (f32[8,16,128]{2,1,0:T(8,128)S(1)}, f32[8,16,128]{2,1,0:T(8,128)S(1)}, u32[]{:S(2)}, u32[]{:S(2)}) collective-permute-start(f32[8,16,128]{2,1,0:T(8,128)S(1)} %get-tuple-element.55.refs_0_), channel_id=1, source_target_pairs={{0,1},{1,2},{2,3},{3,0},{4,5},{5,6},{6,7},{7,4},{8,9},{9,10},{10,1... | collective-permute-start | bytes 196616 | tf_op jit(solution)/shard_map/ppermute | solution.py:632
  63.9 6.4 %collective-permute-start.13 = (f32[8,16,128]{2,1,0:T(8,128)S(1)}, f32[8,16,128]{2,1,0:T(8,128)S(1)}, u32[]{:S(2)}, u32[]{:S(2)}) collective-permute-start(f32[8,16,128]{2,1,0:T(8,128)S(1)} %get-tuple-element.55.refs_0_), channel_id=1, source_target_pairs={{0,4},{4,0},{1,5},{5,1},{2,6},{6,2},{3,7},{7,3},{8,12},{12,8},{9,1... | collective-permute-start | bytes 196616 | tf_op jit(solution)/shard_map/ppermute | solution.py:619
  64.7 5.6 %collective-permute-start.16 = (f32[8,16,128]{2,1,0:T(8,128)S(1)}, f32[8,16,128]{2,1,0:T(8,128)S(1)}, u32[]{:S(2)}, u32[]{:S(2)}) collective-permute-start(f32[8,16,128]{2,1,0:T(8,128)S(1)} %collective-permute-done.12.refs_3_), channel_id=1, source_target_pairs={{0,4},{4,0},{1,5},{5,1},{2,6},{6,2},{3,7},{7,3},{8,12},{12,8},{9,1... | collective-permute-start | bytes 196616 | tf_op jit(solution)/shard_map/ppermute | solution.py:619
  67.2 3.4 %collective-permute-start.15 = (f32[8,16,128]{2,1,0:T(8,128)S(1)}, f32[8,16,128]{2,1,0:T(8,128)S(1)}, u32[]{:S(2)}, u32[]{:S(2)}) collective-permute-start(f32[8,16,128]{2,1,0:T(8,128)S(1)} %collective-permute-done.11.refs_2_), channel_id=1, source_target_pairs={{0,4},{4,0},{1,5},{5,1},{2,6},{6,2},{3,7},{7,3},{8,12},{12,8},{9,1... | collective-permute-start | bytes 196616 | tf_op jit(solution)/shard_map/ppermute | solution.py:619
  69.7 1.6 %collective-permute-start.14 = (f32[8,16,128]{2,1,0:T(8,128)S(1)}, f32[8,16,128]{2,1,0:T(8,128)S(1)}, u32[]{:S(2)}, u32[]{:S(2)}) collective-permute-start(f32[8,16,128]{2,1,0:T(8,128)S(1)} %collective-permute-done.10.refs_1_), channel_id=1, source_target_pairs={{0,4},{4,0},{1,5},{5,1},{2,6},{6,2},{3,7},{7,3},{8,12},{12,8},{9,1... | collective-permute-start | bytes 196616 | tf_op jit(solution)/shard_map/ppermute | solution.py:619
  72.0 6.3 %collective-permute-start.17 = (f32[4,5,16,128]{3,2,1,0:T(8,128)S(1)}, f32[4,5,16,128]{3,2,1,0:T(8,128)S(1)}, u32[]{:S(2)}, u32[]{:S(2)}) collective-permute-start(f32[4,5,16,128]{3,2,1,0:T(8,128)S(1)} %shard_map.51), channel_id=1, source_target_pairs={{0,8},{1,9},{2,10},{3,11},{12,4},{13,5},{14,6},{15,7},{8,16},{9,17... | collective-permute-start | bytes 491528 | tf_op jit(solution)/shard_map/ppermute | solution.py:628
  78.2 3.3 %collective-permute-start.18 = (f32[4,5,16,128]{3,2,1,0:T(8,128)S(1)}, f32[4,5,16,128]{3,2,1,0:T(8,128)S(1)}, u32[]{:S(2)}, u32[]{:S(2)}) collective-permute-start(f32[4,5,16,128]{3,2,1,0:T(8,128)S(1)} %collective-permute-done.17.refs_8_), channel_id=1, source_target_pairs={{0,4},{4,0},{1,5},{5,1},{2,6},{6,2},{3,7},{7,3},{8,12},{12,8},{9,1... | collective-permute-start | bytes 491528 | tf_op jit(solution)/shard_map/ppermute | solution.py:619
  84.2 9.4 %collective-permute-start.19 = (f32[19,16,128]{2,1,0:T(8,128)S(1)}, f32[19,16,128]{2,1,0:T(8,128)S(1)}, u32[]{:S(2)}, u32[]{:S(2)}) collective-permute-start(f32[19,16,128]{2,1,0:T(8,128)S(1)} %get-tuple-element.73), channel_id=1, source_target_pairs={{0,8},{1,9},{2,10},{3,11},{12,4},{13,5},{14,6},{15,7},{8,16},{9,17... | collective-permute-start | bytes 466952 | tf_op jit(solution)/shard_map/ppermute | solution.py:628
  89.3 4.3 %collective-permute-start.20 = (f32[8,128]{1,0:T(8,128)S(1)}, f32[8,128]{1,0:T(8,128)S(1)}, u32[]{:S(2)}, u32[]{:S(2)}) collective-permute-start(f32[8,128]{1,0:T(8,128)S(1)} %get-tuple-element.72), channel_id=1, source_target_pairs={{0,112},{8,120},{16,0},{24,8},{32,16},{40,24},{48,32},{56,40},{64,... | collective-permute-start | bytes 12296 | tf_op jit(solution)/shard_map/ppermute | solution.py:693
  93.5 1.5 %collective-permute-start.21 = (f32[19,16,128]{2,1,0:T(8,128)S(1)}, f32[19,16,128]{2,1,0:T(8,128)S(1)}, u32[]{:S(2)}, u32[]{:S(2)}) collective-permute-start(f32[19,16,128]{2,1,0:T(8,128)S(1)} %collective-permute-done.19.one), channel_id=1, source_target_pairs={{0,4},{4,0},{1,5},{5,1},{2,6},{6,2},{3,7},{7,3},{8,12},{12,8},{9,1... | collective-permute-start | bytes 466952 | tf_op jit(solution)/shard_map/ppermute | solution.py:619
  95.0 5.8 %collective-permute-start.22 = (f32[8,128]{1,0:T(8,128)S(1)}, f32[8,128]{1,0:T(8,128)S(1)}, u32[]{:S(2)}, u32[]{:S(2)}) collective-permute-start(f32[8,128]{1,0:T(8,128)S(1)} %fusion.1.sum_0), channel_id=1, source_target_pairs={{0,32},{1,33},{2,34},{3,35},{4,100},{5,101},{6,102},{7,103},{8,40}... | collective-permute-start | bytes 12296 | tf_op jit(solution)/shard_map/ppermute | solution.py:642
  100.1 4.2 %collective-permute-start.23 = (f32[8,128]{1,0:T(8,128)S(1)}, f32[8,128]{1,0:T(8,128)S(1)}, u32[]{:S(2)}, u32[]{:S(2)}) collective-permute-start(f32[8,128]{1,0:T(8,128)S(1)} %fusion.1.sum_0), channel_id=1, source_target_pairs={{0,64},{8,72},{16,80},{24,88},{32,96},{40,104},{48,112},{56,120},{... | collective-permute-start | bytes 12296 | tf_op jit(solution)/shard_map/ppermute | solution.py:642
  100.9 3.5 %collective-permute-start.24 = (f32[8,128]{1,0:T(8,128)S(1)}, f32[8,128]{1,0:T(8,128)S(1)}, u32[]{:S(2)}, u32[]{:S(2)}) collective-permute-start(f32[8,128]{1,0:T(8,128)S(1)} %collective-permute-done.22.sum_1), channel_id=1, source_target_pairs={{0,4},{4,0},{1,5},{5,1},{2,6},{6,2},{3,7},{7,3},{8,12},{12,8},{9,1... | collective-permute-start | bytes 12296 | tf_op jit(solution)/shard_map/ppermute | solution.py:619

commit v12 on v11

--- a/solution.py
+++ b/solution.py
@@ -519,19 +519,17 @@
         t = i_r[k] * (1.0 + 0.0625 * around(t_b, k, True, mask, 1))
         t_r[k] = t
         w_r[k] = t
-
-    def sweep(n, carry):
-        for k in range(1, 25):
-            t = i_b[k] * (0.0625 * around(t_r, k, False, mask, 1))
-            t_b[k] = t
-            w_b[k] = w_b[k] + t
-        for k in range(1, 25):
-            t = i_r[k] * (0.0625 * around(t_b, k, True, mask, 1))
-            t_r[k] = t
-            w_r[k] = w_r[k] + t
-        return carry
-
-    lax.fori_loop(0, 7, sweep, 0)
+    for n in range(3, 17):
+        far = (17 - n) // 2
+        for k in range(9 - far, 17 + far):
+            if n % 2:
+                t = i_b[k] * (0.0625 * around(t_r, k, False, mask, 1))
+                t_b[k] = t
+                w_b[k] = w_b[k] + t
+            else:
+                t = i_r[k] * (0.0625 * around(t_b, k, True, mask, 1))
+                t_r[k] = t
+                w_r[k] = w_r[k] + t
     for j in range(8):
         red, black = w_r[9 + j], w_b[9 + j]
         out[2 * j] = jnp.where(mask, black, red)

time: 109 us -> 109 us (level)
  waiting for transfers between devices: 21.8 us -> 23.4 us
  Pallas kernels: 24.1 us -> 23 us
    ppermute x12, starting transfers between devices: 11.8 us -> 10.7 us  [swap_cores(): return lax.ppermute(x, 'level', [(0, 1), (1, 0)])]
  transfers between devices with their start and end apart: 26 -> 26, of which waited for: 18 -> 18; matrix products, arithmetic and copies ran while one was open for 0% -> 0% of each run, Pallas kernels for 9% -> 8%
where the time goes in v12:
time: 109 us
  starting transfers between devices  37.7 us (35%)
  waiting for transfers between devices  23.4 us (21%)
  Pallas kernels  23 us (21%)
  blocking collectives  19.7 us (18%)
  local copies, waits for them, and re-layouts  4.58 us (4%)
    pallas_call x11, Pallas kernels, run(): pl.pallas_call(kernel, out_shape=shapes[0] if single else shapes, in_spec...  23 us
    all_to_all x1, blocking collectives, among(): return lax.all_to_all(x, LB, split_axis=0, concat_axis=0, tiled=True)  19.7 us
    ppermute x4, starting transfers between devices, to_slabs(): return lax.ppermute(x, ALL, pairs)  11.7 us
    ppermute x12, starting transfers between devices, swap_cores(): return lax.ppermute(x, 'level', [(0, 1), (1, 0)])  10.7 us
    ppermute x4, waiting for transfers between devices, to_slabs(): return lax.ppermute(x, ALL, pairs)  8.38 us
    ppermute x2, starting transfers between devices, fours_apart(): return (lax.ppermute(x, ALL, beside), lax.ppermute(x, 'slab', across))  5.35 us
    ppermute x12, waiting for transfers between devices, swap_cores(): return lax.ppermute(x, 'level', [(0, 1), (1, 0)])  5.15 us
    ppermute x6, starting transfers between devices, around_chips(): lax.ppermute(x, 'bottom', [(i, (i + d) % 4) for i in range(4)])  4.94 us
  transfers between devices with their start and end apart: 26, of which 18 were waited for; matrix products, arithmetic and copies ran while one was open for 0% of the time, Pallas kernels for 8%

profile of v12, /device:TPU:1, one launch (start us, length us, event | category | flops | bytes accessed | tf_op | source)
XLA Modules:
  0.0 108.7 jit_solution(16719688887135503971)
XLA Ops:
  0.0 0.8 copy.13.bricks
  0.8 0.1 pad_add_fusion.meta
  0.8 1.0 copy-done
  1.9 1.0 copy-done.2
  2.9 1.0 copy-done.4
  4.0 1.7 %shard_map.46 = (f32[8,29,8,128]{3,2,1,0:T(8,128)S(1)}, f32[9,16,128]{2,1,0:T(8,128)S(1)}) custom-call(s32[2]{0:T(128)S(1)} %pad_add_fusion.meta, s32[16,8]{1,0:T(8,128)S(1)} %copy.13.bricks, f32[1,32,32,128]{3,2,1,0:T(8,128)S(1)} %copy-done, f32[1,32,32,128]{3,2,1,0:T(8,128)S(1)} %copy-done.2, f32[1,32,32,128]{3,2,1,0:T(8,128)S(1)} %copy-done.4), custom_call_target="tpu_custom_call" | custom-call | tf_op jit(solution)/shard_map/pallas_call | solution.py:21
  5.7 19.7 %all_to_all.10.recv = f32[8,29,8,128]{3,2,1,0:T(8,128)S(1)} all-to-all(f32[8,29,8,128]{3,2,1,0:T(8,128)S(1)} %get-tuple-element.45), channel_id=1, replica_groups=mesh['slab'=16,'level'=2,'bottom'=4] {'level','bottom'}, dimensions={0} | all-to-all | bytes 1900544 | tf_op jit(solution)/shard_map/all_to_all | solution.py:644
  25.4 0.7 shard_map.47
  26.1 3.1 %collective-permute-start = (f32[4,17,8,128]{3,2,1,0:T(8,128)S(1)}, f32[4,17,8,128]{3,2,1,0:T(8,128)S(1)}, u32[]{:S(2)}, u32[]{:S(2)}) collective-permute-start(f32[4,17,8,128]{3,2,1,0:T(8,128)S(1)} %shard_map.47), channel_id=1, source_target_pairs={{8,0},{9,1},{10,2},{11,3},{4,12},{5,13},{6,14},{7,15},{16,8},{17,9... | collective-permute-start | bytes 835592 | tf_op jit(solution)/shard_map/ppermute | solution.py:626
  29.2 1.0 collective-permute-start.3
  30.3 1.5 %collective-permute-start.2 = (f32[9,16,128]{2,1,0:T(8,128)S(1)}, f32[9,16,128]{2,1,0:T(8,128)S(1)}, u32[]{:S(2)}, u32[]{:S(2)}) collective-permute-start(f32[9,16,128]{2,1,0:T(8,128)S(1)} %get-tuple-element.50.refs_0_), channel_id=1, source_target_pairs={{0,2},{1,3},{2,0},{3,1},{4,6},{5,7},{6,4},{7,5},{8,10},{9,11},{10,... | collective-permute-start | bytes 221192 | tf_op jit(solution)/shard_map/ppermute | solution.py:630
  31.7 0.0 collective-permute-start.1
  31.7 0.9 collective-permute-done.cross
  32.7 2.3 %shard_map.48 = f32[8,34,8,128]{3,2,1,0:T(8,128)} custom-call(s32[2]{0:T(128)S(1)} %pad_add_fusion.meta, s32[16,8]{1,0:T(8,128)S(1)} %copy.13.bricks, f32[8,29,8,128]{3,2,1,0:T(8,128)S(1)} %all_to_all.10.recv, f32[4,17,8,128]{3,2,1,0:T(8,128)S(1)} %collective-permute-done.cross), custom_call_target="tpu_custom_call" | custom-call | tf_op jit(solution)/shard_map/pallas_call | solution.py:21
  35.0 0.7 collective-permute-done.2.refs_2_
  35.8 1.6 %collective-permute-done.1.refs_1_ = f32[9,16,128]{2,1,0:T(8,128)S(1)} collective-permute-done((f32[9,16,128]{2,1,0:T(8,128)S(1)}, f32[9,16,128]{2,1,0:T(8,128)S(1)}, u32[]{:S(2)}, u32[]{:S(2)}) %collective-permute-start.1) | collective-permute-done | bytes 73760 | tf_op jit(solution)/shard_map/ppermute | solution.py:630
  37.4 3.9 %all-to-all-start.1 = ((f32[8,34,8,128]{3,2,1,0:T(8,128)}), f32[8,34,8,128]{3,2,1,0:T(8,128)S(1)}, u32[]{:S(2)}, u32[]{:S(2)}) async-start(f32[8,34,8,128]{3,2,1,0:T(8,128)} %shard_map.48), calls=%async_computation.1 | async-start | bytes 2228224 | tf_op jit(solution)/shard_map/all_to_all | solution.py:644
  41.3 0.2 collective-permute-start.4
  41.5 0.3 collective-permute-start.5
  41.8 0.2 collective-permute-start.6
  42.0 0.3 collective-permute-start.7
  42.3 0.2 collective-permute-done.4.refs_4_
  42.6 0.2 collective-permute-done.5.refs_5_
  42.7 0.3 collective-permute-done.6.refs_6_
  43.1 0.2 collective-permute-done.7.refs_7_
  43.2 0.7 shard_map.49
  44.0 1.3 %collective-permute-start.8 = (f32[4,7,16,128]{3,2,1,0:T(8,128)S(1)}, f32[4,7,16,128]{3,2,1,0:T(8,128)S(1)}, u32[]{:S(2)}, u32[]{:S(2)}) collective-permute-start(f32[4,7,16,128]{3,2,1,0:T(8,128)S(1)} %shard_map.49), channel_id=1, source_target_pairs={{0,8},{1,9},{2,10},{3,11},{12,4},{13,5},{14,6},{15,7},{8,16},{9,17... | collective-permute-start | bytes 688136 | tf_op jit(solution)/shard_map/ppermute | solution.py:626
  45.3 5.9 %collective-permute-done.8.refs_8_ = f32[4,7,16,128]{3,2,1,0:T(8,128)S(1)} collective-permute-done((f32[4,7,16,128]{3,2,1,0:T(8,128)S(1)}, f32[4,7,16,128]{3,2,1,0:T(8,128)S(1)}, u32[]{:S(2)}, u32[]{:S(2)}) %collective-permute-start.8) | collective-permute-done | bytes 229408 | tf_op jit(solution)/shard_map/ppermute | solution.py:626
  51.2 0.5 collective-permute-start.9
  51.7 1.1 %collective-permute-done.9.refs_9_ = f32[4,7,16,128]{3,2,1,0:T(8,128)S(1)} collective-permute-done((f32[4,7,16,128]{3,2,1,0:T(8,128)S(1)}, f32[4,7,16,128]{3,2,1,0:T(8,128)S(1)}, u32[]{:S(2)}, u32[]{:S(2)}) %collective-permute-start.9) | collective-permute-done | bytes 229408 | tf_op jit(solution)/shard_map/ppermute | solution.py:617
  52.8 0.7 copy-done.6
  53.5 3.5 %all-to-all-done.1.recv = f32[8,34,8,128]{3,2,1,0:T(8,128)S(1)} async-done(((f32[8,34,8,128]{3,2,1,0:T(8,128)}), f32[8,34,8,128]{3,2,1,0:T(8,128)S(1)}, u32[]{:S(2)}, u32[]{:S(2)}) %all-to-all-start.1) | async-done | bytes 1114144 | tf_op jit(solution)/shard_map/all_to_all | solution.py:644
  57.0 4.5 %shard_map.50 = (f32[8,16,128]{2,1,0:T(8,128)S(1)}, f32[26,40,256]{2,1,0:T(8,128)S(1)}, f32[26,40,256]{2,1,0:T(8,128)S(1)}, f32[26,40,256]{2,1,0:T(8,128)S(1)}, ...) custom-call(s32[2]{0:T(128)S(1)} %pad_add_fusion.meta, s32[16,8]{1,0:T(8,128)S(1)} %copy.13.bricks, ...), custom_call_target="tpu_custom_call" | custom-call | tf_op jit(solution)/shard_map/pallas_call | solution.py:21
  61.5 1.1 collective-permute-start.12
  62.6 1.4 %collective-permute-start.11 = (f32[8,16,128]{2,1,0:T(8,128)S(1)}, f32[8,16,128]{2,1,0:T(8,128)S(1)}, u32[]{:S(2)}, u32[]{:S(2)}) collective-permute-start(f32[8,16,128]{2,1,0:T(8,128)S(1)} %get-tuple-element.55.refs_0_), channel_id=1, source_target_pairs={{0,2},{1,3},{2,0},{3,1},{4,6},{5,7},{6,4},{7,5},{8,10},{9,11},{10,... | collective-permute-start | bytes 196616 | tf_op jit(solution)/shard_map/ppermute | solution.py:630
  63.9 0.0 collective-permute-start.10
  63.9 0.8 collective-permute-start.13
  64.7 0.0 collective-permute-done.12.refs_3_
  64.7 2.1 %collective-permute-start.16 = (f32[8,16,128]{2,1,0:T(8,128)S(1)}, f32[8,16,128]{2,1,0:T(8,128)S(1)}, u32[]{:S(2)}, u32[]{:S(2)}) collective-permute-start(f32[8,16,128]{2,1,0:T(8,128)S(1)} %collective-permute-done.12.refs_3_), channel_id=1, source_target_pairs={{0,4},{4,0},{1,5},{5,1},{2,6},{6,2},{3,7},{7,3},{8,12},{12,8},{9,1... | collective-permute-start | bytes 196616 | tf_op jit(solution)/shard_map/ppermute | solution.py:617
  66.8 0.4 collective-permute-done.11.refs_2_
  67.2 2.5 %collective-permute-start.15 = (f32[8,16,128]{2,1,0:T(8,128)S(1)}, f32[8,16,128]{2,1,0:T(8,128)S(1)}, u32[]{:S(2)}, u32[]{:S(2)}) collective-permute-start(f32[8,16,128]{2,1,0:T(8,128)S(1)} %collective-permute-done.11.refs_2_), channel_id=1, source_target_pairs={{0,4},{4,0},{1,5},{5,1},{2,6},{6,2},{3,7},{7,3},{8,12},{12,8},{9,1... | collective-permute-start | bytes 196616 | tf_op jit(solution)/shard_map/ppermute | solution.py:617
  69.7 0.7 collective-permute-start.14
  70.4 0.0 collective-permute-done.13.refs_4_
  70.4 0.0 collective-permute-done.16.refs_7_
  70.4 0.2 collective-permute-done.15.refs_6_
  70.6 0.7 collective-permute-done.14.refs_5_
  71.3 0.7 shard_map.51
  72.0 1.3 %collective-permute-start.17 = (f32[4,5,16,128]{3,2,1,0:T(8,128)S(1)}, f32[4,5,16,128]{3,2,1,0:T(8,128)S(1)}, u32[]{:S(2)}, u32[]{:S(2)}) collective-permute-start(f32[4,5,16,128]{3,2,1,0:T(8,128)S(1)} %shard_map.51), channel_id=1, source_target_pairs={{0,8},{1,9},{2,10},{3,11},{12,4},{13,5},{14,6},{15,7},{8,16},{9,17... | collective-permute-start | bytes 491528 | tf_op jit(solution)/shard_map/ppermute | solution.py:626
  73.3 1.5 %shard_map.52 = (f32[28,32,128]{2,1,0:T(8,128)S(1)}, f32[28,32,128]{2,1,0:T(8,128)S(1)}, f32[28,32,128]{2,1,0:T(8,128)S(1)}, f32[22,16,128]{2,1,0:T(8,128)S(1)}, f32[3,8,16,128]{3,2,1,0:T(8,128)S(1)}) custom-call(s32[2]{0:T(128)S(1)} %pad_add_fusion.meta, s32[16,8]{1,0:T(8,128)S(1)} %copy.13.bricks, f32[9,16,128]{2,1,0:T(8,128)S(1)} %get-tuple-element.50.refs_0_, ...), custom_call_target="tpu_custom_call" | custom-call | tf_op jit(solution)/shard_map/pallas_call | solution.py:21
  74.8 1.9 %shard_map.53.refs_10_ = f32[16,16,128]{2,1,0:T(8,128)S(1)} custom-call(s32[2]{0:T(128)S(1)} %pad_add_fusion.meta, f32[3,8,16,128]{3,2,1,0:T(8,128)S(1)} %get-tuple-element.61.coef), custom_call_target="tpu_custom_call" | custom-call | tf_op jit(solution)/shard_map/pallas_call | solution.py:21
  76.7 1.5 %collective-permute-done.17.refs_8_ = f32[4,5,16,128]{3,2,1,0:T(8,128)S(1)} collective-permute-done((f32[4,5,16,128]{3,2,1,0:T(8,128)S(1)}, f32[4,5,16,128]{3,2,1,0:T(8,128)S(1)}, u32[]{:S(2)}, u32[]{:S(2)}) %collective-permute-start.17) | collective-permute-done | bytes 163872 | tf_op jit(solution)/shard_map/ppermute | solution.py:626
  78.2 1.5 %collective-permute-start.18 = (f32[4,5,16,128]{3,2,1,0:T(8,128)S(1)}, f32[4,5,16,128]{3,2,1,0:T(8,128)S(1)}, u32[]{:S(2)}, u32[]{:S(2)}) collective-permute-start(f32[4,5,16,128]{3,2,1,0:T(8,128)S(1)} %collective-permute-done.17.refs_8_), channel_id=1, source_target_pairs={{0,4},{4,0},{1,5},{5,1},{2,6},{6,2},{3,7},{7,3},{8,12},{12,8},{9,1... | collective-permute-start | bytes 491528 | tf_op jit(solution)/shard_map/ppermute | solution.py:617
  79.7 1.0 collective-permute-done.18.refs_9_
  80.7 2.4 %shard_map.54 = (f32[22,16,128]{2,1,0:T(8,128)S(1)}, f32[19,16,128]{2,1,0:T(8,128)S(1)}, f32[8,128]{1,0:T(8,128)S(1)}, f32[28,32,128]{2,1,0:T(8,128)S(1)}, f32[2...) custom-call(s32[2]{0:T(128)S(1)} %pad_add_fusion.meta, s32[16,8]{1,0:T(8,128)S(1)} %copy.13.bricks, ...), custom_call_target="tpu_custom_call" | custom-call | tf_op jit(solution)/shard_map/pallas_call | solution.py:21
  83.1 5.9 %collective-permute-start.19 = (f32[19,16,128]{2,1,0:T(8,128)S(1)}, f32[19,16,128]{2,1,0:T(8,128)S(1)}, u32[]{:S(2)}, u32[]{:S(2)}) collective-permute-start(f32[19,16,128]{2,1,0:T(8,128)S(1)} %get-tuple-element.73), channel_id=1, source_target_pairs={{0,8},{1,9},{2,10},{3,11},{12,4},{13,5},{14,6},{15,7},{8,16},{9,17... | collective-permute-start | bytes 466952 | tf_op jit(solution)/shard_map/ppermute | solution.py:626
  89.1 1.2 %collective-permute-start.20 = (f32[8,128]{1,0:T(8,128)S(1)}, f32[8,128]{1,0:T(8,128)S(1)}, u32[]{:S(2)}, u32[]{:S(2)}) collective-permute-start(f32[8,128]{1,0:T(8,128)S(1)} %get-tuple-element.72), channel_id=1, source_target_pairs={{0,112},{8,120},{16,0},{24,8},{32,16},{40,24},{48,32},{56,40},{64,... | collective-permute-start | bytes 12296 | tf_op jit(solution)/shard_map/ppermute | solution.py:691
  90.3 2.9 %collective-permute-done.20 = f32[8,128]{1,0:T(8,128)S(1)} collective-permute-done((f32[8,128]{1,0:T(8,128)S(1)}, f32[8,128]{1,0:T(8,128)S(1)}, u32[]{:S(2)}, u32[]{:S(2)}) %collective-permute-start.20) | collective-permute-done | bytes 4128 | tf_op jit(solution)/shard_map/ppermute | solution.py:691
  93.1 0.2 collective-permute-start.21
  93.3 1.2 %collective-permute-done.21.two = f32[19,16,128]{2,1,0:T(8,128)S(1)} collective-permute-done((f32[19,16,128]{2,1,0:T(8,128)S(1)}, f32[19,16,128]{2,1,0:T(8,128)S(1)}, u32[]{:S(2)}, u32[]{:S(2)}) %collective-permute-start.21) | collective-permute-done | bytes 155680 | tf_op jit(solution)/shard_map/ppermute | solution.py:617
  94.5 5.3 %collective-permute-start.22 = (f32[8,128]{1,0:T(8,128)S(1)}, f32[8,128]{1,0:T(8,128)S(1)}, u32[]{:S(2)}, u32[]{:S(2)}) collective-permute-start(f32[8,128]{1,0:T(8,128)S(1)} %fusion.1.sum_0), channel_id=1, source_target_pairs={{0,32},{1,33},{2,34},{3,35},{4,100},{5,101},{6,102},{7,103},{8,40}... | collective-permute-start | bytes 12296 | tf_op jit(solution)/shard_map/ppermute | solution.py:640
  99.9 0.8 collective-permute-done.22.sum_1
  100.6 1.5 %collective-permute-start.24 = (f32[8,128]{1,0:T(8,128)S(1)}, f32[8,128]{1,0:T(8,128)S(1)}, u32[]{:S(2)}, u32[]{:S(2)}) collective-permute-start(f32[8,128]{1,0:T(8,128)S(1)} %collective-permute-done.22.sum_1), channel_id=1, source_target_pairs={{0,4},{4,0},{1,5},{5,1},{2,6},{6,2},{3,7},{7,3},{8,12},{12,8},{9,1... | collective-permute-start | bytes 12296 | tf_op jit(solution)/shard_map/ppermute | solution.py:617
  102.1 2.0 %shard_map.55.es = f32[22,16,128]{2,1,0:T(8,128)S(1)} custom-call(s32[2]{0:T(128)S(1)} %pad_add_fusion.meta, f32[22,16,128]{2,1,0:T(8,128)S(1)} %get-tuple-element.76.rb, f32[19,16,128]{2,1,0:T(8,128)S(1)} %collective-permute-done.19.one, f32[19,16,128]{2,1,0:T(8,128)S(1)} %collective-permute-done.21.two), custom_call_target="tpu_custom_call" | custom-call | tf_op jit(solution)/shard_map/pallas_call | solution.py:21
  104.1 4.5 %shard_map.56 = f32[1,32,32,128]{3,2,1,0:T(8,128)} custom-call(s32[2]{0:T(128)S(1)} %pad_add_fusion.meta, s32[16,8]{1,0:T(8,128)S(1)} %copy.13.bricks, f32[8,128]{1,0:T(8,128)S(1)} %fusion.1.sum_0, f32[8,128]{1,0:T(8,128)S(1)} %collective-permute-done.22.sum_1, f32[8,128]{1,0:T(8,128)S(1)} %collective-permute-done.23.sum_2, ...), custom_call_target="tpu_custom_call" | custom-call | tf_op jit(solution)/shard_map/pallas_call | solution.py:21
  (19 shorter events, 0.0 us)
Async XLA Ops:
  0.8 1.0 copy-start
  1.9 1.0 copy-start.2
  2.9 1.0 copy-start.4
  26.1 6.6 %collective-permute-start = (f32[4,17,8,128]{3,2,1,0:T(8,128)S(1)}, f32[4,17,8,128]{3,2,1,0:T(8,128)S(1)}, u32[]{:S(2)}, u32[]{:S(2)}) collective-permute-start(f32[4,17,8,128]{3,2,1,0:T(8,128)S(1)} %shard_map.47), channel_id=1, source_target_pairs={{8,0},{9,1},{10,2},{11,3},{4,12},{5,13},{6,14},{7,15},{16,8},{17,9... | collective-permute-start | bytes 835592 | tf_op jit(solution)/shard_map/ppermute | solution.py:626
  29.2 5.8 %collective-permute-start.3 = (f32[9,16,128]{2,1,0:T(8,128)S(1)}, f32[9,16,128]{2,1,0:T(8,128)S(1)}, u32[]{:S(2)}, u32[]{:S(2)}) collective-permute-start(f32[9,16,128]{2,1,0:T(8,128)S(1)} %get-tuple-element.50.refs_0_), channel_id=1, source_target_pairs={{0,3},{1,0},{2,1},{3,2},{4,7},{5,4},{6,5},{7,6},{8,11},{9,8},{10,9... | collective-permute-start | bytes 221192 | tf_op jit(solution)/shard_map/ppermute | solution.py:630
  30.3 5.5 %collective-permute-start.2 = (f32[9,16,128]{2,1,0:T(8,128)S(1)}, f32[9,16,128]{2,1,0:T(8,128)S(1)}, u32[]{:S(2)}, u32[]{:S(2)}) collective-permute-start(f32[9,16,128]{2,1,0:T(8,128)S(1)} %get-tuple-element.50.refs_0_), channel_id=1, source_target_pairs={{0,2},{1,3},{2,0},{3,1},{4,6},{5,7},{6,4},{7,5},{8,10},{9,11},{10,... | collective-permute-start | bytes 221192 | tf_op jit(solution)/shard_map/ppermute | solution.py:630
  31.7 5.7 %collective-permute-start.1 = (f32[9,16,128]{2,1,0:T(8,128)S(1)}, f32[9,16,128]{2,1,0:T(8,128)S(1)}, u32[]{:S(2)}, u32[]{:S(2)}) collective-permute-start(f32[9,16,128]{2,1,0:T(8,128)S(1)} %get-tuple-element.50.refs_0_), channel_id=1, source_target_pairs={{0,1},{1,2},{2,3},{3,0},{4,5},{5,6},{6,7},{7,4},{8,9},{9,10},{10,1... | collective-permute-start | bytes 221192 | tf_op jit(solution)/shard_map/ppermute | solution.py:630
  35.0 22.0 %copy-start.1 = (f32[1,32,32,128]{3,2,1,0:T(8,128)S(1)}, f32[1,32,32,128]{3,2,1,0:T(8,128)}, u32[]{:S(2)}) copy-start(f32[1,32,32,128]{3,2,1,0:T(8,128)} %u.3) | copy-start | bytes 1572868
  35.0 22.0 %copy-start.3 = (f32[1,32,32,128]{3,2,1,0:T(8,128)S(1)}, f32[1,32,32,128]{3,2,1,0:T(8,128)}, u32[]{:S(2)}) copy-start(f32[1,32,32,128]{3,2,1,0:T(8,128)} %f.3) | copy-start | bytes 1572868
  35.0 22.0 %copy-start.5 = (f32[1,32,32,128]{3,2,1,0:T(8,128)S(1)}, f32[1,32,32,128]{3,2,1,0:T(8,128)}, u32[]{:S(2)}) copy-start(f32[1,32,32,128]{3,2,1,0:T(8,128)} %a.3) | copy-start | bytes 1572868
  37.4 19.6 %all-to-all-start.1 = ((f32[8,34,8,128]{3,2,1,0:T(8,128)}), f32[8,34,8,128]{3,2,1,0:T(8,128)S(1)}, u32[]{:S(2)}, u32[]{:S(2)}) async-start(f32[8,34,8,128]{3,2,1,0:T(8,128)} %shard_map.48), calls=%async_computation.1 | async-start | bytes 2228224 | tf_op jit(solution)/shard_map/all_to_all | solution.py:644
  41.3 1.3 %collective-permute-start.4 = (f32[9,16,128]{2,1,0:T(8,128)S(1)}, f32[9,16,128]{2,1,0:T(8,128)S(1)}, u32[]{:S(2)}, u32[]{:S(2)}) collective-permute-start(f32[9,16,128]{2,1,0:T(8,128)S(1)} %get-tuple-element.50.refs_0_), channel_id=1, source_target_pairs={{0,4},{4,0},{1,5},{5,1},{2,6},{6,2},{3,7},{7,3},{8,12},{12,8},{9,1... | collective-permute-start | bytes 221192 | tf_op jit(solution)/shard_map/ppermute | solution.py:617
  41.5 1.3 %collective-permute-start.5 = (f32[9,16,128]{2,1,0:T(8,128)S(1)}, f32[9,16,128]{2,1,0:T(8,128)S(1)}, u32[]{:S(2)}, u32[]{:S(2)}) collective-permute-start(f32[9,16,128]{2,1,0:T(8,128)S(1)} %collective-permute-done.1.refs_1_), channel_id=1, source_target_pairs={{0,4},{4,0},{1,5},{5,1},{2,6},{6,2},{3,7},{7,3},{8,12},{12,8},{9,1... | collective-permute-start | bytes 221192 | tf_op jit(solution)/shard_map/ppermute | solution.py:617
  41.8 1.3 %collective-permute-start.6 = (f32[9,16,128]{2,1,0:T(8,128)S(1)}, f32[9,16,128]{2,1,0:T(8,128)S(1)}, u32[]{:S(2)}, u32[]{:S(2)}) collective-permute-start(f32[9,16,128]{2,1,0:T(8,128)S(1)} %collective-permute-done.2.refs_2_), channel_id=1, source_target_pairs={{0,4},{4,0},{1,5},{5,1},{2,6},{6,2},{3,7},{7,3},{8,12},{12,8},{9,1... | collective-permute-start | bytes 221192 | tf_op jit(solution)/shard_map/ppermute | solution.py:617
  42.0 1.3 %collective-permute-start.7 = (f32[9,16,128]{2,1,0:T(8,128)S(1)}, f32[9,16,128]{2,1,0:T(8,128)S(1)}, u32[]{:S(2)}, u32[]{:S(2)}) collective-permute-start(f32[9,16,128]{2,1,0:T(8,128)S(1)} %collective-permute-done.3.refs_3_), channel_id=1, source_target_pairs={{0,4},{4,0},{1,5},{5,1},{2,6},{6,2},{3,7},{7,3},{8,12},{12,8},{9,1... | collective-permute-start | bytes 221192 | tf_op jit(solution)/shard_map/ppermute | solution.py:617
  44.0 7.2 %collective-permute-start.8 = (f32[4,7,16,128]{3,2,1,0:T(8,128)S(1)}, f32[4,7,16,128]{3,2,1,0:T(8,128)S(1)}, u32[]{:S(2)}, u32[]{:S(2)}) collective-permute-start(f32[4,7,16,128]{3,2,1,0:T(8,128)S(1)} %shard_map.49), channel_id=1, source_target_pairs={{0,8},{1,9},{2,10},{3,11},{12,4},{13,5},{14,6},{15,7},{8,16},{9,17... | collective-permute-start | bytes 688136 | tf_op jit(solution)/shard_map/ppermute | solution.py:626
  51.2 1.6 %collective-permute-start.9 = (f32[4,7,16,128]{3,2,1,0:T(8,128)S(1)}, f32[4,7,16,128]{3,2,1,0:T(8,128)S(1)}, u32[]{:S(2)}, u32[]{:S(2)}) collective-permute-start(f32[4,7,16,128]{3,2,1,0:T(8,128)S(1)} %collective-permute-done.8.refs_8_), channel_id=1, source_target_pairs={{0,4},{4,0},{1,5},{5,1},{2,6},{6,2},{3,7},{7,3},{8,12},{12,8},{9,1... | collective-permute-start | bytes 688136 | tf_op jit(solution)/shard_map/ppermute | solution.py:617
  52.8 0.7 copy-start.6
  57.0 16.3 %copy-start.7 = (f32[4,7,16,128]{3,2,1,0:T(8,128)S(1)}, f32[4,7,16,128]{3,2,1,0:T(8,128)}, u32[]{:S(2)}) copy-start(f32[4,7,16,128]{3,2,1,0:T(8,128)} %copy-done.6) | copy-start | bytes 688132
  61.5 3.2 %collective-permute-start.12 = (f32[8,16,128]{2,1,0:T(8,128)S(1)}, f32[8,16,128]{2,1,0:T(8,128)S(1)}, u32[]{:S(2)}, u32[]{:S(2)}) collective-permute-start(f32[8,16,128]{2,1,0:T(8,128)S(1)} %get-tuple-element.55.refs_0_), channel_id=1, source_target_pairs={{0,3},{1,0},{2,1},{3,2},{4,7},{5,4},{6,5},{7,6},{8,11},{9,8},{10,9... | collective-permute-start | bytes 196616 | tf_op jit(solution)/shard_map/ppermute | solution.py:630
  62.6 4.6 %collective-permute-start.11 = (f32[8,16,128]{2,1,0:T(8,128)S(1)}, f32[8,16,128]{2,1,0:T(8,128)S(1)}, u32[]{:S(2)}, u32[]{:S(2)}) collective-permute-start(f32[8,16,128]{2,1,0:T(8,128)S(1)} %get-tuple-element.55.refs_0_), channel_id=1, source_target_pairs={{0,2},{1,3},{2,0},{3,1},{4,6},{5,7},{6,4},{7,5},{8,10},{9,11},{10,... | collective-permute-start | bytes 196616 | tf_op jit(solution)/shard_map/ppermute | solution.py:630
  63.9 5.7 %collective-permute-start.10 = (f32[8,16,128]{2,1,0:T(8,128)S(1)}, f32[8,16,128]{2,1,0:T(8,128)S(1)}, u32[]{:S(2)}, u32[]{:S(2)}) collective-permute-start(f32[8,16,128]{2,1,0:T(8,128)S(1)} %get-tuple-element.55.refs_0_), channel_id=1, source_target_pairs={{0,1},{1,2},{2,3},{3,0},{4,5},{5,6},{6,7},{7,4},{8,9},{9,10},{10,1... | collective-permute-start | bytes 196616 | tf_op jit(solution)/shard_map/ppermute | solution.py:630
  63.9 6.4 %collective-permute-start.13 = (f32[8,16,128]{2,1,0:T(8,128)S(1)}, f32[8,16,128]{2,1,0:T(8,128)S(1)}, u32[]{:S(2)}, u32[]{:S(2)}) collective-permute-start(f32[8,16,128]{2,1,0:T(8,128)S(1)} %get-tuple-element.55.refs_0_), channel_id=1, source_target_pairs={{0,4},{4,0},{1,5},{5,1},{2,6},{6,2},{3,7},{7,3},{8,12},{12,8},{9,1... | collective-permute-start | bytes 196616 | tf_op jit(solution)/shard_map/ppermute | solution.py:617
  64.7 5.6 %collective-permute-start.16 = (f32[8,16,128]{2,1,0:T(8,128)S(1)}, f32[8,16,128]{2,1,0:T(8,128)S(1)}, u32[]{:S(2)}, u32[]{:S(2)}) collective-permute-start(f32[8,16,128]{2,1,0:T(8,128)S(1)} %collective-permute-done.12.refs_3_), channel_id=1, source_target_pairs={{0,4},{4,0},{1,5},{5,1},{2,6},{6,2},{3,7},{7,3},{8,12},{12,8},{9,1... | collective-permute-start | bytes 196616 | tf_op jit(solution)/shard_map/ppermute | solution.py:617
  67.2 3.4 %collective-permute-start.15 = (f32[8,16,128]{2,1,0:T(8,128)S(1)}, f32[8,16,128]{2,1,0:T(8,128)S(1)}, u32[]{:S(2)}, u32[]{:S(2)}) collective-permute-start(f32[8,16,128]{2,1,0:T(8,128)S(1)} %collective-permute-done.11.refs_2_), channel_id=1, source_target_pairs={{0,4},{4,0},{1,5},{5,1},{2,6},{6,2},{3,7},{7,3},{8,12},{12,8},{9,1... | collective-permute-start | bytes 196616 | tf_op jit(solution)/shard_map/ppermute | solution.py:617
  69.7 1.6 %collective-permute-start.14 = (f32[8,16,128]{2,1,0:T(8,128)S(1)}, f32[8,16,128]{2,1,0:T(8,128)S(1)}, u32[]{:S(2)}, u32[]{:S(2)}) collective-permute-start(f32[8,16,128]{2,1,0:T(8,128)S(1)} %collective-permute-done.10.refs_1_), channel_id=1, source_target_pairs={{0,4},{4,0},{1,5},{5,1},{2,6},{6,2},{3,7},{7,3},{8,12},{12,8},{9,1... | collective-permute-start | bytes 196616 | tf_op jit(solution)/shard_map/ppermute | solution.py:617
  72.0 6.3 %collective-permute-start.17 = (f32[4,5,16,128]{3,2,1,0:T(8,128)S(1)}, f32[4,5,16,128]{3,2,1,0:T(8,128)S(1)}, u32[]{:S(2)}, u32[]{:S(2)}) collective-permute-start(f32[4,5,16,128]{3,2,1,0:T(8,128)S(1)} %shard_map.51), channel_id=1, source_target_pairs={{0,8},{1,9},{2,10},{3,11},{12,4},{13,5},{14,6},{15,7},{8,16},{9,17... | collective-permute-start | bytes 491528 | tf_op jit(solution)/shard_map/ppermute | solution.py:626
  78.2 2.5 %collective-permute-start.18 = (f32[4,5,16,128]{3,2,1,0:T(8,128)S(1)}, f32[4,5,16,128]{3,2,1,0:T(8,128)S(1)}, u32[]{:S(2)}, u32[]{:S(2)}) collective-permute-start(f32[4,5,16,128]{3,2,1,0:T(8,128)S(1)} %collective-permute-done.17.refs_8_), channel_id=1, source_target_pairs={{0,4},{4,0},{1,5},{5,1},{2,6},{6,2},{3,7},{7,3},{8,12},{12,8},{9,1... | collective-permute-start | bytes 491528 | tf_op jit(solution)/shard_map/ppermute | solution.py:617
  83.1 10.0 %collective-permute-start.19 = (f32[19,16,128]{2,1,0:T(8,128)S(1)}, f32[19,16,128]{2,1,0:T(8,128)S(1)}, u32[]{:S(2)}, u32[]{:S(2)}) collective-permute-start(f32[19,16,128]{2,1,0:T(8,128)S(1)} %get-tuple-element.73), channel_id=1, source_target_pairs={{0,8},{1,9},{2,10},{3,11},{12,4},{13,5},{14,6},{15,7},{8,16},{9,17... | collective-permute-start | bytes 466952 | tf_op jit(solution)/shard_map/ppermute | solution.py:626
  89.1 4.1 %collective-permute-start.20 = (f32[8,128]{1,0:T(8,128)S(1)}, f32[8,128]{1,0:T(8,128)S(1)}, u32[]{:S(2)}, u32[]{:S(2)}) collective-permute-start(f32[8,128]{1,0:T(8,128)S(1)} %get-tuple-element.72), channel_id=1, source_target_pairs={{0,112},{8,120},{16,0},{24,8},{32,16},{40,24},{48,32},{56,40},{64,... | collective-permute-start | bytes 12296 | tf_op jit(solution)/shard_map/ppermute | solution.py:691
  93.1 1.4 %collective-permute-start.21 = (f32[19,16,128]{2,1,0:T(8,128)S(1)}, f32[19,16,128]{2,1,0:T(8,128)S(1)}, u32[]{:S(2)}, u32[]{:S(2)}) collective-permute-start(f32[19,16,128]{2,1,0:T(8,128)S(1)} %collective-permute-done.19.one), channel_id=1, source_target_pairs={{0,4},{4,0},{1,5},{5,1},{2,6},{6,2},{3,7},{7,3},{8,12},{12,8},{9,1... | collective-permute-start | bytes 466952 | tf_op jit(solution)/shard_map/ppermute | solution.py:617
  94.5 6.1 %collective-permute-start.22 = (f32[8,128]{1,0:T(8,128)S(1)}, f32[8,128]{1,0:T(8,128)S(1)}, u32[]{:S(2)}, u32[]{:S(2)}) collective-permute-start(f32[8,128]{1,0:T(8,128)S(1)} %fusion.1.sum_0), channel_id=1, source_target_pairs={{0,32},{1,33},{2,34},{3,35},{4,100},{5,101},{6,102},{7,103},{8,40}... | collective-permute-start | bytes 12296 | tf_op jit(solution)/shard_map/ppermute | solution.py:640
  99.9 4.2 %collective-permute-start.23 = (f32[8,128]{1,0:T(8,128)S(1)}, f32[8,128]{1,0:T(8,128)S(1)}, u32[]{:S(2)}, u32[]{:S(2)}) collective-permute-start(f32[8,128]{1,0:T(8,128)S(1)} %fusion.1.sum_0), channel_id=1, source_target_pairs={{0,64},{8,72},{16,80},{24,88},{32,96},{40,104},{48,112},{56,120},{... | collective-permute-start | bytes 12296 | tf_op jit(solution)/shard_map/ppermute | solution.py:640
  100.6 3.5 %collective-permute-start.24 = (f32[8,128]{1,0:T(8,128)S(1)}, f32[8,128]{1,0:T(8,128)S(1)}, u32[]{:S(2)}, u32[]{:S(2)}) collective-permute-start(f32[8,128]{1,0:T(8,128)S(1)} %collective-permute-done.22.sum_1), channel_id=1, source_target_pairs={{0,4},{4,0},{1,5},{5,1},{2,6},{6,2},{3,7},{7,3},{8,12},{12,8},{9,1... | collective-permute-start | bytes 12296 | tf_op jit(solution)/shard_map/ppermute | solution.py:617
